TPU v7x, 32 devices: a whole 2x2x4 slice. The times are simulated.
32 devices in a mesh: seq: 8 (over y, x, core), tp: 4 (over z).
Axes of the slice: x: 2, y: 2, z: 4, core: 2. Of those that a mesh axis runs over, the one named last changes fastest.
Arguments:
- tokens: bfloat16 [2, 16384, 768], P(None, ('seq', 'tp')), may hold values from -6 to 6
- doc_lengths: int32 [2, 18], replicated, may hold values from 8 to 64, as said below
- rand_blocks: int32 [2, 256, 12, 3], P(None, 'seq', 'tp'), may hold values from 0 to 255, as said below
- query_weight: bfloat16 [768, 768], P(None, 'tp'), may hold values from -0.21875 to 0.21875
- key_weight: bfloat16 [768, 768], P(None, 'tp'), may hold values from -0.21875 to 0.21875
- value_weight: bfloat16 [768, 768], P(None, 'tp'), may hold values from -0.21875 to 0.21875
- query_bias: bfloat16 [768], P('tp'), may hold values from -3 to 3
- value_bias: bfloat16 [768], P('tp'), may hold values from -0.59765625 to 0.59765625
- proj_weight: bfloat16 [768, 768], P('tp'), may hold values from -1.75 to 1.75
- proj_bias: bfloat16 [768], replicated, may hold values from -2 to 2
- first_gain: bfloat16 [768], replicated, may hold values from 0.5 to 1.5
- first_bias: bfloat16 [768], replicated, may hold values from -1.1953125 to 1.1953125
- second_gain: bfloat16 [768], replicated, may hold values from 0.5 to 1.5
- second_bias: bfloat16 [768], replicated, may hold values from -1.1953125 to 1.1953125
- inner_weight: bfloat16 [768, 3072], P(None, 'tp'), may hold values from -0.21875 to 0.21875
- inner_bias: bfloat16 [3072], P('tp'), may hold values from -3 to 3
- outer_weight: bfloat16 [3072, 768], P('tp'), may hold values from -0.109375 to 0.109375
- outer_bias: bfloat16 [768], replicated, may hold values from -2 to 2
- out_grad: bfloat16 [2, 16384, 768], P(None, ('seq', 'tp')), may hold values from -6 to 6
Outputs:
- output: bfloat16 [2, 16384, 768], P(None, ('seq', 'tp'))
- input_grad: float32 [2, 16384, 768], P(None, ('seq', 'tp'))
- query_weight_grad: float32 [768, 768], P(None, 'tp')
- key_weight_grad: float32 [768, 768], P(None, 'tp')
- value_weight_grad: float32 [768, 768], P(None, 'tp')
- query_bias_grad: float32 [768], P('tp')
- value_bias_grad: float32 [768], P('tp')
- proj_weight_grad: float32 [768, 768], P('tp')
- proj_bias_grad: float32 [768], replicated
- first_gain_grad: float32 [768], replicated
- first_bias_grad: float32 [768], replicated
- second_gain_grad: float32 [768], replicated
- second_bias_grad: float32 [768], replicated
- inner_weight_grad: float32 [768, 3072], P(None, 'tp')
- inner_bias_grad: float32 [3072], P('tp')
- outer_weight_grad: float32 [3072, 768], P('tp')
- outer_bias_grad: float32 [768], replicated
Inputs may be any that keep to these rules, and one draw needn't show every extreme that they name: `doc_lengths`: each row holds exactly 2 entries 64 and 16 entries 8, in an order drawn from the seed; they sum to 256. `rand_blocks`: every entry is a block of the same window as its query block (the block of the second index), by doc_lengths of the same micro-batch.
All inputs are finite; a program needn't handle non-finite values.
Results may differ from a plain program's by a relative error of at most 0.017.
Values may be sent and summed in bfloat16 or wider, within the bound.
A program may use at most 320 MiB of HBM per device.

v0:
```python
import math

import jax
import jax.numpy as jnp
from jax import lax
from jax.sharding import PartitionSpec as P

BLOCK = 64
LONG_BLK = 64


NORM_EPS = 1e-05
MASKED = -1000000000.0


def from_behind(block, axis, distance):
    devices = range(lax.axis_size(axis))
    route = [(i - distance, i) for i in devices if i - distance in devices]
    return lax.ppermute(block, axis, route)


def gelu_exact(values):
    return 0.5 * values * (1.0 + lax.erf(values / math.sqrt(2.0)))


def gelu_grad(values, grad_rows):
    _, pull_back = jax.vjp(gelu_exact, values)
    return pull_back(grad_rows)[0]


def layer_stats(values, norm_gain, norm_shift):
    row_mean = jnp.mean(values, axis=-1, keepdims=True)
    centred = values - row_mean
    inverse = lax.rsqrt(jnp.mean(centred * centred, axis=-1, keepdims=True) + NORM_EPS)
    normed = centred * inverse
    return (normed * norm_gain + norm_shift, normed, inverse)


def layer_back(grad_rows, normed, inverse, norm_gain):
    scaled = grad_rows * norm_gain
    inner_term = (
        scaled
        - jnp.mean(scaled, axis=-1, keepdims=True)
        - normed * jnp.mean(scaled * normed, axis=-1, keepdims=True)
    )
    return (inverse * inner_term, jnp.sum(grad_rows * normed, axis=0), jnp.sum(grad_rows, axis=0))


def block_keys(lengths, randoms, blocks, top_block):
    doc_ends = jnp.cumsum(lengths)
    doc_starts = doc_ends - lengths
    doc_owner = jnp.sum((blocks[:, None] >= doc_ends[None, :]).astype(jnp.int32), axis=1)
    doc_ids = jnp.arange(lengths.shape[0], dtype=jnp.int32)
    doc_hit = doc_owner[:, None] == doc_ids[None, :]
    doc_first = jnp.sum(jnp.where(doc_hit, doc_starts[None, :], 0), axis=1)
    doc_final = jnp.sum(jnp.where(doc_hit, doc_ends[None, :], 0), axis=1)
    fixed_keys = jnp.stack(
        [
            jnp.maximum(blocks - 1, 0),
            blocks,
            jnp.minimum(blocks + 1, top_block),
            doc_first,
            doc_first + 1,
        ],
        axis=1,
    )
    block_count = randoms.shape[0]
    head_count = randoms.shape[1]
    key_index = jnp.concatenate(
        [jnp.broadcast_to(fixed_keys[:, None, :], (block_count, head_count, 5)), randoms], axis=2
    )
    always_on = blocks >= 0
    key_valid = jnp.stack(
        [
            blocks > doc_first,
            always_on,
            blocks + 1 < doc_final,
            always_on,
            always_on,
            always_on,
            always_on,
            always_on,
        ],
        axis=1,
    )
    return (key_index, key_valid)


def gather_scores(query_part, index_part, valid_part, keys_all, values_all, head_ids):
    group_size = index_part.shape[0]
    local_heads = index_part.shape[1]
    keys_part = keys_all[head_ids, index_part].reshape(
        group_size, local_heads, -1, keys_all.shape[-1]
    )
    values_part = values_all[head_ids, index_part].reshape(
        group_size, local_heads, -1, values_all.shape[-1]
    )
    scores = jnp.einsum(
        "ghqd,ghkd->ghqk", query_part, keys_part, preferred_element_type=jnp.float32
    )
    key_mask = jnp.repeat(valid_part, keys_all.shape[2], axis=1)[:, None, None, :]
    return (keys_part, values_part, jnp.where(key_mask, scores, MASKED))


def body(
    tokens,
    doc_lengths,
    rand_blocks,
    query_weight,
    key_weight,
    value_weight,
    query_bias,
    value_bias,
    proj_weight,
    proj_bias,
    first_gain,
    first_bias,
    second_gain,
    second_bias,
    inner_weight,
    inner_bias,
    outer_weight,
    outer_bias,
    out_grad,
):
    micro_count, local_rows, model_width = tokens.shape
    seq_count = lax.axis_size("seq")
    block_dev = rand_blocks.shape[1]
    local_heads = rand_blocks.shape[2]
    local_width = query_weight.shape[1]
    head_size = local_width // local_heads
    group_rows = block_dev * BLOCK
    reach_dev = (block_dev + LONG_BLK - 2) // block_dev
    window = 2 * reach_dev + 1
    per_step = math.gcd(block_dev, max(1, 512 // BLOCK))
    step_count = block_dev // per_step
    score_scale = 1.0 / math.sqrt(head_size)
    seq_place = lax.axis_index("seq")
    lowest = (seq_place - reach_dev) * block_dev
    blocks = seq_place * block_dev + jnp.arange(block_dev, dtype=jnp.int32)
    top_block = block_dev * seq_count - 1
    head_ids = jnp.arange(local_heads, dtype=jnp.int32)[None, :, None]
    f32 = jnp.float32
    bf16 = jnp.bfloat16
    acc_inner = jnp.zeros(inner_weight.shape, f32)
    acc_inner_bias = jnp.zeros(inner_bias.shape, f32)
    acc_outer = jnp.zeros(outer_weight.shape, f32)
    acc_proj = jnp.zeros(proj_weight.shape, f32)
    acc_query = jnp.zeros(query_weight.shape, f32)
    acc_key = jnp.zeros(key_weight.shape, f32)
    acc_value = jnp.zeros(value_weight.shape, f32)
    acc_query_bias = jnp.zeros((local_width,), f32)
    acc_value_bias = jnp.zeros((local_width,), f32)
    acc_first_gain = jnp.zeros((model_width,), f32)
    acc_first_bias = jnp.zeros((model_width,), f32)
    acc_second_gain = jnp.zeros((model_width,), f32)
    acc_second_bias = jnp.zeros((model_width,), f32)
    acc_proj_bias = jnp.zeros((model_width,), f32)
    acc_outer_bias = jnp.zeros((model_width,), f32)
    outputs = []
    input_grads = []
    for micro_index in range(micro_count):
        inputs = tokens[micro_index].astype(f32)
        key_index, key_valid = block_keys(
            doc_lengths[micro_index], rand_blocks[micro_index], blocks, top_block
        )
        slot_index = jnp.clip(key_index - lowest, 0, window * block_dev - 1)
        key_slots = key_index.shape[2]
        shifted_one, stats_one, inverse_one = layer_stats(inputs, first_gain, first_bias)
        low_one = shifted_one.astype(bf16)
        gathered_one = lax.all_gather(low_one, "tp", axis=0, tiled=True)
        queries = (
            (jnp.dot(gathered_one, query_weight, preferred_element_type=f32) + query_bias)
            * score_scale
        ).astype(bf16)
        keys_now = jnp.dot(gathered_one, key_weight, preferred_element_type=f32).astype(bf16)
        values_now = (
            jnp.dot(gathered_one, value_weight, preferred_element_type=f32) + value_bias
        ).astype(bf16)
        pair_rows = jnp.stack([keys_now, values_now])
        pieces = []
        for offset in range(-reach_dev, reach_dev + 1):
            if offset == 0:
                pieces.append(pair_rows)
            else:
                pieces.append(from_behind(pair_rows, "seq", -offset))
        spread = jnp.concatenate(pieces, axis=1)
        keys_all = (
            spread[0]
            .reshape(window * block_dev, BLOCK, local_heads, head_size)
            .transpose(2, 0, 1, 3)
        )
        values_all = (
            spread[1]
            .reshape(window * block_dev, BLOCK, local_heads, head_size)
            .transpose(2, 0, 1, 3)
        )
        query_blocks = (
            queries.reshape(block_dev, BLOCK, local_heads, head_size)
            .transpose(0, 2, 1, 3)
            .reshape(step_count, per_step, local_heads, BLOCK, head_size)
        )
        index_steps = slot_index.reshape(step_count, per_step, local_heads, key_slots)
        valid_steps = key_valid.reshape(step_count, per_step, key_slots)

        def forward_step(operands):
            query_part, index_part, valid_part = operands
            keys_part, values_part, scores = gather_scores(
                query_part, index_part, valid_part, keys_all, values_all, head_ids
            )
            row_top = jnp.max(scores, axis=-1, keepdims=True)
            raised = jnp.exp(scores - row_top)
            row_total = jnp.sum(raised, axis=-1, keepdims=True)
            weights = raised / row_total
            context_part = jnp.einsum(
                "ghqk,ghkd->ghqd", weights.astype(bf16), values_part, preferred_element_type=f32
            ).astype(bf16)
            return (context_part, row_top + jnp.log(row_total))

        context_steps, logsum_steps = lax.map(
            forward_step, (query_blocks, index_steps, valid_steps)
        )
        context = (
            context_steps.reshape(block_dev, local_heads, BLOCK, head_size)
            .transpose(0, 2, 1, 3)
            .reshape(group_rows, local_width)
        )
        attended = lax.psum_scatter(
            jnp.dot(context, proj_weight, preferred_element_type=f32),
            "tp",
            scatter_dimension=0,
            tiled=True,
        )
        hidden = inputs + attended + proj_bias
        shifted_two, stats_two, inverse_two = layer_stats(hidden, second_gain, second_bias)
        low_two = shifted_two.astype(bf16)
        gathered_two = lax.all_gather(low_two, "tp", axis=0, tiled=True)
        before = jnp.dot(gathered_two, inner_weight, preferred_element_type=f32) + inner_bias
        active = gelu_exact(before).astype(bf16)
        mixed_rows = lax.psum_scatter(
            jnp.dot(active, outer_weight, preferred_element_type=f32).astype(jnp.bfloat16),
            "tp",
            scatter_dimension=0,
            tiled=True,
        ).astype(jnp.float32)
        result = hidden + mixed_rows + outer_bias
        outputs.append(result.astype(bf16))
        grad_out = out_grad[micro_index]
        grad_float = grad_out.astype(f32)
        acc_outer_bias = acc_outer_bias + jnp.sum(grad_float, axis=0)
        shard_rows = lax.all_gather(grad_out, "tp", axis=0, tiled=True)
        outer_store = acc_outer
        grad_store = jnp.dot(shard_rows, outer_weight.T, preferred_element_type=f32)
        acc_outer = outer_store + jnp.dot(active.T, shard_rows, preferred_element_type=f32)
        grad_before = gelu_grad(before, grad_store).astype(bf16)
        acc_inner = acc_inner + jnp.dot(gathered_two.T, grad_before, preferred_element_type=f32)
        acc_inner_bias = acc_inner_bias + jnp.sum(grad_before.astype(f32), axis=0)
        grad_two = lax.psum_scatter(
            jnp.dot(grad_before, inner_weight.T, preferred_element_type=f32).astype(jnp.bfloat16),
            "tp",
            scatter_dimension=0,
            tiled=True,
        ).astype(jnp.float32)
        back_two, gain_two, shift_two = layer_back(grad_two, stats_two, inverse_two, second_gain)
        acc_second_gain = acc_second_gain + gain_two
        acc_second_bias = acc_second_bias + shift_two
        grad_hidden = grad_float + back_two
        grad_branch = grad_hidden.astype(bf16)
        acc_proj_bias = acc_proj_bias + jnp.sum(grad_branch.astype(f32), axis=0)
        proj_shard_rows = lax.all_gather(grad_branch, "tp", axis=0, tiled=True)
        proj_store = acc_proj
        proj_grad_store = jnp.dot(proj_shard_rows, proj_weight.T, preferred_element_type=f32)
        grad_context = proj_grad_store
        acc_proj = proj_store + jnp.dot(context.T, proj_shard_rows, preferred_element_type=f32)
        grad_context = grad_context.astype(bf16)
        grad_steps = (
            grad_context.reshape(block_dev, BLOCK, local_heads, head_size)
            .transpose(0, 2, 1, 3)
            .reshape(step_count, per_step, local_heads, BLOCK, head_size)
        )

        def backward_step(running, operands):
            keys_store, values_store = running
            query_part, index_part, valid_part, logsum_part, grad_part = operands
            keys_part, values_part, scores = gather_scores(
                query_part, index_part, valid_part, keys_all, values_all, head_ids
            )
            weights = jnp.exp(scores - logsum_part)
            low_weights = weights.astype(bf16)
            grad_weights = jnp.einsum(
                "ghqd,ghkd->ghqk", grad_part, values_part, preferred_element_type=f32
            )
            row_delta = jnp.sum(grad_weights * weights, axis=-1, keepdims=True)
            grad_scores = (weights * (grad_weights - row_delta)).astype(bf16)
            grad_query = jnp.einsum(
                "ghqk,ghkd->ghqd", grad_scores, keys_part, preferred_element_type=f32
            )
            grad_keys = jnp.einsum(
                "ghqk,ghqd->ghkd", grad_scores, query_part, preferred_element_type=f32
            )
            grad_values = jnp.einsum(
                "ghqk,ghqd->ghkd", low_weights, grad_part, preferred_element_type=f32
            )
            shaped = index_part.shape + (BLOCK, head_size)
            keys_store = keys_store.at[head_ids, index_part].add(grad_keys.reshape(shaped))
            values_store = values_store.at[head_ids, index_part].add(grad_values.reshape(shaped))
            return ((keys_store, values_store), grad_query)

        zero_window = jnp.zeros((local_heads, window * block_dev, BLOCK, head_size), f32)
        (keys_store, values_store), query_steps = lax.scan(
            backward_step,
            (zero_window, zero_window),
            (query_blocks, index_steps, valid_steps, logsum_steps, grad_steps),
        )
        grad_pair = (
            jnp.stack([keys_store, values_store])
            .transpose(0, 2, 3, 1, 4)
            .reshape(2, window * group_rows, local_width)
        )
        returned = grad_pair[:, reach_dev * group_rows : (reach_dev + 1) * group_rows]
        for offset in range(-reach_dev, reach_dev + 1):
            if offset != 0:
                shard_part = grad_pair[
                    :, (offset + reach_dev) * group_rows : (offset + reach_dev + 1) * group_rows
                ]
                returned = returned + from_behind(
                    shard_part.astype(jnp.bfloat16), "seq", offset
                ).astype(shard_part.dtype)
        grad_key_rows = returned[0].astype(bf16)
        grad_value_rows = returned[1].astype(bf16)
        grad_query_rows = (
            query_steps.reshape(block_dev, local_heads, BLOCK, head_size)
            .transpose(0, 2, 1, 3)
            .reshape(group_rows, local_width)
            .astype(bf16)
        )
        acc_query = (
            acc_query
            + jnp.dot(gathered_one.T, grad_query_rows, preferred_element_type=f32) * score_scale
        )
        acc_query_bias = acc_query_bias + jnp.sum(grad_query_rows.astype(f32), axis=0) * score_scale
        acc_key = acc_key + jnp.dot(gathered_one.T, grad_key_rows, preferred_element_type=f32)
        acc_value = acc_value + jnp.dot(gathered_one.T, grad_value_rows, preferred_element_type=f32)
        acc_value_bias = acc_value_bias + jnp.sum(grad_value_rows.astype(f32), axis=0)
        total_rows = (
            jnp.dot(grad_query_rows, query_weight.T, preferred_element_type=f32) * score_scale
        )
        total_rows = total_rows + jnp.dot(grad_key_rows, key_weight.T, preferred_element_type=f32)
        grad_one = lax.psum_scatter(
            (
                total_rows + jnp.dot(grad_value_rows, value_weight.T, preferred_element_type=f32)
            ).astype(jnp.bfloat16),
            "tp",
            scatter_dimension=0,
            tiled=True,
        ).astype(jnp.float32)
        back_one, gain_one, shift_one = layer_back(grad_one, stats_one, inverse_one, first_gain)
        acc_first_gain = acc_first_gain + gain_one
        acc_first_bias = acc_first_bias + shift_one
        input_grads.append(grad_hidden + back_one)
    summed = lax.psum(
        (
            acc_query,
            acc_key,
            acc_value,
            acc_proj,
            acc_inner,
            acc_outer,
            acc_query_bias,
            acc_value_bias,
            acc_inner_bias,
        ),
        "seq",
    )
    norm_sums = lax.psum(
        (
            acc_first_gain,
            acc_first_bias,
            acc_second_gain,
            acc_second_bias,
            acc_proj_bias,
            acc_outer_bias,
        ),
        ("seq", "tp"),
    )
    return (
        jnp.stack(outputs),
        jnp.stack(input_grads),
        summed[0],
        summed[1],
        summed[2],
        summed[6],
        summed[7],
        summed[3],
        norm_sums[4],
        norm_sums[0],
        norm_sums[1],
        norm_sums[2],
        norm_sums[3],
        summed[4],
        summed[8],
        summed[5],
        norm_sums[5],
    )


def solution(mesh):
    return jax.shard_map(
        body,
        mesh=mesh,
        in_specs=(
            P(None, ("seq", "tp"), None),
            P(),
            P(None, "seq", "tp", None),
            P(None, "tp"),
            P(None, "tp"),
            P(None, "tp"),
            P("tp"),
            P("tp"),
            P("tp", None),
            P(),
            P(),
            P(),
            P(),
            P(),
            P(None, "tp"),
            P("tp"),
            P("tp", None),
            P(),
            P(None, ("seq", "tp"), None),
        ),
        out_specs=(
            P(None, ("seq", "tp"), None),
            P(None, ("seq", "tp"), None),
            P(None, "tp"),
            P(None, "tp"),
            P(None, "tp"),
            P("tp"),
            P("tp"),
            P("tp", None),
            P(),
            P(),
            P(),
            P(),
            P(),
            P(None, "tp"),
            P("tp"),
            P("tp", None),
            P(),
        ),
        check_vma=False,
    )
```

profile of v0, /device:TPU:13, one launch (start us, length us, event | category | flops | bytes accessed | tf_op | source)
XLA Modules:
  0.0 2626.9 jit_solution(4489959617192319292)
XLA Ops:
  17.0 59.8 %all-gather.15.cloned.1.call-done = bf16[2048,768]{1,0:T(8,128)(2,1)} async-done(((bf16[512,768]{1,0:T(8,128)(2,1)}), bf16[2048,768]{1,0:T(8,128)(2,1)}) %all-gather.15.cloned.1.call-update) | async-done | bytes 3145744 | tf_op jit(solution)/shard_map/all_gather | solution.py:171
  106.7 34.4 %all-gather.11.cloned.1.call-done = bf16[2048,768]{1,0:T(8,128)(2,1)} async-done(((bf16[512,768]{1,0:T(8,128)(2,1)}), bf16[2048,768]{1,0:T(8,128)(2,1)}) %all-gather.11.cloned.1.call-update) | async-done | bytes 3145744 | tf_op jit(solution)/shard_map/all_gather | solution.py:171
  237.7 102.0 %while.57 = (s32[]{:T(128)}, bf16[4,8,3,64,64]{4,3,2,1,0:T(8,128)(2,1)}, f32[4,8,3,64,1]{3,2,1,4,0:T(4,128)S(1)}, pred[4,8,8]{2,1,0:T(8,128)(4,1)S(1)}, bf16[4,8...) while((s32[]{:T(128)}, ...), condition=%wide.region_23.24_spmd.clone, body=%wide.region_20.23_spmd.clone.sunk | while | flops 208502400 | bytes 33927532 | solution.py:220
  417.4 102.4 %while.56 = (s32[]{:T(128)}, bf16[4,8,3,64,64]{4,3,2,1,0:T(8,128)(2,1)}, f32[4,8,3,64,1]{3,2,1,4,0:T(4,128)S(1)}, pred[4,8,8]{2,1,0:T(8,128)(4,1)S(1)}, bf16[4,8...) while((s32[]{:T(128)}, ...), condition=%wide.region_9.10_spmd.clone, body=%wide.region_6.9_spmd.clone.sunk | while | flops 208502400 | bytes 33927532 | solution.py:220
  531.9 118.3 %reduce-scatter.9.cloned.1.call-done = f32[512,768]{1,0:T(8,128)} async-done(((f32[2048,768]{1,0:T(8,128)}), f32[512,768]{1,0:T(8,128)}) %reduce-scatter.9.cloned.1.call-update) | async-done | bytes 1572880 | tf_op jit(solution)/shard_map/reduce_scatter | solution.py:228
  658.5 58.3 %all-gather.17.cloned.1.call-done = bf16[2048,768]{1,0:T(8,128)(2,1)} async-done(((bf16[512,768]{1,0:T(8,128)(2,1)}), bf16[2048,768]{1,0:T(8,128)(2,1)}) %all-gather.17.cloned.1.call-update) | async-done | bytes 3145744 | tf_op jit(solution)/shard_map/all_gather | solution.py:237
  723.9 57.1 %all-gather.25.cloned.1.call-done = bf16[1,2048,768]{2,1,0:T(8,128)(2,1)} async-done(((bf16[1,512,768]{2,1,0:T(8,128)(2,1)}), bf16[1,2048,768]{2,1,0:T(8,128)(2,1)}) %all-gather.25.cloned.1.call-update) | async-done | bytes 3145744 | tf_op jit(solution)/shard_map/all_gather | solution.py:251
  795.1 49.6 %all-gather.13.cloned.1.call-done = bf16[2048,768]{1,0:T(8,128)(2,1)} async-done(((bf16[512,768]{1,0:T(8,128)(2,1)}), bf16[2048,768]{1,0:T(8,128)(2,1)}) %all-gather.13.cloned.1.call-update) | async-done | bytes 3145744 | tf_op jit(solution)/shard_map/all_gather | solution.py:237
  855.6 52.9 %all-gather.23.cloned.1.call-done = bf16[1,2048,768]{2,1,0:T(8,128)(2,1)} async-done(((bf16[1,512,768]{2,1,0:T(8,128)(2,1)}), bf16[1,2048,768]{2,1,0:T(8,128)(2,1)}) %all-gather.23.cloned.1.call-update) | async-done | bytes 3145744 | tf_op jit(solution)/shard_map/all_gather | solution.py:251
  936.4 35.2 %reduce-scatter.21.cloned.1.call-done = bf16[512,768]{1,0:T(8,128)(2,1)} async-done(((bf16[2048,768]{1,0:T(8,128)(2,1)}), bf16[512,768]{1,0:T(8,128)(2,1)}) %reduce-scatter.21.cloned.1.call-update) | async-done | bytes 786448 | tf_op jit(solution)/shard_map/reduce_scatter | solution.py:258
  971.6 62.5 %reduce-scatter.17.cloned.1.call-done = bf16[512,768]{1,0:T(8,128)(2,1)} async-done(((bf16[2048,768]{1,0:T(8,128)(2,1)}), bf16[512,768]{1,0:T(8,128)(2,1)}) %reduce-scatter.17.cloned.1.call-update) | async-done | bytes 786448 | tf_op jit(solution)/shard_map/reduce_scatter | solution.py:258
  1037.4 59.3 %reduce-scatter.15.cloned.1.call-done = bf16[512,768]{1,0:T(8,128)(2,1)} async-done(((bf16[2048,768]{1,0:T(8,128)(2,1)}), bf16[512,768]{1,0:T(8,128)(2,1)}) %reduce-scatter.15.cloned.1.call-update) | async-done | bytes 786448 | tf_op jit(solution)/shard_map/reduce_scatter | solution.py:240
  1096.7 62.5 %reduce-scatter.11.cloned.1.call-done = bf16[512,768]{1,0:T(8,128)(2,1)} async-done(((bf16[2048,768]{1,0:T(8,128)(2,1)}), bf16[512,768]{1,0:T(8,128)(2,1)}) %reduce-scatter.11.cloned.1.call-update) | async-done | bytes 786448 | tf_op jit(solution)/shard_map/reduce_scatter | solution.py:240
  1165.6 61.1 %all-gather.19.cloned.1.call-done = bf16[2048,768]{1,0:T(8,128)(2,1)} async-done(((bf16[512,768]{1,0:T(8,128)(2,1)}), bf16[2048,768]{1,0:T(8,128)(2,1)}) %all-gather.19.cloned.1.call-update) | async-done | bytes 3145744 | tf_op jit(solution)/shard_map/all_gather | solution.py:270
  1250.4 369.6 %while.58 = (s32[]{:T(128)}, f32[3,160,64,64]{3,2,1,0:T(8,128)}, f32[3,160,64,64]{3,2,1,0:T(8,128)}, bf16[4,8,3,64,64]{4,3,2,1,0:T(8,128)(2,1)}, s32[4,8,3,8]{3,...) while((s32[]{:T(128)}, f32[3,160,64,64]{3,2,1,0:T(8,128)}, ...), condition=%wide.region_35.36_spmd.clone, body=%wide.region_31.35_spmd.clone.sunk | while | flops 514326720 | bytes 81102576 | solution.py:310
  1372.0 31.7 %scatter_fusion = f32[3,160,64,64]{3,2,1,0:T(8,128)} fusion(f32[3,160,64,64]{3,2,1,0:T(8,128)} %get-tuple-element.1041, s32[192]{0:T(256)S(1)} %reshape.844, f32[192,64,64]{2,1,0:T(8,128)} %bitcast.524), kind=kCustom, calls=%fused_computation.8.clone.clone.1 | custom fusion | flops 786432 | bytes 9438720 | tf_op jit(solution)/shard_map/while/body/eval_jaxpr/scatter-add | solution.py:305
  1403.7 31.6 %scatter_fusion.1 = f32[3,160,64,64]{3,2,1,0:T(8,128)} fusion(f32[3,160,64,64]{3,2,1,0:T(8,128)} %get-tuple-element.1042, s32[192]{0:T(256)S(1)} %reshape.844, f32[192,64,64]{2,1,0:T(8,128)} %bitcast.522), kind=kCustom, calls=%fused_computation.9.clone.clone.1 | custom fusion | flops 786432 | bytes 9438720 | tf_op jit(solution)/shard_map/while/body/eval_jaxpr/scatter-add | solution.py:306
  1464.4 31.7 %scatter_fusion = f32[3,160,64,64]{3,2,1,0:T(8,128)} fusion(f32[3,160,64,64]{3,2,1,0:T(8,128)} %get-tuple-element.1041, s32[192]{0:T(256)S(1)} %reshape.844, f32[192,64,64]{2,1,0:T(8,128)} %bitcast.524), kind=kCustom, calls=%fused_computation.8.clone.clone.1 | custom fusion | flops 786432 | bytes 9438720 | tf_op jit(solution)/shard_map/while/body/eval_jaxpr/scatter-add | solution.py:305
  1496.0 31.6 %scatter_fusion.1 = f32[3,160,64,64]{3,2,1,0:T(8,128)} fusion(f32[3,160,64,64]{3,2,1,0:T(8,128)} %get-tuple-element.1042, s32[192]{0:T(256)S(1)} %reshape.844, f32[192,64,64]{2,1,0:T(8,128)} %bitcast.522), kind=kCustom, calls=%fused_computation.9.clone.clone.1 | custom fusion | flops 786432 | bytes 9438720 | tf_op jit(solution)/shard_map/while/body/eval_jaxpr/scatter-add | solution.py:306
  1588.3 31.6 %scatter_fusion.1 = f32[3,160,64,64]{3,2,1,0:T(8,128)} fusion(f32[3,160,64,64]{3,2,1,0:T(8,128)} %get-tuple-element.1042, s32[192]{0:T(256)S(1)} %reshape.844, f32[192,64,64]{2,1,0:T(8,128)} %bitcast.522), kind=kCustom, calls=%fused_computation.9.clone.clone.1 | custom fusion | flops 786432 | bytes 9438720 | tf_op jit(solution)/shard_map/while/body/eval_jaxpr/scatter-add | solution.py:306
  1643.6 32.4 %copy.262 = f32[2,160,64,3,64]{2,1,4,3,0:T(8,128)} copy(f32[2,160,64,3,64]{4,2,1,3,0:T(8,128)} %maximum_bitcast_fusion) | data formatting | bytes 31457280 | tf_op jit(solution)/shard_map/transpose | solution.py:317
  1753.9 33.2 %collective-permute-done.11 = bf16[2,2048,192]{1,2,0:T(8,128)(2,1)} collective-permute-done((bf16[2,2048,192]{1,2,0:T(8,128)(2,1)}, bf16[2,2048,192]{1,2,0:T(8,128)(2,1)}, u32[]{:S(2)}, u32[]{:S(2)}) %collective-permute-start.11) | collective-permute-done | bytes 1572896 | tf_op jit(solution)/shard_map/ppermute | solution.py:19
  1844.3 372.1 %while.59 = (s32[]{:T(128)}, f32[3,160,64,64]{3,2,1,0:T(8,128)}, f32[3,160,64,64]{3,2,1,0:T(8,128)}, bf16[4,8,3,64,64]{4,3,2,1,0:T(8,128)(2,1)}, s32[4,8,3,8]{3,...) while((s32[]{:T(128)}, f32[3,160,64,64]{3,2,1,0:T(8,128)}, ...), condition=%wide.region_46.47_spmd.clone, body=%wide.region_42.46_spmd.clone.sunk | while | flops 514326720 | bytes 81102576 | solution.py:310
  1874.3 31.7 %scatter_fusion.2 = f32[3,160,64,64]{3,2,1,0:T(8,128)} fusion(f32[3,160,64,64]{3,2,1,0:T(8,128)} %get-tuple-element.1077, s32[192]{0:T(256)S(1)} %reshape.854, f32[192,64,64]{2,1,0:T(8,128)} %bitcast.525), kind=kCustom, calls=%fused_computation.10.clone.clone.1 | custom fusion | flops 786432 | bytes 9438720 | tf_op jit(solution)/shard_map/while/body/eval_jaxpr/scatter-add | solution.py:305
  1906.0 31.7 %scatter_fusion.3 = f32[3,160,64,64]{3,2,1,0:T(8,128)} fusion(f32[3,160,64,64]{3,2,1,0:T(8,128)} %get-tuple-element.1078, s32[192]{0:T(256)S(1)} %reshape.854, f32[192,64,64]{2,1,0:T(8,128)} %bitcast.523), kind=kCustom, calls=%fused_computation.11.clone.clone.1 | custom fusion | flops 786432 | bytes 9438720 | tf_op jit(solution)/shard_map/while/body/eval_jaxpr/scatter-add | solution.py:306
  1999.0 31.7 %scatter_fusion.3 = f32[3,160,64,64]{3,2,1,0:T(8,128)} fusion(f32[3,160,64,64]{3,2,1,0:T(8,128)} %get-tuple-element.1078, s32[192]{0:T(256)S(1)} %reshape.854, f32[192,64,64]{2,1,0:T(8,128)} %bitcast.523), kind=kCustom, calls=%fused_computation.11.clone.clone.1 | custom fusion | flops 786432 | bytes 9438720 | tf_op jit(solution)/shard_map/while/body/eval_jaxpr/scatter-add | solution.py:306
  2092.0 31.7 %scatter_fusion.3 = f32[3,160,64,64]{3,2,1,0:T(8,128)} fusion(f32[3,160,64,64]{3,2,1,0:T(8,128)} %get-tuple-element.1078, s32[192]{0:T(256)S(1)} %reshape.854, f32[192,64,64]{2,1,0:T(8,128)} %bitcast.523), kind=kCustom, calls=%fused_computation.11.clone.clone.1 | custom fusion | flops 786432 | bytes 9438720 | tf_op jit(solution)/shard_map/while/body/eval_jaxpr/scatter-add | solution.py:306
  2240.1 32.4 %copy.269 = f32[2,160,64,3,64]{2,1,4,3,0:T(8,128)} copy(f32[2,160,64,3,64]{4,2,1,3,0:T(8,128)} %maximum_bitcast_fusion.1) | data formatting | bytes 31457280 | tf_op jit(solution)/shard_map/transpose | solution.py:317
  2353.1 34.5 %collective-permute-done.15 = bf16[2,2048,192]{1,2,0:T(8,128)(2,1)} collective-permute-done((bf16[2,2048,192]{1,2,0:T(8,128)(2,1)}, bf16[2,2048,192]{1,2,0:T(8,128)(2,1)}, u32[]{:S(2)}, u32[]{:S(2)}) %collective-permute-start.15) | collective-permute-done | bytes 1572896 | tf_op jit(solution)/shard_map/ppermute | solution.py:19
  2387.6 32.7 %collective-permute-done.14 = bf16[2,2048,192]{1,2,0:T(8,128)(2,1)} collective-permute-done((bf16[2,2048,192]{1,2,0:T(8,128)(2,1)}, bf16[2,2048,192]{1,2,0:T(8,128)(2,1)}, u32[]{:S(2)}, u32[]{:S(2)}) %collective-permute-start.14) | collective-permute-done | bytes 1572896 | tf_op jit(solution)/shard_map/ppermute | solution.py:19
  2493.6 40.7 %all-reduce = (f32[768]{0:T(1024)}, f32[768]{0:T(1024)}, f32[768]{0:T(1024)}, f32[768]{0:T(1024)}, f32[768]{0:T(1024)}, /*index=5*/f32[768]{0:T(1024)}) all-reduce(f32[768]{0:T(1024)S(1)} %add.663, f32[768]{0:T(1024)S(1)} %add.664, f32[768]{0:T(1024)S(1)} %add.665, f32[768]{0:T(1024)S(1)} %add.666, ...), channel_id=1, replica_groups=mesh['seq'=8,'tp'=4] {'seq','tp'}, use_global_device_ids=true, to_apply=%region_62.63 | all-reduce | flops 4608 | bytes 36864 | tf_op jit(solution)/shard_map/psum | solution.py:375
  2538.9 71.7 %all-reduce.5.cloned.1.call-done = (f32[768,192]{0,1:T(8,128)}, f32[768,192]{0,1:T(8,128)}, f32[768,192]{0,1:T(8,128)}, f32[192,768]{1,0:T(8,128)}, f32[768,768]{1,0:T(8,128)}, /*index=5*/f32[768,768]{1,0:T(8,128)}) async-done(((f32[768,192]{0,1:T(8,128)}, f32[768,192]{0,1:T(8,128)}, f32[768,192]{0,1:T(8,128)}, f32[192,768]{1,0:T(8,128)}, f32[768,768]{1,0:T(8,128)}, /*index=5*/f32[768,768]{1,0:T(8,128)}), ...) | async-done | bytes 7077904 | tf_op jit(solution)/shard_map/psum | solution.py:361
  (785 shorter events, 1336.3 us)
Async XLA Ops:
  7.2 69.6 %all-gather.15.cloned.1.call-start = ((), (), s32[]{:S(2)}) async-start(), calls=%async_computation.12 | async-start | bytes 3932160 | tf_op jit(solution)/shard_map/all_gather | solution.py:171
  14.4 126.8 %all-gather.11.cloned.1.call-start = ((), (), s32[]{:S(2)}) async-start(), calls=%async_computation.8 | async-start | bytes 3932160 | tf_op jit(solution)/shard_map/all_gather | solution.py:171
  15.1 516.8 %reduce-scatter.13.cloned.1.call-start = ((), (), s32[]{:S(2)}) async-start(), calls=%async_computation.13 | async-start | bytes 7864320 | tf_op jit(solution)/shard_map/reduce_scatter | solution.py:228
  82.5 67.6 %collective-permute-start.4 = (bf16[2,2048,192]{1,2,0:T(8,128)(2,1)}, bf16[2,2048,192]{1,2,0:T(8,128)(2,1)}, u32[]{:S(2)}, u32[]{:S(2)}) collective-permute-start(bf16[2,2048,192]{1,2,0:T(8,128)(2,1)} %pad_maximum_fusion.2), channel_id=1, source_target_pairs={{0,8},{4,12},{8,16},{12,20},{16,24},{20,28},{1,9},{5,13},{9,17},{1... | collective-permute-start | bytes 4718600 | tf_op jit(solution)/shard_map/ppermute | solution.py:19
  86.3 68.4 %collective-permute-start.5 = (bf16[2,2048,192]{1,2,0:T(8,128)(2,1)}, bf16[2,2048,192]{1,2,0:T(8,128)(2,1)}, u32[]{:S(2)}, u32[]{:S(2)}) collective-permute-start(bf16[2,2048,192]{1,2,0:T(8,128)(2,1)} %pad_maximum_fusion.2), channel_id=1, source_target_pairs={{0,4},{4,8},{8,12},{12,16},{16,20},{20,24},{24,28},{1,5},{5,9},{9,... | collective-permute-start | bytes 4718600 | tf_op jit(solution)/shard_map/ppermute | solution.py:19
  89.6 96.7 %collective-permute-start.7 = (bf16[2,2048,192]{1,2,0:T(8,128)(2,1)}, bf16[2,2048,192]{1,2,0:T(8,128)(2,1)}, u32[]{:S(2)}, u32[]{:S(2)}) collective-permute-start(bf16[2,2048,192]{1,2,0:T(8,128)(2,1)} %pad_maximum_fusion.2), channel_id=1, source_target_pairs={{8,0},{12,4},{16,8},{20,12},{24,16},{28,20},{9,1},{13,5},{17,9},{2... | collective-permute-start | bytes 4718600 | tf_op jit(solution)/shard_map/ppermute | solution.py:19
  94.8 64.8 %collective-permute-start.6 = (bf16[2,2048,192]{1,2,0:T(8,128)(2,1)}, bf16[2,2048,192]{1,2,0:T(8,128)(2,1)}, u32[]{:S(2)}, u32[]{:S(2)}) collective-permute-start(bf16[2,2048,192]{1,2,0:T(8,128)(2,1)} %pad_maximum_fusion.2), channel_id=1, source_target_pairs={{4,0},{8,4},{12,8},{16,12},{20,16},{24,20},{28,24},{5,1},{9,5},{13... | collective-permute-start | bytes 4718600 | tf_op jit(solution)/shard_map/ppermute | solution.py:19
  147.0 218.4 %collective-permute-start.3 = (bf16[2,2048,192]{1,2,0:T(8,128)(2,1)}, bf16[2,2048,192]{1,2,0:T(8,128)(2,1)}, u32[]{:S(2)}, u32[]{:S(2)}) collective-permute-start(bf16[2,2048,192]{1,2,0:T(8,128)(2,1)} %pad_maximum_fusion.1), channel_id=1, source_target_pairs={{8,0},{12,4},{16,8},{20,12},{24,16},{28,20},{9,1},{13,5},{17,9},{2... | collective-permute-start | bytes 4718600 | tf_op jit(solution)/shard_map/ppermute | solution.py:19
  150.2 213.6 %collective-permute-start.2 = (bf16[2,2048,192]{1,2,0:T(8,128)(2,1)}, bf16[2,2048,192]{1,2,0:T(8,128)(2,1)}, u32[]{:S(2)}, u32[]{:S(2)}) collective-permute-start(bf16[2,2048,192]{1,2,0:T(8,128)(2,1)} %pad_maximum_fusion.1), channel_id=1, source_target_pairs={{4,0},{8,4},{12,8},{16,12},{20,16},{24,20},{28,24},{5,1},{9,5},{13... | collective-permute-start | bytes 4718600 | tf_op jit(solution)/shard_map/ppermute | solution.py:19
  154.7 207.4 %collective-permute-start.1 = (bf16[2,2048,192]{1,2,0:T(8,128)(2,1)}, bf16[2,2048,192]{1,2,0:T(8,128)(2,1)}, u32[]{:S(2)}, u32[]{:S(2)}) collective-permute-start(bf16[2,2048,192]{1,2,0:T(8,128)(2,1)} %pad_maximum_fusion.1), channel_id=1, source_target_pairs={{0,4},{4,8},{8,12},{12,16},{16,20},{20,24},{24,28},{1,5},{5,9},{9,... | collective-permute-start | bytes 4718600 | tf_op jit(solution)/shard_map/ppermute | solution.py:19
  159.6 200.9 %collective-permute-start = (bf16[2,2048,192]{1,2,0:T(8,128)(2,1)}, bf16[2,2048,192]{1,2,0:T(8,128)(2,1)}, u32[]{:S(2)}, u32[]{:S(2)}) collective-permute-start(bf16[2,2048,192]{1,2,0:T(8,128)(2,1)} %pad_maximum_fusion.1), channel_id=1, source_target_pairs={{0,8},{4,12},{8,16},{12,20},{16,24},{20,28},{1,9},{5,13},{9,17},{1... | collective-permute-start | bytes 4718600 | tf_op jit(solution)/shard_map/ppermute | solution.py:19
  351.1 299.1 %reduce-scatter.9.cloned.1.call-start = ((), (), s32[]{:S(2)}) async-start(), calls=%async_computation.9 | async-start | bytes 7864320 | tf_op jit(solution)/shard_map/reduce_scatter | solution.py:228
  531.2 185.5 %all-gather.17.cloned.1.call-start = ((), (), s32[]{:S(2)}) async-start(), calls=%async_computation.14 | async-start | bytes 3932160 | tf_op jit(solution)/shard_map/all_gather | solution.py:237
  655.0 125.9 %all-gather.25.cloned.1.call-start = ((), (), s32[]{:S(2)}) async-start(), calls=%async_computation.23 | async-start | bytes 3932160 | tf_op jit(solution)/shard_map/all_gather | solution.py:251
  656.9 187.8 %all-gather.13.cloned.1.call-start = ((), (), s32[]{:S(2)}) async-start(), calls=%async_computation.10 | async-start | bytes 3932160 | tf_op jit(solution)/shard_map/all_gather | solution.py:237
  657.7 250.8 %all-gather.23.cloned.1.call-start = ((), (), s32[]{:S(2)}) async-start(), calls=%async_computation.22 | async-start | bytes 3932160 | tf_op jit(solution)/shard_map/all_gather | solution.py:251
  658.4 313.2 %reduce-scatter.21.cloned.1.call-start = ((), (), s32[]{:S(2)}) async-start(), calls=%async_computation.19 | async-start | bytes 3932160 | tf_op jit(solution)/shard_map/reduce_scatter | solution.py:258
  795.0 239.1 %reduce-scatter.17.cloned.1.call-start = ((), (), s32[]{:S(2)}) async-start(), calls=%async_computation.16 | async-start | bytes 3932160 | tf_op jit(solution)/shard_map/reduce_scatter | solution.py:258
  922.3 174.4 %reduce-scatter.15.cloned.1.call-start = ((), (), s32[]{:S(2)}) async-start(), calls=%async_computation.15 | async-start | bytes 3932160 | tf_op jit(solution)/shard_map/reduce_scatter | solution.py:240
  928.6 230.6 %reduce-scatter.11.cloned.1.call-start = ((), (), s32[]{:S(2)}) async-start(), calls=%async_computation.11 | async-start | bytes 3932160 | tf_op jit(solution)/shard_map/reduce_scatter | solution.py:240
  935.7 291.0 %all-gather.19.cloned.1.call-start = ((), (), s32[]{:S(2)}) async-start(), calls=%async_computation.17 | async-start | bytes 3932160 | tf_op jit(solution)/shard_map/all_gather | solution.py:270
  1165.0 561.7 %all-gather.21.cloned.1.call-start = ((), (), s32[]{:S(2)}) async-start(), calls=%async_computation.20 | async-start | bytes 3932160 | tf_op jit(solution)/shard_map/all_gather | solution.py:270
  1165.5 1315.4 %reduce-scatter.19.cloned.1.call-start = ((), (), s32[]{:S(2)}) async-start(), calls=%async_computation.18 | async-start | bytes 3932160 | tf_op jit(solution)/shard_map/reduce_scatter | solution.py:349
  1718.5 68.6 %collective-permute-start.11 = (bf16[2,2048,192]{1,2,0:T(8,128)(2,1)}, bf16[2,2048,192]{1,2,0:T(8,128)(2,1)}, u32[]{:S(2)}, u32[]{:S(2)}) collective-permute-start(bf16[2,2048,192]{1,2,0:T(8,128)(2,1)} %get-tuple-element.671), channel_id=1, source_target_pairs={{0,8},{4,12},{8,16},{12,20},{16,24},{20,28},{1,9},{5,13},{9,17},{1... | collective-permute-start | bytes 4718600 | tf_op jit(solution)/shard_map/ppermute | solution.py:19
  1722.2 96.5 %collective-permute-start.10 = (bf16[2,2048,192]{1,2,0:T(8,128)(2,1)}, bf16[2,2048,192]{1,2,0:T(8,128)(2,1)}, u32[]{:S(2)}, u32[]{:S(2)}) collective-permute-start(bf16[2,2048,192]{1,2,0:T(8,128)(2,1)} %get-tuple-element.672), channel_id=1, source_target_pairs={{0,4},{4,8},{8,12},{12,16},{16,20},{20,24},{24,28},{1,5},{5,9},{9,... | collective-permute-start | bytes 4718600 | tf_op jit(solution)/shard_map/ppermute | solution.py:19
  1724.1 94.6 %collective-permute-start.9 = (bf16[2,2048,192]{1,2,0:T(8,128)(2,1)}, bf16[2,2048,192]{1,2,0:T(8,128)(2,1)}, u32[]{:S(2)}, u32[]{:S(2)}) collective-permute-start(bf16[2,2048,192]{1,2,0:T(8,128)(2,1)} %get-tuple-element.673), channel_id=1, source_target_pairs={{4,0},{8,4},{12,8},{16,12},{20,16},{24,20},{28,24},{5,1},{9,5},{13... | collective-permute-start | bytes 4718600 | tf_op jit(solution)/shard_map/ppermute | solution.py:19
  1827.8 663.0 %reduce-scatter.23.cloned.1.call-start = ((), (), s32[]{:S(2)}) async-start(), calls=%async_computation.21 | async-start | bytes 3932160 | tf_op jit(solution)/shard_map/reduce_scatter | solution.py:349
  2312.5 40.6 %collective-permute-start.12 = (bf16[2,2048,192]{1,2,0:T(8,128)(2,1)}, bf16[2,2048,192]{1,2,0:T(8,128)(2,1)}, u32[]{:S(2)}, u32[]{:S(2)}) collective-permute-start(bf16[2,2048,192]{1,2,0:T(8,128)(2,1)} %get-tuple-element.674), channel_id=1, source_target_pairs={{8,0},{12,4},{16,8},{20,12},{24,16},{28,20},{9,1},{13,5},{17,9},{2... | collective-permute-start | bytes 4718600 | tf_op jit(solution)/shard_map/ppermute | solution.py:19
  2318.7 68.9 %collective-permute-start.15 = (bf16[2,2048,192]{1,2,0:T(8,128)(2,1)}, bf16[2,2048,192]{1,2,0:T(8,128)(2,1)}, u32[]{:S(2)}, u32[]{:S(2)}) collective-permute-start(bf16[2,2048,192]{1,2,0:T(8,128)(2,1)} %get-tuple-element.675), channel_id=1, source_target_pairs={{0,8},{4,12},{8,16},{12,20},{16,24},{20,28},{1,9},{5,13},{9,17},{1... | collective-permute-start | bytes 4718600 | tf_op jit(solution)/shard_map/ppermute | solution.py:19
  2320.6 99.6 %collective-permute-start.14 = (bf16[2,2048,192]{1,2,0:T(8,128)(2,1)}, bf16[2,2048,192]{1,2,0:T(8,128)(2,1)}, u32[]{:S(2)}, u32[]{:S(2)}) collective-permute-start(bf16[2,2048,192]{1,2,0:T(8,128)(2,1)} %get-tuple-element.676), channel_id=1, source_target_pairs={{0,4},{4,8},{8,12},{12,16},{16,20},{20,24},{24,28},{1,5},{5,9},{9,... | collective-permute-start | bytes 4718600 | tf_op jit(solution)/shard_map/ppermute | solution.py:19
  2323.6 96.7 %collective-permute-start.13 = (bf16[2,2048,192]{1,2,0:T(8,128)(2,1)}, bf16[2,2048,192]{1,2,0:T(8,128)(2,1)}, u32[]{:S(2)}, u32[]{:S(2)}) collective-permute-start(bf16[2,2048,192]{1,2,0:T(8,128)(2,1)} %get-tuple-element.677), channel_id=1, source_target_pairs={{4,0},{8,4},{12,8},{16,12},{20,16},{24,20},{28,24},{5,1},{9,5},{13... | collective-permute-start | bytes 4718600 | tf_op jit(solution)/shard_map/ppermute | solution.py:19
  2429.4 181.2 %all-reduce.5.cloned.1.call-start = ((), (), s32[]{:S(2)}) async-start(), calls=%async_computation.24 | async-start | bytes 14155776 | tf_op jit(solution)/shard_map/psum | solution.py:361
  (137 other events, 2411.5 us)
Sparse Core Ops, SparseCore 0:
  14.5 62.2 all-gather.14
  78.9 62.1 all-gather.10
  351.2 119.4 reduce-scatter.12
  531.4 118.7 reduce-scatter.8
  655.1 61.5 all-gather.16
  718.8 62.1 all-gather.24
  782.5 62.1 all-gather.12
  846.3 62.1 all-gather.22
  910.8 60.8 reduce-scatter.20
  973.8 60.2 reduce-scatter.16
  1036.4 60.2 reduce-scatter.14
  1098.9 60.2 reduce-scatter.10
  1165.1 61.5 all-gather.18
  1228.1 62.1 all-gather.20
  1827.9 62.8 reduce-scatter.18
  2429.5 61.2 reduce-scatter.22
  2495.9 114.6 all-reduce.4
where the time goes:
time: 2650 us; the launch traced here: 2630 us
  waiting for transfers between devices  985 us (37%)
  other arithmetic  650 us (25%)
  local copies, waits for them, and re-layouts  580 us (22%)
  matrix products  291 us (11%)
  blocking collectives  53.7 us (2%)
  starting transfers between devices  49.9 us (2%)
    scatter-add x8, other arithmetic, backward_step(): values_store.at[head_ids, index_part].add(grad_values.reshape(shaped))  253 us
    scatter-add x8, other arithmetic, backward_step(): keys_store.at[head_ids, index_part].add(grad_keys.reshape(shaped))  253 us
    ppermute x16, waiting for transfers between devices, from_behind(): return lax.ppermute(block, axis, route)  189 us
    reduce_scatter x2, waiting for transfers between devices, body(): lax.psum_scatter(jnp.dot(active, outer_weight, preferred_element_type=f32...  122 us
    reduce_scatter x2, waiting for transfers between devices, body(): lax.psum_scatter(jnp.dot(context, proj_weight, preferred_element_type=f32...  118 us
    gather x16, local copies, waits for them, and re-layouts, gather_scores(): values_all[head_ids, index_part]  110 us
    all_gather x2, waiting for transfers between devices, body(): shard_rows = lax.all_gather(grad_out, 'tp', axis=0, tiled=True)  110 us
    all_gather x2, waiting for transfers between devices, body(): gathered_two = lax.all_gather(low_two, 'tp', axis=0, tiled=True)  108 us
  transfers between devices with their start and end apart: 33, of which 21 were waited for; matrix products, arithmetic and copies ran while one was open for 55% of the time, Pallas kernels for 0%

commit v1 on v0

v1 whole, which is shorter than its diff:
```python
import functools
import math

import jax
import jax.numpy as jnp
from jax import lax
from jax.experimental import pallas as pl
from jax.experimental.pallas import tpu as pltpu
from jax.sharding import PartitionSpec as P

BLOCK = 64
LONG_BLK = 64
PAIR = 2 * BLOCK
UNROLL = 4

NORM_EPS = 1e-05
MASKED = -1000000000.0

f32 = jnp.float32
bf16 = jnp.bfloat16

NN = (((1,), (0,)), ((), ()))
NT = (((1,), (1,)), ((), ()))
TN = (((0,), (0,)), ((), ()))


def contract(left, right, dims):
    return lax.dot_general(left, right, dims, preferred_element_type=f32)


def from_behind(block, axis, distance):
    devices = range(lax.axis_size(axis))
    route = [(i - distance, i) for i in devices if i - distance in devices]
    return lax.ppermute(block, axis, route)


def gelu_exact(values):
    return 0.5 * values * (1.0 + lax.erf(values / math.sqrt(2.0)))


def gelu_grad(values, grad_rows):
    _, pull_back = jax.vjp(gelu_exact, values)
    return pull_back(grad_rows)[0]


def layer_stats(values, norm_gain, norm_shift):
    row_mean = jnp.mean(values, axis=-1, keepdims=True)
    centred = values - row_mean
    inverse = lax.rsqrt(jnp.mean(centred * centred, axis=-1, keepdims=True) + NORM_EPS)
    normed = centred * inverse
    return (normed * norm_gain + norm_shift, normed, inverse)


def layer_back(grad_rows, normed, inverse, norm_gain):
    scaled = grad_rows * norm_gain
    inner_term = (
        scaled
        - jnp.mean(scaled, axis=-1, keepdims=True)
        - normed * jnp.mean(scaled * normed, axis=-1, keepdims=True)
    )
    return (inverse * inner_term, jnp.sum(grad_rows * normed, axis=0), jnp.sum(grad_rows, axis=0))


def block_keys(lengths, randoms, blocks, top_block):
    doc_ends = jnp.cumsum(lengths)
    doc_starts = doc_ends - lengths
    doc_owner = jnp.sum((blocks[:, None] >= doc_ends[None, :]).astype(jnp.int32), axis=1)
    doc_ids = jnp.arange(lengths.shape[0], dtype=jnp.int32)
    doc_hit = doc_owner[:, None] == doc_ids[None, :]
    doc_first = jnp.sum(jnp.where(doc_hit, doc_starts[None, :], 0), axis=1)
    doc_final = jnp.sum(jnp.where(doc_hit, doc_ends[None, :], 0), axis=1)
    fixed_keys = jnp.stack(
        [
            jnp.maximum(blocks - 1, 0),
            jnp.minimum(blocks + 1, top_block),
            blocks,
            doc_first,
            doc_first + 1,
        ],
        axis=1,
    )
    block_count = randoms.shape[0]
    head_count = randoms.shape[1]
    key_index = jnp.concatenate(
        [jnp.broadcast_to(fixed_keys[:, None, :], (block_count, head_count, 5)), randoms], axis=2
    )
    key_valid = jnp.stack([blocks > doc_first, blocks + 1 < doc_final], axis=1)
    return (key_index, key_valid.astype(jnp.int32))


def block_rows(block):
    return pl.ds(pl.multiple_of(block * BLOCK, BLOCK), BLOCK)


def listed_blocks(index_ref, store, base, slots):
    return jnp.concatenate(
        [store[block_rows(index_ref[base + slot]), :] for slot in range(slots)], axis=0
    )


def mask_scores(scores, valid_ref, block):
    lane = lax.broadcasted_iota(jnp.int32, (1, PAIR), 1)
    keep = jnp.where(lane < BLOCK, valid_ref[2 * block], valid_ref[2 * block + 1]) > 0
    return jnp.concatenate([jnp.where(keep, scores[:, :PAIR], MASKED), scores[:, PAIR:]], axis=1)


def forward_kernel(slots, index_ref, valid_ref, query_ref, *refs):
    *pieces, context_ref, logsum_ref, store = refs
    rows = query_ref.shape[0]
    blocks = rows // BLOCK
    head = pl.program_id(0)
    for place, piece in enumerate(pieces):
        store[place * rows : (place + 1) * rows, :] = piece[...]

    def step(group, carry):
        ids = [group * UNROLL + unit for unit in range(UNROLL)]
        listed = [
            listed_blocks(index_ref, store, (head * blocks + block) * slots, slots)
            for block in ids
        ]
        scores = [
            mask_scores(contract(query_ref[block_rows(block), :], pairs, NT), valid_ref, block)
            for block, pairs in zip(ids, listed)
        ]
        probs = []
        for block, score in zip(ids, scores):
            top = jnp.max(score, axis=1, keepdims=True)
            raised = jnp.exp(score - top)
            total = jnp.sum(raised, axis=1, keepdims=True)
            probs.append((raised * (1.0 / total)).astype(bf16))
            logsum_ref[block_rows(block), :] = jnp.broadcast_to(
                top + jnp.log(total), (BLOCK, PAIR)
            )
        for block, prob, pairs in zip(ids, probs, listed):
            context_ref[block_rows(block), :] = contract(prob, pairs, NN).astype(bf16)
        return carry

    lax.fori_loop(0, blocks // UNROLL, step, 0)


def backward_kernel(slots, count, index_ref, valid_ref, both_ref, logsum_ref, *refs):
    pieces = refs[:count]
    grad_query_ref = refs[count]
    grad_pieces = refs[count + 1 : 2 * count + 1]
    store, sums = refs[2 * count + 1 :]
    rows = both_ref.shape[0]
    blocks = rows // BLOCK
    head = pl.program_id(0)
    for place, piece in enumerate(pieces):
        store[place * rows : (place + 1) * rows, :] = piece[...]
    sums[...] = jnp.zeros_like(sums)
    lane = lax.broadcasted_iota(jnp.int32, (BLOCK, PAIR), 1)

    def step(group, carry):
        ids = [group * UNROLL + unit for unit in range(UNROLL)]
        listed = [
            listed_blocks(index_ref, store, (head * blocks + block) * slots, slots)
            for block in ids
        ]
        lefts = []
        for block in ids:
            both = both_ref[block_rows(block), :]
            lefts.append(
                jnp.concatenate(
                    [
                        jnp.where(lane < BLOCK, both, 0).astype(bf16),
                        jnp.where(lane < BLOCK, 0, both).astype(bf16),
                    ],
                    axis=0,
                )
            )
        products = [contract(left, pairs, NT) for left, pairs in zip(lefts, listed)]
        mixes = []
        for block, product in zip(ids, products):
            score = mask_scores(product[:BLOCK], valid_ref, block)
            grad_prob = product[BLOCK:]
            logsum = jnp.concatenate([logsum_ref[block_rows(block), :]] * (slots // 2), axis=1)
            prob = jnp.exp(score - logsum)
            delta = jnp.sum(prob * grad_prob, axis=1, keepdims=True)
            grad_score = prob * (grad_prob - delta)
            mixes.append(jnp.concatenate([grad_score.astype(bf16), prob.astype(bf16)], axis=0))
        for block, mix, pairs in zip(ids, mixes, listed):
            grad_query_ref[block_rows(block), :] = contract(mix[:BLOCK], pairs, NN).astype(bf16)
        terms = [contract(mix, left, TN) for mix, left in zip(mixes, lefts)]
        for block, term in zip(ids, terms):
            base = (head * blocks + block) * slots
            for slot in range(slots):
                sums[block_rows(index_ref[base + slot]), :] += term[
                    slot * BLOCK : (slot + 1) * BLOCK
                ]
        return carry

    lax.fori_loop(0, blocks // UNROLL, step, 0)
    for place, grad_piece in enumerate(grad_pieces):
        grad_piece[...] = sums[place * rows : (place + 1) * rows, :].astype(bf16)


def attend_forward(index, valid, queries, pieces, heads, slots):
    rows = queries.shape[0]
    spec = pl.BlockSpec((rows, PAIR), lambda head, *_: (0, head))
    work = heads * rows * slots * BLOCK
    return pl.pallas_call(
        functools.partial(forward_kernel, slots),
        grid_spec=pltpu.PrefetchScalarGridSpec(
            num_scalar_prefetch=2,
            grid=(heads,),
            in_specs=[spec] * (1 + len(pieces)),
            out_specs=[spec, spec],
            scratch_shapes=[pltpu.VMEM((rows * len(pieces), PAIR), bf16)],
        ),
        out_shape=[
            jax.ShapeDtypeStruct((rows, heads * PAIR), bf16),
            jax.ShapeDtypeStruct((rows, heads * PAIR), f32),
        ],
        compiler_params=pltpu.CompilerParams(vmem_limit_bytes=40 * 2**20),
        cost_estimate=pl.CostEstimate(
            flops=work * PAIR * 4, bytes_accessed=rows * heads * PAIR * 18, transcendentals=work
        ),
    )(index, valid, queries, *pieces)


def attend_backward(index, valid, both, logsum, pieces, heads, slots):
    rows = both.shape[0]
    count = len(pieces)
    spec = pl.BlockSpec((rows, PAIR), lambda head, *_: (0, head))
    work = heads * rows * slots * BLOCK
    return pl.pallas_call(
        functools.partial(backward_kernel, slots, count),
        grid_spec=pltpu.PrefetchScalarGridSpec(
            num_scalar_prefetch=2,
            grid=(heads,),
            in_specs=[spec] * (2 + count),
            out_specs=[spec] * (1 + count),
            scratch_shapes=[
                pltpu.VMEM((rows * count, PAIR), bf16),
                pltpu.VMEM((rows * count, PAIR), f32),
            ],
        ),
        out_shape=[jax.ShapeDtypeStruct((rows, heads * PAIR), bf16)] * (1 + count),
        compiler_params=pltpu.CompilerParams(vmem_limit_bytes=50 * 2**20),
        cost_estimate=pl.CostEstimate(
            flops=work * PAIR * 10, bytes_accessed=rows * heads * PAIR * 28, transcendentals=work
        ),
    )(index, valid, both, logsum, *pieces)


def body(
    tokens,
    doc_lengths,
    rand_blocks,
    query_weight,
    key_weight,
    value_weight,
    query_bias,
    value_bias,
    proj_weight,
    proj_bias,
    first_gain,
    first_bias,
    second_gain,
    second_bias,
    inner_weight,
    inner_bias,
    outer_weight,
    outer_bias,
    out_grad,
):
    micro_count, local_rows, model_width = tokens.shape
    seq_count = lax.axis_size("seq")
    tp_count = lax.axis_size("tp")
    seq_place = lax.axis_index("seq")
    tp_place = lax.axis_index("tp")
    block_dev = rand_blocks.shape[1]
    heads = rand_blocks.shape[2]
    local_width = query_weight.shape[1]
    head_size = local_width // heads
    hidden_units = inner_weight.shape[1]
    group_rows = block_dev * BLOCK
    reach_dev = (block_dev + LONG_BLK - 2) // block_dev
    window = 2 * reach_dev + 1
    score_scale = 1.0 / math.sqrt(head_size)
    lowest = (seq_place - reach_dev) * block_dev
    blocks = seq_place * block_dev + jnp.arange(block_dev, dtype=jnp.int32)
    top_block = block_dev * seq_count - 1

    held = jnp.concatenate([inner_weight.T, outer_weight, proj_weight, inner_bias[None]], axis=0)
    used_rows = held.shape[0]
    piece_rows = -(-used_rows // (16 * seq_count)) * 16
    held_rows = piece_rows * seq_count
    held = jnp.pad(held, ((0, held_rows - used_rows), (0, 0)))
    share = lax.dynamic_slice_in_dim(held, seq_place * piece_rows, piece_rows, axis=0)
    spread = lax.all_gather(share, ("tp", "seq"), axis=0, tiled=True)
    spread = spread.reshape(tp_count, held_rows, model_width)
    cuts = [0, hidden_units, 2 * hidden_units, 2 * hidden_units + local_width, used_rows]
    inner_full = spread[:, cuts[0] : cuts[1]].reshape(-1, model_width)
    outer_full = spread[:, cuts[1] : cuts[2]].reshape(-1, model_width)
    proj_full = spread[:, cuts[2] : cuts[3]].reshape(-1, model_width)
    inner_bias_full = spread[:, cuts[3] : cuts[4]].reshape(-1)

    def by_head(weight):
        return weight.reshape(weight.shape[:-1] + (heads, head_size))

    def side_by_side(first, second):
        paired = jnp.concatenate([by_head(first), by_head(second)], axis=-1)
        return paired.reshape(paired.shape[:-2] + (heads * PAIR,))

    query_wide = side_by_side(query_weight, jnp.zeros_like(query_weight))
    query_wide_bias = side_by_side(query_bias, jnp.zeros_like(query_bias))
    pair_wide = side_by_side(key_weight, value_weight)
    pair_wide_bias = side_by_side(jnp.zeros_like(value_bias), value_bias)

    stage = [{} for _ in range(micro_count)]
    for micro, held_in in enumerate(stage):
        inputs = tokens[micro].astype(f32)
        shifted, stats, inverse = layer_stats(inputs, first_gain, first_bias)
        held_in["inputs"], held_in["stats_one"], held_in["inverse_one"] = inputs, stats, inverse
        held_in["one"] = lax.all_gather(shifted.astype(bf16), "tp", axis=0, tiled=True)

    for micro, held_in in enumerate(stage):
        one = held_in["one"]
        pair_rows = (contract(one, pair_wide, NN) + pair_wide_bias).astype(bf16)
        pieces = [
            pair_rows if offset == 0 else from_behind(pair_rows, "seq", -offset)
            for offset in range(-reach_dev, reach_dev + 1)
        ]
        queries = ((contract(one, query_wide, NN) + query_wide_bias) * score_scale).astype(bf16)
        key_index, key_valid = block_keys(
            doc_lengths[micro], rand_blocks[micro], blocks, top_block
        )
        slots = key_index.shape[2]
        slot_index = jnp.clip(key_index - lowest, 0, window * block_dev - 1)
        held_in["index"] = slot_index.transpose(1, 0, 2).reshape(-1)
        held_in["valid"] = key_valid.reshape(-1)
        held_in["queries"], held_in["pieces"] = queries, pieces

    for held_in in stage:
        wide_context, held_in["logsum"] = attend_forward(
            held_in["index"],
            held_in["valid"],
            held_in["queries"],
            held_in["pieces"],
            heads,
            slots,
        )
        context = wide_context.reshape(group_rows, heads, PAIR)[:, :, head_size:]
        held_in["context"] = lax.all_to_all(
            context.reshape(group_rows, local_width), "tp", split_axis=0, concat_axis=1, tiled=True
        )

    outputs = []
    for micro, held_in in enumerate(stage):
        context = held_in["context"]
        hidden = held_in["inputs"] + contract(context, proj_full, NN) + proj_bias
        shifted, stats, inverse = layer_stats(hidden, second_gain, second_bias)
        two = shifted.astype(bf16)
        before = contract(two, inner_full, NT) + inner_bias_full
        active = gelu_exact(before).astype(bf16)
        result = hidden + contract(active, outer_full, NN) + outer_bias
        outputs.append(result.astype(bf16))
        grad_out = out_grad[micro]
        grad_float = grad_out.astype(f32)
        grad_active = contract(grad_out, outer_full, NT)
        grad_before = gelu_grad(before, grad_active).astype(bf16)
        grad_two = contract(grad_before, inner_full, NN)
        back, gain_sum, shift_sum = layer_back(grad_two, stats, inverse, second_gain)
        grad_hidden = grad_float + back
        branch = grad_hidden.astype(bf16)
        grad_context = contract(branch, proj_full, NT).astype(bf16)
        held_in["grad_context"] = lax.all_to_all(
            grad_context, "tp", split_axis=1, concat_axis=0, tiled=True
        )
        held_in["grad_hidden"] = grad_hidden
        held_in["dense"] = (two, grad_before, active, grad_out, context, branch)
        held_in["row_sums"] = (
            jnp.sum(grad_before.astype(f32), axis=0),
            gain_sum,
            shift_sum,
            jnp.sum(branch.astype(f32), axis=0),
            jnp.sum(grad_float, axis=0),
        )

    two, grad_before, active, grad_out, context, branch = (
        jnp.concatenate(group, axis=0) for group in zip(*(h["dense"] for h in stage))
    )
    inner_part = contract(grad_before, two, TN).astype(bf16)
    outer_part = contract(active, grad_out, TN).astype(bf16)
    proj_part = contract(context, branch, TN).astype(bf16)
    grad_rows = 2 * hidden_units + local_width
    grad_piece = -(-grad_rows // (16 * seq_count)) * 16
    grad_held = grad_piece * seq_count
    parts = jnp.concatenate(
        [
            inner_part.reshape(tp_count, hidden_units, model_width),
            outer_part.reshape(tp_count, hidden_units, model_width),
            proj_part.reshape(tp_count, local_width, model_width),
            jnp.zeros((tp_count, grad_held - grad_rows, model_width), bf16),
        ],
        axis=1,
    ).reshape(tp_count * grad_held, model_width)
    own_part = lax.psum_scatter(parts, ("tp", "seq"), scatter_dimension=0, tiled=True)
    dense_sum = lax.all_gather(own_part, "seq", axis=0, tiled=True).astype(f32)
    inner_weight_grad = dense_sum[cuts[0] : cuts[1]].T
    outer_weight_grad = dense_sum[cuts[1] : cuts[2]]
    proj_weight_grad = dense_sum[cuts[2] : cuts[3]]

    for held_in in stage:
        queries = held_in["queries"].reshape(group_rows, heads, PAIR)[:, :, :head_size]
        both = jnp.concatenate([queries, by_head(held_in["grad_context"])], axis=-1)
        held_in["grad_query"], *grad_pieces = attend_backward(
            held_in["index"],
            held_in["valid"],
            both.reshape(group_rows, heads * PAIR),
            held_in["logsum"],
            held_in["pieces"],
            heads,
            slots,
        )
        returned = grad_pieces[reach_dev].astype(f32)
        for offset in range(-reach_dev, reach_dev + 1):
            if offset != 0:
                returned = returned + from_behind(
                    grad_pieces[offset + reach_dev], "seq", offset
                ).astype(f32)
        held_in["grad_pair"] = returned.astype(bf16)

    scaled_wide = (query_wide * score_scale).astype(bf16)
    input_grads = []
    query_sum = pair_sum = 0.0
    query_bias_sum = pair_bias_sum = 0.0
    first_gain_sum = first_bias_sum = 0.0
    for held_in in stage:
        grad_query, grad_pair, one = held_in["grad_query"], held_in["grad_pair"], held_in["one"]
        rows = contract(grad_query, scaled_wide, NT) + contract(grad_pair, pair_wide, NT)
        grad_one = lax.psum_scatter(
            rows.astype(bf16), "tp", scatter_dimension=0, tiled=True
        ).astype(f32)
        query_sum = query_sum + contract(one, grad_query, TN)
        pair_sum = pair_sum + contract(one, grad_pair, TN)
        query_bias_sum = query_bias_sum + jnp.sum(grad_query.astype(f32), axis=0)
        pair_bias_sum = pair_bias_sum + jnp.sum(grad_pair.astype(f32), axis=0)
        back, gain_sum, shift_sum = layer_back(
            grad_one, held_in["stats_one"], held_in["inverse_one"], first_gain
        )
        first_gain_sum = first_gain_sum + gain_sum
        first_bias_sum = first_bias_sum + shift_sum
        input_grads.append(held_in["grad_hidden"] + back)

    def low_half(wide):
        return wide.reshape(wide.shape[:-1] + (heads, PAIR))[..., :head_size].reshape(
            wide.shape[:-1] + (local_width,)
        )

    def high_half(wide):
        return wide.reshape(wide.shape[:-1] + (heads, PAIR))[..., head_size:].reshape(
            wide.shape[:-1] + (local_width,)
        )

    query_grad, key_grad, value_grad = lax.psum(
        (low_half(query_sum) * score_scale, low_half(pair_sum), high_half(pair_sum)), "seq"
    )
    inner_bias_sum, second_gain_sum, second_bias_sum, proj_bias_sum, outer_bias_sum = (
        sum(group) for group in zip(*(h["row_sums"] for h in stage))
    )

    def own_columns(values):
        wide = jnp.zeros((tp_count, local_width), f32)
        return lax.dynamic_update_slice_in_dim(wide, values[None], tp_place, axis=0).reshape(-1)

    early = lax.psum(
        jnp.concatenate(
            [
                inner_bias_sum,
                second_gain_sum,
                second_bias_sum,
                proj_bias_sum,
                outer_bias_sum,
            ]
        ),
        ("seq", "tp"),
    )
    late = lax.psum(
        jnp.concatenate(
            [
                first_gain_sum,
                first_bias_sum,
                own_columns(low_half(query_bias_sum) * score_scale),
                own_columns(high_half(pair_bias_sum)),
            ]
        ),
        ("seq", "tp"),
    )
    inner_bias_all = early[: tp_count * hidden_units].reshape(tp_count, hidden_units)
    early_rows = early[tp_count * hidden_units :].reshape(-1, model_width)
    late_rows = late.reshape(-1, model_width)

    def my_columns(row):
        return lax.dynamic_slice_in_dim(row, tp_place * local_width, local_width)

    return (
        jnp.stack(outputs),
        jnp.stack(input_grads),
        query_grad,
        key_grad,
        value_grad,
        my_columns(late_rows[2]),
        my_columns(late_rows[3]),
        proj_weight_grad,
        early_rows[2],
        late_rows[0],
        late_rows[1],
        early_rows[0],
        early_rows[1],
        inner_weight_grad,
        lax.dynamic_index_in_dim(inner_bias_all, tp_place, axis=0, keepdims=False),
        outer_weight_grad,
        early_rows[3],
    )


def solution(mesh):
    return jax.shard_map(
        body,
        mesh=mesh,
        in_specs=(
            P(None, ("seq", "tp"), None),
            P(),
            P(None, "seq", "tp", None),
            P(None, "tp"),
            P(None, "tp"),
            P(None, "tp"),
            P("tp"),
            P("tp"),
            P("tp", None),
            P(),
            P(),
            P(),
            P(),
            P(),
            P(None, "tp"),
            P("tp"),
            P("tp", None),
            P(),
            P(None, ("seq", "tp"), None),
        ),
        out_specs=(
            P(None, ("seq", "tp"), None),
            P(None, ("seq", "tp"), None),
            P(None, "tp"),
            P(None, "tp"),
            P(None, "tp"),
            P("tp"),
            P("tp"),
            P("tp", None),
            P(),
            P(),
            P(),
            P(),
            P(),
            P(None, "tp"),
            P("tp"),
            P("tp", None),
            P(),
        ),
        check_vma=False,
    )
```

time: 2650 us -> 1010 us (0.38)
  other arithmetic: 650 us -> 50.7 us
  local copies, waits for them, and re-layouts: 580 us -> 83.4 us
  waiting for transfers between devices: 985 us -> 536 us
  matrix products: 291 us -> 106 us
  Pallas kernels: 0 us -> 88.9 us
    scatter-add x16 -> x0, other arithmetic: 506 us -> none  [the longest x8 253 us: backward_step(): values_store.at[head_ids, index_part].add(grad_values.reshape(shaped))]
    reduce_scatter x8 -> x3, waiting for transfers between devices: 348 us -> 33 us  [the longest x2 33 us: body(): lax.psum_scatter(rows.astype(bf16), 'tp', scatter_dimension=0, tiled=True)]
    all_gather x8 -> x4, waiting for transfers between devices: 373 us -> 103 us  [the longest x2 103 us: body(): lax.all_gather(shifted.astype(bf16), 'tp', axis=0, tiled=True)]
    gather x32 -> x0, local copies, waits for them, and re-layouts: 208 us -> none  [the longest x16 110 us: gather_scores(): values_all[head_ids, index_part]]
    ppermute x16, waiting for transfers between devices: 189 us -> 320 us  [from_behind(): return lax.ppermute(block, axis, route)]
    dot_general x76 -> x27, matrix products: 221 us -> 106 us  [contract(): return lax.dot_general(left, right, dims, preferred_element_type=f32)]
    pallas_call x0 -> x4, Pallas kernels: none -> 88.9 us  [the longest x2 51.2 us: attend_backward(): pl.pallas_call(functools.partial(backward_kernel, slots, count), grid_spe...]
    another operation x20 -> x7, local copies, waits for them, and re-layouts: 80.1 us -> 0.24 us
  transfers between devices with their start and end apart: 33 -> 28, of which waited for: 21 -> 19; matrix products, arithmetic and copies ran while one was open for 55% -> 15% of each run, Pallas kernels for 0% -> 9%
where the time goes in v1:
time: 1010 us; the launch traced here: 996 us
  waiting for transfers between devices  536 us (53%)
  matrix products  106 us (10%)
  Pallas kernels  88.9 us (9%)
  local copies, waits for them, and re-layouts  83.4 us (8%)
  starting transfers between devices  75 us (7%)
  other arithmetic  50.7 us (5%)
  blocking collectives  39.7 us (4%)
  between operations  16 us (2%)
    ppermute x16, waiting for transfers between devices, from_behind(): return lax.ppermute(block, axis, route)  320 us
    dot_general x27, matrix products, contract(): return lax.dot_general(left, right, dims, preferred_element_type=f32)  106 us
    all_gather x2, waiting for transfers between devices, body(): lax.all_gather(shifted.astype(bf16), 'tp', axis=0, tiled=True)  103 us
    pallas_call x2, Pallas kernels, attend_backward(): pl.pallas_call(functools.partial(backward_kernel, slots, count), grid_spe...  51.2 us
    ppermute x16, starting transfers between devices, from_behind(): return lax.ppermute(block, axis, route)  47.5 us
    all_to_all x2, waiting for transfers between devices, body(): lax.all_to_all(grad_context, 'tp', split_axis=1, concat_axis=0, tiled=True)  44.2 us
    psum x1, blocking collectives, body(): lax.psum(jnp.concatenate([first_gain_sum, first_bias_sum, own_columns(low...  39.7 us
    pallas_call x2, Pallas kernels, attend_forward(): pl.pallas_call(functools.partial(forward_kernel, slots), grid_spec=pltpu....  37.7 us
  transfers between devices with their start and end apart: 28, of which 19 were waited for; matrix products, arithmetic and copies ran while one was open for 15% of the time, Pallas kernels for 9%

profile of v1, /device:TPU:13, one launch (start us, length us, event | category | flops | bytes accessed | tf_op | source)
XLA Modules:
  0.0 995.6 jit_solution(1786329020346540533)
XLA Ops:
  18.6 56.7 %all-gather.9.cloned.1.call-done = bf16[2048,768]{1,0:T(8,128)(2,1)} async-done(((bf16[512,768]{1,0:T(8,128)(2,1)}), bf16[2048,768]{1,0:T(8,128)(2,1)}) %all-gather.9.cloned.1.call-update) | async-done | bytes 3145744 | tf_op jit(solution)/shard_map/all_gather | solution.py:317
  92.9 46.7 %all-gather.5.cloned.1.call-done = bf16[2048,768]{1,0:T(8,128)(2,1)} async-done(((bf16[512,768]{1,0:T(8,128)(2,1)}), bf16[2048,768]{1,0:T(8,128)(2,1)}) %all-gather.5.cloned.1.call-update) | async-done | bytes 3145744 | tf_op jit(solution)/shard_map/all_gather | solution.py:317
  159.8 36.1 %collective-permute-done.4.refs_0_ = bf16[2048,384]{1,0:T(8,128)(2,1)} collective-permute-done((bf16[2048,384]{1,0:T(8,128)(2,1)S(1)}, bf16[2048,384]{1,0:T(8,128)(2,1)}, u32[]{:S(2)}, u32[]{:S(2)}) %collective-permute-start.4) | collective-permute-done | bytes 1572896 | tf_op jit(solution)/shard_map/ppermute | solution.py:34
  195.9 18.8 %shard_map.315 = (bf16[2048,384]{1,0:T(8,128)(2,1)S(1)}, f32[2048,384]{1,0:T(8,128)S(1)}) custom-call(s32[768]{0:T(1024)S(1)} %reshape.428.index_ref, s32[64]{0:T(128)S(1)} %reshape.451.valid_ref, bf16[2048,384]{1,0:T(8,128)(2,1)S(1)} %multiply_convert_fusion.2.query_ref, bf16[2048,384]{1,0:T(8,128)(2,1)} %collective-permute-done.4.refs_0_, ...), custom_call_target="tpu_custom_call" | custom-call | flops 1610612736 | bytes 14155776 | tf_op jit(solution)/shard_map/pallas_call | solution.py:202
  222.9 7.0 all-to-all-start.1
  235.1 9.2 collective-permute-done.3.refs_4_
  244.3 37.7 %collective-permute-done.1.refs_1_ = bf16[2048,384]{1,0:T(8,128)(2,1)} collective-permute-done((bf16[2048,384]{1,0:T(8,128)(2,1)}, bf16[2048,384]{1,0:T(8,128)(2,1)}, u32[]{:S(2)}, u32[]{:S(2)}) %collective-permute-start.1) | collective-permute-done | bytes 1572896 | tf_op jit(solution)/shard_map/ppermute | solution.py:34
  282.1 34.6 %collective-permute-done.refs_0_ = bf16[2048,384]{1,0:T(8,128)(2,1)} collective-permute-done((bf16[2048,384]{1,0:T(8,128)(2,1)}, bf16[2048,384]{1,0:T(8,128)(2,1)}, u32[]{:S(2)}, u32[]{:S(2)}) %collective-permute-start) | collective-permute-done | bytes 1572896 | tf_op jit(solution)/shard_map/ppermute | solution.py:34
  316.7 18.9 %shard_map.314 = (bf16[2048,384]{1,0:T(8,128)(2,1)S(1)}, f32[2048,384]{1,0:T(8,128)S(1)}) custom-call(s32[768]{0:T(1024)S(1)} %reshape.414.index_ref, s32[64]{0:T(128)S(1)} %reshape.447.valid_ref, bf16[2048,384]{1,0:T(8,128)(2,1)S(1)} %multiply_convert_fusion.3.query_ref, bf16[2048,384]{1,0:T(8,128)(2,1)} %collective-permute-done.refs_0_, ...), custom_call_target="tpu_custom_call" | custom-call | flops 1610612736 | bytes 14155776 | tf_op jit(solution)/shard_map/pallas_call | solution.py:202
  348.2 6.9 all-to-all-start
  360.4 7.9 fusion.110
  387.7 7.5 multiply_convert_fusion.1
  395.1 8.0 convert_reduce_fusion.1
  427.5 12.4 %maximum_maximum_fusion = bf16[4,1792,768]{2,1,0:T(8,128)(2,1)} fusion(bf16[4,192,768]{2,1,0:T(8,128)(2,1)S(1)} %bitcast.318, bf16[4,768,768]{2,1,0:T(8,128)(2,1)S(1)} %bitcast.308, bf16[4,768,768]{2,1,0:T(8,128)(2,1)S(1)} %bitcast.303, bf16[1792]{0:T(1024)(128)(2,1)S(1)} %pad.11.clone), kind=kLoop, calls=%fused_computation | loop fusion | flops 44040192 | bytes 21630464 | tf_op jit(solution)/shard_map/concatenate | solution.py:391
  446.4 8.3 all-to-all-start.2
  458.8 11.5 %all-to-all-done.2 = bf16[512,4,192]{0,2,1:T(8,128)(2,1)} async-done(((bf16[512,4,192]{0,2,1:T(8,128)(2,1)}), bf16[512,4,192]{0,2,1:T(8,128)(2,1)}, u32[]{:S(2)}, u32[]{:S(2)}) %all-to-all-start.2) | async-done | bytes 786464 | tf_op jit(solution)/shard_map/all_to_all | solution.py:369
  476.7 25.6 %shard_map.316 = (bf16[2048,384]{1,0:T(8,128)(2,1)S(1)}, bf16[2048,384]{1,0:T(8,128)(2,1)S(1)}, bf16[2048,384]{1,0:T(8,128)(2,1)}, bf16[2048,384]{1,0:T(8,128)(2...) custom-call(s32[768]{0:T(1024)S(1)} %reshape.414.index_ref, s32[64]{0:T(128)S(1)} %reshape.447.valid_ref, ...), custom_call_target="tpu_custom_call" | custom-call | flops 4026531840 | bytes 22020096 | tf_op jit(solution)/shard_map/pallas_call | solution.py:227
  514.3 36.4 %collective-permute-done.8 = bf16[2048,384]{1,0:T(8,128)(2,1)S(1)} collective-permute-done((bf16[2048,384]{1,0:T(8,128)(2,1)S(1)}, bf16[2048,384]{1,0:T(8,128)(2,1)S(1)}, u32[]{:S(2)}, u32[]{:S(2)}) %collective-permute-start.8) | collective-permute-done | bytes 1572896 | tf_op jit(solution)/shard_map/ppermute | solution.py:34
  550.7 23.2 %collective-permute-done.9 = bf16[2048,384]{1,0:T(8,128)(2,1)S(1)} collective-permute-done((bf16[2048,384]{1,0:T(8,128)(2,1)}, bf16[2048,384]{1,0:T(8,128)(2,1)S(1)}, u32[]{:S(2)}, u32[]{:S(2)}) %collective-permute-start.9) | collective-permute-done | bytes 1572896 | tf_op jit(solution)/shard_map/ppermute | solution.py:34
  573.9 14.1 %collective-permute-done.10 = bf16[2048,384]{1,0:T(8,128)(2,1)S(1)} collective-permute-done((bf16[2048,384]{1,0:T(8,128)(2,1)}, bf16[2048,384]{1,0:T(8,128)(2,1)S(1)}, u32[]{:S(2)}, u32[]{:S(2)}) %collective-permute-start.10) | collective-permute-done | bytes 1572896 | tf_op jit(solution)/shard_map/ppermute | solution.py:34
  588.0 38.1 %collective-permute-done.11 = bf16[2048,384]{1,0:T(8,128)(2,1)S(1)} collective-permute-done((bf16[2048,384]{1,0:T(8,128)(2,1)}, bf16[2048,384]{1,0:T(8,128)(2,1)S(1)}, u32[]{:S(2)}, u32[]{:S(2)}) %collective-permute-start.11) | collective-permute-done | bytes 1572896 | tf_op jit(solution)/shard_map/ppermute | solution.py:34
  648.3 32.7 %all-to-all-done.3 = bf16[512,4,192]{0,2,1:T(8,128)(2,1)} async-done(((bf16[512,4,192]{0,2,1:T(8,128)(2,1)}), bf16[512,4,192]{0,2,1:T(8,128)(2,1)}, u32[]{:S(2)}, u32[]{:S(2)}) %all-to-all-start.3) | async-done | bytes 786464 | tf_op jit(solution)/shard_map/all_to_all | solution.py:369
  687.4 25.6 %shard_map.317 = (bf16[2048,384]{1,0:T(8,128)(2,1)S(1)}, bf16[2048,384]{1,0:T(8,128)(2,1)S(1)}, bf16[2048,384]{1,0:T(8,128)(2,1)}, bf16[2048,384]{1,0:T(8,128)(2...) custom-call(s32[768]{0:T(1024)S(1)} %reshape.428.index_ref, s32[64]{0:T(128)S(1)} %reshape.451.valid_ref, ...), custom_call_target="tpu_custom_call" | custom-call | flops 4026531840 | bytes 22020096 | tf_op jit(solution)/shard_map/pallas_call | solution.py:227
  725.9 21.2 %collective-permute-done.12 = bf16[2048,384]{1,0:T(8,128)(2,1)S(1)} collective-permute-done((bf16[2048,384]{1,0:T(8,128)(2,1)S(1)}, bf16[2048,384]{1,0:T(8,128)(2,1)S(1)}, u32[]{:S(2)}, u32[]{:S(2)}) %collective-permute-start.12) | collective-permute-done | bytes 1572896 | tf_op jit(solution)/shard_map/ppermute | solution.py:34
  747.2 20.9 %collective-permute-done.13 = bf16[2048,384]{1,0:T(8,128)(2,1)S(1)} collective-permute-done((bf16[2048,384]{1,0:T(8,128)(2,1)}, bf16[2048,384]{1,0:T(8,128)(2,1)S(1)}, u32[]{:S(2)}, u32[]{:S(2)}) %collective-permute-start.13) | collective-permute-done | bytes 1572896 | tf_op jit(solution)/shard_map/ppermute | solution.py:34
  768.1 12.9 %collective-permute-done.14 = bf16[2048,384]{1,0:T(8,128)(2,1)S(1)} collective-permute-done((bf16[2048,384]{1,0:T(8,128)(2,1)}, bf16[2048,384]{1,0:T(8,128)(2,1)S(1)}, u32[]{:S(2)}, u32[]{:S(2)}) %collective-permute-start.14) | collective-permute-done | bytes 1572896 | tf_op jit(solution)/shard_map/ppermute | solution.py:34
  781.0 35.7 %collective-permute-done.15 = bf16[2048,384]{1,0:T(8,128)(2,1)S(1)} collective-permute-done((bf16[2048,384]{1,0:T(8,128)(2,1)}, bf16[2048,384]{1,0:T(8,128)(2,1)S(1)}, u32[]{:S(2)}, u32[]{:S(2)}) %collective-permute-start.15) | collective-permute-done | bytes 1572896 | tf_op jit(solution)/shard_map/ppermute | solution.py:34
  825.4 7.2 fusion.82
  833.0 7.0 fusion.83
  855.1 33.0 %reduce-scatter.6.cloned.1.call-done = bf16[512,768]{1,0:T(8,128)(2,1)} async-done(((bf16[2048,768]{1,0:T(8,128)(2,1)}), bf16[512,768]{1,0:T(8,128)(2,1)}) %reduce-scatter.6.cloned.1.call-update) | async-done | bytes 786448 | tf_op jit(solution)/shard_map/reduce_scatter | solution.py:434
  891.0 39.7 %all-reduce.4 = (f32[3072]{0:T(1024)S(1)}, f32[6144]{0:T(1024)S(1)}) all-reduce(f32[3072]{0:T(1024)S(1)} %pad_maximum_fusion.5, f32[6144]{0:T(1024)S(1)} %constant_dynamic-update-slice_fusion), channel_id=1, replica_groups=mesh['seq'=8,'tp'=4] {'seq','tp'}, use_global_device_ids=true, to_apply=%region_37.38 | all-reduce | flops 9216 | bytes 73728 | tf_op jit(solution)/shard_map/psum | solution.py:481
  952.9 31.7 %all-reduce.8.cloned.1.call-done = (f32[768,192]{0,1:T(8,128)}, f32[768,192]{0,1:T(8,128)}, f32[768,192]{0,1:T(8,128)}) async-done(((f32[768,192]{0,1:T(8,128)}, f32[768,192]{0,1:T(8,128)}, f32[768,192]{0,1:T(8,128)}), (f32[768,192]{0,1:T(8,128)}, f32[768,192]{0,1:T(8,128)}, f32[768,192]{0,1:T(8,128)})) %all-reduce.8.cloned.1.call-update) | async-done | bytes 1769488 | tf_op jit(solution)/shard_map/psum | solution.py:458
  (348 shorter events, 246.3 us)
Async XLA Ops:
  7.2 68.1 %all-gather.9.cloned.1.call-start = ((), (), s32[]{:S(2)}) async-start(), calls=%async_computation.9 | async-start | bytes 3932160 | tf_op jit(solution)/shard_map/all_gather | solution.py:317
  12.9 126.7 %all-gather.5.cloned.1.call-start = ((), (), s32[]{:S(2)}) async-start(), calls=%async_computation.7 | async-start | bytes 3932160 | tf_op jit(solution)/shard_map/all_gather | solution.py:317
  13.7 341.7 %all-gather.7.cloned.1.call-start = ((), (), s32[]{:S(2)}) async-start(), calls=%async_computation.8 | async-start | bytes 11354112 | tf_op jit(solution)/shard_map/all_gather | solution.py:292
  18.6 56.7 %copy-start.17 = (bf16[768,3,128]{0,2,1:T(8,128)(2,1)}, bf16[768,3,128]{0,2,1:T(8,128)(2,1)S(1)}, u32[]{:S(2)}) copy-start(bf16[768,3,128]{0,2,1:T(8,128)(2,1)S(1)} %pad_maximum_fusion.4) | copy-start | bytes 1769476
  79.1 65.6 %copy-start.1 = (bf16[2048,384]{1,0:T(8,128)(2,1)}, bf16[2048,384]{1,0:T(8,128)(2,1)S(1)}, u32[]{:S(2)}) copy-start(bf16[2048,384]{1,0:T(8,128)(2,1)S(1)} %add_convert_fusion.4.refs_2_) | copy-start | bytes 4718596
  79.1 68.7 %collective-permute-start.7 = (bf16[2048,384]{1,0:T(8,128)(2,1)S(1)}, bf16[2048,384]{1,0:T(8,128)(2,1)S(1)}, u32[]{:S(2)}, u32[]{:S(2)}) collective-permute-start(bf16[2048,384]{1,0:T(8,128)(2,1)S(1)} %add_convert_fusion.4.refs_2_), channel_id=1, source_target_pairs={{8,0},{12,4},{16,8},{20,12},{24,16},{28,20},{9,1},{13,5},{17,9},{2... | collective-permute-start | bytes 4718600 | tf_op jit(solution)/shard_map/ppermute | solution.py:34
  82.2 69.7 %collective-permute-start.6 = (bf16[2048,384]{1,0:T(8,128)(2,1)S(1)}, bf16[2048,384]{1,0:T(8,128)(2,1)}, u32[]{:S(2)}, u32[]{:S(2)}) collective-permute-start(bf16[2048,384]{1,0:T(8,128)(2,1)S(1)} %add_convert_fusion.4.refs_2_), channel_id=1, source_target_pairs={{4,0},{8,4},{12,8},{16,12},{20,16},{24,20},{28,24},{5,1},{9,5},{13... | collective-permute-start | bytes 4718600 | tf_op jit(solution)/shard_map/ppermute | solution.py:34
  85.2 70.0 %collective-permute-start.5 = (bf16[2048,384]{1,0:T(8,128)(2,1)S(1)}, bf16[2048,384]{1,0:T(8,128)(2,1)}, u32[]{:S(2)}, u32[]{:S(2)}) collective-permute-start(bf16[2048,384]{1,0:T(8,128)(2,1)S(1)} %add_convert_fusion.4.refs_2_), channel_id=1, source_target_pairs={{0,4},{4,8},{8,12},{12,16},{16,20},{20,24},{24,28},{1,5},{5,9},{9,... | collective-permute-start | bytes 4718600 | tf_op jit(solution)/shard_map/ppermute | solution.py:34
  87.9 108.0 %collective-permute-start.4 = (bf16[2048,384]{1,0:T(8,128)(2,1)S(1)}, bf16[2048,384]{1,0:T(8,128)(2,1)}, u32[]{:S(2)}, u32[]{:S(2)}) collective-permute-start(bf16[2048,384]{1,0:T(8,128)(2,1)S(1)} %add_convert_fusion.4.refs_2_), channel_id=1, source_target_pairs={{0,8},{4,12},{8,16},{12,20},{16,24},{20,28},{1,9},{5,13},{9,17},{1... | collective-permute-start | bytes 4718600 | tf_op jit(solution)/shard_map/ppermute | solution.py:34
  144.8 99.5 %collective-permute-start.3 = (bf16[2048,384]{1,0:T(8,128)(2,1)}, bf16[2048,384]{1,0:T(8,128)(2,1)}, u32[]{:S(2)}, u32[]{:S(2)}) collective-permute-start(bf16[2048,384]{1,0:T(8,128)(2,1)} %add_convert_fusion.5.refs_2_), channel_id=1, source_target_pairs={{8,0},{12,4},{16,8},{20,12},{24,16},{28,20},{9,1},{13,5},{17,9},{2... | collective-permute-start | bytes 4718600 | tf_op jit(solution)/shard_map/ppermute | solution.py:34
  149.0 95.3 %collective-permute-start.2 = (bf16[2048,384]{1,0:T(8,128)(2,1)}, bf16[2048,384]{1,0:T(8,128)(2,1)}, u32[]{:S(2)}, u32[]{:S(2)}) collective-permute-start(bf16[2048,384]{1,0:T(8,128)(2,1)} %add_convert_fusion.5.refs_2_), channel_id=1, source_target_pairs={{4,0},{8,4},{12,8},{16,12},{20,16},{24,20},{28,24},{5,1},{9,5},{13... | collective-permute-start | bytes 4718600 | tf_op jit(solution)/shard_map/ppermute | solution.py:34
  152.0 130.1 %collective-permute-start.1 = (bf16[2048,384]{1,0:T(8,128)(2,1)}, bf16[2048,384]{1,0:T(8,128)(2,1)}, u32[]{:S(2)}, u32[]{:S(2)}) collective-permute-start(bf16[2048,384]{1,0:T(8,128)(2,1)} %add_convert_fusion.5.refs_2_), channel_id=1, source_target_pairs={{0,4},{4,8},{8,12},{12,16},{16,20},{20,24},{24,28},{1,5},{5,9},{9,... | collective-permute-start | bytes 4718600 | tf_op jit(solution)/shard_map/ppermute | solution.py:34
  155.2 161.4 %collective-permute-start = (bf16[2048,384]{1,0:T(8,128)(2,1)}, bf16[2048,384]{1,0:T(8,128)(2,1)}, u32[]{:S(2)}, u32[]{:S(2)}) collective-permute-start(bf16[2048,384]{1,0:T(8,128)(2,1)} %add_convert_fusion.5.refs_2_), channel_id=1, source_target_pairs={{0,8},{4,12},{8,16},{12,20},{16,24},{20,28},{1,9},{5,13},{9,17},{1... | collective-permute-start | bytes 4718600 | tf_op jit(solution)/shard_map/ppermute | solution.py:34
  157.9 38.0 %copy-start.2 = (bf16[2048,384]{1,0:T(8,128)(2,1)S(1)}, bf16[2048,384]{1,0:T(8,128)(2,1)}, u32[]{:S(2)}) copy-start(bf16[2048,384]{1,0:T(8,128)(2,1)} %copy-done.1) | copy-start | bytes 4718596
  222.9 125.4 %all-to-all-start.1 = ((bf16[4,512,192]{1,2,0:T(8,128)(2,1)}), bf16[4,512,192]{1,2,0:T(8,128)(2,1)}, u32[]{:S(2)}, u32[]{:S(2)}) async-start(bf16[4,512,192]{1,2,0:T(8,128)(2,1)} %copy.108), calls=%async_computation.1 | async-start | bytes 1572864 | tf_op jit(solution)/shard_map/all_to_all | solution.py:346
  348.2 22.5 %all-to-all-start = ((bf16[4,512,192]{1,2,0:T(8,128)(2,1)}), bf16[4,512,192]{1,2,0:T(8,128)(2,1)}, u32[]{:S(2)}, u32[]{:S(2)}) async-start(bf16[4,512,192]{1,2,0:T(8,128)(2,1)} %copy.101), calls=%async_computation | async-start | bytes 1572864 | tf_op jit(solution)/shard_map/all_to_all | solution.py:346
  355.2 477.5 %reduce-scatter.8.cloned.1.call-start = ((), (), s32[]{:S(2)}) async-start(), calls=%async_computation.12 | async-start | bytes 11354112 | tf_op jit(solution)/shard_map/reduce_scatter | solution.py:400
  373.4 48.0 %copy-start.11 = (f32[512,768]{1,0:T(8,128)}, f32[512,768]{1,0:T(8,128)S(1)}, u32[]{:S(2)}) copy-start(f32[512,768]{1,0:T(8,128)S(1)} %get-tuple-element.204) | copy-start | bytes 4718596
  446.4 23.9 %all-to-all-start.2 = ((bf16[512,4,192]{0,2,1:T(8,128)(2,1)}), bf16[512,4,192]{0,2,1:T(8,128)(2,1)}, u32[]{:S(2)}, u32[]{:S(2)}) async-start(bf16[512,4,192]{0,2,1:T(8,128)(2,1)} %bitcast.313), calls=%async_computation.2 | async-start | bytes 1572864 | tf_op jit(solution)/shard_map/all_to_all | solution.py:369
  454.7 400.4 %reduce-scatter.4.cloned.1.call-start = ((), (), s32[]{:S(2)}) async-start(), calls=%async_computation.10 | async-start | bytes 3932160 | tf_op jit(solution)/shard_map/reduce_scatter | solution.py:434
  502.3 48.3 %collective-permute-start.8 = (bf16[2048,384]{1,0:T(8,128)(2,1)S(1)}, bf16[2048,384]{1,0:T(8,128)(2,1)S(1)}, u32[]{:S(2)}, u32[]{:S(2)}) collective-permute-start(bf16[2048,384]{1,0:T(8,128)(2,1)S(1)} %get-tuple-element.38), channel_id=1, source_target_pairs={{8,0},{12,4},{16,8},{20,12},{24,16},{28,20},{9,1},{13,5},{17,9},{2... | collective-permute-start | bytes 4718600 | tf_op jit(solution)/shard_map/ppermute | solution.py:34
  504.3 69.6 %collective-permute-start.9 = (bf16[2048,384]{1,0:T(8,128)(2,1)}, bf16[2048,384]{1,0:T(8,128)(2,1)S(1)}, u32[]{:S(2)}, u32[]{:S(2)}) collective-permute-start(bf16[2048,384]{1,0:T(8,128)(2,1)} %get-tuple-element.39), channel_id=1, source_target_pairs={{4,0},{8,4},{12,8},{16,12},{20,16},{24,20},{28,24},{5,1},{9,5},{13... | collective-permute-start | bytes 4718600 | tf_op jit(solution)/shard_map/ppermute | solution.py:34
  508.7 79.3 %collective-permute-start.10 = (bf16[2048,384]{1,0:T(8,128)(2,1)}, bf16[2048,384]{1,0:T(8,128)(2,1)S(1)}, u32[]{:S(2)}, u32[]{:S(2)}) collective-permute-start(bf16[2048,384]{1,0:T(8,128)(2,1)} %get-tuple-element.40), channel_id=1, source_target_pairs={{0,4},{4,8},{8,12},{12,16},{16,20},{20,24},{24,28},{1,5},{5,9},{9,... | collective-permute-start | bytes 4718600 | tf_op jit(solution)/shard_map/ppermute | solution.py:34
  512.3 113.7 %collective-permute-start.11 = (bf16[2048,384]{1,0:T(8,128)(2,1)}, bf16[2048,384]{1,0:T(8,128)(2,1)S(1)}, u32[]{:S(2)}, u32[]{:S(2)}) collective-permute-start(bf16[2048,384]{1,0:T(8,128)(2,1)} %get-tuple-element.41), channel_id=1, source_target_pairs={{0,8},{4,12},{8,16},{12,20},{16,24},{20,28},{1,9},{5,13},{9,17},{1... | collective-permute-start | bytes 4718600 | tf_op jit(solution)/shard_map/ppermute | solution.py:34
  639.7 41.3 %all-to-all-start.3 = ((bf16[512,4,192]{0,2,1:T(8,128)(2,1)}), bf16[512,4,192]{0,2,1:T(8,128)(2,1)}, u32[]{:S(2)}, u32[]{:S(2)}) async-start(bf16[512,4,192]{0,2,1:T(8,128)(2,1)} %bitcast.314), calls=%async_computation.4 | async-start | bytes 1572864 | tf_op jit(solution)/shard_map/all_to_all | solution.py:369
  644.3 243.8 %reduce-scatter.6.cloned.1.call-start = ((), (), s32[]{:S(2)}) async-start(), calls=%async_computation.11 | async-start | bytes 3932160 | tf_op jit(solution)/shard_map/reduce_scatter | solution.py:434
  713.0 34.2 %collective-permute-start.12 = (bf16[2048,384]{1,0:T(8,128)(2,1)S(1)}, bf16[2048,384]{1,0:T(8,128)(2,1)S(1)}, u32[]{:S(2)}, u32[]{:S(2)}) collective-permute-start(bf16[2048,384]{1,0:T(8,128)(2,1)S(1)} %get-tuple-element.45), channel_id=1, source_target_pairs={{8,0},{12,4},{16,8},{20,12},{24,16},{28,20},{9,1},{13,5},{17,9},{2... | collective-permute-start | bytes 4718600 | tf_op jit(solution)/shard_map/ppermute | solution.py:34
  715.8 52.3 %collective-permute-start.13 = (bf16[2048,384]{1,0:T(8,128)(2,1)}, bf16[2048,384]{1,0:T(8,128)(2,1)S(1)}, u32[]{:S(2)}, u32[]{:S(2)}) collective-permute-start(bf16[2048,384]{1,0:T(8,128)(2,1)} %get-tuple-element.46), channel_id=1, source_target_pairs={{4,0},{8,4},{12,8},{16,12},{20,16},{24,20},{28,24},{5,1},{9,5},{13... | collective-permute-start | bytes 4718600 | tf_op jit(solution)/shard_map/ppermute | solution.py:34
  720.4 60.6 %collective-permute-start.14 = (bf16[2048,384]{1,0:T(8,128)(2,1)}, bf16[2048,384]{1,0:T(8,128)(2,1)S(1)}, u32[]{:S(2)}, u32[]{:S(2)}) collective-permute-start(bf16[2048,384]{1,0:T(8,128)(2,1)} %get-tuple-element.47), channel_id=1, source_target_pairs={{0,4},{4,8},{8,12},{12,16},{16,20},{20,24},{24,28},{1,5},{5,9},{9,... | collective-permute-start | bytes 4718600 | tf_op jit(solution)/shard_map/ppermute | solution.py:34
  724.0 92.7 %collective-permute-start.15 = (bf16[2048,384]{1,0:T(8,128)(2,1)}, bf16[2048,384]{1,0:T(8,128)(2,1)S(1)}, u32[]{:S(2)}, u32[]{:S(2)}) collective-permute-start(bf16[2048,384]{1,0:T(8,128)(2,1)} %get-tuple-element.48), channel_id=1, source_target_pairs={{0,8},{4,12},{8,16},{12,20},{16,24},{20,28},{1,9},{5,13},{9,17},{1... | collective-permute-start | bytes 4718600 | tf_op jit(solution)/shard_map/ppermute | solution.py:34
  824.8 116.6 %all-gather.11.cloned.1.call-start = ((), (), s32[]{:S(2)}) async-start(), calls=%async_computation.13 | async-start | bytes 3096576 | tf_op jit(solution)/shard_map/all_gather | solution.py:401
  832.7 151.9 %all-reduce.8.cloned.1.call-start = ((), (), s32[]{:S(2)}) async-start(), calls=%async_computation.14 | async-start | bytes 3538944 | tf_op jit(solution)/shard_map/psum | solution.py:458
  (64 other events, 532.5 us)
Sparse Core Ops, SparseCore 0:
  13.0 62.2 all-gather.8
  77.5 62.1 all-gather.4
  143.1 115.4 all-gather.6
  440.1 160.3 reduce-scatter.7
  634.3 77.2 reduce-scatter.3
  824.9 63.1 reduce-scatter.5
  890.0 31.7 all-gather.10
  925.9 58.6 all-reduce.7

commit v2 on v1

v2 whole, which is shorter than its diff:
```python
import functools
import math

import jax
import jax.numpy as jnp
from jax import lax
from jax.experimental import pallas as pl
from jax.experimental.pallas import tpu as pltpu
from jax.sharding import PartitionSpec as P

BLOCK = 64
LONG_BLK = 64
SHORT_BLK = 8
PAIR = 2 * BLOCK
UNROLL = 4
SEQ = "seq"
TP = "tp"

NORM_EPS = 1e-05
MASKED = -1000000000.0

f32 = jnp.float32
bf16 = jnp.bfloat16

NN = (((1,), (0,)), ((), ()))
NT = (((1,), (1,)), ((), ()))
TN = (((0,), (0,)), ((), ()))


def contract(left, right, dims):
    return lax.dot_general(left, right, dims, preferred_element_type=f32)


def from_behind(block, axis, distance):
    devices = range(lax.axis_size(axis))
    route = [(i - distance, i) for i in devices if i - distance in devices]
    return lax.ppermute(block, axis, route)


def gelu_exact(values):
    return 0.5 * values * (1.0 + lax.erf(values / math.sqrt(2.0)))


def gelu_grad(values, grad_rows):
    _, pull_back = jax.vjp(gelu_exact, values)
    return pull_back(grad_rows)[0]


def layer_stats(values, norm_gain, norm_shift):
    row_mean = jnp.mean(values, axis=-1, keepdims=True)
    centred = values - row_mean
    inverse = lax.rsqrt(jnp.mean(centred * centred, axis=-1, keepdims=True) + NORM_EPS)
    normed = centred * inverse
    return (normed * norm_gain + norm_shift, normed, inverse)


def layer_back(grad_rows, normed, inverse, norm_gain):
    scaled = grad_rows * norm_gain
    inner_term = (
        scaled
        - jnp.mean(scaled, axis=-1, keepdims=True)
        - normed * jnp.mean(scaled * normed, axis=-1, keepdims=True)
    )
    return (inverse * inner_term, jnp.sum(grad_rows * normed, axis=0), jnp.sum(grad_rows, axis=0))


def block_keys(lengths, randoms, blocks):
    doc_ends = jnp.cumsum(lengths)
    doc_starts = doc_ends - lengths
    doc_owner = jnp.sum((blocks[:, None] >= doc_ends[None, :]).astype(jnp.int32), axis=1)
    doc_ids = jnp.arange(lengths.shape[0], dtype=jnp.int32)
    doc_hit = doc_owner[:, None] == doc_ids[None, :]
    doc_first = jnp.sum(jnp.where(doc_hit, doc_starts[None, :], 0), axis=1)
    doc_final = jnp.sum(jnp.where(doc_hit, doc_ends[None, :], 0), axis=1)
    fixed_keys = jnp.stack(
        [
            jnp.maximum(blocks - 1, doc_first),
            jnp.minimum(blocks + 1, doc_final - 1),
            blocks,
            doc_first,
            doc_first + 1,
        ],
        axis=1,
    )
    block_count = randoms.shape[0]
    head_count = randoms.shape[1]
    key_index = jnp.concatenate(
        [jnp.broadcast_to(fixed_keys[:, None, :], (block_count, head_count, 5)), randoms], axis=2
    )
    key_valid = jnp.stack([blocks > doc_first, blocks + 1 < doc_final], axis=1)
    return (key_index, key_valid.astype(jnp.int32))


def block_rows(block):
    return pl.ds(pl.multiple_of(block * BLOCK, BLOCK), BLOCK)


def listed_blocks(index_ref, store, base, slots):
    return jnp.concatenate(
        [store[block_rows(index_ref[base + slot]), :] for slot in range(slots)], axis=0
    )


def mask_scores(scores, valid_ref, block):
    lane = lax.broadcasted_iota(jnp.int32, (1, PAIR), 1)
    keep = jnp.where(lane < BLOCK, valid_ref[2 * block], valid_ref[2 * block + 1]) > 0
    return jnp.concatenate([jnp.where(keep, scores[:, :PAIR], MASKED), scores[:, PAIR:]], axis=1)


def fill_store(store, pieces):
    place = 0
    for piece in pieces:
        store[place : place + piece.shape[0], :] = piece[...]
        place += piece.shape[0]


def each_head(heads, work):
    for head in range(heads):

        @pl.when(pl.program_id(0) == head)
        def _():
            work(slice(head * BLOCK, (head + 1) * BLOCK))


def forward_kernel(slots, heads, index_ref, valid_ref, query_ref, *refs):
    *pieces, context_ref, logsum_ref, store, wide_query, wide_context = refs
    rows = query_ref.shape[0]
    blocks = rows // BLOCK
    head = pl.program_id(0)
    fill_store(store, pieces)

    def take_query(columns):
        query = query_ref[:, columns]
        wide_query[...] = jnp.concatenate([query, jnp.zeros_like(query)], axis=1)

    each_head(heads, take_query)

    def step(group, carry):
        ids = [group * UNROLL + unit for unit in range(UNROLL)]
        listed = [
            listed_blocks(index_ref, store, (head * blocks + block) * slots, slots)
            for block in ids
        ]
        scores = [
            mask_scores(contract(wide_query[block_rows(block), :], pairs, NT), valid_ref, block)
            for block, pairs in zip(ids, listed)
        ]
        probs = []
        for block, score in zip(ids, scores):
            top = jnp.max(score, axis=1, keepdims=True)
            raised = jnp.exp(score - top)
            total = jnp.sum(raised, axis=1, keepdims=True)
            probs.append((raised * (1.0 / total)).astype(bf16))
            logsum_ref[block_rows(block), :] = jnp.broadcast_to(
                top + jnp.log(total), (BLOCK, PAIR)
            )
        for block, prob, pairs in zip(ids, probs, listed):
            wide_context[block_rows(block), :] = contract(prob, pairs, NN).astype(bf16)
        return carry

    lax.fori_loop(0, blocks // UNROLL, step, 0)

    def give_context(columns):
        context_ref[:, columns] = wide_context[:, BLOCK:]

    each_head(heads, give_context)


def backward_kernel(slots, heads, count, index_ref, valid_ref, query_ref, grad_ref, logsum_ref, *refs):
    pieces = refs[:count]
    grad_query_ref = refs[count]
    grad_pieces = refs[count + 1 : 2 * count + 1]
    store, sums, both_rows, wide_grad = refs[2 * count + 1 :]
    rows = query_ref.shape[0]
    blocks = rows // BLOCK
    head = pl.program_id(0)
    fill_store(store, pieces)
    sums[...] = jnp.zeros_like(sums)
    lane = lax.broadcasted_iota(jnp.int32, (BLOCK, PAIR), 1)

    def take_both(columns):
        both_rows[...] = jnp.concatenate([query_ref[:, columns], grad_ref[:, columns]], axis=1)

    each_head(heads, take_both)

    def step(group, carry):
        ids = [group * UNROLL + unit for unit in range(UNROLL)]
        listed = [
            listed_blocks(index_ref, store, (head * blocks + block) * slots, slots)
            for block in ids
        ]
        lefts = []
        for block in ids:
            both = both_rows[block_rows(block), :]
            lefts.append(
                jnp.concatenate(
                    [
                        jnp.where(lane < BLOCK, both, 0).astype(bf16),
                        jnp.where(lane < BLOCK, 0, both).astype(bf16),
                    ],
                    axis=0,
                )
            )
        products = [contract(left, pairs, NT) for left, pairs in zip(lefts, listed)]
        mixes = []
        for block, product in zip(ids, products):
            score = mask_scores(product[:BLOCK], valid_ref, block)
            grad_prob = product[BLOCK:]
            logsum = jnp.concatenate([logsum_ref[block_rows(block), :]] * (slots // 2), axis=1)
            prob = jnp.exp(score - logsum)
            delta = jnp.sum(prob * grad_prob, axis=1, keepdims=True)
            grad_score = prob * (grad_prob - delta)
            mixes.append(jnp.concatenate([grad_score.astype(bf16), prob.astype(bf16)], axis=0))
        for block, mix, pairs in zip(ids, mixes, listed):
            wide_grad[block_rows(block), :] = contract(mix[:BLOCK], pairs, NN).astype(bf16)
        terms = [contract(mix, left, TN) for mix, left in zip(mixes, lefts)]
        for block, term in zip(ids, terms):
            base = (head * blocks + block) * slots
            for slot in range(slots):
                sums[block_rows(index_ref[base + slot]), :] += term[
                    slot * BLOCK : (slot + 1) * BLOCK
                ]
        return carry

    lax.fori_loop(0, blocks // UNROLL, step, 0)
    place = 0
    for grad_piece in grad_pieces:
        grad_piece[...] = sums[place : place + grad_piece.shape[0], :].astype(bf16)
        place += grad_piece.shape[0]

    def give_grad(columns):
        grad_query_ref[:, columns] = wide_grad[:, :BLOCK]

    each_head(heads, give_grad)


def lasting(microseconds):
    return pl.CostEstimate(
        flops=0, bytes_accessed=int(microseconds * 3.69e6), transcendentals=0
    )


def per_head(array):
    return pl.BlockSpec((array.shape[0], PAIR), lambda head, *_: (0, head))


def whole(array):
    return pl.BlockSpec(array.shape, lambda head, *_: (0, 0))


def attend_forward(index, valid, queries, pieces, heads, slots):
    rows = queries.shape[0]
    stored = sum(piece.shape[0] for piece in pieces)
    logsum = jax.ShapeDtypeStruct((rows, heads * PAIR), f32)
    return pl.pallas_call(
        functools.partial(forward_kernel, slots, heads),
        grid_spec=pltpu.PrefetchScalarGridSpec(
            num_scalar_prefetch=2,
            grid=(heads,),
            in_specs=[whole(queries)] + [per_head(piece) for piece in pieces],
            out_specs=[whole(queries), per_head(logsum)],
            scratch_shapes=[
                pltpu.VMEM((stored, PAIR), bf16),
                pltpu.VMEM((rows, PAIR), bf16),
                pltpu.VMEM((rows, PAIR), bf16),
            ],
        ),
        out_shape=[jax.ShapeDtypeStruct(queries.shape, bf16), logsum],
        compiler_params=pltpu.CompilerParams(vmem_limit_bytes=40 * 2**20),
        cost_estimate=lasting(18),
    )(index, valid, queries, *pieces)


def attend_backward(index, valid, queries, grads, logsum, pieces, heads, slots):
    rows = queries.shape[0]
    stored = sum(piece.shape[0] for piece in pieces)
    piece_specs = [per_head(piece) for piece in pieces]
    return pl.pallas_call(
        functools.partial(backward_kernel, slots, heads, len(pieces)),
        grid_spec=pltpu.PrefetchScalarGridSpec(
            num_scalar_prefetch=2,
            grid=(heads,),
            in_specs=[whole(queries), whole(grads), per_head(logsum)] + piece_specs,
            out_specs=[whole(queries)] + piece_specs,
            scratch_shapes=[
                pltpu.VMEM((stored, PAIR), bf16),
                pltpu.VMEM((stored, PAIR), f32),
                pltpu.VMEM((rows, PAIR), bf16),
                pltpu.VMEM((rows, PAIR), bf16),
            ],
        ),
        out_shape=[jax.ShapeDtypeStruct(queries.shape, bf16)]
        + [jax.ShapeDtypeStruct(piece.shape, bf16) for piece in pieces],
        compiler_params=pltpu.CompilerParams(vmem_limit_bytes=50 * 2**20),
        cost_estimate=lasting(25),
    )(index, valid, queries, grads, logsum, *pieces)


def plane_exchange(values, split_axis, concat_axis):
    count = lax.axis_size(SEQ)
    groups = [list(range(place, count, 2)) for place in range(2)]
    return lax.all_to_all(
        values,
        SEQ,
        split_axis=split_axis,
        concat_axis=concat_axis,
        axis_index_groups=groups,
        tiled=True,
    )


def plane_gather(values):
    count = lax.axis_size(SEQ) // 2
    return plane_exchange(jnp.concatenate([values] * count, axis=0), 0, 0)


def core_swap(block):
    route = [(place, place ^ 1) for place in range(lax.axis_size(SEQ))]
    return lax.ppermute(block, SEQ, route)


def column_shift(block, step):
    count = lax.axis_size(TP)
    return lax.ppermute(block, TP, [(place, (place + step) % count) for place in range(count)])


def column_gather(values):
    count = lax.axis_size(TP)
    place = lax.axis_index(TP)
    spread = jnp.zeros((count,) + values.shape, values.dtype)
    spread = lax.dynamic_update_index_in_dim(spread, values, place, axis=0)
    for step in range(1, count):
        spread = lax.dynamic_update_index_in_dim(
            spread, column_shift(values, step), (place - step) % count, axis=0
        )
    return spread


def after(values, *earlier):
    return lax.optimization_barrier((values, earlier))[0]


def sum_parts(parts):
    total = parts[0].astype(f32)
    for place in range(1, len(parts)):
        total = total + parts[place].astype(f32)
    return total


def partner_of(place):
    return place + 1 - 2 * (place % 2)


def enter(neighbours):
    barrier = pltpu.get_barrier_semaphore()
    count = 0
    for exists, device in neighbours:

        @pl.when(exists)
        def _():
            pl.semaphore_signal(
                barrier, inc=1, device_id=device, device_id_type=pl.DeviceIdType.MESH
            )

        count = count + jnp.where(exists, 1, 0)
    pl.semaphore_wait(barrier, count)


def remote(source, target, send, receive, device):
    return pltpu.make_async_remote_copy(
        src_ref=source,
        dst_ref=target,
        send_sem=send,
        recv_sem=receive,
        device_id=device,
        device_id_type=pl.DeviceIdType.MESH,
    )


def column_reduce_kernel(
    parts,
    near_ref,
    far_ref,
    out_ref,
    sums,
    given,
    came,
    load_sem,
    send_far,
    recv_far,
    send_z,
    recv_z,
):
    count = lax.axis_size(TP)
    place = lax.axis_index(TP)
    other = {SEQ: partner_of(lax.axis_index(SEQ))}
    rows = out_ref.shape[0] // parts
    step_rows = 128
    load = pltpu.make_async_copy(near_ref, sums, load_sem)
    load.start()
    enter(
        [
            (place >= 0, other),
            (place < count - 1, {TP: place + 1}),
            (place > 0, {TP: place - 1}),
        ]
    )

    def cut(part):
        return pl.ds(part * rows, rows)

    def across(owner):
        return remote(
            far_ref.at[owner], given.at[owner], send_far.at[owner], recv_far.at[owner], other
        )

    def along(way, owner, part):
        return remote(
            sums.at[owner, cut(part)],
            came.at[way, owner, cut(part)],
            send_z.at[way, owner, part],
            recv_z.at[way, owner, part],
            {TP: place - 1 if way == 0 else place + 1},
        )

    def add(owner, source, part):
        @pl.loop(0, rows // step_rows)
        def _(step):
            at = pl.ds(pl.multiple_of(part * rows + step * step_rows, step_rows), step_rows)
            total = sums[owner, at, :].astype(f32) + source[at, :].astype(f32)
            sums[owner, at, :] = total.astype(sums.dtype)

    order = []
    for step in range(count):
        for owner in (step, count - 1 - step):
            if owner not in order:
                order.append(owner)
    for owner in order:
        across(owner).start()
    load.wait()
    for owner in order:
        across(owner).wait_recv()
        for part in range(parts):
            add(owner, given.at[owner], part)
            for way in range(2):
                passes = place > owner if way == 0 else place < owner
                takes = (place < count - 1) if way == 0 else (place > 0)

                @pl.when(passes)
                def _():
                    @pl.when(takes)
                    def _():
                        along(way, owner, part).wait_recv()
                        add(owner, came.at[way, owner], part)

                    along(way, owner, part).start()

    for part in range(parts):
        for way in range(2):
            for owner in range(count):
                takes = (place < count - 1) if way == 0 else (place > 0)

                @pl.when((place == owner) & takes)
                def _():
                    along(way, owner, part).wait_recv()
                    add(owner, came.at[way, owner], part)

    for owner in range(count):

        @pl.when(place == owner)
        def _():
            out_ref[...] = sums[owner]

        across(owner).wait_send()
        for part in range(parts):
            for way in range(2):

                @pl.when(place > owner if way == 0 else place < owner)
                def _():
                    along(way, owner, part).wait_send()


def column_reduce_both(near, far, collective_id, parts=2):
    count = lax.axis_size(TP)
    block = near.shape[1:]
    return pl.pallas_call(
        functools.partial(column_reduce_kernel, parts),
        out_shape=jax.ShapeDtypeStruct(block, near.dtype),
        in_specs=[pl.BlockSpec(memory_space=pl.ANY), pl.BlockSpec(memory_space=pltpu.VMEM)],
        out_specs=pl.BlockSpec(memory_space=pltpu.VMEM),
        scratch_shapes=[
            pltpu.VMEM((count,) + block, near.dtype),
            pltpu.VMEM((count,) + block, near.dtype),
            pltpu.VMEM((2, count) + block, near.dtype),
            pltpu.SemaphoreType.DMA,
            pltpu.SemaphoreType.DMA((count,)),
            pltpu.SemaphoreType.DMA((count,)),
            pltpu.SemaphoreType.DMA((2, count, parts)),
            pltpu.SemaphoreType.DMA((2, count, parts)),
        ],
        compiler_params=pltpu.CompilerParams(
            collective_id=collective_id, has_side_effects=True, vmem_limit_bytes=32 * 2**20
        ),
        cost_estimate=lasting(55),
    )(near, far)


def plane_ids():
    seq_place = lax.axis_index(SEQ)
    chip, core = seq_place // 2, seq_place % 2
    beside = chip + 1 - 2 * (chip % 2)
    above = chip + 2 - 4 * (chip // 2)
    facing = 3 - chip
    return chip, core, beside, above, facing


def column_way(place, way, distance):
    return place - distance if way == 0 else place + distance


class ColumnSpread:

    def __init__(self, parts, own, near, far, other, keep_sem, along_sems, across_sems):
        self.parts, self.own, self.near, self.far = parts, own, near, far
        self.other, self.keep_sem = other, keep_sem
        self.along_sems, self.across_sems = along_sems, across_sems
        self.count = lax.axis_size(TP)
        self.place = lax.axis_index(TP)
        self.rows = own.shape[0] // parts

    def cut(self, part):
        return pl.ds(part * self.rows, self.rows)

    def block(self, way, distance, part):
        if distance == 0:
            return self.own.at[self.cut(part)]
        return self.near.at[column_way(self.place, way, distance), self.cut(part)]

    def along(self, way, distance, part):
        return remote(
            self.block(way, distance, part),
            self.near.at[column_way(self.place, way, distance), self.cut(part)],
            self.along_sems[0].at[way, distance, part],
            self.along_sems[1].at[way, distance, part],
            {TP: self.place + 1 if way == 0 else self.place - 1},
        )

    def landed(self, way, distance, part):
        block = self.near.at[column_way(self.place, way, distance), self.cut(part)]
        return remote(
            block,
            block,
            self.along_sems[0].at[way, distance, part],
            self.along_sems[1].at[way, distance - 1, part],
            self.other,
        )

    def across(self, way, distance, part):
        return remote(
            self.block(way, distance, part),
            self.far.at[column_way(self.place, way, distance), self.cut(part)],
            self.across_sems[0].at[way, distance, part],
            self.across_sems[1].at[way, distance, part],
            self.other,
        )

    def keep(self):
        return pltpu.make_async_copy(self.own, self.near.at[self.place], self.keep_sem)

    def goes_on(self, way):
        return self.place < self.count - 1 if way == 0 else self.place > 0

    def has_come(self, way, distance):
        if way == 0:
            return self.place >= distance
        return self.place + distance < self.count

    def start(self):
        for part in range(self.parts):
            for way in range(2):

                @pl.when(self.goes_on(way))
                def _():
                    self.along(way, 0, part).start()

        if self.far is not None:
            for part in range(self.parts):
                self.across(0, 0, part).start()
        self.keep().start()

    def step(self, distance, part):
        for way in range(2):

            @pl.when(self.has_come(way, distance))
            def _():
                self.landed(way, distance, part).wait_recv()
                if distance < self.count - 1:

                    @pl.when(self.goes_on(way))
                    def _():
                        self.along(way, distance, part).start()

                if self.far is not None:
                    self.across(way, distance, part).start()

    def finish(self):
        self.keep().wait()
        for part in range(self.parts):
            if self.far is not None:
                self.across(0, 0, part).wait()
            for way in range(2):

                @pl.when(self.goes_on(way))
                def _():
                    self.along(way, 0, part).wait_send()

        for distance in range(1, self.count):
            for part in range(self.parts):
                for way in range(2):

                    @pl.when(self.has_come(way, distance))
                    def _():
                        if distance < self.count - 1:

                            @pl.when(self.goes_on(way))
                            def _():
                                self.along(way, distance, part).wait_send()

                        if self.far is not None:
                            self.across(way, distance, part).wait()


class PlaneSpread:

    def __init__(self, own, out, sems):
        self.own, self.out = own, out
        self.send_row, self.recv_row, self.send_on, self.recv_on = sems
        self.chip, core, beside, above, self.facing = plane_ids()
        self.ways = ({SEQ: 2 * beside + core}, {SEQ: 2 * above + core})
        self.chips = (beside, above)

    def first(self, way, part):
        return remote(
            self.own(part),
            self.out(self.chip, part),
            self.send_row.at[way, part],
            self.recv_row.at[way, part],
            self.ways[way],
        )

    def second(self, way):
        return remote(
            self.out(self.chips[way], way),
            self.out(self.chips[way], way),
            self.send_on.at[way],
            self.recv_on.at[way],
            self.ways[1 - way],
        )

    def start(self):
        self.first(0, 0).start()
        self.first(1, 1).start()

    def forward(self):
        for way in range(2):
            self.first(way, way).wait_recv()
            self.second(way).start()
        for way in range(2):
            self.first(way, 1 - way).start()

    def arrive(self):
        for way in range(2):
            self.first(way, 1 - way).wait_recv()
        for way in range(2):
            self.second(way).wait_recv()

    def finish(self):
        for way in range(2):
            self.second(way).wait_send()
            for part in range(2):
                self.first(way, part).wait_send()


def plane_sems():
    dma = pltpu.SemaphoreType.DMA
    return [dma((2, 2)), dma((2, 2)), dma((2,)), dma((2,))]


def column_sems(parts):
    sems = pltpu.SemaphoreType.DMA((2, 4, parts))
    return [sems, sems, sems, sems]


def halves_of(own, out, keep_sem):
    half = own.shape[0] // 2
    chip = plane_ids()[0]
    return (
        lambda part: own.at[pl.ds(part * half, half)],
        lambda place, part: out.at[place, pl.ds(part * half, half)],
        pltpu.make_async_copy(own, out.at[chip], keep_sem),
    )


def neighbours(facing_too, column_too):
    chip, core, beside, above, facing = plane_ids()
    count = lax.axis_size(TP)
    place = lax.axis_index(TP)
    always = place >= 0
    devices = [(always, {SEQ: 2 * chip + 1 - core})]
    devices += [(always, {SEQ: 2 * beside + core}), (always, {SEQ: 2 * above + core})]
    if facing_too:
        devices.append((always, {SEQ: 2 * facing + core}))
    if column_too:
        for step in range(1, count):
            devices.append((always, {TP: lax.rem(place + step, count)}))
    else:
        devices.append((place < count - 1, {TP: place + 1}))
        devices.append((place > 0, {TP: place - 1}))
    return devices


def first_kernel(
    parts,
    own_ref,
    weight_ref,
    share_ref,
    random_ref,
    out_ref,
    spread_ref,
    column_ref,
    random_out_ref,
    randoms,
    own_sem,
    send_row,
    recv_row,
    send_on,
    recv_on,
    send_z,
    recv_z,
    send_far,
    recv_far,
    send_random,
    recv_random,
    send_column,
    recv_column,
    send_share,
    recv_share,
):
    chip, core, beside, above, facing = plane_ids()
    tp_count = lax.axis_size(TP)
    place = lax.axis_index(TP)
    other = {SEQ: 2 * chip + 1 - core}
    weight_rows = weight_ref.shape[0] // (2 * parts)
    column = [{TP: lax.rem(place + step, tp_count)} for step in range(1, tp_count)]
    enter(neighbours(True, True))
    own, out, keep_rows = halves_of(own_ref, out_ref, own_sem.at[0])
    rows = PlaneSpread(own, out, (send_row, recv_row, send_on, recv_on))
    shares = ColumnSpread(
        1, share_ref, column_ref, None, other, own_sem.at[2], (send_share, recv_share), None
    )

    def weight_cut(part, holder):
        return pl.ds((holder * parts + part) * weight_rows, weight_rows)

    def weight_along(source, way, part):
        at = weight_cut(part, core)
        return remote(
            source.at[at],
            spread_ref.at[at],
            send_z.at[way, part],
            recv_z.at[part],
            {TP: place + 1 if way == 0 else place - 1},
        )

    def weight_across(part):
        at = weight_cut(part, core)
        return remote(
            spread_ref.at[at], spread_ref.at[at], send_far.at[part], recv_far.at[part], other
        )

    def goes_on(way):
        if way == 0:
            return (place >= chip) & (place < tp_count - 1)
        return (place <= chip) & (place > 0)

    def random_to_holder(sender):
        return remote(
            random_ref,
            randoms.at[sender],
            send_random,
            recv_random.at[sender],
            {SEQ: 2 * place + core},
        )

    def random_along(step):
        return remote(
            randoms,
            random_out_ref,
            send_column.at[step],
            recv_column,
            column[step],
        )

    rows.start()

    @pl.when(place != chip)
    def _():
        random_to_holder(chip).start()

    for part in range(parts):
        for way in range(2):

            @pl.when((place == chip) & goes_on(way))
            def _():
                weight_along(weight_ref, way, part).start()

    shares.start()
    keep_rows.start()

    @pl.when(place == chip)
    def _():
        keep = pltpu.make_async_copy(weight_ref, spread_ref, own_sem.at[1])
        keep.start()
        keep.wait()
        randoms[chip] = random_ref[...]
        for step in range(1, tp_count):
            random_to_holder(lax.rem(chip + step, tp_count)).wait_recv()
        random_out_ref[...] = randoms[...]
        for step in range(tp_count - 1):
            random_along(step).start()

    rows.forward()
    for part in range(parts):

        @pl.when(place != chip)
        def _():
            weight_along(spread_ref, 0, part).wait_recv()
            for way in range(2):

                @pl.when(goes_on(way))
                def _():
                    weight_along(spread_ref, way, part).start()

            weight_across(part).start()

    for distance in range(1, tp_count):
        shares.step(distance, 0)
    rows.arrive()
    rows.finish()
    shares.finish()
    keep_rows.wait()

    @pl.when(place != chip)
    def _():
        random_to_holder(chip).wait_send()
        random_along(0).wait_recv()

    @pl.when(place == chip)
    def _():
        for step in range(tp_count - 1):
            random_along(step).wait_send()

    for part in range(parts):

        @pl.when(place != chip)
        def _():
            weight_across(part).wait()

        for way in range(2):

            @pl.when(goes_on(way))
            def _():
                weight_along(spread_ref, way, part).wait_send()


def first_exchange(own, weight, share, randoms, collective_id, parts=2):
    chips = lax.axis_size(SEQ) // 2
    count = lax.axis_size(TP)
    resident = pl.BlockSpec(memory_space=pltpu.VMEM)
    dma = pltpu.SemaphoreType.DMA
    return pl.pallas_call(
        functools.partial(first_kernel, parts),
        out_shape=[
            jax.ShapeDtypeStruct((chips,) + own.shape, own.dtype),
            jax.ShapeDtypeStruct(weight.shape, weight.dtype),
            jax.ShapeDtypeStruct((count,) + share.shape, share.dtype),
            jax.ShapeDtypeStruct((chips,) + randoms.shape, randoms.dtype),
        ],
        in_specs=[resident] * 4,
        out_specs=[resident] * 4,
        scratch_shapes=[pltpu.VMEM((chips,) + randoms.shape, randoms.dtype), dma((3,))]
        + plane_sems()
        + [
            dma((2, parts)),
            dma((parts,)),
            dma((parts,)),
            dma((parts,)),
            dma,
            dma((chips,)),
            dma((chips - 1,)),
            dma,
        ]
        + column_sems(1)[:2],
        compiler_params=pltpu.CompilerParams(
            collective_id=collective_id, has_side_effects=True, vmem_limit_bytes=32 * 2**20
        ),
        cost_estimate=lasting(30),
    )(own, weight, share, randoms)


def second_kernel(parts, longs_ref, own_ref, near_ref, far_ref, out_ref, keep_sem, *sems):
    chip, core = plane_ids()[:2]
    enter(neighbours(False, False))
    other = {SEQ: 2 * chip + 1 - core}
    longs = ColumnSpread(
        parts, longs_ref, near_ref, far_ref, other, keep_sem.at[0], sems[:2], sems[2:4]
    )
    own, out, keep_rows = halves_of(own_ref, out_ref, keep_sem.at[1])
    rows = PlaneSpread(own, out, sems[4:])
    longs.start()
    rows.start()
    keep_rows.start()
    rows.forward()
    for distance in range(1, longs.count):
        for part in range(parts):
            longs.step(distance, part)
    rows.arrive()
    rows.finish()
    longs.finish()
    keep_rows.wait()


def second_exchange(longs, own, collective_id, parts=2):
    chips = lax.axis_size(SEQ) // 2
    near = jax.ShapeDtypeStruct((lax.axis_size(TP),) + longs.shape, longs.dtype)
    resident = pl.BlockSpec(memory_space=pltpu.VMEM)
    return pl.pallas_call(
        functools.partial(second_kernel, parts),
        out_shape=[near, near, jax.ShapeDtypeStruct((chips,) + own.shape, own.dtype)],
        in_specs=[resident] * 2,
        out_specs=[resident] * 3,
        scratch_shapes=[pltpu.SemaphoreType.DMA((2,))] + column_sems(parts) + plane_sems(),
        compiler_params=pltpu.CompilerParams(
            collective_id=collective_id, has_side_effects=True, vmem_limit_bytes=32 * 2**20
        ),
        cost_estimate=lasting(55),
    )(longs, own)


def third_kernel(parts, cuts, longs_ref, column_ref, near_ref, far_ref, *refs):
    count = len(cuts) - 1
    outs, refs = refs[:count], refs[count:]
    keep_sem, cross_sems, sems = refs[0], refs[1:3], refs[3:]
    chip, core, beside, above, facing = plane_ids()
    enter(neighbours(False, False))
    other = {SEQ: 2 * chip + 1 - core}
    longs = ColumnSpread(
        parts, longs_ref, near_ref, far_ref, other, keep_sem.at[0], sems[:2], sems[2:4]
    )
    half = column_ref.shape[0] // 2
    weights = []
    keeps = []
    for place in range(count):
        rows = pl.ds(cuts[place], cuts[place + 1] - cuts[place])
        out = outs[place]
        weights.append(
            PlaneSpread(
                lambda part, rows=rows: column_ref.at[pl.ds(part * half, half), rows],
                lambda where, part, out=out: out.at[core, where, pl.ds(part * half, half)],
                [sem.at[place] for sem in sems[4:]],
            )
        )
        keeps.append(
            pltpu.make_async_copy(
                column_ref.at[:, rows], out.at[core, chip], keep_sem.at[1 + place]
            )
        )

    def across(place, where):
        block = outs[place].at[core, (chip, beside, above, facing)[where]]
        return remote(
            block, block, cross_sems[0].at[place, where], cross_sems[1].at[place, where], other
        )

    longs.start()
    for weight, keep in zip(weights, keeps):
        weight.start()
        keep.start()
    for part in range(parts):
        longs.step(1, part)
    for place in range(count):
        weights[place].forward()
        keeps[place].wait()
        across(place, 0).start()
    for part in range(parts):
        longs.step(2, part)
    for place in range(count):
        weights[place].arrive()
        for where in range(1, 4):
            across(place, where).start()
    for part in range(parts):
        longs.step(3, part)
    longs.finish()
    for place in range(count):
        weights[place].finish()
        for where in range(4):
            across(place, where).wait()


def third_exchange(longs, column, cuts, collective_id, parts=2):
    chips = lax.axis_size(SEQ) // 2
    tp_count, _, width = column.shape
    near = jax.ShapeDtypeStruct((tp_count,) + longs.shape, longs.dtype)
    count = len(cuts) - 1
    outs = [
        jax.ShapeDtypeStruct((2, chips, tp_count, last - first, width), column.dtype)
        for first, last in zip(cuts, cuts[1:])
    ]
    resident = pl.BlockSpec(memory_space=pltpu.VMEM)
    dma = pltpu.SemaphoreType.DMA
    return pl.pallas_call(
        functools.partial(third_kernel, parts, cuts),
        out_shape=[near, near] + outs,
        in_specs=[resident] * 2,
        out_specs=[resident] * (2 + count),
        scratch_shapes=[dma((1 + count,)), dma((count, 4)), dma((count, 4))]
        + column_sems(parts)
        + [dma((count, 2, 2)), dma((count, 2, 2)), dma((count, 2)), dma((count, 2))],
        compiler_params=pltpu.CompilerParams(
            collective_id=collective_id, has_side_effects=True, vmem_limit_bytes=48 * 2**20
        ),
        cost_estimate=lasting(55),
    )(longs, column)


def plane_reduce_kernel(
    parts_ref, out_ref, came, facing_came, sent, last, send_near, recv_near, send_far, recv_far, send_on, recv_on
):
    chip, core, beside, above, facing = plane_ids()
    ways = ({SEQ: 2 * beside + core}, {SEQ: 2 * above + core})
    chips = (beside, above)
    half = out_ref.shape[0] // 2
    always = lax.axis_index(TP) >= 0
    enter([(always, ways[0]), (always, ways[1])])

    def rows_of(way):
        return pl.ds(way * half, half)

    def facing_term(way):
        return remote(
            parts_ref.at[facing, rows_of(way)],
            facing_came.at[way],
            send_far.at[way],
            recv_far.at[way],
            ways[way],
        )

    def near_term(way):
        return remote(
            parts_ref.at[chips[way], rows_of(way)],
            came.at[way],
            send_near.at[way],
            recv_near.at[way],
            ways[way],
        )

    def summed(way):
        return remote(
            sent.at[way], last.at[way], send_on.at[way], recv_on.at[way], ways[1 - way]
        )

    for way in range(2):
        facing_term(way).start()
    for way in range(2):
        near_term(way).start()
    step_rows = 64

    def each_step(work):
        @pl.loop(0, half // step_rows)
        def _(step):
            work(pl.multiple_of(step * step_rows, step_rows))

    for way in range(2):
        facing_term(way).wait_recv()

        def add_term(start):
            total = parts_ref[
                chips[1 - way], pl.ds(way * half + start, step_rows), :
            ].astype(f32) + facing_came[way, pl.ds(start, step_rows), :].astype(f32)
            sent[way, pl.ds(start, step_rows), :] = total.astype(sent.dtype)

        each_step(add_term)
        summed(way).start()
    for way in range(2):
        near_term(way).wait_recv()

        def add_near(start):
            at = pl.ds(way * half + start, step_rows)
            out_ref[at, :] = parts_ref[chip, at, :].astype(f32) + came[
                way, pl.ds(start, step_rows), :
            ].astype(f32)

        each_step(add_near)
    for way in range(2):
        summed(way).wait_recv()

        def add_last(start):
            out_ref[pl.ds(way * half + start, step_rows), :] += last[
                way, pl.ds(start, step_rows), :
            ].astype(f32)

        each_step(add_last)
    for way in range(2):
        facing_term(way).wait_send()
        near_term(way).wait_send()
        summed(way).wait_send()


def plane_reduce_now(parts, collective_id):
    chips, rows, width = parts.shape
    half = pltpu.VMEM((2, rows // 2, width), parts.dtype)
    dma = pltpu.SemaphoreType.DMA((2,))
    return pl.pallas_call(
        plane_reduce_kernel,
        out_shape=jax.ShapeDtypeStruct((rows, width), f32),
        in_specs=[pl.BlockSpec(memory_space=pltpu.VMEM)],
        out_specs=pl.BlockSpec(memory_space=pltpu.VMEM),
        scratch_shapes=[half] * 4 + [dma] * 6,
        compiler_params=pltpu.CompilerParams(
            collective_id=collective_id, has_side_effects=True, vmem_limit_bytes=32 * 2**20
        ),
        cost_estimate=lasting(28),
    )(parts)


def all_sum_kernel(rows_ref, out_ref, sums, came, send, receive):
    chip, core, beside, above, facing = plane_ids()
    place = lax.axis_index(TP)
    peers = [
        {SEQ: 2 * chip + 1 - core},
        {SEQ: 2 * beside + core},
        {SEQ: 2 * above + core},
        {TP: place + 1 - 2 * (place % 2)},
        {TP: place + 2 - 4 * (place // 2)},
    ]
    enter([(place >= 0, peer) for peer in peers])
    sums[0] = rows_ref[...]
    for step, peer in enumerate(peers):
        copy = remote(sums.at[step], came.at[step], send.at[step], receive.at[step], peer)
        copy.start()
        copy.wait()
        sums[step + 1] = sums[step] + came[step]
    out_ref[...] = sums[len(peers)]


def all_sum(rows, collective_id):
    steps = 5
    return pl.pallas_call(
        all_sum_kernel,
        out_shape=jax.ShapeDtypeStruct(rows.shape, rows.dtype),
        in_specs=[pl.BlockSpec(memory_space=pltpu.VMEM)],
        out_specs=pl.BlockSpec(memory_space=pltpu.VMEM),
        scratch_shapes=[
            pltpu.VMEM((steps + 1,) + rows.shape, rows.dtype),
            pltpu.VMEM((steps,) + rows.shape, rows.dtype),
            pltpu.SemaphoreType.DMA((steps,)),
            pltpu.SemaphoreType.DMA((steps,)),
        ],
        compiler_params=pltpu.CompilerParams(
            collective_id=collective_id, has_side_effects=True
        ),
        cost_estimate=lasting(12),
    )(rows)


def holder_sum_kernel(
    parts,
    terms_ref,
    out_ref,
    sums,
    given,
    came,
    send_far,
    recv_far,
    send_z,
    recv_z,
    send_plane,
    recv_plane,
    send_on,
    send_back,
    recv_back,
):
    chip, core, beside, above, facing = plane_ids()
    count = lax.axis_size(TP)
    place = lax.axis_index(TP)
    other = {SEQ: 2 * chip + 1 - core}
    ways = ({SEQ: 2 * beside + core}, {SEQ: 2 * above + core})
    rows = sums.shape[0]
    part_rows = rows // parts
    always = place >= 0
    holds = place == chip
    enter(
        [
            (always, other),
            (always, ways[0]),
            (always, ways[1]),
            (place < count - 1, {TP: place + 1}),
            (place > 0, {TP: place - 1}),
        ]
    )

    def cut(part):
        return pl.ds(part * part_rows, part_rows)

    def own_cut(part):
        return pl.ds(pl.multiple_of(core * rows + part * part_rows, 16), part_rows)

    across = remote(
        terms_ref.at[pl.ds(pl.multiple_of((1 - core) * rows, 16), rows)], given, send_far, recv_far, other
    )
    across.start()

    def along(way, part):
        return remote(
            sums.at[cut(part)],
            came.at[way, cut(part)],
            send_z.at[way, part],
            recv_z.at[way, part],
            {TP: place - 1 if way == 0 else place + 1},
        )

    def add(source, part):
        total = sums[cut(part), :].astype(f32) + source[cut(part), :].astype(f32)
        sums[cut(part), :] = total.astype(sums.dtype)

    def to_plane(way, part):
        return remote(
            out_ref.at[own_cut(part)],
            out_ref.at[own_cut(part)],
            send_plane.at[way, part],
            recv_plane.at[part],
            ways[way],
        )

    def onward(part):
        return remote(
            out_ref.at[own_cut(part)],
            out_ref.at[own_cut(part)],
            send_on,
            recv_plane.at[part],
            ways[1 - part],
        )

    def back(part):
        return remote(
            out_ref.at[own_cut(part)],
            out_ref.at[own_cut(part)],
            send_back.at[part],
            recv_back.at[part],
            other,
        )

    across.wait_recv()
    for part in range(parts):
        sums[cut(part), :] = terms_ref[own_cut(part), :]
        add(given, part)
        for way in range(2):
            passes = place > chip if way == 0 else place < chip
            takes = place < count - 1 if way == 0 else place > 0

            @pl.when(passes)
            def _():
                @pl.when(takes)
                def _():
                    along(way, part).wait_recv()
                    add(came.at[way], part)

                along(way, part).start()

    for part in range(parts):
        for way in range(2):
            takes = place < count - 1 if way == 0 else place > 0

            @pl.when(holds & takes)
            def _():
                along(way, part).wait_recv()
                add(came.at[way], part)

        @pl.when(holds)
        def _():
            out_ref[own_cut(part), :] = sums[cut(part), :]
            for way in range(2):
                to_plane(way, part).start()
            back(part).start()

    for part in range(parts):

        @pl.when(place != chip)
        def _():
            to_plane(0, part).wait_recv()

        @pl.when((beside if part == 0 else above) == place)
        def _():
            onward(part).start()

        @pl.when(place != chip)
        def _():
            back(part).start()

    across.wait_send()
    for part in range(parts):
        back(part).wait()

        @pl.when((beside if part == 0 else above) == place)
        def _():
            onward(part).wait_send()

        for way in range(2):

            @pl.when(holds)
            def _():
                to_plane(way, part).wait_send()

            @pl.when(place > chip if way == 0 else place < chip)
            def _():
                along(way, part).wait_send()


def holder_sum(terms, collective_id):
    parts = 2
    rows = terms.shape[0] // 2
    half = (rows,) + terms.shape[1:]
    dma = pltpu.SemaphoreType.DMA
    resident = pl.BlockSpec(memory_space=pltpu.VMEM)
    return pl.pallas_call(
        functools.partial(holder_sum_kernel, parts),
        out_shape=jax.ShapeDtypeStruct(terms.shape, terms.dtype),
        in_specs=[resident],
        out_specs=resident,
        scratch_shapes=[
            pltpu.VMEM(half, terms.dtype),
            pltpu.VMEM(half, terms.dtype),
            pltpu.VMEM((2,) + half, terms.dtype),
            dma,
            dma,
            dma((2, parts)),
            dma((2, parts)),
            dma((2, parts)),
            dma((parts,)),
            dma,
            dma((parts,)),
            dma((parts,)),
        ],
        compiler_params=pltpu.CompilerParams(
            collective_id=collective_id, has_side_effects=True, vmem_limit_bytes=32 * 2**20
        ),
        cost_estimate=lasting(35),
    )(terms)


def plane_applies(mesh, blocks, docs):
    seq_count, tp_count = mesh.shape[SEQ], mesh.shape[TP]
    groups = seq_count * tp_count
    return (
        tp_count == 4
        and seq_count == 2 * tp_count
        and blocks == groups * SHORT_BLK
        and 2 * tp_count * SHORT_BLK == LONG_BLK
        and blocks - SHORT_BLK * docs == 2 * (LONG_BLK - SHORT_BLK)
    )


class Micro:
    pass


def plane_body(
    tokens,
    doc_lengths,
    rand_blocks,
    query_weight,
    key_weight,
    value_weight,
    query_bias,
    value_bias,
    proj_weight,
    proj_bias,
    first_gain,
    first_bias,
    second_gain,
    second_bias,
    inner_weight,
    inner_bias,
    outer_weight,
    outer_bias,
    out_grad,
):
    micro_count, own_rows, model_width = tokens.shape
    seq_count = lax.axis_size(SEQ)
    tp_count = lax.axis_size(TP)
    chips = seq_count // 2
    seq_place = lax.axis_index(SEQ)
    tp_place = lax.axis_index(TP)
    chip = seq_place // 2
    core = seq_place % 2
    heads = rand_blocks.shape[2]
    rands = rand_blocks.shape[3]
    local_width = query_weight.shape[1]
    head_size = local_width // heads
    pair_width = heads * PAIR
    hidden_units = inner_weight.shape[1]
    classes = 2 * tp_count
    own_class = core * tp_count + tp_place
    long_docs = 2
    slots = 5 + rands
    group_rows = chips * own_rows
    score_scale = 1.0 / math.sqrt(head_size)

    def by_head(values):
        return values.reshape(values.shape[:-1] + (heads, -1))

    def side_by_side(first, second):
        paired = jnp.concatenate([by_head(first), by_head(second)], axis=-1)
        return paired.reshape(paired.shape[:-2] + (pair_width,))

    def low_half(wide):
        return by_head(wide)[..., :head_size].reshape(wide.shape[:-1] + (local_width,))

    def high_half(wide):
        return by_head(wide)[..., head_size:].reshape(wide.shape[:-1] + (local_width,))

    def slot_rows(values, slot):
        return values[slot * own_rows : (slot + 1) * own_rows]

    stage = [Micro() for _ in range(micro_count)]
    spare_rows = 64
    packed = jnp.concatenate([side_by_side(key_weight, value_weight), query_weight], axis=1)
    packed_bias = jnp.concatenate(
        [side_by_side(jnp.zeros_like(value_bias), value_bias), query_bias]
    )
    packed = jnp.concatenate([packed, packed_bias[None]], axis=0)
    packed = jnp.pad(packed, ((0, spare_rows - 1), (0, -packed.shape[1] % 128)))
    randoms = rand_blocks.reshape(-1)
    random_count = randoms.shape[0]
    randoms = jnp.pad(randoms, (0, -random_count % 1024)).reshape(-1, 128)
    for micro, held in enumerate(stage):
        held.inputs = tokens[micro].astype(f32)
        shifted, held.stats_one, held.inverse_one = layer_stats(
            held.inputs, first_gain, first_bias
        )
        held.low = shifted.astype(bf16)
    unit_cut = hidden_units // seq_count
    proj_cut = local_width // seq_count
    rest_rows = -(-(proj_cut + 1) // 16) * 16
    cuts = (0, rest_rows, rest_rows + unit_cut, rest_rows + 2 * unit_cut)

    def padded(row_values):
        return jnp.pad(row_values, [(0, 0)] * (row_values.ndim - 1) + [(0, model_width - unit_cut)])

    share = jnp.concatenate(
        [
            lax.dynamic_slice_in_dim(proj_weight, seq_place * proj_cut, proj_cut, axis=0),
            padded(lax.dynamic_slice_in_dim(inner_bias, seq_place * unit_cut, unit_cut)[None]),
            jnp.zeros((rest_rows - proj_cut - 1, model_width), bf16),
            lax.dynamic_slice_in_dim(inner_weight, seq_place * unit_cut, unit_cut, axis=1).T,
            lax.dynamic_slice_in_dim(outer_weight, seq_place * unit_cut, unit_cut, axis=0),
        ],
        axis=0,
    )
    one, packed, column, randoms = first_exchange(stage[0].low, packed, share, randoms, 1)
    stage[0].one = one.reshape(group_rows, model_width)
    pair_wide = packed[:model_width, :pair_width]
    pair_wide_bias = packed[model_width, :pair_width]
    query_part = packed[:model_width, pair_width : pair_width + local_width]
    query_part_bias = packed[model_width, pair_width : pair_width + local_width]

    starts = jnp.cumsum(doc_lengths, axis=1) - doc_lengths
    is_long = doc_lengths == LONG_BLK
    long_firsts = jnp.min(jnp.where(is_long, starts, jnp.iinfo(jnp.int32).max), axis=1)
    long_lasts = jnp.max(jnp.where(is_long, starts, -1), axis=1)
    randoms = randoms.reshape(chips, -1)[:, :random_count]
    randoms = randoms.reshape(chips, micro_count, tp_count, SHORT_BLK, heads, rands)
    randoms = lax.dynamic_index_in_dim(randoms, tp_place, axis=2, keepdims=False)
    randoms = jnp.pad(randoms.transpose(1, 3, 0, 2, 4), [(0, 0)] * 4 + [(slots - rands, 0)])
    shape = (heads, chips, SHORT_BLK, slots)
    slot, block, entry = (lax.broadcasted_iota(jnp.int32, shape, axis) for axis in (1, 2, 3))
    for micro, held in enumerate(stage):
        group = slot * classes + own_class
        number = group * SHORT_BLK + block
        in_long = [
            (number >= start[micro]) & (number < start[micro] + LONG_BLK)
            for start in (long_firsts, long_lasts)
        ]
        window_first = jnp.where(
            in_long[0],
            long_firsts[micro],
            jnp.where(in_long[1], long_lasts[micro], group * SHORT_BLK),
        )
        any_long = in_long[0] | in_long[1]
        window_final = window_first + jnp.where(any_long, LONG_BLK, SHORT_BLK)
        key = randoms[micro]
        for place, value in enumerate(
            (
                jnp.maximum(number - 1, window_first),
                jnp.minimum(number + 1, window_final - 1),
                number,
                window_first,
                window_first + 1,
            )
        ):
            key = jnp.where(entry == place, value, key)
        inside = key % SHORT_BLK
        key_class = (key // SHORT_BLK) % classes
        piece = key_class % tp_count + jnp.where(key_class // tp_count == core, 0, tp_count)
        long_place = piece * long_docs + jnp.where(in_long[1], 1, 0)
        short_place = classes * long_docs + slot
        held.index = (jnp.where(any_long, long_place, short_place) * SHORT_BLK + inside).reshape(-1)
        counts = jnp.where(entry == 0, number > window_first, number + 1 < window_final)
        held.valid = counts[0, :, :, :2].astype(jnp.int32).reshape(-1)
        held.long_rows = []
        for start in (long_firsts[micro], long_lasts[micro]):
            first_group = start // SHORT_BLK
            own_group = first_group + (own_class - first_group) % classes
            held.long_rows.append((own_group // classes) * own_rows)

    def long_blocks(micro):
        held = stage[micro]
        pair_rows = (contract(held.one, pair_wide, NN) + pair_wide_bias).astype(bf16)
        longs = jnp.concatenate(
            [
                lax.dynamic_slice_in_dim(pair_rows, start, own_rows, axis=0)
                for start in held.long_rows
            ],
            axis=0,
        )
        return pair_rows, longs

    def keep_pieces(micro, near, far, pair_rows):
        stage[micro].pieces = [
            near.reshape(-1, pair_width), far.reshape(-1, pair_width), pair_rows
        ]

    def attend(micro):
        held = stage[micro]
        one = held.one
        if micro:
            one = after(one, stage[micro - 1].grad_context_sent)
        held.queries = (
            (contract(one, query_part, NN) + query_part_bias) * score_scale
        ).astype(bf16)
        held.context_sent, held.logsum = attend_forward(
            held.index, held.valid, held.queries, held.pieces, heads, slots
        )
        held.context = plane_exchange(held.context_sent, 0, 1)

    def feed_forward(micro):
        held = stage[micro]
        if micro:
            held.context = after(
                held.context, stage[micro - 1].grad_query, stage[micro - 1].long_sum_sent
            )
        else:
            held.context = after(held.context, stage[1].pieces[0])
        hidden = held.inputs + contract(held.context, proj_full, NN) + proj_bias
        shifted, stats, inverse = layer_stats(hidden, second_gain, second_bias)
        held.two = shifted.astype(bf16)
        before = contract(held.two, inner_full, NT) + inner_bias_full
        held.active = gelu_exact(before).astype(bf16)
        result = hidden + contract(held.active, outer_full, NN) + outer_bias
        held.output = result.astype(bf16)
        held.grad_out = out_grad[micro]
        grad_float = held.grad_out.astype(f32)
        grad_active = contract(held.grad_out, outer_full, NT)
        held.grad_before = gelu_grad(before, grad_active).astype(bf16)
        grad_two = contract(held.grad_before, inner_full, NN)
        back, gain_sum, shift_sum = layer_back(grad_two, stats, inverse, second_gain)
        held.grad_hidden = grad_float + back
        held.branch = held.grad_hidden.astype(bf16)
        held.grad_context_sent = jnp.stack(
            [
                contract(
                    held.branch, proj_full[part * local_width : (part + 1) * local_width], NT
                ).astype(bf16)
                for part in range(chips)
            ]
        )
        held.grad_context = plane_exchange(held.grad_context_sent, 0, 0).reshape(
            group_rows, local_width
        )
        held.unit_sum = jnp.sum(held.grad_before.astype(f32), axis=0)
        held.row_sums = jnp.stack(
            [
                gain_sum,
                shift_sum,
                jnp.sum(held.branch.astype(f32), axis=0),
                jnp.sum(grad_float, axis=0),
            ]
        )

    def attend_back(micro, *earlier):
        held = stage[micro]
        held.grad_query, near, far, held.grad_pair = attend_backward(
            held.index,
            held.valid,
            held.queries,
            after(held.grad_context, *earlier),
            held.logsum,
            held.pieces,
            heads,
            slots,
        )
        return near, far

    def input_rows(micro, long_sum):
        held = stage[micro]
        for doc, start in enumerate(held.long_rows):
            held.grad_pair = lax.dynamic_update_slice_in_dim(
                held.grad_pair, slot_rows(long_sum, doc), start, axis=0
            )
        rows = contract(held.grad_query, query_part * score_scale, NT) + contract(
            held.grad_pair, pair_wide, NT
        )
        return rows.astype(bf16).reshape(chips, own_rows, model_width)

    def input_back(micro, grad_one):
        held = stage[micro]
        back, gain_sum, shift_sum = layer_back(
            grad_one, held.stats_one, held.inverse_one, first_gain
        )
        held.input_grad = held.grad_hidden + back
        held.first_sums = jnp.stack([gain_sum, shift_sum])

    pair_rows, longs = long_blocks(0)
    near, far, one = second_exchange(longs, stage[1].low, 2)
    stage[1].one = one.reshape(group_rows, model_width)
    keep_pieces(0, near, far, pair_rows)
    attend(0)
    pair_rows, longs = long_blocks(1)
    near, far, rest, inner_full, outer_full = third_exchange(
        after(longs, stage[0].context_sent), column, cuts, 7
    )
    keep_pieces(1, near, far, pair_rows)
    inner_full = inner_full.reshape(-1, model_width)
    outer_full = outer_full.reshape(-1, model_width)
    inner_bias_full = rest[:, :, :, proj_cut, :unit_cut].reshape(-1)
    proj_full = rest[:, :, :, :proj_cut].transpose(2, 1, 0, 3, 4)
    proj_full = proj_full.reshape(tp_count * local_width, model_width)
    feed_forward(0)
    attend(1)
    near, far = attend_back(0, stage[1].logsum, stage[1].context_sent)
    stage[0].long_sum_sent = sum_parts([near, core_swap(far)]).astype(bf16)
    long_sum = lax.psum_scatter(stage[0].long_sum_sent, TP, scatter_dimension=0, tiled=True)
    feed_forward(1)

    two, grad_before, active, grad_out, context, branch = (
        jnp.concatenate(group, axis=0)
        for group in zip(
            *((h.two, h.grad_before, h.active, h.grad_out, h.context, h.branch) for h in stage)
        )
    )
    two, active, context = after((two, active, context), stage[1].grad_context_sent)
    proj_part = contract(context, branch, TN).astype(bf16)
    proj_part = proj_part.reshape(tp_count, chips, 2, proj_cut, model_width)
    unit_shape = (2, chips, tp_count)
    unit_sum = sum(h.unit_sum for h in stage).astype(bf16)
    rest_part = jnp.concatenate(
        [
            proj_part.transpose(2, 1, 0, 3, 4),
            padded(unit_sum.reshape(unit_shape + (1, unit_cut))),
            jnp.zeros(unit_shape + (rest_rows - proj_cut - 1, model_width), bf16),
        ],
        axis=3,
    )
    halves = []
    for part in (
        contract(grad_before, two, TN).astype(bf16),
        contract(active, grad_out, TN).astype(bf16),
        rest_part,
    ):
        part = part.reshape(2, chips, -1, model_width)
        kept = lax.dynamic_index_in_dim(part, core, axis=0, keepdims=False)
        given = lax.dynamic_index_in_dim(part, 1 - core, axis=0, keepdims=False)
        halves.append(sum_parts([kept, core_swap(given)]).astype(bf16))
    halves = jnp.concatenate(halves, axis=1)
    by_chip = plane_exchange(halves, 0, 0)

    rows = input_rows(0, after(long_sum, stage[1].grad_context_sent))
    grad_one = [lax.dynamic_index_in_dim(rows, chip, axis=0, keepdims=False)]
    for step in range(1, chips):
        part = lax.dynamic_index_in_dim(rows, chip ^ step, axis=0, keepdims=False)
        route = [(place, place ^ (2 * step)) for place in range(seq_count)]
        grad_one.append(lax.ppermute(part, SEQ, route))
    near, far = attend_back(1, halves, rows)

    query_sum = sum(contract(h.one, h.grad_query, TN) for h in stage) * score_scale
    query_sum = query_sum.astype(bf16)
    half_rows = model_width // 2
    kept = lax.dynamic_slice_in_dim(query_sum, core * half_rows, half_rows, axis=0)
    given = core_swap(
        lax.dynamic_slice_in_dim(query_sum, (1 - core) * half_rows, half_rows, axis=0)
    )
    near = after(near, query_sum)
    column_shape = (tp_count, long_docs * own_rows, pair_width)
    long_sum = column_reduce_both(near.reshape(column_shape), far.reshape(column_shape), 3)
    input_back(0, sum_parts(after(grad_one, long_sum)))
    rows = input_rows(1, long_sum)

    half = sum_parts([kept, given]).astype(bf16)
    came = [
        lax.ppermute(
            after(half, rows),
            (SEQ, TP),
            [
                (place * tp_count + (place // 2 + step) % tp_count, place * tp_count + place // 2)
                for place in range(seq_count)
            ],
        )
        for step in range(1, tp_count)
    ]
    quarters = jnp.sum(after(by_chip, rows).astype(f32), axis=0).astype(bf16)
    cuts = [0, tp_count * unit_cut, 2 * tp_count * unit_cut, quarters.shape[0]]
    quarters = jnp.concatenate(
        [
            quarters[first:last].reshape(tp_count, -1, model_width)
            for first, last in zip(cuts, cuts[1:])
        ],
        axis=1,
    )
    by_column = lax.all_to_all(quarters, TP, split_axis=0, concat_axis=0, tiled=True)
    grad_one = plane_reduce_now(after(rows, quarters, half), 4)
    input_back(1, grad_one)

    ones = after([h.one for h in stage], grad_one)
    pair_sum = sum(contract(one, h.grad_pair, TN) for one, h in zip(ones, stage)).astype(bf16)
    half = sum_parts([half] + after(came, grad_one)).astype(bf16)
    came = [
        lax.ppermute(
            half,
            (SEQ, TP),
            [
                (place * tp_count + place // 2, (place ^ (2 * step)) * tp_count + place // 2)
                for place in range(seq_count)
            ],
        )
        for step in range(1, chips)
    ]
    own_sum = jnp.sum(after(by_column, grad_one).astype(f32), axis=0).astype(bf16)
    other_sum = core_swap(own_sum)
    pair_sum = holder_sum(after(pair_sum, half, own_sum), 6).astype(f32)
    key_grad = low_half(pair_sum)
    value_grad = high_half(pair_sum)

    other_sum = after(other_sum, pair_sum)
    chip_sum = jnp.where(
        core == 0, jnp.stack([own_sum, other_sum]), jnp.stack([other_sum, own_sum])
    )
    dense_sum = plane_gather(chip_sum)
    near = jnp.where(tp_place == chip, half, sum(after(came, pair_sum)))
    far = core_swap(near)

    def own_columns(values):
        wide = jnp.zeros((chips, local_width), f32)
        return lax.dynamic_update_slice_in_dim(wide, values[None], chip, axis=0).reshape(-1)

    query_bias_sum = sum(jnp.sum(h.grad_query.astype(f32), axis=0) for h in stage)
    pair_bias_sum = sum(jnp.sum(h.grad_pair.astype(f32), axis=0) for h in stage)
    all_rows = all_sum(
        after(
            jnp.concatenate(
                [
                    sum(h.row_sums for h in stage),
                    sum(h.first_sums for h in stage),
                    own_columns(query_bias_sum * score_scale)[None],
                    own_columns(high_half(pair_bias_sum))[None],
                ],
                axis=0,
            ),
            near,
            chip_sum,
        ),
        5,
    )
    query_grad = jnp.where(
        core == 0, jnp.concatenate([near, far], axis=0), jnp.concatenate([far, near], axis=0)
    ).astype(f32)
    dense_sum = dense_sum.reshape(seq_count, -1, model_width).astype(f32)
    inner_weight_grad = dense_sum[:, :unit_cut].reshape(hidden_units, model_width).T
    outer_weight_grad = dense_sum[:, unit_cut : 2 * unit_cut].reshape(hidden_units, model_width)
    rest = dense_sum[:, 2 * unit_cut :]
    proj_weight_grad = rest[:, :proj_cut].reshape(local_width, model_width)
    inner_bias_grad = rest[:, proj_cut, :unit_cut].reshape(hidden_units)

    def my_columns(row):
        return lax.dynamic_slice_in_dim(row, tp_place * local_width, local_width)

    return (
        jnp.stack([h.output for h in stage]),
        jnp.stack([h.input_grad for h in stage]),
        query_grad,
        key_grad,
        value_grad,
        my_columns(all_rows[6]),
        my_columns(all_rows[7]),
        proj_weight_grad,
        all_rows[2],
        all_rows[4],
        all_rows[5],
        all_rows[0],
        all_rows[1],
        inner_weight_grad,
        inner_bias_grad,
        outer_weight_grad,
        all_rows[3],
    )


def general_body(
    tokens,
    doc_lengths,
    rand_blocks,
    query_weight,
    key_weight,
    value_weight,
    query_bias,
    value_bias,
    proj_weight,
    proj_bias,
    first_gain,
    first_bias,
    second_gain,
    second_bias,
    inner_weight,
    inner_bias,
    outer_weight,
    outer_bias,
    out_grad,
):
    micro_count, local_rows, model_width = tokens.shape
    seq_count = lax.axis_size(SEQ)
    tp_count = lax.axis_size(TP)
    seq_place = lax.axis_index(SEQ)
    tp_place = lax.axis_index(TP)
    block_dev = rand_blocks.shape[1]
    heads = rand_blocks.shape[2]
    local_width = query_weight.shape[1]
    head_size = local_width // heads
    hidden_units = inner_weight.shape[1]
    group_rows = block_dev * BLOCK
    reach_dev = (block_dev + LONG_BLK - 2) // block_dev
    window = 2 * reach_dev + 1
    score_scale = 1.0 / math.sqrt(head_size)
    lowest = (seq_place - reach_dev) * block_dev
    blocks = seq_place * block_dev + jnp.arange(block_dev, dtype=jnp.int32)

    held = jnp.concatenate([inner_weight.T, outer_weight, proj_weight, inner_bias[None]], axis=0)
    used_rows = held.shape[0]
    piece_rows = -(-used_rows // (16 * seq_count)) * 16
    held_rows = piece_rows * seq_count
    held = jnp.pad(held, ((0, held_rows - used_rows), (0, 0)))
    share = lax.dynamic_slice_in_dim(held, seq_place * piece_rows, piece_rows, axis=0)
    spread = lax.all_gather(share, (TP, SEQ), axis=0, tiled=True)
    spread = spread.reshape(tp_count, held_rows, model_width)
    cuts = [0, hidden_units, 2 * hidden_units, 2 * hidden_units + local_width, used_rows]
    inner_full = spread[:, cuts[0] : cuts[1]].reshape(-1, model_width)
    outer_full = spread[:, cuts[1] : cuts[2]].reshape(-1, model_width)
    proj_full = spread[:, cuts[2] : cuts[3]].reshape(-1, model_width)
    inner_bias_full = spread[:, cuts[3] : cuts[4]].reshape(-1)

    def by_head(weight):
        return weight.reshape(weight.shape[:-1] + (heads, head_size))

    def side_by_side(first, second):
        paired = jnp.concatenate([by_head(first), by_head(second)], axis=-1)
        return paired.reshape(paired.shape[:-2] + (heads * PAIR,))

    pair_wide = side_by_side(key_weight, value_weight)
    pair_wide_bias = side_by_side(jnp.zeros_like(value_bias), value_bias)

    stage = [Micro() for _ in range(micro_count)]
    for micro, held in enumerate(stage):
        inputs = tokens[micro].astype(f32)
        shifted, stats, inverse = layer_stats(inputs, first_gain, first_bias)
        held.inputs, held.stats_one, held.inverse_one = inputs, stats, inverse
        held.one = lax.all_gather(shifted.astype(bf16), TP, axis=0, tiled=True)

    for micro, held in enumerate(stage):
        one = held.one
        pair_rows = (contract(one, pair_wide, NN) + pair_wide_bias).astype(bf16)
        pieces = [
            pair_rows if offset == 0 else from_behind(pair_rows, SEQ, -offset)
            for offset in range(-reach_dev, reach_dev + 1)
        ]
        queries = ((contract(one, query_weight, NN) + query_bias) * score_scale).astype(bf16)
        key_index, key_valid = block_keys(doc_lengths[micro], rand_blocks[micro], blocks)
        slots = key_index.shape[2]
        slot_index = jnp.clip(key_index - lowest, 0, window * block_dev - 1)
        held.index = slot_index.transpose(1, 0, 2).reshape(-1)
        held.valid = key_valid.reshape(-1)
        held.queries, held.pieces = queries, pieces

    for held in stage:
        context, held.logsum = attend_forward(
            held.index,
            held.valid,
            held.queries,
            held.pieces,
            heads,
            slots,
        )
        held.context = lax.all_to_all(context, TP, split_axis=0, concat_axis=1, tiled=True)

    outputs = []
    for micro, held in enumerate(stage):
        context = held.context
        hidden = held.inputs + contract(context, proj_full, NN) + proj_bias
        shifted, stats, inverse = layer_stats(hidden, second_gain, second_bias)
        two = shifted.astype(bf16)
        before = contract(two, inner_full, NT) + inner_bias_full
        active = gelu_exact(before).astype(bf16)
        result = hidden + contract(active, outer_full, NN) + outer_bias
        outputs.append(result.astype(bf16))
        grad_out = out_grad[micro]
        grad_float = grad_out.astype(f32)
        grad_active = contract(grad_out, outer_full, NT)
        grad_before = gelu_grad(before, grad_active).astype(bf16)
        grad_two = contract(grad_before, inner_full, NN)
        back, gain_sum, shift_sum = layer_back(grad_two, stats, inverse, second_gain)
        grad_hidden = grad_float + back
        branch = grad_hidden.astype(bf16)
        grad_context = contract(branch, proj_full, NT).astype(bf16)
        held.grad_context = lax.all_to_all(
            grad_context, TP, split_axis=1, concat_axis=0, tiled=True
        )
        held.grad_hidden = grad_hidden
        held.dense = (two, grad_before, active, grad_out, context, branch)
        held.row_sums = (
            jnp.sum(grad_before.astype(f32), axis=0),
            gain_sum,
            shift_sum,
            jnp.sum(branch.astype(f32), axis=0),
            jnp.sum(grad_float, axis=0),
        )

    two, grad_before, active, grad_out, context, branch = (
        jnp.concatenate(group, axis=0) for group in zip(*(h.dense for h in stage))
    )
    inner_part = contract(grad_before, two, TN).astype(bf16)
    outer_part = contract(active, grad_out, TN).astype(bf16)
    proj_part = contract(context, branch, TN).astype(bf16)
    grad_rows = 2 * hidden_units + local_width
    grad_piece = -(-grad_rows // (16 * seq_count)) * 16
    grad_held = grad_piece * seq_count
    parts = jnp.concatenate(
        [
            inner_part.reshape(tp_count, hidden_units, model_width),
            outer_part.reshape(tp_count, hidden_units, model_width),
            proj_part.reshape(tp_count, local_width, model_width),
            jnp.zeros((tp_count, grad_held - grad_rows, model_width), bf16),
        ],
        axis=1,
    ).reshape(tp_count * grad_held, model_width)
    own_part = lax.psum_scatter(parts, (TP, SEQ), scatter_dimension=0, tiled=True)
    dense_sum = lax.all_gather(own_part, SEQ, axis=0, tiled=True).astype(f32)
    inner_weight_grad = dense_sum[cuts[0] : cuts[1]].T
    outer_weight_grad = dense_sum[cuts[1] : cuts[2]]
    proj_weight_grad = dense_sum[cuts[2] : cuts[3]]

    for held in stage:
        held.grad_query, *grad_pieces = attend_backward(
            held.index,
            held.valid,
            held.queries,
            held.grad_context,
            held.logsum,
            held.pieces,
            heads,
            slots,
        )
        returned = grad_pieces[reach_dev].astype(f32)
        for offset in range(-reach_dev, reach_dev + 1):
            if offset != 0:
                returned = returned + from_behind(
                    grad_pieces[offset + reach_dev], SEQ, offset
                ).astype(f32)
        held.grad_pair = returned.astype(bf16)

    input_grads = []
    query_sum = pair_sum = 0.0
    query_bias_sum = pair_bias_sum = 0.0
    first_gain_sum = first_bias_sum = 0.0
    for held in stage:
        grad_query, grad_pair, one = held.grad_query, held.grad_pair, held.one
        rows = contract(grad_query, query_weight * score_scale, NT) + contract(grad_pair, pair_wide, NT)
        grad_one = lax.psum_scatter(
            rows.astype(bf16), TP, scatter_dimension=0, tiled=True
        ).astype(f32)
        query_sum = query_sum + contract(one, grad_query, TN)
        pair_sum = pair_sum + contract(one, grad_pair, TN)
        query_bias_sum = query_bias_sum + jnp.sum(grad_query.astype(f32), axis=0)
        pair_bias_sum = pair_bias_sum + jnp.sum(grad_pair.astype(f32), axis=0)
        back, gain_sum, shift_sum = layer_back(
            grad_one, held.stats_one, held.inverse_one, first_gain
        )
        first_gain_sum = first_gain_sum + gain_sum
        first_bias_sum = first_bias_sum + shift_sum
        input_grads.append(held.grad_hidden + back)

    def low_half(wide):
        return wide.reshape(wide.shape[:-1] + (heads, PAIR))[..., :head_size].reshape(
            wide.shape[:-1] + (local_width,)
        )

    def high_half(wide):
        return wide.reshape(wide.shape[:-1] + (heads, PAIR))[..., head_size:].reshape(
            wide.shape[:-1] + (local_width,)
        )

    query_grad, key_grad, value_grad = lax.psum(
        (query_sum * score_scale, low_half(pair_sum), high_half(pair_sum)), SEQ
    )
    inner_bias_sum, second_gain_sum, second_bias_sum, proj_bias_sum, outer_bias_sum = (
        sum(group) for group in zip(*(h.row_sums for h in stage))
    )

    def own_columns(values):
        wide = jnp.zeros((tp_count, local_width), f32)
        return lax.dynamic_update_slice_in_dim(wide, values[None], tp_place, axis=0).reshape(-1)

    early = lax.psum(
        jnp.concatenate(
            [
                inner_bias_sum,
                second_gain_sum,
                second_bias_sum,
                proj_bias_sum,
                outer_bias_sum,
            ]
        ),
        (SEQ, TP),
    )
    late = lax.psum(
        jnp.concatenate(
            [
                first_gain_sum,
                first_bias_sum,
                own_columns(query_bias_sum * score_scale),
                own_columns(high_half(pair_bias_sum)),
            ]
        ),
        (SEQ, TP),
    )
    inner_bias_all = early[: tp_count * hidden_units].reshape(tp_count, hidden_units)
    early_rows = early[tp_count * hidden_units :].reshape(-1, model_width)
    late_rows = late.reshape(-1, model_width)

    def my_columns(row):
        return lax.dynamic_slice_in_dim(row, tp_place * local_width, local_width)

    return (
        jnp.stack(outputs),
        jnp.stack(input_grads),
        query_grad,
        key_grad,
        value_grad,
        my_columns(late_rows[2]),
        my_columns(late_rows[3]),
        proj_weight_grad,
        early_rows[2],
        late_rows[0],
        late_rows[1],
        early_rows[0],
        early_rows[1],
        inner_weight_grad,
        lax.dynamic_index_in_dim(inner_bias_all, tp_place, axis=0, keepdims=False),
        outer_weight_grad,
        early_rows[3],
    )


def solution(mesh):
    def choose(tokens, doc_lengths, rand_blocks, *rest):
        blocks = rand_blocks.shape[1] * mesh.shape[SEQ]
        if plane_applies(mesh, blocks, doc_lengths.shape[1]):
            return plane_body(tokens, doc_lengths, rand_blocks, *rest)
        return general_body(tokens, doc_lengths, rand_blocks, *rest)

    return jax.shard_map(
        choose,
        mesh=mesh,
        in_specs=(
            P(None, (SEQ, TP), None),
            P(),
            P(None, SEQ, TP, None),
            P(None, TP),
            P(None, TP),
            P(None, TP),
            P(TP),
            P(TP),
            P(TP, None),
            P(),
            P(),
            P(),
            P(),
            P(),
            P(None, TP),
            P(TP),
            P(TP, None),
            P(),
            P(None, (SEQ, TP), None),
        ),
        out_specs=(
            P(None, (SEQ, TP), None),
            P(None, (SEQ, TP), None),
            P(None, TP),
            P(None, TP),
            P(None, TP),
            P(TP),
            P(TP),
            P(TP, None),
            P(),
            P(),
            P(),
            P(),
            P(),
            P(None, TP),
            P(TP),
            P(TP, None),
            P(),
        ),
        check_vma=False,
    )
```

time: 1010 us -> 758 us (0.75)
  the two profiles are of different devices: /device:TPU:13 before, /device:TPU:0 now
where the time goes in v2:
time: 758 us; the launch traced here: 748 us
  Pallas kernels  391 us (52%)
  matrix products  96.9 us (13%)
  other arithmetic  78.6 us (10%)
  local copies, waits for them, and re-layouts  76.1 us (10%)
  starting transfers between devices  67.2 us (9%)
  between operations  29.7 us (4%)
  waiting for transfers between devices  8.61 us (1%)
    dot_general x33, matrix products, contract(): return lax.dot_general(left, right, dims, preferred_element_type=f32)  96.9 us
    pallas_call x1, Pallas kernels, third_exchange(): pl.pallas_call(functools.partial(third_kernel, parts, cuts), out_shape=[n...  61.8 us
    pallas_call x1, Pallas kernels, second_exchange(): pl.pallas_call(functools.partial(second_kernel, parts), out_shape=[near,...  58.6 us
    pallas_call x1, Pallas kernels, column_reduce_both(): pl.pallas_call(functools.partial(column_reduce_kernel, parts), out_shape=...  55.4 us
    pallas_call x2, Pallas kernels, attend_backward(): pl.pallas_call(functools.partial(backward_kernel, slots, heads, len(piece...  51.6 us
    pallas_call x1, Pallas kernels, first_exchange(): pl.pallas_call(functools.partial(first_kernel, parts), out_shape=[jax.Sha...  42.3 us
    pallas_call x2, Pallas kernels, attend_forward(): pl.pallas_call(functools.partial(forward_kernel, slots, heads), grid_spec...  37.6 us
    pallas_call x1, Pallas kernels, all_sum(): pl.pallas_call(all_sum_kernel, out_shape=jax.ShapeDtypeStruct(rows.shape,...  34.7 us
  transfers between devices with their start and end apart: 24, of which 3 were waited for; matrix products, arithmetic and copies ran while one was open for 16% of the time, Pallas kernels for 33%

profile of v2, /device:TPU:0, one launch (start us, length us, event | category | flops | bytes accessed | tf_op | source)
XLA Modules:
  0.0 748.2 jit_solution(1324710107241537709)
XLA Ops:
  31.9 42.3 %shard_map.314 = (bf16[4,512,768]{2,1,0:T(8,128)(2,1)S(1)}, bf16[832,640]{1,0:T(8,128)(2,1)S(1)}, bf16[4,224,768]{2,1,0:T(8,128)(2,1)S(1)}, s32[4,8,128]{2,1,0:T(8,128)S(1)}) custom-call(bf16[512,768]{1,0:T(8,128)(2,1)S(1)} %get-tuple-element.205.own_ref, bf16[832,640]{1,0:T(8,128)(2,1)S(1)} %fusion.97.weight_ref, ...), custom_call_target="tpu_custom_call" | custom-call | bytes 110700000 | tf_op jit(solution)/shard_map/pallas_call | solution.py:881
  91.2 3.8 add_convert_fusion.4.refs_2_
  97.8 58.6 %shard_map.315 = (bf16[4,1024,384]{2,1,0:T(8,128)(2,1)S(1)}, bf16[4,1024,384]{2,1,0:T(8,128)(2,1)S(1)}, bf16[4,512,768]{2,1,0:T(8,128)(2,1)S(1)}) custom-call(bf16[1024,384]{1,0:T(8,128)(2,1)S(1)} %pad_maximum_fusion.8.longs_ref, bf16[512,768]{1,0:T(8,128)(2,1)S(1)} %get-tuple-element.204.own_ref), custom_call_target="tpu_custom_call" | custom-call | bytes 202950000 | tf_op jit(solution)/shard_map/pallas_call | solution.py:937
  158.1 18.8 %shard_map.316 = (bf16[2048,192]{1,0:T(8,128)(2,1)S(1)}, f32[2048,384]{1,0:T(8,128)S(1)}) custom-call(s32[768]{0:T(1024)S(1)} %fusion.134.index_ref, s32[64]{0:T(128)S(1)} %reshape.373.valid_ref, bf16[2048,192]{1,0:T(8,128)(2,1)S(1)} %fusion.25.query_ref, bf16[4096,384]{1,0:T(8,128)(2,1)S(1)} %bitcast.334, bf16[4096,384]{1,0:T(8,128)(2,1)S(1)} %bitcast.336, ...), custom_call_target="tpu_custom_call" | custom-call | bytes 66420000 | tf_op jit(solution)/shard_map/pallas_call | solution.py:255
  181.9 5.2 all-to-all-start
  192.4 3.7 add_convert_fusion.3.refs_2_
  198.0 61.8 %shard_map.317 = (bf16[4,1024,384]{2,1,0:T(8,128)(2,1)}, bf16[4,1024,384]{2,1,0:T(8,128)(2,1)}, bf16[2,4,4,32,768]{4,3,2,1,0:T(8,128)(2,1)S(1)}, bf16[2,4,4,96,7...) custom-call(bf16[1024,384]{1,0:T(8,128)(2,1)S(1)} %pad_maximum_fusion.9.longs_ref, bf16[4,224,768]{2,1,0:T(8,128)(2,1)S(1)} %copy-done.26), custom_call_target="tpu_custom_call" | custom-call | bytes 202950000 | tf_op jit(solution)/shard_map/pallas_call | solution.py:1021
  267.4 5.2 fusion.163
  272.8 5.8 convert_reduce_fusion.1
  287.1 4.1 all-to-all-start.2
  297.2 18.8 %shard_map.318 = (bf16[2048,192]{1,0:T(8,128)(2,1)S(1)}, f32[2048,384]{1,0:T(8,128)S(1)}) custom-call(s32[768]{0:T(1024)S(1)} %fusion.142.index_ref, s32[64]{0:T(128)S(1)} %reshape.377.valid_ref, bf16[2048,192]{1,0:T(8,128)(2,1)S(1)} %fusion.26.query_ref, bf16[4096,384]{1,0:T(8,128)(2,1)S(1)} %bitcast.331, bf16[4096,384]{1,0:T(8,128)(2,1)S(1)} %bitcast.333, ...), custom_call_target="tpu_custom_call" | custom-call | bytes 66420000 | tf_op jit(solution)/shard_map/pallas_call | solution.py:255
  320.9 25.7 %shard_map.319 = (bf16[2048,192]{1,0:T(8,128)(2,1)S(1)}, bf16[4096,384]{1,0:T(8,128)(2,1)}, bf16[4096,384]{1,0:T(8,128)(2,1)}, bf16[2048,384]{1,0:T(8,128)(2,1)}) custom-call(s32[768]{0:T(1024)S(1)} %fusion.134.index_ref, s32[64]{0:T(128)S(1)} %reshape.373.valid_ref, bf16[2048,192]{1,0:T(8,128)(2,1)S(1)} %copy-done.13, bf16[2048,192]{1,0:T(8,128)(2,1)S(1)} %bitcast.340, ...), custom_call_target="tpu_custom_call" | custom-call | bytes 92250000 | tf_op jit(solution)/shard_map/pallas_call | solution.py:278
  350.9 3.9 all-to-all-start.1
  362.6 4.5 add_convert_fusion.2
  370.4 10.9 %multiply_convert_fusion.1 = (bf16[512,3072]{1,0:T(8,128)(2,1)}, bf16[512,3072]{1,0:T(8,128)(2,1)}, f32[512,3072]{1,0:T(8,128)S(1)}) fusion(f32[512,3072]{1,0:T(8,128)} %copy-done.147, f32[3072]{0:T(1024)S(1)} %copy-done.108, bf16[512,768]{1,0:T(8,128)(2,1)S(1)} %add_convert_fusion.6, bf16[3072,768]{1,0:T(8,128)(2,1)} %bitcast.412), kind=kOutput, calls=%fused_computation.28 | convolution fusion | flops 2434793472 | bytes 24391680 | tf_op jit(solution)/shard_map/dot_general | solution.py:31
  381.3 5.3 convert_reduce_fusion
  400.9 4.4 all-to-all-start.3
  405.5 4.0 pad_maximum_fusion
  413.9 5.5 convolution_convert_fusion
  423.3 5.8 fusion.16
  452.6 5.6 all-to-all-start.4
  464.4 5.2 add_convert_fusion.1
  469.6 25.9 %shard_map.320 = (bf16[2048,192]{1,0:T(8,128)(2,1)S(1)}, bf16[4096,384]{1,0:T(8,128)(2,1)}, bf16[4096,384]{1,0:T(8,128)(2,1)}, bf16[2048,384]{1,0:T(8,128)(2,1)}) custom-call(s32[768]{0:T(1024)S(1)} %fusion.142.index_ref, s32[64]{0:T(128)S(1)} %reshape.377.valid_ref, bf16[2048,192]{1,0:T(8,128)(2,1)S(1)} %copy-done.11, bf16[2048,192]{1,0:T(8,128)(2,1)S(1)} %bitcast.339, ...), custom_call_target="tpu_custom_call" | custom-call | bytes 92250000 | tf_op jit(solution)/shard_map/pallas_call | solution.py:278
  502.1 55.4 %shard_map.321 = bf16[1024,384]{1,0:T(8,128)(2,1)S(1)} custom-call(bf16[4,1024,384]{2,1,0:T(8,128)(2,1)S(1)} %bitcast.341, bf16[4,1024,384]{2,1,0:T(8,128)(2,1)S(1)} %bitcast.342), custom_call_target="tpu_custom_call" | custom-call | bytes 202950000 | tf_op jit(solution)/shard_map/pallas_call | solution.py:486
  567.6 4.2 reduce_sum.346
  573.2 19.7 %all-to-all-start.5 = ((bf16[4,224,768]{2,1,0:T(8,128)(2,1)}), bf16[4,224,768]{2,1,0:T(8,128)(2,1)}, u32[]{:S(2)}, u32[]{:S(2)}) async-start(bf16[4,224,768]{2,1,0:T(8,128)(2,1)} %pad_maximum_fusion.7), calls=%async_computation.6 | async-start | bytes 2752512 | tf_op jit(solution)/shard_map/all_to_all | solution.py:1729
  598.3 31.0 %shard_map.322 = f32[512,768]{1,0:T(8,128)S(1)} custom-call(bf16[4,512,768]{2,1,0:T(8,128)(2,1)S(1)} %bitcast.338), custom_call_target="tpu_custom_call" | custom-call | bytes 103320000 | tf_op jit(solution)/shard_map/pallas_call | solution.py:1123
  634.4 5.6 collective-permute-done.10
  646.7 4.6 fusion.63
  653.1 18.2 %shard_map.323 = bf16[768,384]{1,0:T(8,128)(2,1)S(1)} custom-call(bf16[768,384]{1,0:T(8,128)(2,1)S(1)} %fusion.80.terms_ref), custom_call_target="tpu_custom_call" | custom-call | bytes 129150000 | tf_op jit(solution)/shard_map/pallas_call | solution.py:1335
  673.3 9.7 %all-to-all-start.6 = ((bf16[8,224,768]{2,1,0:T(8,128)(2,1)}), bf16[8,224,768]{2,1,0:T(8,128)(2,1)}, u32[]{:S(2)}, u32[]{:S(2)}) async-start(bf16[8,224,768]{2,1,0:T(8,128)(2,1)} %pad_maximum_fusion.3), calls=%async_computation.7 | async-start | bytes 5505024 | tf_op jit(solution)/shard_map/all_to_all | solution.py:302
  693.0 34.7 %shard_map.324 = f32[8,768]{1,0:T(8,128)} custom-call(f32[8,768]{1,0:T(8,128)} %pad_maximum_fusion.13.rows_ref), custom_call_target="tpu_custom_call" | custom-call | bytes 44280000 | tf_op jit(solution)/shard_map/pallas_call | solution.py:1158
  (588 shorter events, 200.5 us)
Async XLA Ops:
  78.8 77.6 %copy-start.90 = (s32[768]{0:T(1024)}, s32[768]{0:T(1024)S(1)}, u32[]{:S(2)}) copy-start(s32[768]{0:T(1024)S(1)} %iota.122) | copy-start | bytes 9220
  83.1 73.3 %copy-start.92 = (s32[768]{0:T(1024)}, s32[768]{0:T(1024)S(1)}, u32[]{:S(2)}) copy-start(s32[768]{0:T(1024)S(1)} %mul.322) | copy-start | bytes 9220
  95.1 63.1 %copy-start.9 = (bf16[2048,384]{1,0:T(8,128)(2,1)}, bf16[2048,384]{1,0:T(8,128)(2,1)S(1)}, u32[]{:S(2)}) copy-start(bf16[2048,384]{1,0:T(8,128)(2,1)S(1)} %add_convert_fusion.4.refs_2_) | copy-start | bytes 4718596
  97.5 60.6 %copy-start.12 = (bf16[2048,192]{1,0:T(8,128)(2,1)}, bf16[2048,192]{1,0:T(8,128)(2,1)S(1)}, u32[]{:S(2)}) copy-start(bf16[2048,192]{1,0:T(8,128)(2,1)S(1)} %fusion.25.query_ref) | copy-start | bytes 2359300
  97.6 58.8 %copy-start.94 = (s32[768]{0:T(1024)S(1)}, s32[768]{0:T(1024)}, u32[]{:S(2)}) copy-start(s32[768]{0:T(1024)} %iota.104) | copy-start | bytes 9220
  97.6 58.8 %copy-start.106 = (s32[768]{0:T(1024)S(1)}, s32[768]{0:T(1024)}, u32[]{:S(2)}) copy-start(s32[768]{0:T(1024)} %squeeze.96) | copy-start | bytes 9220
  97.6 58.8 %copy-start.112 = (pred[768]{0:T(1024)(128)(4,1)S(1)}, pred[768]{0:T(1024)(128)(4,1)}, u32[]{:S(2)}) copy-start(pred[768]{0:T(1024)(128)(4,1)} %iota.107) | copy-start | bytes 2308
  181.9 82.3 %all-to-all-start = ((bf16[4,512,192]{1,2,0:T(8,128)(2,1)}), bf16[4,512,192]{1,2,0:T(8,128)(2,1)S(1)}, u32[]{:S(2)}, u32[]{:S(2)}) async-start(bf16[4,512,192]{1,2,0:T(8,128)(2,1)} %copy.74), calls=%async_computation | async-start | bytes 1572864 | tf_op jit(solution)/shard_map/all_to_all | solution.py:302
  192.3 71.9 %copy-start.127 = (f32[768]{0:T(1024)}, f32[768]{0:T(1024)S(1)}, u32[]{:S(2)}) copy-start(f32[768]{0:T(1024)S(1)} %convert_element_type.320) | copy-start | bytes 9220
  287.1 32.5 %all-to-all-start.2 = ((bf16[4,512,192]{1,2,0:T(8,128)(2,1)}), bf16[4,512,192]{1,2,0:T(8,128)(2,1)S(1)}, u32[]{:S(2)}, u32[]{:S(2)}) async-start(bf16[4,512,192]{1,2,0:T(8,128)(2,1)} %pad_maximum_fusion.10), calls=%async_computation.2 | async-start | bytes 1572864 | tf_op jit(solution)/shard_map/all_to_all | solution.py:302
  346.6 16.1 %collective-permute-start = (bf16[4096,384]{1,0:T(8,128)(2,1)}, bf16[4096,384]{1,0:T(8,128)(2,1)}, u32[]{:S(2)}, u32[]{:S(2)}) collective-permute-start(bf16[4096,384]{1,0:T(8,128)(2,1)} %get-tuple-element.93), channel_id=1, source_target_pairs={{0,4},{4,0},{8,12},{12,8},{16,20},{20,16},{24,28},{28,24},{1,5},{5... | collective-permute-start | bytes 9437192 | tf_op jit(solution)/shard_map/ppermute | solution.py:319
  350.9 16.2 %all-to-all-start.1 = ((bf16[4,512,192]{1,2,0:T(8,128)(2,1)}), bf16[4,512,192]{1,2,0:T(8,128)(2,1)S(1)}, u32[]{:S(2)}, u32[]{:S(2)}) async-start(bf16[4,512,192]{1,2,0:T(8,128)(2,1)} %copy.82), calls=%async_computation.1 | async-start | bytes 1572864 | tf_op jit(solution)/shard_map/all_to_all | solution.py:302
  354.8 106.0 %reduce-scatter.2.cloned.1.call-start = ((), (), s32[]{:S(2)}) async-start(), calls=%async_computation.8 | async-start | bytes 3932160 | tf_op jit(solution)/shard_map/reduce_scatter | solution.py:1652
  400.9 40.4 %all-to-all-start.3 = ((bf16[4,512,192]{1,2,0:T(8,128)(2,1)}), bf16[4,512,192]{1,2,0:T(8,128)(2,1)}, u32[]{:S(2)}, u32[]{:S(2)}) async-start(bf16[4,512,192]{1,2,0:T(8,128)(2,1)} %pad_maximum_fusion.11), calls=%async_computation.4 | async-start | bytes 1572864 | tf_op jit(solution)/shard_map/all_to_all | solution.py:302
  413.7 29.1 %collective-permute-start.6 = (bf16[4,128,768]{2,1,0:T(8,128)(2,1)}, bf16[4,128,768]{2,1,0:T(8,128)(2,1)}, u32[]{:S(2)}, u32[]{:S(2)}) collective-permute-start(bf16[4,128,768]{2,1,0:T(8,128)(2,1)} %dynamic-slice_bitcast_fusion.2), channel_id=1, source_target_pairs={{0,4},{4,0},{8,12},{12,8},{16,20},{20,16},{24,28},{28,24},{1,5},{5... | collective-permute-start | bytes 2359304 | tf_op jit(solution)/shard_map/ppermute | solution.py:319
  423.0 21.5 %collective-permute-start.5 = (bf16[4,384,768]{2,1,0:T(8,128)(2,1)}, bf16[4,384,768]{2,1,0:T(8,128)(2,1)}, u32[]{:S(2)}, u32[]{:S(2)}) collective-permute-start(bf16[4,384,768]{2,1,0:T(8,128)(2,1)} %dynamic-slice_bitcast_fusion), channel_id=1, source_target_pairs={{0,4},{4,0},{8,12},{12,8},{16,20},{20,16},{24,28},{28,24},{1,5},{5... | collective-permute-start | bytes 7077896 | tf_op jit(solution)/shard_map/ppermute | solution.py:319
  432.6 14.8 %collective-permute-start.4 = (bf16[4,384,768]{2,1,0:T(8,128)(2,1)}, bf16[4,384,768]{2,1,0:T(8,128)(2,1)}, u32[]{:S(2)}, u32[]{:S(2)}) collective-permute-start(bf16[4,384,768]{2,1,0:T(8,128)(2,1)} %dynamic-slice_bitcast_fusion.1), channel_id=1, source_target_pairs={{0,4},{4,0},{8,12},{12,8},{16,20},{20,16},{24,28},{28,24},{1,5},{5... | collective-permute-start | bytes 7077896 | tf_op jit(solution)/shard_map/ppermute | solution.py:319
  452.6 115.1 %all-to-all-start.4 = ((bf16[4,896,768]{2,1,0:T(8,128)(2,1)}), bf16[4,896,768]{2,1,0:T(8,128)(2,1)}, u32[]{:S(2)}, u32[]{:S(2)}) async-start(bf16[4,896,768]{2,1,0:T(8,128)(2,1)} %pad_maximum_fusion.1), calls=%async_computation.5 | async-start | bytes 11010048 | tf_op jit(solution)/shard_map/all_to_all | solution.py:302
  497.1 95.7 %collective-permute-start.7 = (bf16[384,192]{0,1:T(8,128)(2,1)}, bf16[384,192]{0,1:T(8,128)(2,1)}, u32[]{:S(2)}, u32[]{:S(2)}) collective-permute-start(bf16[384,192]{0,1:T(8,128)(2,1)} %constant_dynamic-slice_fusion.2), channel_id=1, source_target_pairs={{0,4},{4,0},{8,12},{12,8},{16,20},{20,16},{24,28},{28,24},{1,5},{5... | collective-permute-start | bytes 442376 | tf_op jit(solution)/shard_map/ppermute | solution.py:319
  498.6 146.1 %collective-permute-start.1 = (bf16[512,768]{1,0:T(8,128)(2,1)}, bf16[512,768]{1,0:T(8,128)(2,1)}, u32[]{:S(2)}, u32[]{:S(2)}) collective-permute-start(bf16[512,768]{1,0:T(8,128)(2,1)} %get-tuple-element.200), channel_id=1, source_target_pairs={{0,8},{4,12},{8,0},{12,4},{16,24},{20,28},{24,16},{28,20},{1,9},{5... | collective-permute-start | bytes 2359304 | tf_op jit(solution)/shard_map/ppermute | solution.py:1692
  500.1 146.6 %collective-permute-start.2 = (bf16[512,768]{1,0:T(8,128)(2,1)}, bf16[512,768]{1,0:T(8,128)(2,1)}, u32[]{:S(2)}, u32[]{:S(2)}) collective-permute-start(bf16[512,768]{1,0:T(8,128)(2,1)} %get-tuple-element.199), channel_id=1, source_target_pairs={{0,16},{4,20},{8,24},{12,28},{16,0},{20,4},{24,8},{28,12},{1,17},{... | collective-permute-start | bytes 2359304 | tf_op jit(solution)/shard_map/ppermute | solution.py:1692
  501.6 145.1 %collective-permute-start.3 = (bf16[512,768]{1,0:T(8,128)(2,1)}, bf16[512,768]{1,0:T(8,128)(2,1)}, u32[]{:S(2)}, u32[]{:S(2)}) collective-permute-start(bf16[512,768]{1,0:T(8,128)(2,1)} %get-tuple-element.198), channel_id=1, source_target_pairs={{0,24},{4,28},{8,16},{12,20},{16,8},{20,12},{24,0},{28,4},{1,25},{... | collective-permute-start | bytes 2359304 | tf_op jit(solution)/shard_map/ppermute | solution.py:1692
  573.2 78.1 %all-to-all-start.5 = ((bf16[4,224,768]{2,1,0:T(8,128)(2,1)}), bf16[4,224,768]{2,1,0:T(8,128)(2,1)}, u32[]{:S(2)}, u32[]{:S(2)}) async-start(bf16[4,224,768]{2,1,0:T(8,128)(2,1)} %pad_maximum_fusion.7), calls=%async_computation.6 | async-start | bytes 2752512 | tf_op jit(solution)/shard_map/all_to_all | solution.py:1729
  593.8 37.4 %collective-permute-start.8 = (bf16[384,192]{0,1:T(8,128)(2,1)S(1)}, bf16[384,192]{0,1:T(8,128)(2,1)S(1)}, u32[]{:S(2)}, u32[]{:S(2)}) collective-permute-start(bf16[384,192]{0,1:T(8,128)(2,1)S(1)} %add_convert_fusion.10), channel_id=1, source_target_pairs={{1,0},{5,4},{10,9},{14,13},{19,18},{23,22},{24,27},{28,31}} | collective-permute-start | bytes 442376 | tf_op jit(solution)/shard_map/ppermute | solution.py:1710
  595.1 39.3 %collective-permute-start.9 = (bf16[384,192]{0,1:T(8,128)(2,1)S(1)}, bf16[384,192]{0,1:T(8,128)(2,1)S(1)}, u32[]{:S(2)}, u32[]{:S(2)}) collective-permute-start(bf16[384,192]{0,1:T(8,128)(2,1)S(1)} %add_convert_fusion.10), channel_id=1, source_target_pairs={{2,0},{6,4},{11,9},{15,13},{16,18},{20,22},{25,27},{29,31}} | collective-permute-start | bytes 442376 | tf_op jit(solution)/shard_map/ppermute | solution.py:1710
  631.2 8.8 %collective-permute-start.10 = (bf16[384,192]{0,1:T(8,128)(2,1)S(1)}, bf16[384,192]{0,1:T(8,128)(2,1)S(1)}, u32[]{:S(2)}, u32[]{:S(2)}) collective-permute-start(bf16[384,192]{0,1:T(8,128)(2,1)S(1)} %add_convert_fusion.10), channel_id=1, source_target_pairs={{3,0},{7,4},{8,9},{12,13},{17,18},{21,22},{26,27},{30,31}} | collective-permute-start | bytes 442376 | tf_op jit(solution)/shard_map/ppermute | solution.py:1710
  640.8 48.6 %collective-permute-start.11 = (bf16[384,192]{0,1:T(8,128)(2,1)}, bf16[384,192]{0,1:T(8,128)(2,1)}, u32[]{:S(2)}, u32[]{:S(2)}) collective-permute-start(bf16[384,192]{0,1:T(8,128)(2,1)} %add_convert_fusion.9), channel_id=1, source_target_pairs={{0,8},{4,12},{9,1},{13,5},{18,26},{22,30},{27,19},{31,23}} | collective-permute-start | bytes 442376 | tf_op jit(solution)/shard_map/ppermute | solution.py:1737
  642.7 46.7 %collective-permute-start.12 = (bf16[384,192]{0,1:T(8,128)(2,1)}, bf16[384,192]{0,1:T(8,128)(2,1)}, u32[]{:S(2)}, u32[]{:S(2)}) collective-permute-start(bf16[384,192]{0,1:T(8,128)(2,1)} %add_convert_fusion.9), channel_id=1, source_target_pairs={{0,16},{4,20},{9,25},{13,29},{18,2},{22,6},{27,11},{31,15}} | collective-permute-start | bytes 442376 | tf_op jit(solution)/shard_map/ppermute | solution.py:1737
  644.7 44.7 %collective-permute-start.13 = (bf16[384,192]{0,1:T(8,128)(2,1)}, bf16[384,192]{0,1:T(8,128)(2,1)}, u32[]{:S(2)}, u32[]{:S(2)}) collective-permute-start(bf16[384,192]{0,1:T(8,128)(2,1)} %add_convert_fusion.9), channel_id=1, source_target_pairs={{0,24},{4,28},{9,17},{13,21},{18,10},{22,14},{27,3},{31,7}} | collective-permute-start | bytes 442376 | tf_op jit(solution)/shard_map/ppermute | solution.py:1737
  653.0 18.3 %collective-permute-start.15 = (bf16[224,768]{1,0:T(8,128)(2,1)S(1)}, bf16[224,768]{1,0:T(8,128)(2,1)S(1)}, u32[]{:S(2)}, u32[]{:S(2)}) collective-permute-start(bf16[224,768]{1,0:T(8,128)(2,1)S(1)} %reduce_sum.349), channel_id=1, source_target_pairs={{0,4},{4,0},{8,12},{12,8},{16,20},{20,16},{24,28},{28,24},{1,5},{5... | collective-permute-start | bytes 1032200 | tf_op jit(solution)/shard_map/ppermute | solution.py:319
  673.3 57.5 %all-to-all-start.6 = ((bf16[8,224,768]{2,1,0:T(8,128)(2,1)}), bf16[8,224,768]{2,1,0:T(8,128)(2,1)}, u32[]{:S(2)}, u32[]{:S(2)}) async-start(bf16[8,224,768]{2,1,0:T(8,128)(2,1)} %pad_maximum_fusion.3), calls=%async_computation.7 | async-start | bytes 5505024 | tf_op jit(solution)/shard_map/all_to_all | solution.py:302
  690.6 1.4 collective-permute-start.14
  (156 other events, 1576.4 us)
Sparse Core Ops, SparseCore 0:
  398.9 61.9 reduce-scatter.1

commit v3 on v2

--- a/solution.py
+++ b/solution.py
@@ -3,6 +3,7 @@
 
 import jax
 import jax.numpy as jnp
+import numpy as np
 from jax import lax
 from jax.experimental import pallas as pl
 from jax.experimental.pallas import tpu as pltpu
@@ -377,134 +378,6 @@
     )
 
 
-def column_reduce_kernel(
-    parts,
-    near_ref,
-    far_ref,
-    out_ref,
-    sums,
-    given,
-    came,
-    load_sem,
-    send_far,
-    recv_far,
-    send_z,
-    recv_z,
-):
-    count = lax.axis_size(TP)
-    place = lax.axis_index(TP)
-    other = {SEQ: partner_of(lax.axis_index(SEQ))}
-    rows = out_ref.shape[0] // parts
-    step_rows = 128
-    load = pltpu.make_async_copy(near_ref, sums, load_sem)
-    load.start()
-    enter(
-        [
-            (place >= 0, other),
-            (place < count - 1, {TP: place + 1}),
-            (place > 0, {TP: place - 1}),
-        ]
-    )
-
-    def cut(part):
-        return pl.ds(part * rows, rows)
-
-    def across(owner):
-        return remote(
-            far_ref.at[owner], given.at[owner], send_far.at[owner], recv_far.at[owner], other
-        )
-
-    def along(way, owner, part):
-        return remote(
-            sums.at[owner, cut(part)],
-            came.at[way, owner, cut(part)],
-            send_z.at[way, owner, part],
-            recv_z.at[way, owner, part],
-            {TP: place - 1 if way == 0 else place + 1},
-        )
-
-    def add(owner, source, part):
-        @pl.loop(0, rows // step_rows)
-        def _(step):
-            at = pl.ds(pl.multiple_of(part * rows + step * step_rows, step_rows), step_rows)
-            total = sums[owner, at, :].astype(f32) + source[at, :].astype(f32)
-            sums[owner, at, :] = total.astype(sums.dtype)
-
-    order = []
-    for step in range(count):
-        for owner in (step, count - 1 - step):
-            if owner not in order:
-                order.append(owner)
-    for owner in order:
-        across(owner).start()
-    load.wait()
-    for owner in order:
-        across(owner).wait_recv()
-        for part in range(parts):
-            add(owner, given.at[owner], part)
-            for way in range(2):
-                passes = place > owner if way == 0 else place < owner
-                takes = (place < count - 1) if way == 0 else (place > 0)
-
-                @pl.when(passes)
-                def _():
-                    @pl.when(takes)
-                    def _():
-                        along(way, owner, part).wait_recv()
-                        add(owner, came.at[way, owner], part)
-
-                    along(way, owner, part).start()
-
-    for part in range(parts):
-        for way in range(2):
-            for owner in range(count):
-                takes = (place < count - 1) if way == 0 else (place > 0)
-
-                @pl.when((place == owner) & takes)
-                def _():
-                    along(way, owner, part).wait_recv()
-                    add(owner, came.at[way, owner], part)
-
-    for owner in range(count):
-
-        @pl.when(place == owner)
-        def _():
-            out_ref[...] = sums[owner]
-
-        across(owner).wait_send()
-        for part in range(parts):
-            for way in range(2):
-
-                @pl.when(place > owner if way == 0 else place < owner)
-                def _():
-                    along(way, owner, part).wait_send()
-
-
-def column_reduce_both(near, far, collective_id, parts=2):
-    count = lax.axis_size(TP)
-    block = near.shape[1:]
-    return pl.pallas_call(
-        functools.partial(column_reduce_kernel, parts),
-        out_shape=jax.ShapeDtypeStruct(block, near.dtype),
-        in_specs=[pl.BlockSpec(memory_space=pl.ANY), pl.BlockSpec(memory_space=pltpu.VMEM)],
-        out_specs=pl.BlockSpec(memory_space=pltpu.VMEM),
-        scratch_shapes=[
-            pltpu.VMEM((count,) + block, near.dtype),
-            pltpu.VMEM((count,) + block, near.dtype),
-            pltpu.VMEM((2, count) + block, near.dtype),
-            pltpu.SemaphoreType.DMA,
-            pltpu.SemaphoreType.DMA((count,)),
-            pltpu.SemaphoreType.DMA((count,)),
-            pltpu.SemaphoreType.DMA((2, count, parts)),
-            pltpu.SemaphoreType.DMA((2, count, parts)),
-        ],
-        compiler_params=pltpu.CompilerParams(
-            collective_id=collective_id, has_side_effects=True, vmem_limit_bytes=32 * 2**20
-        ),
-        cost_estimate=lasting(55),
-    )(near, far)
-
-
 def plane_ids():
     seq_place = lax.axis_index(SEQ)
     chip, core = seq_place // 2, seq_place % 2
@@ -756,7 +629,7 @@
     own, out, keep_rows = halves_of(own_ref, out_ref, own_sem.at[0])
     rows = PlaneSpread(own, out, (send_row, recv_row, send_on, recv_on))
     shares = ColumnSpread(
-        1, share_ref, column_ref, None, other, own_sem.at[2], (send_share, recv_share), None
+        2, share_ref, column_ref, None, other, own_sem.at[2], (send_share, recv_share), None
     )
 
     def weight_cut(part, holder):
@@ -844,7 +717,8 @@
             weight_across(part).start()
 
     for distance in range(1, tp_count):
-        shares.step(distance, 0)
+        for part in range(2):
+            shares.step(distance, part)
     rows.arrive()
     rows.finish()
     shares.finish()
@@ -873,7 +747,7 @@
                 weight_along(spread_ref, way, part).wait_send()
 
 
-def first_exchange(own, weight, share, randoms, collective_id, parts=2):
+def first_exchange(own, weight, share, randoms, collective_id, parts=4):
     chips = lax.axis_size(SEQ) // 2
     count = lax.axis_size(TP)
     resident = pl.BlockSpec(memory_space=pltpu.VMEM)
@@ -900,7 +774,7 @@
             dma((chips - 1,)),
             dma,
         ]
-        + column_sems(1)[:2],
+        + column_sems(2)[:2],
         compiler_params=pltpu.CompilerParams(
             collective_id=collective_id, has_side_effects=True, vmem_limit_bytes=32 * 2**20
         ),
@@ -947,12 +821,14 @@
     )(longs, own)
 
 
-def third_kernel(parts, cuts, longs_ref, column_ref, near_ref, far_ref, *refs):
+def third_kernel(
+    parts, cuts, longs_ref, column_ref, sent_ref, near_ref, far_ref, context_ref, *refs
+):
     count = len(cuts) - 1
     outs, refs = refs[:count], refs[count:]
-    keep_sem, cross_sems, sems = refs[0], refs[1:3], refs[3:]
+    keep_sem, cross_sems, block_sems, sems = refs[0], refs[1:3], refs[3:5], refs[5:]
     chip, core, beside, above, facing = plane_ids()
-    enter(neighbours(False, False))
+    enter(neighbours(True, False))
     other = {SEQ: 2 * chip + 1 - core}
     longs = ColumnSpread(
         parts, longs_ref, near_ref, far_ref, other, keep_sem.at[0], sems[:2], sems[2:4]
@@ -976,38 +852,60 @@
             )
         )
 
-    def across(place, where):
-        block = outs[place].at[core, (chip, beside, above, facing)[where]]
+    def across(place, where, part):
+        block = outs[place].at[
+            core, (chip, beside, above, facing)[where], pl.ds(part * half, half)
+        ]
+        at = (place, where, part)
+        return remote(block, block, cross_sems[0].at[at], cross_sems[1].at[at], other)
+
+    def send_block(index):
+        target = (beside, above, facing)[index]
         return remote(
-            block, block, cross_sems[0].at[place, where], cross_sems[1].at[place, where], other
-        )
-
+            sent_ref.at[target],
+            context_ref.at[chip],
+            block_sems[0].at[index],
+            block_sems[1].at[index],
+            {SEQ: 2 * target + core},
+        )
+
+    keep_block = pltpu.make_async_copy(
+        sent_ref.at[chip], context_ref.at[chip], keep_sem.at[1 + count]
+    )
     longs.start()
     for weight, keep in zip(weights, keeps):
         weight.start()
         keep.start()
+    for index in range(3):
+        send_block(index).start()
+    keep_block.start()
     for part in range(parts):
         longs.step(1, part)
     for place in range(count):
         weights[place].forward()
         keeps[place].wait()
-        across(place, 0).start()
+        for where, part in ((0, 0), (0, 1), (1, 0), (2, 1)):
+            across(place, where, part).start()
     for part in range(parts):
         longs.step(2, part)
     for place in range(count):
         weights[place].arrive()
-        for where in range(1, 4):
-            across(place, where).start()
+        for where, part in ((1, 1), (2, 0), (3, 0), (3, 1)):
+            across(place, where, part).start()
     for part in range(parts):
         longs.step(3, part)
     longs.finish()
     for place in range(count):
         weights[place].finish()
         for where in range(4):
-            across(place, where).wait()
-
-
-def third_exchange(longs, column, cuts, collective_id, parts=2):
+            for part in range(2):
+                across(place, where, part).wait()
+    for index in range(3):
+        send_block(index).wait()
+    keep_block.wait()
+
+
+def third_exchange(longs, column, sent, cuts, collective_id, parts=2):
     chips = lax.axis_size(SEQ) // 2
     tp_count, _, width = column.shape
     near = jax.ShapeDtypeStruct((tp_count,) + longs.shape, longs.dtype)
@@ -1020,163 +918,376 @@
     dma = pltpu.SemaphoreType.DMA
     return pl.pallas_call(
         functools.partial(third_kernel, parts, cuts),
-        out_shape=[near, near] + outs,
-        in_specs=[resident] * 2,
-        out_specs=[resident] * (2 + count),
-        scratch_shapes=[dma((1 + count,)), dma((count, 4)), dma((count, 4))]
+        out_shape=[near, near, jax.ShapeDtypeStruct(sent.shape, sent.dtype)] + outs,
+        in_specs=[resident] * 3,
+        out_specs=[resident] * (3 + count),
+        scratch_shapes=[dma((2 + count,)), dma((count, 4, 2)), dma((count, 4, 2)), dma((3,)), dma((3,))]
         + column_sems(parts)
         + [dma((count, 2, 2)), dma((count, 2, 2)), dma((count, 2)), dma((count, 2))],
         compiler_params=pltpu.CompilerParams(
             collective_id=collective_id, has_side_effects=True, vmem_limit_bytes=48 * 2**20
         ),
         cost_estimate=lasting(55),
-    )(longs, column)
-
-
-def plane_reduce_kernel(
-    parts_ref, out_ref, came, facing_came, sent, last, send_near, recv_near, send_far, recv_far, send_on, recv_on
-):
-    chip, core, beside, above, facing = plane_ids()
-    ways = ({SEQ: 2 * beside + core}, {SEQ: 2 * above + core})
-    chips = (beside, above)
-    half = out_ref.shape[0] // 2
-    always = lax.axis_index(TP) >= 0
-    enter([(always, ways[0]), (always, ways[1])])
-
-    def rows_of(way):
-        return pl.ds(way * half, half)
-
-    def facing_term(way):
+    )(longs, column, sent)
+
+
+class ColumnReduce:
+
+    def __init__(self, parts, step_rows, sums, came, sems):
+        self.parts, self.step_rows = parts, step_rows
+        self.sums, self.came, self.sems = sums, came, sems
+        self.count = lax.axis_size(TP)
+        self.place = lax.axis_index(TP)
+        self.rows = sums.shape[1] // parts
+        self.order = []
+        for step in range(self.count):
+            for owner in (step, self.count - 1 - step):
+                if owner not in self.order:
+                    self.order.append(owner)
+
+    def along(self, way, owner, part):
+        at = pl.ds(part * self.rows, self.rows)
         return remote(
-            parts_ref.at[facing, rows_of(way)],
-            facing_came.at[way],
-            send_far.at[way],
-            recv_far.at[way],
-            ways[way],
-        )
-
-    def near_term(way):
+            self.sums.at[owner, at],
+            self.came.at[way, owner, at],
+            self.sems[0].at[way, owner, part],
+            self.sems[1].at[way, owner, part],
+            {TP: self.place - 1 if way == 0 else self.place + 1},
+        )
+
+    def add(self, owner, source, part):
+        @pl.loop(0, self.rows // self.step_rows)
+        def _(step):
+            start = pl.multiple_of(part * self.rows + step * self.step_rows, self.step_rows)
+            at = pl.ds(start, self.step_rows)
+            total = self.sums[owner, at, :].astype(f32) + source[at, :].astype(f32)
+            self.sums[owner, at, :] = total.astype(self.sums.dtype)
+
+    def takes(self, way):
+        return self.place < self.count - 1 if way == 0 else self.place > 0
+
+    def passes(self, way, owner):
+        return self.place > owner if way == 0 else self.place < owner
+
+    def begin(self, owner, part):
+        for way in range(2):
+
+            @pl.when(self.passes(way, owner) & ~self.takes(way))
+            def _():
+                self.along(way, owner, part).start()
+
+    def move(self, way, owner, part):
+        @pl.when(self.passes(way, owner) & self.takes(way))
+        def _():
+            self.along(way, owner, part).wait_recv()
+            self.add(owner, self.came.at[way, owner], part)
+            self.along(way, owner, part).start()
+
+    def end(self):
+        for part in range(self.parts):
+            for way in range(2):
+                for owner in range(self.count):
+
+                    @pl.when((self.place == owner) & self.takes(way))
+                    def _():
+                        self.along(way, owner, part).wait_recv()
+                        self.add(owner, self.came.at[way, owner], part)
+
+    def finish(self):
+        for owner in range(self.count):
+            for part in range(self.parts):
+                for way in range(2):
+
+                    @pl.when(self.passes(way, owner))
+                    def _():
+                        self.along(way, owner, part).wait_send()
+
+    def give(self, out):
+        for owner in range(self.count):
+
+            @pl.when(self.place == owner)
+            def _():
+                out[...] = self.sums[owner]
+
+
+class PlaneReduce:
+
+    def __init__(self, step_rows, terms, out, buffers, sems):
+        self.step_rows, self.terms, self.out = step_rows, terms, out
+        self.came, self.facing_came, self.sent, self.last = buffers
+        self.sems = sems
+        self.chip, core, beside, above, self.facing = plane_ids()
+        self.ways = ({SEQ: 2 * beside + core}, {SEQ: 2 * above + core})
+        self.chips = (beside, above)
+        self.half = terms.shape[1] // 2
+
+    def copy(self, kind, way, source, target, device):
         return remote(
-            parts_ref.at[chips[way], rows_of(way)],
-            came.at[way],
-            send_near.at[way],
-            recv_near.at[way],
-            ways[way],
-        )
-
-    def summed(way):
+            source, target.at[way], self.sems[0].at[kind, way], self.sems[1].at[kind, way], device
+        )
+
+    def pieces(self, way):
+        return pl.ds(way * self.half, self.half)
+
+    def facing_term(self, way):
+        source = self.terms.at[self.facing, self.pieces(way)]
+        return self.copy(0, way, source, self.facing_came, self.ways[way])
+
+    def near_term(self, way):
+        source = self.terms.at[self.chips[way], self.pieces(way)]
+        return self.copy(1, way, source, self.came, self.ways[way])
+
+    def summed(self, way):
+        return self.copy(2, way, self.sent.at[way], self.last, self.ways[1 - way])
+
+    def each_step(self, work):
+        steps = self.terms.shape[2] // self.step_rows
+
+        @pl.loop(0, self.half * steps)
+        def _(step):
+            start = pl.multiple_of((step % steps) * self.step_rows, self.step_rows)
+            work(step // steps, pl.ds(start, self.step_rows))
+
+    def start(self):
+        for way in range(2):
+            self.facing_term(way).start()
+        for way in range(2):
+            self.near_term(way).start()
+
+    def move(self):
+        for way in range(2):
+            self.facing_term(way).wait_recv()
+
+            def add_term(piece, at):
+                total = self.terms[self.chips[1 - way], way * self.half + piece, at, :].astype(f32)
+                total = total + self.facing_came[way, piece, at, :].astype(f32)
+                self.sent[way, piece, at, :] = total.astype(self.sent.dtype)
+
+            self.each_step(add_term)
+            self.summed(way).start()
+
+    def end(self):
+        for way in range(2):
+            self.near_term(way).wait_recv()
+            self.summed(way).wait_recv()
+
+            def add_last(piece, at):
+                total = self.terms[self.chip, way * self.half + piece, at, :].astype(f32)
+                total = total + self.came[way, piece, at, :].astype(f32)
+                total = total + self.last[way, piece, at, :].astype(f32)
+                self.out[way * self.half + piece, at, :] = total.astype(self.out.dtype)
+
+            self.each_step(add_last)
+
+    def finish(self):
+        for way in range(2):
+            self.facing_term(way).wait_send()
+            self.near_term(way).wait_send()
+            self.summed(way).wait_send()
+
+
+def reduce_scratch(shape, dtype):
+    half = pltpu.VMEM((2, shape[1] // 2) + shape[2:], dtype)
+    sems = pltpu.SemaphoreType.DMA((3, 2))
+    return [half] * 4 + [sems, sems]
+
+
+def fourth_kernel(parts, cuts, near_ref, far_ref, rows_ref, *refs):
+    count = len(cuts) - 1
+    terms, givens, refs = refs[:count], refs[count : 2 * count], refs[2 * count :]
+    out_ref, dense_ref, rows_out_ref, sums, given, came, dense, more = refs[:8]
+    load_sem, send_far, recv_far, send_z, recv_z = refs[8:13]
+    buffers, sems = refs[13:17], refs[17:19]
+    row_buffers, row_sems = refs[19:23], refs[23:25]
+    place = lax.axis_index(TP)
+    chip, core = plane_ids()[:2]
+    other = {SEQ: 2 * chip + 1 - core}
+    loads = [pltpu.make_async_copy(near_ref, sums, load_sem.at[0])]
+    for index in range(count):
+        rows = pl.ds(cuts[index], cuts[index + 1] - cuts[index])
+        loads.append(
+            pltpu.make_async_copy(
+                terms[index].at[core], dense.at[:, :, rows], load_sem.at[1 + 2 * index]
+            )
+        )
+        loads.append(
+            pltpu.make_async_copy(givens[index], more.at[:, :, rows], load_sem.at[2 + 2 * index])
+        )
+    for load in loads:
+        load.start()
+    enter(neighbours(False, False))
+    column = ColumnReduce(parts, 128, sums, came, (send_z, recv_z))
+    plane = PlaneReduce(32, dense, dense_ref, buffers, sems)
+    rows = PlaneReduce(64, rows_ref, rows_out_ref, row_buffers, row_sems)
+
+    def across(owner):
         return remote(
-            sent.at[way], last.at[way], send_on.at[way], recv_on.at[way], ways[1 - way]
-        )
-
-    for way in range(2):
-        facing_term(way).start()
-    for way in range(2):
-        near_term(way).start()
-    step_rows = 64
-
-    def each_step(work):
-        @pl.loop(0, half // step_rows)
-        def _(step):
-            work(pl.multiple_of(step * step_rows, step_rows))
-
-    for way in range(2):
-        facing_term(way).wait_recv()
-
-        def add_term(start):
-            total = parts_ref[
-                chips[1 - way], pl.ds(way * half + start, step_rows), :
-            ].astype(f32) + facing_came[way, pl.ds(start, step_rows), :].astype(f32)
-            sent[way, pl.ds(start, step_rows), :] = total.astype(sent.dtype)
-
-        each_step(add_term)
-        summed(way).start()
-    for way in range(2):
-        near_term(way).wait_recv()
-
-        def add_near(start):
-            at = pl.ds(way * half + start, step_rows)
-            out_ref[at, :] = parts_ref[chip, at, :].astype(f32) + came[
-                way, pl.ds(start, step_rows), :
-            ].astype(f32)
-
-        each_step(add_near)
-    for way in range(2):
-        summed(way).wait_recv()
-
-        def add_last(start):
-            out_ref[pl.ds(way * half + start, step_rows), :] += last[
-                way, pl.ds(start, step_rows), :
-            ].astype(f32)
-
-        each_step(add_last)
-    for way in range(2):
-        facing_term(way).wait_send()
-        near_term(way).wait_send()
-        summed(way).wait_send()
-
-
-def plane_reduce_now(parts, collective_id):
-    chips, rows, width = parts.shape
-    half = pltpu.VMEM((2, rows // 2, width), parts.dtype)
-    dma = pltpu.SemaphoreType.DMA((2,))
+            far_ref.at[owner], given.at[owner], send_far.at[owner], recv_far.at[owner], other
+        )
+
+    def move(steps):
+        for part in range(parts):
+            for way, owner in steps:
+                column.move(way, owner, part)
+
+    rows.start()
+    for owner in column.order:
+        across(owner).start()
+    for load in loads:
+        load.wait()
+    pieces, steps = dense.shape[1], dense.shape[2] // 32
+
+    @pl.loop(0, dense.shape[0] * pieces * steps)
+    def _(step):
+        at = pl.ds(pl.multiple_of((step % steps) * 32, 32), 32)
+        piece = (step // steps) % pieces
+        where = step // (steps * pieces)
+        total = dense[where, piece, at, :].astype(f32) + more[where, piece, at, :].astype(f32)
+        dense[where, piece, at, :] = total.astype(dense.dtype)
+
+    plane.start()
+    for owner in column.order:
+        across(owner).wait_recv()
+        for part in range(parts):
+            column.add(owner, given.at[owner], part)
+            column.begin(owner, part)
+    rows.move()
+    last = column.count - 1
+
+    @pl.when(place == last - 1)
+    def _():
+        move([(0, 0)])
+
+    @pl.when(place == 1)
+    def _():
+        move([(1, last)])
+
+    plane.move()
+
+    @pl.when(place == last - 1)
+    def _():
+        move([(0, 1), (1, last)])
+
+    @pl.when(place == 1)
+    def _():
+        move([(1, last - 1), (0, 0)])
+
+    rows.end()
+    column.end()
+    column.give(out_ref)
+    plane.end()
+    column.finish()
+    plane.finish()
+    rows.finish()
+    for owner in column.order:
+        across(owner).wait_send()
+
+
+def fourth_exchange(near, far, rows, terms, givens, cuts, collective_id, parts=2):
+    count = lax.axis_size(TP)
+    block = near.shape[1:]
+    chips = givens[0].shape[0]
+    width = givens[0].shape[-1]
+    dense = (chips, count, cuts[-1], width)
+    resident = pl.BlockSpec(memory_space=pltpu.VMEM)
+    anywhere = pl.BlockSpec(memory_space=pl.ANY)
+    dma = pltpu.SemaphoreType.DMA
+    pieces = len(cuts) - 1
     return pl.pallas_call(
-        plane_reduce_kernel,
-        out_shape=jax.ShapeDtypeStruct((rows, width), f32),
-        in_specs=[pl.BlockSpec(memory_space=pltpu.VMEM)],
-        out_specs=pl.BlockSpec(memory_space=pltpu.VMEM),
-        scratch_shapes=[half] * 4 + [dma] * 6,
+        functools.partial(fourth_kernel, parts, cuts),
+        out_shape=[
+            jax.ShapeDtypeStruct(block, near.dtype),
+            jax.ShapeDtypeStruct(dense[1:], near.dtype),
+            jax.ShapeDtypeStruct(rows.shape[1:], f32),
+        ],
+        in_specs=[anywhere, resident, resident] + [anywhere] * (2 * pieces),
+        out_specs=[resident] * 3,
+        scratch_shapes=[
+            pltpu.VMEM((count,) + block, near.dtype),
+            pltpu.VMEM((count,) + block, near.dtype),
+            pltpu.VMEM((2, count) + block, near.dtype),
+            pltpu.VMEM(dense, near.dtype),
+            pltpu.VMEM(dense, near.dtype),
+            dma((1 + 2 * pieces,)),
+            dma((count,)),
+            dma((count,)),
+            dma((2, count, parts)),
+            dma((2, count, parts)),
+        ]
+        + reduce_scratch(dense, near.dtype)
+        + reduce_scratch(rows.shape, rows.dtype),
         compiler_params=pltpu.CompilerParams(
-            collective_id=collective_id, has_side_effects=True, vmem_limit_bytes=32 * 2**20
+            collective_id=collective_id, has_side_effects=True, vmem_limit_bytes=52 * 2**20
         ),
-        cost_estimate=lasting(28),
-    )(parts)
-
-
-def all_sum_kernel(rows_ref, out_ref, sums, came, send, receive):
-    chip, core, beside, above, facing = plane_ids()
+        cost_estimate=lasting(62),
+    )(near, far, rows, *terms, *givens)
+
+
+def fifth_kernel(rows_ref, dense_ref, out_ref, own_ref, came, send_z, recv_z, *refs):
+    buffers, sems = refs[:4], refs[4:6]
+    count = lax.axis_size(TP)
     place = lax.axis_index(TP)
-    peers = [
-        {SEQ: 2 * chip + 1 - core},
-        {SEQ: 2 * beside + core},
-        {SEQ: 2 * above + core},
-        {TP: place + 1 - 2 * (place % 2)},
-        {TP: place + 2 - 4 * (place // 2)},
-    ]
-    enter([(place >= 0, peer) for peer in peers])
-    sums[0] = rows_ref[...]
-    for step, peer in enumerate(peers):
-        copy = remote(sums.at[step], came.at[step], send.at[step], receive.at[step], peer)
-        copy.start()
-        copy.wait()
-        sums[step + 1] = sums[step] + came[step]
-    out_ref[...] = sums[len(peers)]
-
-
-def all_sum(rows, collective_id):
-    steps = 5
+    enter(neighbours(False, True))
+    plane = PlaneReduce(64, rows_ref, out_ref, buffers, sems)
+
+    def to_owner(step):
+        owner = lax.rem(place + step, count)
+        return remote(
+            dense_ref.at[owner], came.at[step - 1], send_z.at[step], recv_z.at[step], {TP: owner}
+        )
+
+    plane.start()
+    for step in range(1, count):
+        to_owner(step).start()
+    plane.move()
+    plane.end()
+    for step in range(1, count):
+        to_owner(step).wait()
+
+    @pl.loop(0, own_ref.shape[0] // 32)
+    def _(step):
+        at = pl.ds(pl.multiple_of(step * 32, 32), 32)
+        total = dense_ref[place, at, :].astype(f32)
+        for other in range(count - 1):
+            total = total + came[other, at, :].astype(f32)
+        own_ref[at, :] = total.astype(own_ref.dtype)
+
+    plane.finish()
+
+
+def fifth_exchange(rows, dense, collective_id):
+    count = lax.axis_size(TP)
+    resident = pl.BlockSpec(memory_space=pltpu.VMEM)
+    dma = pltpu.SemaphoreType.DMA
     return pl.pallas_call(
-        all_sum_kernel,
-        out_shape=jax.ShapeDtypeStruct(rows.shape, rows.dtype),
-        in_specs=[pl.BlockSpec(memory_space=pltpu.VMEM)],
-        out_specs=pl.BlockSpec(memory_space=pltpu.VMEM),
+        fifth_kernel,
+        out_shape=[
+            jax.ShapeDtypeStruct(rows.shape[1:], f32),
+            jax.ShapeDtypeStruct(dense.shape[1:], dense.dtype),
+        ],
+        in_specs=[resident] * 2,
+        out_specs=[resident] * 2,
         scratch_shapes=[
-            pltpu.VMEM((steps + 1,) + rows.shape, rows.dtype),
-            pltpu.VMEM((steps,) + rows.shape, rows.dtype),
-            pltpu.SemaphoreType.DMA((steps,)),
-            pltpu.SemaphoreType.DMA((steps,)),
-        ],
+            pltpu.VMEM((count - 1,) + dense.shape[1:], dense.dtype),
+            dma((count,)),
+            dma((count,)),
+        ]
+        + reduce_scratch(rows.shape, rows.dtype),
         compiler_params=pltpu.CompilerParams(
-            collective_id=collective_id, has_side_effects=True
+            collective_id=collective_id, has_side_effects=True, vmem_limit_bytes=48 * 2**20
         ),
-        cost_estimate=lasting(12),
-    )(rows)
-
-
-def holder_sum_kernel(
+        cost_estimate=lasting(30),
+    )(rows, dense)
+
+
+def sixth_kernel(
     parts,
     terms_ref,
+    own_ref,
+    rows_ref,
     out_ref,
+    dense_ref,
+    all_ref,
     sums,
     given,
     came,
@@ -1189,6 +1300,17 @@
     send_on,
     send_back,
     recv_back,
+    keep_sem,
+    send_row,
+    recv_row,
+    send_next,
+    recv_next,
+    send_dense,
+    recv_dense,
+    column_came,
+    plane_came,
+    send_all,
+    recv_all,
 ):
     chip, core, beside, above, facing = plane_ids()
     count = lax.axis_size(TP)
@@ -1199,15 +1321,54 @@
     part_rows = rows // parts
     always = place >= 0
     holds = place == chip
-    enter(
-        [
-            (always, other),
-            (always, ways[0]),
-            (always, ways[1]),
-            (place < count - 1, {TP: place + 1}),
-            (place > 0, {TP: place - 1}),
-        ]
-    )
+    far_column = [
+        (always, {SEQ: 2 * chip + 1 - core, TP: lax.rem(place + step, count)})
+        for step in range(1, count)
+    ]
+    enter(neighbours(True, True) + far_column)
+    half = own_ref.shape[0] // 2
+    dense = PlaneSpread(
+        lambda part: own_ref.at[pl.ds(part * half, half)],
+        lambda where, part: dense_ref.at[where, core, pl.ds(part * half, half)],
+        (send_row, recv_row, send_next, recv_next),
+    )
+    keep = pltpu.make_async_copy(own_ref, dense_ref.at[chip, core], keep_sem)
+
+    def dense_across(where):
+        block = dense_ref.at[(chip, beside, above, facing)[where], core]
+        return remote(block, block, send_dense.at[where], recv_dense.at[where], other)
+
+    mine = core * count + place
+
+    def column_copy(index):
+        peer = lax.rem(mine + index, 2 * count)
+        return remote(
+            rows_ref,
+            column_came.at[mine],
+            send_all.at[index],
+            recv_all.at[index],
+            {SEQ: 2 * chip + peer // count, TP: lax.rem(peer, count)},
+        )
+
+    def column_landed(index):
+        sender = lax.rem(mine + 2 * count - index, 2 * count)
+        block = column_came.at[sender]
+        return remote(block, block, send_all.at[index], recv_all.at[index], other)
+
+    def plane_copy(index):
+        return remote(
+            plane_came.at[chip],
+            plane_came.at[chip],
+            send_all.at[2 * count + index],
+            recv_all.at[2 * count + index],
+            {SEQ: 2 * (beside, above, facing)[index] + core},
+        )
+
+    dense.start()
+    keep.start()
+    column_came[mine] = rows_ref[...]
+    for index in range(1, 2 * count):
+        column_copy(index).start()
 
     def cut(part):
         return pl.ds(part * part_rows, part_rows)
@@ -1246,9 +1407,9 @@
         return remote(
             out_ref.at[own_cut(part)],
             out_ref.at[own_cut(part)],
-            send_on,
+            send_on.at[part],
             recv_plane.at[part],
-            ways[1 - part],
+            ways[1 - part // (parts // 2)],
         )
 
     def back(part):
@@ -1261,6 +1422,8 @@
         )
 
     across.wait_recv()
+    keep.wait()
+    dense_across(0).start()
     for part in range(parts):
         sums[cut(part), :] = terms_ref[own_cut(part), :]
         add(given, part)
@@ -1277,6 +1440,7 @@
 
                 along(way, part).start()
 
+    dense.forward()
     for part in range(parts):
         for way in range(2):
             takes = place < count - 1 if way == 0 else place > 0
@@ -1293,13 +1457,24 @@
                 to_plane(way, part).start()
             back(part).start()
 
+    for index in range(1, 2 * count):
+        column_landed(index).wait_recv()
+    total = column_came[0]
+    for index in range(1, 2 * count):
+        total = total + column_came[index]
+    plane_came[chip] = total
+    for index in range(3):
+        plane_copy(index).start()
+    dense.arrive()
+    for where in range(1, 4):
+        dense_across(where).start()
     for part in range(parts):
 
         @pl.when(place != chip)
         def _():
             to_plane(0, part).wait_recv()
 
-        @pl.when((beside if part == 0 else above) == place)
+        @pl.when((beside if part < parts // 2 else above) == place)
         def _():
             onward(part).start()
 
@@ -1307,11 +1482,22 @@
         def _():
             back(part).start()
 
+    for index in range(1, 2 * count):
+        column_copy(index).wait_send()
+    for index in range(3):
+        plane_copy(index).wait()
+    total = plane_came[0]
+    for index in range(1, plane_came.shape[0]):
+        total = total + plane_came[index]
+    all_ref[...] = total
     across.wait_send()
+    dense.finish()
+    for where in range(4):
+        dense_across(where).wait()
     for part in range(parts):
         back(part).wait()
 
-        @pl.when((beside if part == 0 else above) == place)
+        @pl.when((beside if part < parts // 2 else above) == place)
         def _():
             onward(part).wait_send()
 
@@ -1326,17 +1512,23 @@
                 along(way, part).wait_send()
 
 
-def holder_sum(terms, collective_id):
-    parts = 2
+def sixth_exchange(terms, own, small, collective_id):
+    parts = 4
+    chips = lax.axis_size(SEQ) // 2
+    column = 2 * lax.axis_size(TP)
     rows = terms.shape[0] // 2
     half = (rows,) + terms.shape[1:]
     dma = pltpu.SemaphoreType.DMA
     resident = pl.BlockSpec(memory_space=pltpu.VMEM)
     return pl.pallas_call(
-        functools.partial(holder_sum_kernel, parts),
-        out_shape=jax.ShapeDtypeStruct(terms.shape, terms.dtype),
-        in_specs=[resident],
-        out_specs=resident,
+        functools.partial(sixth_kernel, parts),
+        out_shape=[
+            jax.ShapeDtypeStruct(terms.shape, terms.dtype),
+            jax.ShapeDtypeStruct((chips, 2) + own.shape, own.dtype),
+            jax.ShapeDtypeStruct(small.shape, small.dtype),
+        ],
+        in_specs=[resident] * 3,
+        out_specs=[resident] * 3,
         scratch_shapes=[
             pltpu.VMEM(half, terms.dtype),
             pltpu.VMEM(half, terms.dtype),
@@ -1347,15 +1539,25 @@
             dma((2, parts)),
             dma((2, parts)),
             dma((parts,)),
-            dma,
             dma((parts,)),
             dma((parts,)),
+            dma((parts,)),
+            dma,
+        ]
+        + plane_sems()
+        + [
+            dma((4,)),
+            dma((4,)),
+            pltpu.VMEM((column,) + small.shape, small.dtype),
+            pltpu.VMEM((chips,) + small.shape, small.dtype),
+            dma((column + 3,)),
+            dma((column + 3,)),
         ],
         compiler_params=pltpu.CompilerParams(
             collective_id=collective_id, has_side_effects=True, vmem_limit_bytes=32 * 2**20
         ),
         cost_estimate=lasting(35),
-    )(terms)
+    )(terms, own, small)
 
 
 def plane_applies(mesh, blocks, docs):
@@ -1401,8 +1603,8 @@
     chips = seq_count // 2
     seq_place = lax.axis_index(SEQ)
     tp_place = lax.axis_index(TP)
-    chip = seq_place // 2
-    core = seq_place % 2
+    chip = lax.shift_right_logical(seq_place, 1)
+    core = seq_place & 1
     heads = rand_blocks.shape[2]
     rands = rand_blocks.shape[3]
     local_width = query_weight.shape[1]
@@ -1410,6 +1612,8 @@
     pair_width = heads * PAIR
     hidden_units = inner_weight.shape[1]
     classes = 2 * tp_count
+    class_bits = classes.bit_length() - 1
+    group_bits = SHORT_BLK.bit_length() - 1
     own_class = core * tp_count + tp_place
     long_docs = 2
     slots = 5 + rands
@@ -1433,7 +1637,7 @@
         return values[slot * own_rows : (slot + 1) * own_rows]
 
     stage = [Micro() for _ in range(micro_count)]
-    spare_rows = 64
+    spare_rows = 128
     packed = jnp.concatenate([side_by_side(key_weight, value_weight), query_weight], axis=1)
     packed_bias = jnp.concatenate(
         [side_by_side(jnp.zeros_like(value_bias), value_bias), query_bias]
@@ -1473,17 +1677,22 @@
     pair_wide_bias = packed[model_width, :pair_width]
     query_part = packed[:model_width, pair_width : pair_width + local_width]
     query_part_bias = packed[model_width, pair_width : pair_width + local_width]
+    joined_weight = jnp.concatenate([pair_wide, query_part * score_scale], axis=1)
 
     starts = jnp.cumsum(doc_lengths, axis=1) - doc_lengths
     is_long = doc_lengths == LONG_BLK
     long_firsts = jnp.min(jnp.where(is_long, starts, jnp.iinfo(jnp.int32).max), axis=1)
     long_lasts = jnp.max(jnp.where(is_long, starts, -1), axis=1)
+    first_groups = lax.shift_right_logical(jnp.stack([long_firsts, long_lasts]), group_bits)
+    own_groups = first_groups + ((own_class - first_groups) & (classes - 1))
+    long_rows = lax.shift_right_logical(own_groups, class_bits) * own_rows
     randoms = randoms.reshape(chips, -1)[:, :random_count]
     randoms = randoms.reshape(chips, micro_count, tp_count, SHORT_BLK, heads, rands)
     randoms = lax.dynamic_index_in_dim(randoms, tp_place, axis=2, keepdims=False)
     randoms = jnp.pad(randoms.transpose(1, 3, 0, 2, 4), [(0, 0)] * 4 + [(slots - rands, 0)])
+    randoms = randoms.reshape(micro_count, -1)
     shape = (heads, chips, SHORT_BLK, slots)
-    slot, block, entry = (lax.broadcasted_iota(jnp.int32, shape, axis) for axis in (1, 2, 3))
+    slot, block, entry = (part.reshape(-1) for part in np.indices(shape, np.int32)[1:])
     for micro, held in enumerate(stage):
         group = slot * classes + own_class
         number = group * SHORT_BLK + block
@@ -1509,19 +1718,17 @@
             )
         ):
             key = jnp.where(entry == place, value, key)
-        inside = key % SHORT_BLK
-        key_class = (key // SHORT_BLK) % classes
-        piece = key_class % tp_count + jnp.where(key_class // tp_count == core, 0, tp_count)
+        inside = key & (SHORT_BLK - 1)
+        key_class = lax.shift_right_logical(key, group_bits) & (classes - 1)
+        own_core = lax.shift_right_logical(key_class, class_bits - 1) == core
+        piece = (key_class & (tp_count - 1)) + jnp.where(own_core, 0, tp_count)
         long_place = piece * long_docs + jnp.where(in_long[1], 1, 0)
         short_place = classes * long_docs + slot
-        held.index = (jnp.where(any_long, long_place, short_place) * SHORT_BLK + inside).reshape(-1)
+        held.index = jnp.where(any_long, long_place, short_place) * SHORT_BLK + inside
         counts = jnp.where(entry == 0, number > window_first, number + 1 < window_final)
-        held.valid = counts[0, :, :, :2].astype(jnp.int32).reshape(-1)
-        held.long_rows = []
-        for start in (long_firsts[micro], long_lasts[micro]):
-            first_group = start // SHORT_BLK
-            own_group = first_group + (own_class - first_group) % classes
-            held.long_rows.append((own_group // classes) * own_rows)
+        counts = counts.astype(jnp.int32)[: chips * SHORT_BLK * slots]
+        held.valid = counts.reshape(-1, slots)[:, :2].reshape(-1)
+        held.long_rows = [long_rows[doc, micro] for doc in range(long_docs)]
 
     def long_blocks(micro):
         held = stage[micro]
@@ -1551,7 +1758,8 @@
         held.context_sent, held.logsum = attend_forward(
             held.index, held.valid, held.queries, held.pieces, heads, slots
         )
-        held.context = plane_exchange(held.context_sent, 0, 1)
+        if micro:
+            held.context = plane_exchange(held.context_sent, 0, 1)
 
     def feed_forward(micro):
         held = stage[micro]
@@ -1559,8 +1767,6 @@
             held.context = after(
                 held.context, stage[micro - 1].grad_query, stage[micro - 1].long_sum_sent
             )
-        else:
-            held.context = after(held.context, stage[1].pieces[0])
         hidden = held.inputs + contract(held.context, proj_full, NN) + proj_bias
         shifted, stats, inverse = layer_stats(hidden, second_gain, second_bias)
         held.two = shifted.astype(bf16)
@@ -1617,9 +1823,8 @@
             held.grad_pair = lax.dynamic_update_slice_in_dim(
                 held.grad_pair, slot_rows(long_sum, doc), start, axis=0
             )
-        rows = contract(held.grad_query, query_part * score_scale, NT) + contract(
-            held.grad_pair, pair_wide, NT
-        )
+        held.grad_joined = jnp.concatenate([held.grad_pair, held.grad_query], axis=1)
+        rows = contract(held.grad_joined, joined_weight, NT)
         return rows.astype(bf16).reshape(chips, own_rows, model_width)
 
     def input_back(micro, grad_one):
@@ -1636,10 +1841,15 @@
     keep_pieces(0, near, far, pair_rows)
     attend(0)
     pair_rows, longs = long_blocks(1)
-    near, far, rest, inner_full, outer_full = third_exchange(
-        after(longs, stage[0].context_sent), column, cuts, 7
+    near, far, context, rest, inner_full, outer_full = third_exchange(
+        longs,
+        column,
+        stage[0].context_sent.reshape(chips, own_rows, local_width),
+        cuts,
+        7,
     )
     keep_pieces(1, near, far, pair_rows)
+    stage[0].context = context.transpose(1, 0, 2).reshape(own_rows, model_width)
     inner_full = inner_full.reshape(-1, model_width)
     outer_full = outer_full.reshape(-1, model_width)
     inner_bias_full = rest[:, :, :, proj_cut, :unit_cut].reshape(-1)
@@ -1671,92 +1881,42 @@
         ],
         axis=3,
     )
-    halves = []
-    for part in (
-        contract(grad_before, two, TN).astype(bf16),
-        contract(active, grad_out, TN).astype(bf16),
-        rest_part,
-    ):
-        part = part.reshape(2, chips, -1, model_width)
-        kept = lax.dynamic_index_in_dim(part, core, axis=0, keepdims=False)
-        given = lax.dynamic_index_in_dim(part, 1 - core, axis=0, keepdims=False)
-        halves.append(sum_parts([kept, core_swap(given)]).astype(bf16))
-    halves = jnp.concatenate(halves, axis=1)
-    by_chip = plane_exchange(halves, 0, 0)
+    terms = [
+        part.reshape(2, chips, tp_count, -1, model_width)
+        for part in (
+            contract(grad_before, two, TN).astype(bf16),
+            contract(active, grad_out, TN).astype(bf16),
+            rest_part,
+        )
+    ]
+    givens = [
+        core_swap(lax.dynamic_index_in_dim(part, 1 - core, axis=0, keepdims=False))
+        for part in terms
+    ]
 
     rows = input_rows(0, after(long_sum, stage[1].grad_context_sent))
-    grad_one = [lax.dynamic_index_in_dim(rows, chip, axis=0, keepdims=False)]
-    for step in range(1, chips):
-        part = lax.dynamic_index_in_dim(rows, chip ^ step, axis=0, keepdims=False)
-        route = [(place, place ^ (2 * step)) for place in range(seq_count)]
-        grad_one.append(lax.ppermute(part, SEQ, route))
-    near, far = attend_back(1, halves, rows)
-
-    query_sum = sum(contract(h.one, h.grad_query, TN) for h in stage) * score_scale
-    query_sum = query_sum.astype(bf16)
-    half_rows = model_width // 2
-    kept = lax.dynamic_slice_in_dim(query_sum, core * half_rows, half_rows, axis=0)
-    given = core_swap(
-        lax.dynamic_slice_in_dim(query_sum, (1 - core) * half_rows, half_rows, axis=0)
-    )
-    near = after(near, query_sum)
+    near, far = attend_back(1, rows)
+
     column_shape = (tp_count, long_docs * own_rows, pair_width)
-    long_sum = column_reduce_both(near.reshape(column_shape), far.reshape(column_shape), 3)
-    input_back(0, sum_parts(after(grad_one, long_sum)))
+    cuts = (0, unit_cut, 2 * unit_cut, 2 * unit_cut + rest_rows)
+    row_shape = (chips, 2, own_rows // 2, model_width)
+    long_sum, quarters, grad_one = fourth_exchange(
+        near.reshape(column_shape),
+        far.reshape(column_shape),
+        rows.reshape(row_shape),
+        terms,
+        givens,
+        cuts,
+        3,
+    )
     rows = input_rows(1, long_sum)
-
-    half = sum_parts([kept, given]).astype(bf16)
-    came = [
-        lax.ppermute(
-            after(half, rows),
-            (SEQ, TP),
-            [
-                (place * tp_count + (place // 2 + step) % tp_count, place * tp_count + place // 2)
-                for place in range(seq_count)
-            ],
-        )
-        for step in range(1, tp_count)
-    ]
-    quarters = jnp.sum(after(by_chip, rows).astype(f32), axis=0).astype(bf16)
-    cuts = [0, tp_count * unit_cut, 2 * tp_count * unit_cut, quarters.shape[0]]
-    quarters = jnp.concatenate(
-        [
-            quarters[first:last].reshape(tp_count, -1, model_width)
-            for first, last in zip(cuts, cuts[1:])
-        ],
-        axis=1,
-    )
-    by_column = lax.all_to_all(quarters, TP, split_axis=0, concat_axis=0, tiled=True)
-    grad_one = plane_reduce_now(after(rows, quarters, half), 4)
-    input_back(1, grad_one)
-
-    ones = after([h.one for h in stage], grad_one)
-    pair_sum = sum(contract(one, h.grad_pair, TN) for one, h in zip(ones, stage)).astype(bf16)
-    half = sum_parts([half] + after(came, grad_one)).astype(bf16)
-    came = [
-        lax.ppermute(
-            half,
-            (SEQ, TP),
-            [
-                (place * tp_count + place // 2, (place ^ (2 * step)) * tp_count + place // 2)
-                for place in range(seq_count)
-            ],
-        )
-        for step in range(1, chips)
-    ]
-    own_sum = jnp.sum(after(by_column, grad_one).astype(f32), axis=0).astype(bf16)
-    other_sum = core_swap(own_sum)
-    pair_sum = holder_sum(after(pair_sum, half, own_sum), 6).astype(f32)
-    key_grad = low_half(pair_sum)
-    value_grad = high_half(pair_sum)
-
-    other_sum = after(other_sum, pair_sum)
-    chip_sum = jnp.where(
-        core == 0, jnp.stack([own_sum, other_sum]), jnp.stack([other_sum, own_sum])
-    )
-    dense_sum = plane_gather(chip_sum)
-    near = jnp.where(tp_place == chip, half, sum(after(came, pair_sum)))
-    far = core_swap(near)
+    grad_one_now, own_sum = fifth_exchange(rows.reshape(row_shape), quarters, 4)
+    input_back(0, after(grad_one, rows).reshape(own_rows, model_width))
+    input_back(1, grad_one_now.reshape(own_rows, model_width))
+
+    ones = after([h.one for h in stage], grad_one_now)
+    packed_sum = sum(contract(one, h.grad_joined, TN) for one, h in zip(ones, stage))
+    packed_sum = jnp.pad(packed_sum, ((0, 0), (0, -packed_sum.shape[1] % 128))).astype(bf16)
 
     def own_columns(values):
         wide = jnp.zeros((chips, local_width), f32)
@@ -1764,25 +1924,23 @@
 
     query_bias_sum = sum(jnp.sum(h.grad_query.astype(f32), axis=0) for h in stage)
     pair_bias_sum = sum(jnp.sum(h.grad_pair.astype(f32), axis=0) for h in stage)
-    all_rows = all_sum(
-        after(
-            jnp.concatenate(
-                [
-                    sum(h.row_sums for h in stage),
-                    sum(h.first_sums for h in stage),
-                    own_columns(query_bias_sum * score_scale)[None],
-                    own_columns(high_half(pair_bias_sum))[None],
-                ],
-                axis=0,
-            ),
-            near,
-            chip_sum,
+    packed_sum, dense_sum, all_rows = sixth_exchange(
+        packed_sum,
+        own_sum,
+        jnp.concatenate(
+            [
+                sum(h.row_sums for h in stage),
+                sum(h.first_sums for h in stage),
+                own_columns(query_bias_sum * score_scale)[None],
+                own_columns(high_half(pair_bias_sum))[None],
+            ],
+            axis=0,
         ),
-        5,
-    )
-    query_grad = jnp.where(
-        core == 0, jnp.concatenate([near, far], axis=0), jnp.concatenate([far, near], axis=0)
-    ).astype(f32)
+        6,
+    )
+    key_grad = low_half(packed_sum[:, :pair_width]).astype(f32)
+    value_grad = high_half(packed_sum[:, :pair_width]).astype(f32)
+    query_grad = packed_sum[:, pair_width : pair_width + local_width].astype(f32) * score_scale
     dense_sum = dense_sum.reshape(seq_count, -1, model_width).astype(f32)
     inner_weight_grad = dense_sum[:, :unit_cut].reshape(hidden_units, model_width).T
     outer_weight_grad = dense_sum[:, unit_cut : 2 * unit_cut].reshape(hidden_units, model_width)

time: 758 us -> 688 us (0.908)
  the two profiles are of different devices: /device:TPU:0 before, /device:TPU:13 now
where the time goes in v3:
time: 688 us; the launch traced here: 681 us
  Pallas kernels  411 us (60%)
  matrix products  89.8 us (13%)
  local copies, waits for them, and re-layouts  82.1 us (12%)
  other arithmetic  56.2 us (8%)
  between operations  27.4 us (4%)
  starting transfers between devices  14.5 us (2%)
    dot_general x29, matrix products, contract(): return lax.dot_general(left, right, dims, preferred_element_type=f32)  89.8 us
    pallas_call x1, Pallas kernels, fourth_exchange(): pl.pallas_call(functools.partial(fourth_kernel, parts, cuts), out_shape=[...  79.8 us
    pallas_call x1, Pallas kernels, third_exchange(): pl.pallas_call(functools.partial(third_kernel, parts, cuts), out_shape=[n...  77.6 us
    pallas_call x2, Pallas kernels, attend_backward(): pl.pallas_call(functools.partial(backward_kernel, slots, heads, len(piece...  51.4 us
    pallas_call x1, Pallas kernels, second_exchange(): pl.pallas_call(functools.partial(second_kernel, parts), out_shape=[near,...  51.2 us
    pallas_call x1, Pallas kernels, sixth_exchange(): pl.pallas_call(functools.partial(sixth_kernel, parts), out_shape=[jax.Sha...  39.9 us
    pallas_call x1, Pallas kernels, first_exchange(): pl.pallas_call(functools.partial(first_kernel, parts), out_shape=[jax.Sha...  38.9 us
    pallas_call x2, Pallas kernels, attend_forward(): pl.pallas_call(functools.partial(forward_kernel, slots, heads), grid_spec...  37.5 us
  transfers between devices with their start and end apart: 8, of which 0 were waited for; matrix products, arithmetic and copies ran while one was open for 11% of the time, Pallas kernels for 7%

profile of v3, /device:TPU:13, one launch (start us, length us, event | category | flops | bytes accessed | tf_op | source)
XLA Modules:
  0.0 681.1 jit_solution(5142185919056563354)
XLA Ops:
  26.2 38.9 %shard_map.467 = (bf16[4,512,768]{2,1,0:T(8,128)(2,1)S(1)}, bf16[896,640]{1,0:T(8,128)(2,1)S(1)}, bf16[4,224,768]{2,1,0:T(8,128)(2,1)S(1)}, s32[4,8,128]{2,1,0:T(8,128)S(1)}) custom-call(bf16[512,768]{1,0:T(8,128)(2,1)S(1)} %get-tuple-element.208.own_ref, bf16[896,640]{1,0:T(8,128)(2,1)S(1)} %fusion.70.weight_ref, ...), custom_call_target="tpu_custom_call" | custom-call | bytes 110700000 | tf_op jit(solution)/shard_map/pallas_call | solution.py:755
  71.1 3.7 add_convert_fusion.2.refs_2_
  77.3 51.2 %shard_map.468 = (bf16[4,1024,384]{2,1,0:T(8,128)(2,1)S(1)}, bf16[4,1024,384]{2,1,0:T(8,128)(2,1)S(1)}, bf16[4,512,768]{2,1,0:T(8,128)(2,1)S(1)}) custom-call(bf16[1024,384]{1,0:T(8,128)(2,1)S(1)} %pad_maximum_fusion.14.longs_ref, bf16[512,768]{1,0:T(8,128)(2,1)S(1)} %copy-done.14), custom_call_target="tpu_custom_call" | custom-call | bytes 202950000 | tf_op jit(solution)/shard_map/pallas_call | solution.py:811
  128.5 3.5 add_convert_fusion.1.refs_2_
  132.2 3.2 fusion.114
  135.6 3.9 fusion.23.query_ref
  146.5 18.7 %shard_map.469 = (bf16[2048,192]{1,0:T(8,128)(2,1)S(1)}, f32[2048,384]{1,0:T(8,128)S(1)}) custom-call(s32[768]{0:T(1024)S(1)} %and_add_fusion.1.index_ref, s32[64]{0:T(128)S(1)} %reshape.474.valid_ref, bf16[2048,192]{1,0:T(8,128)(2,1)S(1)} %copy-done.12, bf16[4096,384]{1,0:T(8,128)(2,1)S(1)} %bitcast.275, bf16[4096,384]{1,0:T(8,128)(2,1)S(1)} %bitcast.278, ...), custom_call_target="tpu_custom_call" | custom-call | bytes 66420000 | tf_op jit(solution)/shard_map/pallas_call | solution.py:256
  166.9 77.6 %shard_map.470 = (bf16[4,1024,384]{2,1,0:T(8,128)(2,1)}, bf16[4,1024,384]{2,1,0:T(8,128)(2,1)}, bf16[4,512,192]{2,1,0:T(8,128)(2,1)S(1)}, bf16[2,4,4,32,768]{4,3...) custom-call(bf16[1024,384]{1,0:T(8,128)(2,1)S(1)} %pad_maximum_fusion.15.longs_ref, ...), custom_call_target="tpu_custom_call" | custom-call | bytes 202950000 | tf_op jit(solution)/shard_map/pallas_call | solution.py:919
  254.0 4.8 fusion.135
  258.9 5.8 convert_reduce_fusion.1
  264.7 3.5 multiply_reduce_fusion.3
  274.8 4.4 all-to-all-start.1
  281.0 3.2 fusion.24.query_ref
  285.3 18.8 %shard_map.471 = (bf16[2048,192]{1,0:T(8,128)(2,1)S(1)}, f32[2048,384]{1,0:T(8,128)S(1)}) custom-call(s32[768]{0:T(1024)S(1)} %and_add_fusion.index_ref, s32[64]{0:T(128)S(1)} %reshape.478.valid_ref, bf16[2048,192]{1,0:T(8,128)(2,1)S(1)} %fusion.24.query_ref, bf16[4096,384]{1,0:T(8,128)(2,1)S(1)} %bitcast.272, bf16[4096,384]{1,0:T(8,128)(2,1)S(1)} %bitcast.274, ...), custom_call_target="tpu_custom_call" | custom-call | bytes 66420000 | tf_op jit(solution)/shard_map/pallas_call | solution.py:256
  309.3 25.7 %shard_map.472 = (bf16[2048,192]{1,0:T(8,128)(2,1)S(1)}, bf16[4096,384]{1,0:T(8,128)(2,1)}, bf16[4096,384]{1,0:T(8,128)(2,1)}, bf16[2048,384]{1,0:T(8,128)(2,1)}) custom-call(s32[768]{0:T(1024)S(1)} %and_add_fusion.1.index_ref, s32[64]{0:T(128)S(1)} %reshape.474.valid_ref, bf16[2048,192]{1,0:T(8,128)(2,1)S(1)} %copy-done.13, ...), custom_call_target="tpu_custom_call" | custom-call | bytes 92250000 | tf_op jit(solution)/shard_map/pallas_call | solution.py:279
  337.4 4.3 all-to-all-start
  355.7 4.3 add_convert_fusion
  363.2 11.0 %multiply_convert_fusion.1 = (bf16[512,3072]{1,0:T(8,128)(2,1)}, bf16[512,3072]{1,0:T(8,128)(2,1)}, f32[512,3072]{1,0:T(8,128)S(1)}) fusion(f32[512,3072]{1,0:T(8,128)} %copy-done.136, f32[3072]{0:T(1024)S(1)} %reshape.476, bf16[512,768]{1,0:T(8,128)(2,1)S(1)} %add_convert_fusion.4, bf16[3072,768]{1,0:T(8,128)(2,1)} %bitcast.351), kind=kOutput, calls=%fused_computation.26 | convolution fusion | flops 2434793472 | bytes 24391680 | tf_op jit(solution)/shard_map/dot_general | solution.py:32
  374.3 5.2 convert_reduce_fusion
  379.6 3.5 multiply_reduce_fusion.2
  393.0 4.4 all-to-all-start.2
  397.4 6.0 pad_maximum_fusion
  408.0 5.6 fusion.16
  417.4 5.8 convolution_convert_fusion
  438.2 25.7 %shard_map.473 = (bf16[2048,192]{1,0:T(8,128)(2,1)S(1)}, bf16[4096,384]{1,0:T(8,128)(2,1)}, bf16[4096,384]{1,0:T(8,128)(2,1)}, bf16[2048,384]{1,0:T(8,128)(2,1)}) custom-call(s32[768]{0:T(1024)S(1)} %and_add_fusion.index_ref, s32[64]{0:T(128)S(1)} %reshape.478.valid_ref, bf16[2048,192]{1,0:T(8,128)(2,1)S(1)} %copy-done.11, bf16[2048,192]{1,0:T(8,128)(2,1)S(1)} %bitcast.280, ...), custom_call_target="tpu_custom_call" | custom-call | bytes 92250000 | tf_op jit(solution)/shard_map/pallas_call | solution.py:279
  472.7 4.1 convolution_convert_fusion.2
  476.8 79.8 %shard_map.474 = (bf16[1024,384]{1,0:T(8,128)(2,1)S(1)}, bf16[4,224,768]{2,1,0:T(8,128)(2,1)}, f32[2,256,768]{2,1,0:T(8,128)}) custom-call(bf16[4,1024,384]{2,1,0:T(8,128)(2,1)} %bitcast.303, bf16[4,1024,384]{2,1,0:T(8,128)(2,1)} %bitcast.304, bf16[4,2,256,768]{3,2,1,0:T(8,128)(2,1)} %bitcast.305, bf16[2,4,4,96,768]{4,3,2,1,0:T(8,128)(2,1)} %bitcast.292, ...), custom_call_target="tpu_custom_call" | custom-call | bytes 228780000 | tf_op jit(solution)/shard_map/pallas_call | solution.py:1196
  557.5 3.1 dynamic_update_slice.20
  563.4 5.8 convolution_convert_fusion.1
  570.5 34.7 %shard_map.475 = (f32[2,256,768]{2,1,0:T(8,128)S(1)}, bf16[224,768]{1,0:T(8,128)(2,1)S(1)}) custom-call(bf16[4,2,256,768]{3,2,1,0:T(8,128)(2,1)} %bitcast.306, bf16[4,224,768]{2,1,0:T(8,128)(2,1)S(1)} %copy-done.19), custom_call_target="tpu_custom_call" | custom-call | bytes 110700000 | tf_op jit(solution)/shard_map/pallas_call | solution.py:1262
  615.7 39.9 %shard_map.476 = (bf16[768,640]{1,0:T(8,128)(2,1)S(1)}, bf16[4,2,224,768]{3,2,1,0:T(8,128)(2,1)S(1)}, f32[8,768]{1,0:T(8,128)S(1)}) custom-call(bf16[768,640]{1,0:T(8,128)(2,1)S(1)} %pad.31.terms_ref, bf16[224,768]{1,0:T(8,128)(2,1)S(1)} %get-tuple-element.97.own_ref, f32[8,768]{1,0:T(8,128)S(1)} %pad_maximum_fusion.21.rows_ref), custom_call_target="tpu_custom_call" | custom-call | bytes 129150000 | tf_op jit(solution)/shard_map/pallas_call | solution.py:1523
  665.0 3.2 copy.137
  (514 shorter events, 140.5 us)
Async XLA Ops:
  7.2 13.3 %copy-start = (bf16[768,768]{1,0:T(8,128)(2,1)S(1)}, bf16[768,768]{1,0:T(8,128)(2,1)}, u32[]{:S(2)}) copy-start(bf16[768,768]{1,0:T(8,128)(2,1)} %param.50) | copy-start | bytes 3538948
  7.2 10.1 %copy-start.34 = (bf16[2,512,768]{2,1,0:T(8,128)(2,1)S(1)}, bf16[2,512,768]{2,1,0:T(8,128)(2,1)}, u32[]{:S(2)}) copy-start(bf16[2,512,768]{2,1,0:T(8,128)(2,1)} %param.36) | copy-start | bytes 4718596
  66.2 69.4 %copy-start.132 = (f32[1,192]{1,0:T(1,128)}, f32[1,192]{1,0:T(1,128)S(1)}, u32[]{:S(2)}) copy-start(f32[1,192]{1,0:T(1,128)S(1)} %slice_convert_fusion.4) | copy-start | bytes 2308
  76.3 52.1 %copy-start.28 = (bf16[896,640]{1,0:T(8,128)(2,1)S(1)}, bf16[896,640]{1,0:T(8,128)(2,1)}, u32[]{:S(2)}) copy-start(bf16[896,640]{1,0:T(8,128)(2,1)} %copy-done.27) | copy-start | bytes 3440644
  128.4 15.4 %copy-start.4 = (bf16[4,1024,384]{2,1,0:T(8,128)(2,1)}, bf16[4,1024,384]{2,1,0:T(8,128)(2,1)S(1)}, u32[]{:S(2)}) copy-start(bf16[4,1024,384]{2,1,0:T(8,128)(2,1)S(1)} %get-tuple-element.64) | copy-start | bytes 9437188
  146.5 20.4 %copy-start.18 = (bf16[4,224,768]{2,1,0:T(8,128)(2,1)S(1)}, bf16[4,224,768]{2,1,0:T(8,128)(2,1)}, u32[]{:S(2)}) copy-start(bf16[4,224,768]{2,1,0:T(8,128)(2,1)} %copy-done.17) | copy-start | bytes 4128772
  253.9 10.7 %slice-start.8 = ((s8[4718592]{0:T(1024)(128)(4,1)}), s8[4194304]{0:T(1024)(128)(4,1)S(1)}, s32[]{:S(2)}) async-start(s8[4718592]{0:T(1024)(128)(4,1)} %bitcast.352), calls=%async_computation.13 | async-start | bytes 8388608
  274.8 33.0 %all-to-all-start.1 = ((bf16[4,512,192]{1,2,0:T(8,128)(2,1)}), bf16[4,512,192]{1,2,0:T(8,128)(2,1)}, u32[]{:S(2)}, u32[]{:S(2)}) async-start(bf16[4,512,192]{1,2,0:T(8,128)(2,1)} %pad_maximum_fusion.16), calls=%async_computation.1 | async-start | bytes 1572864 | tf_op jit(solution)/shard_map/all_to_all | solution.py:303
  309.3 26.8 %copy-start.21 = (bf16[2048,192]{1,0:T(8,128)(2,1)S(1)}, bf16[2048,192]{1,0:T(8,128)(2,1)}, u32[]{:S(2)}) copy-start(bf16[2048,192]{1,0:T(8,128)(2,1)} %copy-done.20) | copy-start | bytes 2359300
  335.9 19.3 %collective-permute-start = (bf16[4096,384]{1,0:T(8,128)(2,1)}, bf16[4096,384]{1,0:T(8,128)(2,1)}, u32[]{:S(2)}, u32[]{:S(2)}) collective-permute-start(bf16[4096,384]{1,0:T(8,128)(2,1)} %get-tuple-element.80), channel_id=1, source_target_pairs={{0,4},{4,0},{8,12},{12,8},{16,20},{20,16},{24,28},{28,24},{1,5},{5... | collective-permute-start | bytes 9437192 | tf_op jit(solution)/shard_map/ppermute | solution.py:320
  337.3 9.9 %copy-start.119 = (f32[768]{0:T(1024)S(1)}, f32[768]{0:T(1024)}, u32[]{:S(2)}) copy-start(f32[768]{0:T(1024)} %get-tuple-element.184) | copy-start | bytes 9220
  337.4 10.5 %copy-start.118 = (f32[768]{0:T(1024)S(1)}, f32[768]{0:T(1024)}, u32[]{:S(2)}) copy-start(f32[768]{0:T(1024)} %get-tuple-element.171) | copy-start | bytes 9220
  337.4 13.0 %copy-start.49 = (bf16[2,512,768]{2,1,0:T(8,128)(2,1)S(1)}, bf16[2,512,768]{2,1,0:T(8,128)(2,1)}, u32[]{:S(2)}) copy-start(bf16[2,512,768]{2,1,0:T(8,128)(2,1)} %param.54) | copy-start | bytes 4718596
  337.4 22.7 %all-to-all-start = ((bf16[4,512,192]{1,2,0:T(8,128)(2,1)}), bf16[4,512,192]{1,2,0:T(8,128)(2,1)}, u32[]{:S(2)}, u32[]{:S(2)}) async-start(bf16[4,512,192]{1,2,0:T(8,128)(2,1)} %copy.129), calls=%async_computation | async-start | bytes 1572864 | tf_op jit(solution)/shard_map/all_to_all | solution.py:303
  341.7 124.2 %reduce-scatter.2.cloned.1.call-start = ((), (), s32[]{:S(2)}) async-start(), calls=%async_computation.4 | async-start | bytes 3932160 | tf_op jit(solution)/shard_map/reduce_scatter | solution.py:1862
  362.5 20.5 %copy-start.43 = (f32[512,768]{1,0:T(8,128)}, f32[512,768]{1,0:T(8,128)S(1)}, u32[]{:S(2)}) copy-start(f32[512,768]{1,0:T(8,128)S(1)} %get-tuple-element.256) | copy-start | bytes 4718596
  362.9 11.4 %slice-start.4 = ((s8[4718592]{0:T(1024)(128)(4,1)}), s8[4194304]{0:T(1024)(128)(4,1)S(1)}, s32[]{:S(2)}) async-start(s8[4718592]{0:T(1024)(128)(4,1)} %bitcast.343), calls=%async_computation.9 | async-start | bytes 8388608
  363.2 11.0 %copy-start.56 = (bf16[512,768]{1,0:T(8,128)(2,1)}, bf16[512,768]{1,0:T(8,128)(2,1)S(1)}, u32[]{:S(2)}) copy-start(bf16[512,768]{1,0:T(8,128)(2,1)S(1)} %add_convert_fusion.4) | copy-start | bytes 2359300
  363.2 11.0 %copy-start.50 = (bf16[2,512,768]{2,1,0:T(8,128)(2,1)S(1)}, bf16[2,512,768]{2,1,0:T(8,128)(2,1)}, u32[]{:S(2)}) copy-start(bf16[2,512,768]{2,1,0:T(8,128)(2,1)} %param.54) | copy-start | bytes 4718596
  363.2 11.0 %slice-start.5 = ((s8[4718592]{0:T(1024)(128)(4,1)}), s8[524288]{0:T(1024)(128)(4,1)S(1)}, s32[]{:S(2)}) async-start(s8[4718592]{0:T(1024)(128)(4,1)} %bitcast.343), calls=%async_computation.10 | async-start | bytes 1048576
  363.2 16.3 %slice-start.10 = ((s8[4718592]{0:T(1024)(128)(4,1)}), s8[4194304]{0:T(1024)(128)(4,1)S(1)}, s32[]{:S(2)}) async-start(s8[4718592]{0:T(1024)(128)(4,1)} %bitcast.355), calls=%async_computation.15 | async-start | bytes 8388608
  393.0 43.7 %all-to-all-start.2 = ((bf16[4,512,192]{1,2,0:T(8,128)(2,1)}), bf16[4,512,192]{1,2,0:T(8,128)(2,1)}, u32[]{:S(2)}, u32[]{:S(2)}) async-start(bf16[4,512,192]{1,2,0:T(8,128)(2,1)} %pad_maximum_fusion.17), calls=%async_computation.2 | async-start | bytes 1572864 | tf_op jit(solution)/shard_map/all_to_all | solution.py:303
  406.4 11.0 %slice-start = ((s8[6291456]{0:T(1024)(128)(4,1)}), s8[4194304]{0:T(1024)(128)(4,1)S(1)}, s32[]{:S(2)}) async-start(s8[6291456]{0:T(1024)(128)(4,1)} %bitcast.296), calls=%async_computation.5 | async-start | bytes 8388608
  413.6 13.4 %slice-start.6 = ((s8[4718592]{0:T(1024)(128)(4,1)}), s8[4194304]{0:T(1024)(128)(4,1)S(1)}, s32[]{:S(2)}) async-start(s8[4718592]{0:T(1024)(128)(4,1)} %bitcast.346), calls=%async_computation.11 | async-start | bytes 8388608
  417.1 59.7 %collective-permute-start.1 = (bf16[4,4,96,768]{3,2,1,0:T(8,128)(2,1)}, bf16[4,4,96,768]{3,2,1,0:T(8,128)(2,1)}, u32[]{:S(2)}, u32[]{:S(2)}) collective-permute-start(bf16[4,4,96,768]{3,2,1,0:T(8,128)(2,1)} %dynamic-slice_bitcast_fusion.1), channel_id=1, source_target_pairs={{0,4},{4,0},{8,12},{12,8},{16,20},{20,16},{24,28},{28,24},{1,5},{5... | collective-permute-start | bytes 7077896 | tf_op jit(solution)/shard_map/ppermute | solution.py:320
  417.4 9.5 %copy-start.124 = (f32[768]{0:T(1024)S(1)}, f32[768]{0:T(1024)}, u32[]{:S(2)}) copy-start(f32[768]{0:T(1024)} %convert_element_type.260) | copy-start | bytes 9220
  417.4 9.5 %slice-start.7 = ((s8[4718592]{0:T(1024)(128)(4,1)}), s8[524288]{0:T(1024)(128)(4,1)S(1)}, s32[]{:S(2)}) async-start(s8[4718592]{0:T(1024)(128)(4,1)} %bitcast.346), calls=%async_computation.12 | async-start | bytes 1048576
  426.8 50.1 %collective-permute-start.2 = (bf16[4,4,96,768]{3,2,1,0:T(8,128)(2,1)}, bf16[4,4,96,768]{3,2,1,0:T(8,128)(2,1)}, u32[]{:S(2)}, u32[]{:S(2)}) collective-permute-start(bf16[4,4,96,768]{3,2,1,0:T(8,128)(2,1)} %dynamic-slice_bitcast_fusion), channel_id=1, source_target_pairs={{0,4},{4,0},{8,12},{12,8},{16,20},{20,16},{24,28},{28,24},{1,5},{5... | collective-permute-start | bytes 7077896 | tf_op jit(solution)/shard_map/ppermute | solution.py:320
  435.0 41.8 %collective-permute-start.3 = (bf16[4,4,32,768]{3,2,1,0:T(8,128)(2,1)}, bf16[4,4,32,768]{3,2,1,0:T(8,128)(2,1)}, u32[]{:S(2)}, u32[]{:S(2)}) collective-permute-start(bf16[4,4,32,768]{3,2,1,0:T(8,128)(2,1)} %dynamic-slice_bitcast_fusion.2), channel_id=1, source_target_pairs={{0,4},{4,0},{8,12},{12,8},{16,20},{20,16},{24,28},{28,24},{1,5},{5... | collective-permute-start | bytes 2359304 | tf_op jit(solution)/shard_map/ppermute | solution.py:320
  438.2 27.0 %copy-start.112 = (f32[192]{0:T(256)S(1)}, f32[192]{0:T(256)}, u32[]{:S(2)}) copy-start(f32[192]{0:T(256)} %convert_reduce_fusion.5) | copy-start | bytes 2308
  569.2 36.0 %copy-start.65 = (bf16[2048,384]{1,0:T(8,128)(2,1)S(1)}, bf16[2048,384]{1,0:T(8,128)(2,1)}, u32[]{:S(2)}) copy-start(bf16[2048,384]{1,0:T(8,128)(2,1)} %copy-done.64) | copy-start | bytes 4718596
  570.5 34.7 %copy-start.31 = (bf16[4,512,768]{2,1,0:T(8,128)(2,1)S(1)}, bf16[4,512,768]{2,1,0:T(8,128)(2,1)}, u32[]{:S(2)}) copy-start(bf16[4,512,768]{2,1,0:T(8,128)(2,1)} %copy-done.30) | copy-start | bytes 9437188
  (129 other events, 441.1 us)
Sparse Core Ops, SparseCore 0:
  386.9 62.0 reduce-scatter.1

commit v4 on v3

--- a/solution.py
+++ b/solution.py
@@ -120,7 +120,11 @@
 
         @pl.when(pl.program_id(0) == head)
         def _():
-            work(slice(head * BLOCK, (head + 1) * BLOCK))
+            work(head)
+
+
+def head_columns(head, first=0):
+    return slice(first + head * BLOCK, first + (head + 1) * BLOCK)
 
 
 def forward_kernel(slots, heads, index_ref, valid_ref, query_ref, *refs):
@@ -130,8 +134,8 @@
     head = pl.program_id(0)
     fill_store(store, pieces)
 
-    def take_query(columns):
-        query = query_ref[:, columns]
+    def take_query(own):
+        query = query_ref[:, head_columns(own, heads * PAIR)]
         wide_query[...] = jnp.concatenate([query, jnp.zeros_like(query)], axis=1)
 
     each_head(heads, take_query)
@@ -161,17 +165,16 @@
 
     lax.fori_loop(0, blocks // UNROLL, step, 0)
 
-    def give_context(columns):
-        context_ref[:, columns] = wide_context[:, BLOCK:]
+    def give_context(own):
+        context_ref[:, head_columns(own)] = wide_context[:, BLOCK:]
 
     each_head(heads, give_context)
 
 
 def backward_kernel(slots, heads, count, index_ref, valid_ref, query_ref, grad_ref, logsum_ref, *refs):
-    pieces = refs[:count]
-    grad_query_ref = refs[count]
-    grad_pieces = refs[count + 1 : 2 * count + 1]
-    store, sums, both_rows, wide_grad = refs[2 * count + 1 :]
+    pieces, refs = refs[:count], refs[count:]
+    grad_pieces, joined_ref = refs[: count - 1], refs[count - 1]
+    store, sums, both_rows, wide_grad = refs[count:]
     rows = query_ref.shape[0]
     blocks = rows // BLOCK
     head = pl.program_id(0)
@@ -179,8 +182,9 @@
     sums[...] = jnp.zeros_like(sums)
     lane = lax.broadcasted_iota(jnp.int32, (BLOCK, PAIR), 1)
 
-    def take_both(columns):
-        both_rows[...] = jnp.concatenate([query_ref[:, columns], grad_ref[:, columns]], axis=1)
+    def take_both(own):
+        query = query_ref[:, head_columns(own, heads * PAIR)]
+        both_rows[...] = jnp.concatenate([query, grad_ref[:, head_columns(own)]], axis=1)
 
     each_head(heads, take_both)
 
@@ -229,10 +233,12 @@
         grad_piece[...] = sums[place : place + grad_piece.shape[0], :].astype(bf16)
         place += grad_piece.shape[0]
 
-    def give_grad(columns):
-        grad_query_ref[:, columns] = wide_grad[:, :BLOCK]
-
-    each_head(heads, give_grad)
+    def give_joined(own):
+        joined_ref[:, own * PAIR : (own + 1) * PAIR] = sums[place:, :].astype(bf16)
+        start = heads * PAIR + own * BLOCK
+        joined_ref[:, start : start + BLOCK] = wide_grad[:, :BLOCK]
+
+    each_head(heads, give_joined)
 
 
 def lasting(microseconds):
@@ -249,8 +255,10 @@
     return pl.BlockSpec(array.shape, lambda head, *_: (0, 0))
 
 
-def attend_forward(index, valid, queries, pieces, heads, slots):
-    rows = queries.shape[0]
+def attend_forward(index, valid, joined, pieces, heads, slots):
+    rows = joined.shape[0]
+    pieces = pieces + [joined]
+    context = jax.ShapeDtypeStruct((rows, heads * BLOCK), bf16)
     stored = sum(piece.shape[0] for piece in pieces)
     logsum = jax.ShapeDtypeStruct((rows, heads * PAIR), f32)
     return pl.pallas_call(
@@ -258,22 +266,23 @@
         grid_spec=pltpu.PrefetchScalarGridSpec(
             num_scalar_prefetch=2,
             grid=(heads,),
-            in_specs=[whole(queries)] + [per_head(piece) for piece in pieces],
-            out_specs=[whole(queries), per_head(logsum)],
+            in_specs=[whole(joined)] + [per_head(piece) for piece in pieces],
+            out_specs=[whole(context), per_head(logsum)],
             scratch_shapes=[
                 pltpu.VMEM((stored, PAIR), bf16),
                 pltpu.VMEM((rows, PAIR), bf16),
                 pltpu.VMEM((rows, PAIR), bf16),
             ],
         ),
-        out_shape=[jax.ShapeDtypeStruct(queries.shape, bf16), logsum],
+        out_shape=[context, logsum],
         compiler_params=pltpu.CompilerParams(vmem_limit_bytes=40 * 2**20),
         cost_estimate=lasting(18),
-    )(index, valid, queries, *pieces)
-
-
-def attend_backward(index, valid, queries, grads, logsum, pieces, heads, slots):
-    rows = queries.shape[0]
+    )(index, valid, joined, *pieces)
+
+
+def attend_backward(index, valid, joined, grads, logsum, pieces, heads, slots):
+    rows = joined.shape[0]
+    pieces = pieces + [joined]
     stored = sum(piece.shape[0] for piece in pieces)
     piece_specs = [per_head(piece) for piece in pieces]
     return pl.pallas_call(
@@ -281,8 +290,8 @@
         grid_spec=pltpu.PrefetchScalarGridSpec(
             num_scalar_prefetch=2,
             grid=(heads,),
-            in_specs=[whole(queries), whole(grads), per_head(logsum)] + piece_specs,
-            out_specs=[whole(queries)] + piece_specs,
+            in_specs=[whole(joined), whole(grads), per_head(logsum)] + piece_specs,
+            out_specs=piece_specs[:-1] + [whole(joined)],
             scratch_shapes=[
                 pltpu.VMEM((stored, PAIR), bf16),
                 pltpu.VMEM((stored, PAIR), f32),
@@ -290,11 +299,76 @@
                 pltpu.VMEM((rows, PAIR), bf16),
             ],
         ),
-        out_shape=[jax.ShapeDtypeStruct(queries.shape, bf16)]
-        + [jax.ShapeDtypeStruct(piece.shape, bf16) for piece in pieces],
+        out_shape=[jax.ShapeDtypeStruct(piece.shape, bf16) for piece in pieces],
         compiler_params=pltpu.CompilerParams(vmem_limit_bytes=50 * 2**20),
         cost_estimate=lasting(25),
-    )(index, valid, queries, grads, logsum, *pieces)
+    )(index, valid, joined, grads, logsum, *pieces)
+
+
+def dense_kernel(core_ref, *refs):
+    ins, (given_inner, given_outer, kept_inner, kept_outer, proj) = refs[:12], refs[12:]
+    step = pl.program_id(0)
+    half = pl.num_programs(0) // 2
+
+    def term(first):
+        total = contract(ins[first][...], ins[first + 2][...], TN)
+        return (total + contract(ins[first + 1][...], ins[first + 3][...], TN)).astype(bf16)
+
+    @pl.when(step < half)
+    def _():
+        given_inner[...] = term(0)
+        given_outer[...] = term(4)
+
+    @pl.when(step >= half)
+    def _():
+        kept_inner[...] = term(0)
+        kept_outer[...] = term(4)
+
+    @pl.when(step == 0)
+    def _():
+        proj[...] = term(8)
+
+
+def dense_terms(core, units, rows):
+    steps = 8
+    hidden = units[0][0].shape[1]
+    tile = hidden // steps
+    width = rows[0][0].shape[1]
+
+    def unit_tile(step, core_ref):
+        owner = jnp.where(step < steps // 2, 1 - core_ref[0], core_ref[0])
+        return (0, owner * (steps // 2) + step % (steps // 2))
+
+    def whole_rows(array):
+        return pl.BlockSpec(array.shape, lambda step, *_: (0, 0))
+
+    ins, specs = [], []
+    for place in range(3):
+        for array in units[place]:
+            ins.append(array)
+            if place < 2:
+                specs.append(pl.BlockSpec((array.shape[0], tile), unit_tile))
+            else:
+                specs.append(whole_rows(array))
+        for array in rows[place]:
+            ins.append(array)
+            specs.append(whole_rows(array))
+    half = jax.ShapeDtypeStruct((hidden // 2, width), bf16)
+    proj = jax.ShapeDtypeStruct((units[2][0].shape[1], width), bf16)
+    given = pl.BlockSpec((tile, width), lambda step, *_: (jnp.minimum(step, steps // 2 - 1), 0))
+    kept = pl.BlockSpec((tile, width), lambda step, *_: (jnp.maximum(step - steps // 2, 0), 0))
+    return pl.pallas_call(
+        dense_kernel,
+        grid_spec=pltpu.PrefetchScalarGridSpec(
+            num_scalar_prefetch=1,
+            grid=(steps,),
+            in_specs=specs,
+            out_specs=[given, given, kept, kept, whole_rows(proj)],
+        ),
+        out_shape=[half] * 4 + [proj],
+        compiler_params=pltpu.CompilerParams(vmem_limit_bytes=40 * 2**20),
+        cost_estimate=lasting(15),
+    )(core.reshape(1), *ins)
 
 
 def plane_exchange(values, split_axis, concat_axis):
@@ -782,7 +856,76 @@
     )(own, weight, share, randoms)
 
 
-def second_kernel(parts, longs_ref, own_ref, near_ref, far_ref, out_ref, keep_sem, *sems):
+class WeightSpread:
+
+    def __init__(self, column, rows, out, keep_sem, cross_sems, plane_sems):
+        self.out, self.cross_sems = out, cross_sems
+        self.chip, self.core, self.beside, self.above, self.facing = plane_ids()
+        self.other = {SEQ: 2 * self.chip + 1 - self.core}
+        self.half = column.shape[0] // 2
+        self.plane = PlaneSpread(
+            lambda part: column.at[pl.ds(part * self.half, self.half), rows],
+            lambda where, part: out.at[self.core, where, pl.ds(part * self.half, self.half)],
+            plane_sems,
+        )
+        self.keep = pltpu.make_async_copy(
+            column.at[:, rows], out.at[self.core, self.chip], keep_sem
+        )
+
+    def across(self, where, part):
+        chip = (self.chip, self.beside, self.above, self.facing)[where]
+        block = self.out.at[self.core, chip, pl.ds(part * self.half, self.half)]
+        at = (where, part)
+        return remote(
+            block, block, self.cross_sems[0].at[at], self.cross_sems[1].at[at], self.other
+        )
+
+    def start(self):
+        self.plane.start()
+        self.keep.start()
+
+    def forward(self):
+        self.plane.forward()
+        self.keep.wait()
+        for where, part in ((0, 0), (0, 1), (1, 0), (2, 1)):
+            self.across(where, part).start()
+
+    def arrive(self):
+        self.plane.arrive()
+        for where, part in ((1, 1), (2, 0), (3, 0), (3, 1)):
+            self.across(where, part).start()
+
+    def finish(self):
+        self.plane.finish()
+        for where in range(4):
+            for part in range(2):
+                self.across(where, part).wait()
+
+
+def weight_sems():
+    dma = pltpu.SemaphoreType.DMA
+    return [dma, dma((4, 2)), dma((4, 2))] + plane_sems()
+
+
+def weight_shape(column, rows):
+    tp_count, _, width = column.shape
+    chips = lax.axis_size(SEQ) // 2
+    return jax.ShapeDtypeStruct((2, chips, tp_count, rows[1] - rows[0], width), column.dtype)
+
+
+def second_kernel(
+    parts,
+    rows,
+    longs_ref,
+    own_ref,
+    column_ref,
+    near_ref,
+    far_ref,
+    out_ref,
+    weight_ref,
+    keep_sem,
+    *sems,
+):
     chip, core = plane_ids()[:2]
     enter(neighbours(False, False))
     other = {SEQ: 2 * chip + 1 - core}
@@ -790,74 +933,83 @@
         parts, longs_ref, near_ref, far_ref, other, keep_sem.at[0], sems[:2], sems[2:4]
     )
     own, out, keep_rows = halves_of(own_ref, out_ref, keep_sem.at[1])
-    rows = PlaneSpread(own, out, sems[4:])
+    plane = PlaneSpread(own, out, sems[4:8])
+    weight = WeightSpread(
+        column_ref, pl.ds(rows[0], rows[1] - rows[0]), weight_ref, sems[8], sems[9:11], sems[11:15]
+    )
     longs.start()
-    rows.start()
+    plane.start()
+    weight.start()
     keep_rows.start()
-    rows.forward()
-    for distance in range(1, longs.count):
-        for part in range(parts):
-            longs.step(distance, part)
-    rows.arrive()
-    rows.finish()
+    for part in range(parts):
+        longs.step(1, part)
+    plane.forward()
+    weight.forward()
+    for part in range(parts):
+        longs.step(2, part)
+    plane.arrive()
+    weight.arrive()
+    for part in range(parts):
+        longs.step(3, part)
+    plane.finish()
+    weight.finish()
     longs.finish()
     keep_rows.wait()
 
 
-def second_exchange(longs, own, collective_id, parts=2):
+def second_exchange(longs, own, column, rows, collective_id, parts=2):
     chips = lax.axis_size(SEQ) // 2
     near = jax.ShapeDtypeStruct((lax.axis_size(TP),) + longs.shape, longs.dtype)
     resident = pl.BlockSpec(memory_space=pltpu.VMEM)
     return pl.pallas_call(
-        functools.partial(second_kernel, parts),
-        out_shape=[near, near, jax.ShapeDtypeStruct((chips,) + own.shape, own.dtype)],
-        in_specs=[resident] * 2,
-        out_specs=[resident] * 3,
-        scratch_shapes=[pltpu.SemaphoreType.DMA((2,))] + column_sems(parts) + plane_sems(),
+        functools.partial(second_kernel, parts, rows),
+        out_shape=[
+            near,
+            near,
+            jax.ShapeDtypeStruct((chips,) + own.shape, own.dtype),
+            weight_shape(column, rows),
+        ],
+        in_specs=[resident] * 3,
+        out_specs=[resident] * 4,
+        scratch_shapes=[pltpu.SemaphoreType.DMA((2,))]
+        + column_sems(parts)
+        + plane_sems()
+        + weight_sems(),
         compiler_params=pltpu.CompilerParams(
-            collective_id=collective_id, has_side_effects=True, vmem_limit_bytes=32 * 2**20
+            collective_id=collective_id, has_side_effects=True, vmem_limit_bytes=48 * 2**20
         ),
-        cost_estimate=lasting(55),
-    )(longs, own)
+        cost_estimate=lasting(58),
+    )(longs, own, column)
 
 
 def third_kernel(
-    parts, cuts, longs_ref, column_ref, sent_ref, near_ref, far_ref, context_ref, *refs
+    parts,
+    cuts,
+    longs_ref,
+    column_ref,
+    sent_ref,
+    near_ref,
+    far_ref,
+    context_ref,
+    *refs,
 ):
-    count = len(cuts) - 1
+    count = len(cuts)
     outs, refs = refs[:count], refs[count:]
-    keep_sem, cross_sems, block_sems, sems = refs[0], refs[1:3], refs[3:5], refs[5:]
+    keep_sem, block_sems, sems = refs[0], refs[1:3], refs[3:7]
     chip, core, beside, above, facing = plane_ids()
     enter(neighbours(True, False))
     other = {SEQ: 2 * chip + 1 - core}
     longs = ColumnSpread(
         parts, longs_ref, near_ref, far_ref, other, keep_sem.at[0], sems[:2], sems[2:4]
     )
-    half = column_ref.shape[0] // 2
     weights = []
-    keeps = []
-    for place in range(count):
-        rows = pl.ds(cuts[place], cuts[place + 1] - cuts[place])
-        out = outs[place]
+    for index, (first, last) in enumerate(cuts):
+        own = refs[7 + 7 * index : 14 + 7 * index]
         weights.append(
-            PlaneSpread(
-                lambda part, rows=rows: column_ref.at[pl.ds(part * half, half), rows],
-                lambda where, part, out=out: out.at[core, where, pl.ds(part * half, half)],
-                [sem.at[place] for sem in sems[4:]],
+            WeightSpread(
+                column_ref, pl.ds(first, last - first), outs[index], own[0], own[1:3], own[3:7]
             )
         )
-        keeps.append(
-            pltpu.make_async_copy(
-                column_ref.at[:, rows], out.at[core, chip], keep_sem.at[1 + place]
-            )
-        )
-
-    def across(place, where, part):
-        block = outs[place].at[
-            core, (chip, beside, above, facing)[where], pl.ds(part * half, half)
-        ]
-        at = (place, where, part)
-        return remote(block, block, cross_sems[0].at[at], cross_sems[1].at[at], other)
 
     def send_block(index):
         target = (beside, above, facing)[index]
@@ -869,65 +1021,47 @@
             {SEQ: 2 * target + core},
         )
 
-    keep_block = pltpu.make_async_copy(
-        sent_ref.at[chip], context_ref.at[chip], keep_sem.at[1 + count]
-    )
+    keep_block = pltpu.make_async_copy(sent_ref.at[chip], context_ref.at[chip], keep_sem.at[1])
     longs.start()
-    for weight, keep in zip(weights, keeps):
+    for weight in weights:
         weight.start()
-        keep.start()
     for index in range(3):
         send_block(index).start()
     keep_block.start()
     for part in range(parts):
         longs.step(1, part)
-    for place in range(count):
-        weights[place].forward()
-        keeps[place].wait()
-        for where, part in ((0, 0), (0, 1), (1, 0), (2, 1)):
-            across(place, where, part).start()
+    for weight in weights:
+        weight.forward()
     for part in range(parts):
         longs.step(2, part)
-    for place in range(count):
-        weights[place].arrive()
-        for where, part in ((1, 1), (2, 0), (3, 0), (3, 1)):
-            across(place, where, part).start()
+    for weight in weights:
+        weight.arrive()
     for part in range(parts):
         longs.step(3, part)
     longs.finish()
-    for place in range(count):
-        weights[place].finish()
-        for where in range(4):
-            for part in range(2):
-                across(place, where, part).wait()
+    for weight in weights:
+        weight.finish()
     for index in range(3):
         send_block(index).wait()
     keep_block.wait()
 
 
 def third_exchange(longs, column, sent, cuts, collective_id, parts=2):
-    chips = lax.axis_size(SEQ) // 2
-    tp_count, _, width = column.shape
-    near = jax.ShapeDtypeStruct((tp_count,) + longs.shape, longs.dtype)
-    count = len(cuts) - 1
-    outs = [
-        jax.ShapeDtypeStruct((2, chips, tp_count, last - first, width), column.dtype)
-        for first, last in zip(cuts, cuts[1:])
-    ]
+    near = jax.ShapeDtypeStruct((column.shape[0],) + longs.shape, longs.dtype)
     resident = pl.BlockSpec(memory_space=pltpu.VMEM)
     dma = pltpu.SemaphoreType.DMA
+    sems = [sem for _ in cuts for sem in weight_sems()]
     return pl.pallas_call(
         functools.partial(third_kernel, parts, cuts),
-        out_shape=[near, near, jax.ShapeDtypeStruct(sent.shape, sent.dtype)] + outs,
+        out_shape=[near, near, jax.ShapeDtypeStruct(sent.shape, sent.dtype)]
+        + [weight_shape(column, rows) for rows in cuts],
         in_specs=[resident] * 3,
-        out_specs=[resident] * (3 + count),
-        scratch_shapes=[dma((2 + count,)), dma((count, 4, 2)), dma((count, 4, 2)), dma((3,)), dma((3,))]
-        + column_sems(parts)
-        + [dma((count, 2, 2)), dma((count, 2, 2)), dma((count, 2)), dma((count, 2))],
+        out_specs=[resident] * (3 + len(cuts)),
+        scratch_shapes=[dma((2,)), dma((3,)), dma((3,))] + column_sems(parts) + sems,
         compiler_params=pltpu.CompilerParams(
             collective_id=collective_id, has_side_effects=True, vmem_limit_bytes=48 * 2**20
         ),
-        cost_estimate=lasting(55),
+        cost_estimate=lasting(58),
     )(longs, column, sent)
 
 
@@ -1092,13 +1226,12 @@
     return [half] * 4 + [sems, sems]
 
 
-def fourth_kernel(parts, cuts, near_ref, far_ref, rows_ref, *refs):
+def fourth_kernel(parts, cuts, near_ref, far_ref, *refs):
     count = len(cuts) - 1
     terms, givens, refs = refs[:count], refs[count : 2 * count], refs[2 * count :]
-    out_ref, dense_ref, rows_out_ref, sums, given, came, dense, more = refs[:8]
-    load_sem, send_far, recv_far, send_z, recv_z = refs[8:13]
-    buffers, sems = refs[13:17], refs[17:19]
-    row_buffers, row_sems = refs[19:23], refs[23:25]
+    out_ref, dense_ref, sums, given, came, dense, more = refs[:7]
+    load_sem, send_far, recv_far, send_z, recv_z = refs[7:12]
+    buffers, sems = refs[12:16], refs[16:18]
     place = lax.axis_index(TP)
     chip, core = plane_ids()[:2]
     other = {SEQ: 2 * chip + 1 - core}
@@ -1107,7 +1240,7 @@
         rows = pl.ds(cuts[index], cuts[index + 1] - cuts[index])
         loads.append(
             pltpu.make_async_copy(
-                terms[index].at[core], dense.at[:, :, rows], load_sem.at[1 + 2 * index]
+                terms[index], dense.at[:, :, rows], load_sem.at[1 + 2 * index]
             )
         )
         loads.append(
@@ -1116,9 +1249,9 @@
     for load in loads:
         load.start()
     enter(neighbours(False, False))
-    column = ColumnReduce(parts, 128, sums, came, (send_z, recv_z))
-    plane = PlaneReduce(32, dense, dense_ref, buffers, sems)
-    rows = PlaneReduce(64, rows_ref, rows_out_ref, row_buffers, row_sems)
+    step_rows = dense.shape[2] // 2
+    column = ColumnReduce(parts, sums.shape[1] // parts // 2, sums, came, (send_z, recv_z))
+    plane = PlaneReduce(step_rows, dense, dense_ref, buffers, sems)
 
     def across(owner):
         return remote(
@@ -1130,16 +1263,15 @@
             for way, owner in steps:
                 column.move(way, owner, part)
 
-    rows.start()
     for owner in column.order:
         across(owner).start()
     for load in loads:
         load.wait()
-    pieces, steps = dense.shape[1], dense.shape[2] // 32
+    pieces, steps = dense.shape[1], dense.shape[2] // step_rows
 
     @pl.loop(0, dense.shape[0] * pieces * steps)
     def _(step):
-        at = pl.ds(pl.multiple_of((step % steps) * 32, 32), 32)
+        at = pl.ds(pl.multiple_of((step % steps) * step_rows, step_rows), step_rows)
         piece = (step // steps) % pieces
         where = step // (steps * pieces)
         total = dense[where, piece, at, :].astype(f32) + more[where, piece, at, :].astype(f32)
@@ -1151,7 +1283,6 @@
         for part in range(parts):
             column.add(owner, given.at[owner], part)
             column.begin(owner, part)
-    rows.move()
     last = column.count - 1
 
     @pl.when(place == last - 1)
@@ -1172,18 +1303,16 @@
     def _():
         move([(1, last - 1), (0, 0)])
 
-    rows.end()
     column.end()
     column.give(out_ref)
     plane.end()
     column.finish()
     plane.finish()
-    rows.finish()
     for owner in column.order:
         across(owner).wait_send()
 
 
-def fourth_exchange(near, far, rows, terms, givens, cuts, collective_id, parts=2):
+def fourth_exchange(near, far, terms, givens, cuts, collective_id, parts=2):
     count = lax.axis_size(TP)
     block = near.shape[1:]
     chips = givens[0].shape[0]
@@ -1198,10 +1327,9 @@
         out_shape=[
             jax.ShapeDtypeStruct(block, near.dtype),
             jax.ShapeDtypeStruct(dense[1:], near.dtype),
-            jax.ShapeDtypeStruct(rows.shape[1:], f32),
         ],
-        in_specs=[anywhere, resident, resident] + [anywhere] * (2 * pieces),
-        out_specs=[resident] * 3,
+        in_specs=[anywhere, resident] + [anywhere] * (2 * pieces),
+        out_specs=[resident] * 2,
         scratch_shapes=[
             pltpu.VMEM((count,) + block, near.dtype),
             pltpu.VMEM((count,) + block, near.dtype),
@@ -1214,13 +1342,12 @@
             dma((2, count, parts)),
             dma((2, count, parts)),
         ]
-        + reduce_scratch(dense, near.dtype)
-        + reduce_scratch(rows.shape, rows.dtype),
+        + reduce_scratch(dense, near.dtype),
         compiler_params=pltpu.CompilerParams(
             collective_id=collective_id, has_side_effects=True, vmem_limit_bytes=52 * 2**20
         ),
         cost_estimate=lasting(62),
-    )(near, far, rows, *terms, *givens)
+    )(near, far, *terms, *givens)
 
 
 def fifth_kernel(rows_ref, dense_ref, out_ref, own_ref, came, send_z, recv_z, *refs):
@@ -1228,7 +1355,7 @@
     count = lax.axis_size(TP)
     place = lax.axis_index(TP)
     enter(neighbours(False, True))
-    plane = PlaneReduce(64, rows_ref, out_ref, buffers, sems)
+    plane = PlaneReduce(rows_ref.shape[2] // 2, rows_ref, out_ref, buffers, sems)
 
     def to_owner(step):
         owner = lax.rem(place + step, count)
@@ -1244,9 +1371,11 @@
     for step in range(1, count):
         to_owner(step).wait()
 
-    @pl.loop(0, own_ref.shape[0] // 32)
+    step_rows = own_ref.shape[0] // 2
+
+    @pl.loop(0, 2)
     def _(step):
-        at = pl.ds(pl.multiple_of(step * 32, 32), 32)
+        at = pl.ds(pl.multiple_of(step * step_rows, step_rows), step_rows)
         total = dense_ref[place, at, :].astype(f32)
         for other in range(count - 1):
             total = total + came[other, at, :].astype(f32)
@@ -1678,6 +1807,7 @@
     query_part = packed[:model_width, pair_width : pair_width + local_width]
     query_part_bias = packed[model_width, pair_width : pair_width + local_width]
     joined_weight = jnp.concatenate([pair_wide, query_part * score_scale], axis=1)
+    joined_bias = jnp.concatenate([pair_wide_bias, query_part_bias * score_scale])
 
     starts = jnp.cumsum(doc_lengths, axis=1) - doc_lengths
     is_long = doc_lengths == LONG_BLK
@@ -1732,31 +1862,26 @@
 
     def long_blocks(micro):
         held = stage[micro]
-        pair_rows = (contract(held.one, pair_wide, NN) + pair_wide_bias).astype(bf16)
+        held.joined = (contract(held.one, joined_weight, NN) + joined_bias).astype(bf16)
         longs = jnp.concatenate(
             [
-                lax.dynamic_slice_in_dim(pair_rows, start, own_rows, axis=0)
+                lax.dynamic_slice(held.joined, (start, 0), (own_rows, pair_width))
                 for start in held.long_rows
             ],
             axis=0,
         )
-        return pair_rows, longs
-
-    def keep_pieces(micro, near, far, pair_rows):
-        stage[micro].pieces = [
-            near.reshape(-1, pair_width), far.reshape(-1, pair_width), pair_rows
-        ]
+        return longs
+
+    def keep_pieces(micro, near, far):
+        stage[micro].pieces = [near.reshape(-1, pair_width), far.reshape(-1, pair_width)]
 
     def attend(micro):
         held = stage[micro]
-        one = held.one
+        index = held.index
         if micro:
-            one = after(one, stage[micro - 1].grad_context_sent)
-        held.queries = (
-            (contract(one, query_part, NN) + query_part_bias) * score_scale
-        ).astype(bf16)
+            index = after(index, stage[micro - 1].grad_context_sent)
         held.context_sent, held.logsum = attend_forward(
-            held.index, held.valid, held.queries, held.pieces, heads, slots
+            index, held.valid, held.joined, held.pieces, heads, slots
         )
         if micro:
             held.context = plane_exchange(held.context_sent, 0, 1)
@@ -1765,7 +1890,7 @@
         held = stage[micro]
         if micro:
             held.context = after(
-                held.context, stage[micro - 1].grad_query, stage[micro - 1].long_sum_sent
+                held.context, stage[micro - 1].long_sum_sent
             )
         hidden = held.inputs + contract(held.context, proj_full, NN) + proj_bias
         shifted, stats, inverse = layer_stats(hidden, second_gain, second_bias)
@@ -1805,10 +1930,10 @@
 
     def attend_back(micro, *earlier):
         held = stage[micro]
-        held.grad_query, near, far, held.grad_pair = attend_backward(
+        near, far, held.grad_joined = attend_backward(
             held.index,
             held.valid,
-            held.queries,
+            held.joined,
             after(held.grad_context, *earlier),
             held.logsum,
             held.pieces,
@@ -1819,11 +1944,13 @@
 
     def input_rows(micro, long_sum):
         held = stage[micro]
+        shape = (chips, own_rows, pair_width + local_width)
+        place, lane = np.indices(shape, np.int32, sparse=True)[::2]
+        joined = held.grad_joined.reshape(shape)
         for doc, start in enumerate(held.long_rows):
-            held.grad_pair = lax.dynamic_update_slice_in_dim(
-                held.grad_pair, slot_rows(long_sum, doc), start, axis=0
-            )
-        held.grad_joined = jnp.concatenate([held.grad_pair, held.grad_query], axis=1)
+            long_part = jnp.pad(slot_rows(long_sum, doc), ((0, 0), (0, local_width)))
+            joined = jnp.where((place * own_rows == start) & (lane < pair_width), long_part, joined)
+        held.grad_joined = joined.reshape(group_rows, -1)
         rows = contract(held.grad_joined, joined_weight, NT)
         return rows.astype(bf16).reshape(chips, own_rows, model_width)
 
@@ -1835,20 +1962,20 @@
         held.input_grad = held.grad_hidden + back
         held.first_sums = jnp.stack([gain_sum, shift_sum])
 
-    pair_rows, longs = long_blocks(0)
-    near, far, one = second_exchange(longs, stage[1].low, 2)
+    longs = long_blocks(0)
+    near, far, one, outer_full = second_exchange(longs, stage[1].low, column, cuts[2:4], 2)
     stage[1].one = one.reshape(group_rows, model_width)
-    keep_pieces(0, near, far, pair_rows)
+    keep_pieces(0, near, far)
     attend(0)
-    pair_rows, longs = long_blocks(1)
-    near, far, context, rest, inner_full, outer_full = third_exchange(
+    longs = long_blocks(1)
+    near, far, context, rest, inner_full = third_exchange(
         longs,
         column,
         stage[0].context_sent.reshape(chips, own_rows, local_width),
-        cuts,
+        (cuts[0:2], cuts[1:3]),
         7,
     )
-    keep_pieces(1, near, far, pair_rows)
+    keep_pieces(1, near, far)
     stage[0].context = context.transpose(1, 0, 2).reshape(own_rows, model_width)
     inner_full = inner_full.reshape(-1, model_width)
     outer_full = outer_full.reshape(-1, model_width)
@@ -1862,14 +1989,11 @@
     long_sum = lax.psum_scatter(stage[0].long_sum_sent, TP, scatter_dimension=0, tiled=True)
     feed_forward(1)
 
-    two, grad_before, active, grad_out, context, branch = (
-        jnp.concatenate(group, axis=0)
-        for group in zip(
-            *((h.two, h.grad_before, h.active, h.grad_out, h.context, h.branch) for h in stage)
-        )
-    )
-    two, active, context = after((two, active, context), stage[1].grad_context_sent)
-    proj_part = contract(context, branch, TN).astype(bf16)
+    given_inner, given_outer, kept_inner, kept_outer, proj_part = dense_terms(
+        after(core, stage[1].grad_context_sent),
+        [[h.grad_before for h in stage], [h.active for h in stage], [h.context for h in stage]],
+        [[h.two for h in stage], [h.grad_out for h in stage], [h.branch for h in stage]],
+    )
     proj_part = proj_part.reshape(tp_count, chips, 2, proj_cut, model_width)
     unit_shape = (2, chips, tp_count)
     unit_sum = sum(h.unit_sum for h in stage).astype(bf16)
@@ -1881,37 +2005,33 @@
         ],
         axis=3,
     )
-    terms = [
-        part.reshape(2, chips, tp_count, -1, model_width)
-        for part in (
-            contract(grad_before, two, TN).astype(bf16),
-            contract(active, grad_out, TN).astype(bf16),
-            rest_part,
-        )
-    ]
-    givens = [
-        core_swap(lax.dynamic_index_in_dim(part, 1 - core, axis=0, keepdims=False))
-        for part in terms
-    ]
-
-    rows = input_rows(0, after(long_sum, stage[1].grad_context_sent))
+    unit_shape = (chips, tp_count, -1, model_width)
+    terms = [kept_inner.reshape(unit_shape), kept_outer.reshape(unit_shape)]
+    givens = [core_swap(part.reshape(unit_shape)) for part in (given_inner, given_outer)]
+    terms.append(lax.dynamic_index_in_dim(rest_part, core, axis=0, keepdims=False))
+    givens.append(
+        core_swap(lax.dynamic_index_in_dim(rest_part, 1 - core, axis=0, keepdims=False))
+    )
+
+    rows = input_rows(0, after(long_sum, kept_inner))
+    grad_one = lax.psum_scatter(
+        rows.reshape(group_rows, model_width),
+        SEQ,
+        scatter_dimension=0,
+        axis_index_groups=[list(range(place, seq_count, 2)) for place in range(2)],
+        tiled=True,
+    )
     near, far = attend_back(1, rows)
 
     column_shape = (tp_count, long_docs * own_rows, pair_width)
     cuts = (0, unit_cut, 2 * unit_cut, 2 * unit_cut + rest_rows)
     row_shape = (chips, 2, own_rows // 2, model_width)
-    long_sum, quarters, grad_one = fourth_exchange(
-        near.reshape(column_shape),
-        far.reshape(column_shape),
-        rows.reshape(row_shape),
-        terms,
-        givens,
-        cuts,
-        3,
+    long_sum, quarters = fourth_exchange(
+        near.reshape(column_shape), far.reshape(column_shape), terms, givens, cuts, 3
     )
     rows = input_rows(1, long_sum)
     grad_one_now, own_sum = fifth_exchange(rows.reshape(row_shape), quarters, 4)
-    input_back(0, after(grad_one, rows).reshape(own_rows, model_width))
+    input_back(0, after(grad_one, rows).astype(f32))
     input_back(1, grad_one_now.reshape(own_rows, model_width))
 
     ones = after([h.one for h in stage], grad_one_now)
@@ -1922,8 +2042,7 @@
         wide = jnp.zeros((chips, local_width), f32)
         return lax.dynamic_update_slice_in_dim(wide, values[None], chip, axis=0).reshape(-1)
 
-    query_bias_sum = sum(jnp.sum(h.grad_query.astype(f32), axis=0) for h in stage)
-    pair_bias_sum = sum(jnp.sum(h.grad_pair.astype(f32), axis=0) for h in stage)
+    joined_sum = sum(jnp.sum(h.grad_joined.astype(f32), axis=0) for h in stage)
     packed_sum, dense_sum, all_rows = sixth_exchange(
         packed_sum,
         own_sum,
@@ -1931,8 +2050,8 @@
             [
                 sum(h.row_sums for h in stage),
                 sum(h.first_sums for h in stage),
-                own_columns(query_bias_sum * score_scale)[None],
-                own_columns(high_half(pair_bias_sum))[None],
+                own_columns(joined_sum[pair_width:] * score_scale)[None],
+                own_columns(high_half(joined_sum[:pair_width]))[None],
             ],
             axis=0,
         ),
@@ -2044,23 +2163,25 @@
     for micro, held in enumerate(stage):
         one = held.one
         pair_rows = (contract(one, pair_wide, NN) + pair_wide_bias).astype(bf16)
-        pieces = [
-            pair_rows if offset == 0 else from_behind(pair_rows, SEQ, -offset)
-            for offset in range(-reach_dev, reach_dev + 1)
-        ]
+        offsets = [offset for offset in range(-reach_dev, reach_dev + 1) if offset != 0]
+        pieces = [from_behind(pair_rows, SEQ, -offset) for offset in offsets]
         queries = ((contract(one, query_weight, NN) + query_bias) * score_scale).astype(bf16)
+        held.joined = jnp.concatenate([pair_rows, queries], axis=1)
         key_index, key_valid = block_keys(doc_lengths[micro], rand_blocks[micro], blocks)
         slots = key_index.shape[2]
         slot_index = jnp.clip(key_index - lowest, 0, window * block_dev - 1)
+        piece = slot_index // block_dev
+        piece = jnp.where(piece == reach_dev, 2 * reach_dev, piece - (piece > reach_dev))
+        slot_index = piece * block_dev + slot_index % block_dev
         held.index = slot_index.transpose(1, 0, 2).reshape(-1)
         held.valid = key_valid.reshape(-1)
-        held.queries, held.pieces = queries, pieces
+        held.pieces = pieces
 
     for held in stage:
         context, held.logsum = attend_forward(
             held.index,
             held.valid,
-            held.queries,
+            held.joined,
             held.pieces,
             heads,
             slots,
@@ -2124,22 +2245,21 @@
     proj_weight_grad = dense_sum[cuts[2] : cuts[3]]
 
     for held in stage:
-        held.grad_query, *grad_pieces = attend_backward(
+        *grad_pieces, joined = attend_backward(
             held.index,
             held.valid,
-            held.queries,
+            held.joined,
             held.grad_context,
             held.logsum,
             held.pieces,
             heads,
             slots,
         )
-        returned = grad_pieces[reach_dev].astype(f32)
-        for offset in range(-reach_dev, reach_dev + 1):
-            if offset != 0:
-                returned = returned + from_behind(
-                    grad_pieces[offset + reach_dev], SEQ, offset
-                ).astype(f32)
+        pair_width = heads * PAIR
+        returned = joined[:, :pair_width].astype(f32)
+        held.grad_query = joined[:, pair_width:]
+        for offset, grad_piece in zip(offsets, grad_pieces):
+            returned = returned + from_behind(grad_piece, SEQ, offset).astype(f32)
         held.grad_pair = returned.astype(bf16)
 
     input_grads = []

time: 688 us -> 672 us (0.977)
  waiting for transfers between devices: 0.04 us -> 17.7 us
  matrix products: 89.8 us -> 72.7 us
  other arithmetic: 56.2 us -> 45 us
  local copies, waits for them, and re-layouts: 82.1 us -> 72.9 us
    pallas_call x1 -> x2, Pallas kernels: 51.2 us -> 81 us  [the longest x1 65.3 us: second_exchange(): pl.pallas_call(functools.partial(second_kernel, parts, rows), out_shape=[...]
    pallas_call x1, Pallas kernels: 77.6 us -> 57.1 us  [third_exchange(): pl.pallas_call(functools.partial(third_kernel, parts, cuts), out_shape=[n...]
    dot_general x29 -> x24, matrix products: 89.8 us -> 72.7 us  [contract(): return lax.dot_general(left, right, dims, preferred_element_type=f32)]
    pallas_call x1, Pallas kernels: 79.8 us -> 68.1 us  [fourth_exchange(): pl.pallas_call(functools.partial(fourth_kernel, parts, cuts), out_shape=[...]
    reduce_scatter x1, waiting for transfers between devices: 0.01 us -> 11.6 us  [plane_body(): lax.psum_scatter(stage[0].long_sum_sent, TP, scatter_dimension=0, tiled=T...]
    concatenate x5 -> x2, other arithmetic: 11.3 us -> 0.16 us  [long_blocks(): jnp.concatenate([lax.dynamic_slice(held.joined, (start, 0), (own_rows, pa...]
    dynamic_update_slice x4 -> x0, local copies, waits for them, and re-layouts: 9.99 us -> none  [input_rows(): lax.dynamic_update_slice_in_dim(held.grad_pair, slot_rows(long_sum, doc),...]
    unnamed x316 -> x246, local copies, waits for them, and re-layouts: 32.2 us -> 38.5 us
  transfers between devices with their start and end apart: 8 -> 9, of which waited for: 0 -> 3; matrix products, arithmetic and copies ran while one was open for 11% -> 10% of each run, Pallas kernels for 7% -> 25%
where the time goes in v4:
time: 672 us; the launch traced here: 665 us
  Pallas kernels  414 us (62%)
  local copies, waits for them, and re-layouts  72.9 us (11%)
  matrix products  72.7 us (11%)
  other arithmetic  45 us (7%)
  between operations  26.1 us (4%)
  waiting for transfers between devices  17.7 us (3%)
  starting transfers between devices  16.4 us (2%)
    dot_general x24, matrix products, contract(): return lax.dot_general(left, right, dims, preferred_element_type=f32)  72.7 us
    pallas_call x1, Pallas kernels, fourth_exchange(): pl.pallas_call(functools.partial(fourth_kernel, parts, cuts), out_shape=[...  68.1 us
    pallas_call x1, Pallas kernels, second_exchange(): pl.pallas_call(functools.partial(second_kernel, parts, rows), out_shape=[...  65.3 us
    pallas_call x1, Pallas kernels, third_exchange(): pl.pallas_call(functools.partial(third_kernel, parts, cuts), out_shape=[n...  57.1 us
    pallas_call x2, Pallas kernels, attend_backward(): pl.pallas_call(functools.partial(backward_kernel, slots, heads, len(piece...  54.1 us
    pallas_call x1, Pallas kernels, first_exchange(): pl.pallas_call(functools.partial(first_kernel, parts), out_shape=[jax.Sha...  38.8 us
    pallas_call x1, Pallas kernels, sixth_exchange(): pl.pallas_call(functools.partial(sixth_kernel, parts), out_shape=[jax.Sha...  38.7 us
    pallas_call x1, Pallas kernels, fifth_exchange(): pl.pallas_call(fifth_kernel, out_shape=[jax.ShapeDtypeStruct(rows.shape[1...  38.6 us
  transfers between devices with their start and end apart: 9, of which 3 were waited for; matrix products, arithmetic and copies ran while one was open for 10% of the time, Pallas kernels for 25%

profile of v4, /device:TPU:13, one launch (start us, length us, event | category | flops | bytes accessed | tf_op | source)
XLA Modules:
  0.0 664.8 jit_solution(8192537861648748408)
XLA Ops:
  15.7 2.9 add_convert_fusion.7
  22.1 38.8 %shard_map.539 = (bf16[4,512,768]{2,1,0:T(8,128)(2,1)S(1)}, bf16[896,640]{1,0:T(8,128)(2,1)S(1)}, bf16[4,224,768]{2,1,0:T(8,128)(2,1)S(1)}, s32[4,8,128]{2,1,0:T(8,128)S(1)}) custom-call(bf16[512,768]{1,0:T(8,128)(2,1)S(1)} %get-tuple-element.216.own_ref, bf16[896,640]{1,0:T(8,128)(2,1)S(1)} %fusion.59.weight_ref, bf16[224,768]{1,0:T(8,128)(2,1)S(1)} %copy-done.21, ...), custom_call_target="tpu_custom_call" | custom-call | bytes 110700000 | tf_op jit(solution)/shard_map/pallas_call | solution.py:829
  72.6 4.5 add_convert_fusion.2.query_ref.refs_2_
  78.9 65.3 %shard_map.540 = (bf16[4,1024,384]{2,1,0:T(8,128)(2,1)S(1)}, bf16[4,1024,384]{2,1,0:T(8,128)(2,1)}, bf16[4,512,768]{2,1,0:T(8,128)(2,1)}, bf16[2,4,4,96,768]{4,3,2,1,0:T(8,128)(2,1)}) custom-call(bf16[1024,384]{1,0:T(8,128)(2,1)S(1)} %pad_maximum_fusion.3.longs_ref, bf16[512,768]{1,0:T(8,128)(2,1)S(1)} %copy-done.15, ...), custom_call_target="tpu_custom_call" | custom-call | bytes 214020000 | tf_op jit(solution)/shard_map/pallas_call | solution.py:964
  144.2 5.6 add_convert_fusion.1.query_ref.refs_2_
  151.5 3.1 fusion.102
  162.0 18.7 %shard_map.541 = (bf16[2048,192]{1,0:T(8,128)(2,1)S(1)}, f32[2048,384]{1,0:T(8,128)S(1)}) custom-call(s32[768]{0:T(1024)S(1)} %and_add_fusion.1.index_ref, s32[64]{0:T(128)S(1)} %reshape.565.valid_ref, bf16[2048,576]{1,0:T(8,128)(2,1)S(1)} %copy-done.4, bf16[4096,384]{1,0:T(8,128)(2,1)S(1)} %bitcast.319, bf16[4096,384]{1,0:T(8,128)(2,1)S(1)} %bitcast.321, ...), custom_call_target="tpu_custom_call" | custom-call | bytes 66420000 | tf_op jit(solution)/shard_map/pallas_call | solution.py:264
  182.3 57.1 %shard_map.542 = (bf16[4,1024,384]{2,1,0:T(8,128)(2,1)}, bf16[4,1024,384]{2,1,0:T(8,128)(2,1)}, bf16[4,512,192]{2,1,0:T(8,128)(2,1)S(1)}, bf16[2,4,4,32,768]{4,3...) custom-call(bf16[1024,384]{1,0:T(8,128)(2,1)S(1)} %pad_maximum_fusion.4.longs_ref, bf16[4,224,768]{2,1,0:T(8,128)(2,1)S(1)} %copy-done.11, ...), custom_call_target="tpu_custom_call" | custom-call | bytes 214020000 | tf_op jit(solution)/shard_map/pallas_call | solution.py:1054
  250.4 4.8 fusion.113
  255.3 5.8 convert_reduce_fusion.1
  261.2 3.5 multiply_reduce_fusion.2
  271.0 5.0 all-to-all-start.1
  282.9 18.8 %shard_map.543 = (bf16[2048,192]{1,0:T(8,128)(2,1)S(1)}, f32[2048,384]{1,0:T(8,128)S(1)}) custom-call(s32[768]{0:T(1024)S(1)} %and_add_fusion.index_ref, s32[64]{0:T(128)S(1)} %reshape.568.valid_ref, bf16[2048,576]{1,0:T(8,128)(2,1)S(1)} %add_convert_fusion.1.query_ref.refs_2_, bf16[4096,384]{1,0:T(8,128)(2,1)S(1)} %bitcast.315, ...), custom_call_target="tpu_custom_call" | custom-call | bytes 66420000 | tf_op jit(solution)/shard_map/pallas_call | solution.py:264
  305.8 27.0 %shard_map.544 = (bf16[4096,384]{1,0:T(8,128)(2,1)}, bf16[4096,384]{1,0:T(8,128)(2,1)}, bf16[2048,576]{1,0:T(8,128)(2,1)S(1)}) custom-call(s32[768]{0:T(1024)S(1)} %and_add_fusion.1.index_ref, s32[64]{0:T(128)S(1)} %reshape.565.valid_ref, bf16[2048,576]{1,0:T(8,128)(2,1)} %copy-done.3, bf16[2048,192]{1,0:T(8,128)(2,1)S(1)} %bitcast.322, ...), custom_call_target="tpu_custom_call" | custom-call | bytes 92250000 | tf_op jit(solution)/shard_map/pallas_call | solution.py:288
  336.6 4.3 all-to-all-start
  346.2 4.3 add_convert_fusion
  353.3 2.8 fusion.112
  357.2 10.6 %multiply_convert_fusion.1 = (bf16[512,3072]{1,0:T(8,128)(2,1)}, bf16[512,3072]{1,0:T(8,128)(2,1)}, f32[512,3072]{1,0:T(8,128)S(1)}) fusion(f32[512,3072]{1,0:T(8,128)} %copy-done.108, f32[3072]{0:T(1024)S(1)} %copy-done.84, bf16[512,768]{1,0:T(8,128)(2,1)S(1)} %add_convert_fusion.4.refs_3_, bf16[3072,768]{1,0:T(8,128)(2,1)} %bitcast.381), kind=kOutput, calls=%fused_computation.21 | convolution fusion | flops 2434793472 | bytes 24391680 | tf_op jit(solution)/shard_map/dot_general | solution.py:32
  367.8 5.3 convert_reduce_fusion
  373.1 3.0 multiply_reduce_fusion.1
  380.9 15.7 %shard_map.545 = (bf16[1536,768]{1,0:T(8,128)(2,1)S(1)}, bf16[1536,768]{1,0:T(8,128)(2,1)S(1)}, bf16[1536,768]{1,0:T(8,128)(2,1)S(1)}, bf16[1536,768]{1,0:T(8,128)(2,1)}, bf16[768,768]{1,0:T(8,128)(2,1)S(1)}) custom-call(s32[1]{0:T(128)} %bitcast.58.core_ref, bf16[512,3072]{1,0:T(8,128)(2,1)} %copy-done.46, bf16[512,3072]{1,0:T(8,128)(2,1)} %copy-done.49, ...), custom_call_target="tpu_custom_call" | custom-call | bytes 55350000 | tf_op jit(solution)/shard_map/pallas_call | solution.py:360
  401.9 11.6 %reduce-scatter.3.cloned.1.call-done = bf16[1024,384]{1,0:T(8,128)(2,1)} async-done(((bf16[4096,384]{1,0:T(8,128)(2,1)}), bf16[1024,384]{1,0:T(8,128)(2,1)}) %reduce-scatter.3.cloned.1.call-update) | async-done | bytes 786448 | tf_op jit(solution)/shard_map/reduce_scatter | solution.py:1989
  418.4 4.2 convolution_convert_fusion.1
  425.4 4.4 all-to-all-start.2
  433.7 5.7 fusion.49
  443.4 5.5 all-to-all-done.2
  450.4 27.1 %shard_map.546 = (bf16[4096,384]{1,0:T(8,128)(2,1)}, bf16[4096,384]{1,0:T(8,128)(2,1)}, bf16[2048,576]{1,0:T(8,128)(2,1)S(1)}) custom-call(s32[768]{0:T(1024)S(1)} %and_add_fusion.index_ref, s32[64]{0:T(128)S(1)} %reshape.568.valid_ref, bf16[2048,576]{1,0:T(8,128)(2,1)} %copy-done.2, bf16[2048,192]{1,0:T(8,128)(2,1)S(1)} %bitcast.323, ...), custom_call_target="tpu_custom_call" | custom-call | bytes 92250000 | tf_op jit(solution)/shard_map/pallas_call | solution.py:288
  477.5 68.1 %shard_map.547 = (bf16[1024,384]{1,0:T(8,128)(2,1)S(1)}, bf16[4,224,768]{2,1,0:T(8,128)(2,1)}) custom-call(bf16[4,1024,384]{2,1,0:T(8,128)(2,1)} %bitcast.341, bf16[4,1024,384]{2,1,0:T(8,128)(2,1)} %bitcast.342, bf16[4,4,96,768]{3,2,1,0:T(8,128)(2,1)} %bitcast.324, bf16[4,4,96,768]{3,2,1,0:T(8,128)(2,1)} %bitcast.353, ...), custom_call_target="tpu_custom_call" | custom-call | bytes 228780000 | tf_op jit(solution)/shard_map/pallas_call | solution.py:1325
  547.2 4.0 convolution_convert_fusion
  551.2 38.6 %shard_map.548 = (f32[2,256,768]{2,1,0:T(8,128)S(1)}, bf16[224,768]{1,0:T(8,128)(2,1)S(1)}) custom-call(bf16[4,2,256,768]{3,2,1,0:T(8,128)(2,1)} %bitcast.340, bf16[4,224,768]{2,1,0:T(8,128)(2,1)S(1)} %copy-done.22), custom_call_target="tpu_custom_call" | custom-call | bytes 110700000 | tf_op jit(solution)/shard_map/pallas_call | solution.py:1391
  601.3 38.7 %shard_map.549 = (bf16[768,640]{1,0:T(8,128)(2,1)S(1)}, bf16[4,2,224,768]{3,2,1,0:T(8,128)(2,1)S(1)}, f32[8,768]{1,0:T(8,128)S(1)}) custom-call(bf16[768,640]{1,0:T(8,128)(2,1)S(1)} %pad.48.terms_ref, bf16[224,768]{1,0:T(8,128)(2,1)S(1)} %get-tuple-element.97.own_ref, f32[8,768]{1,0:T(8,128)S(1)} %pad_maximum_fusion.8.rows_ref), custom_call_target="tpu_custom_call" | custom-call | bytes 129150000 | tf_op jit(solution)/shard_map/pallas_call | solution.py:1652
  649.4 3.2 copy.154
  (440 shorter events, 120.5 us)
Async XLA Ops:
  22.1 40.7 %copy-start.94 = (s32[2,18]{1,0:T(2,128)S(1)}, s32[2,18]{1,0:T(2,128)}, u32[]{:S(2)}) copy-start(s32[2,18]{1,0:T(2,128)} %param.45) | copy-start | bytes 436
  62.6 16.0 %copy-start.10 = (bf16[4,224,768]{2,1,0:T(8,128)(2,1)}, bf16[4,224,768]{2,1,0:T(8,128)(2,1)S(1)}, u32[]{:S(2)}) copy-start(bf16[4,224,768]{2,1,0:T(8,128)(2,1)S(1)} %get-tuple-element.61.column_ref) | copy-start | bytes 4128772
  62.7 14.4 %copy-start.67 = (bf16[768,192]{1,0:T(8,128)(2,1)}, bf16[768,192]{1,0:T(8,128)(2,1)S(1)}, u32[]{:S(2)}) copy-start(bf16[768,192]{1,0:T(8,128)(2,1)S(1)} %slice_multiply_fusion) | copy-start | bytes 884740
  62.8 81.4 %copy-start.64 = (bf16[768,384]{1,0:T(8,128)(2,1)}, bf16[768,384]{1,0:T(8,128)(2,1)S(1)}, u32[]{:S(2)}) copy-start(bf16[768,384]{1,0:T(8,128)(2,1)S(1)} %slice.211) | copy-start | bytes 1769476
  78.6 65.6 %copy-start.68 = (bf16[768,192]{1,0:T(8,128)(2,1)S(1)}, bf16[768,192]{1,0:T(8,128)(2,1)}, u32[]{:S(2)}) copy-start(bf16[768,192]{1,0:T(8,128)(2,1)} %copy-done.67) | copy-start | bytes 884740
  144.2 7.3 %copy-start.78 = (s32[768]{0:T(1024)S(1)}, s32[768]{0:T(1024)}, u32[]{:S(2)}) copy-start(s32[768]{0:T(1024)} %constant.137.clone) | copy-start | bytes 9220
  144.2 7.3 %copy-start.79 = (s32[768]{0:T(1024)S(1)}, s32[768]{0:T(1024)}, u32[]{:S(2)}) copy-start(s32[768]{0:T(1024)} %constant.136.clone) | copy-start | bytes 9220
  144.2 7.3 %copy-start.87 = (pred[768]{0:T(1024)(128)(4,1)S(1)}, pred[768]{0:T(1024)(128)(4,1)}, u32[]{:S(2)}) copy-start(pred[768]{0:T(1024)(128)(4,1)} %constant.138.clone) | copy-start | bytes 2308
  149.9 129.2 %copy-start.2 = (bf16[2048,576]{1,0:T(8,128)(2,1)}, bf16[2048,576]{1,0:T(8,128)(2,1)S(1)}, u32[]{:S(2)}) copy-start(bf16[2048,576]{1,0:T(8,128)(2,1)S(1)} %add_convert_fusion.1.query_ref.refs_2_) | copy-start | bytes 7077892
  162.0 20.3 %copy-start.11 = (bf16[4,224,768]{2,1,0:T(8,128)(2,1)S(1)}, bf16[4,224,768]{2,1,0:T(8,128)(2,1)}, u32[]{:S(2)}) copy-start(bf16[4,224,768]{2,1,0:T(8,128)(2,1)} %copy-done.10) | copy-start | bytes 4128772
  250.4 10.8 %slice-start.6 = ((s8[4718592]{0:T(1024)(128)(4,1)}), s8[4194304]{0:T(1024)(128)(4,1)S(1)}, s32[]{:S(2)}) async-start(s8[4718592]{0:T(1024)(128)(4,1)} %bitcast.382), calls=%async_computation.13 | async-start | bytes 8388608
  271.0 33.4 %all-to-all-start.1 = ((bf16[4,512,192]{1,2,0:T(8,128)(2,1)}), bf16[4,512,192]{1,2,0:T(8,128)(2,1)}, u32[]{:S(2)}, u32[]{:S(2)}) async-start(bf16[4,512,192]{1,2,0:T(8,128)(2,1)} %pad_maximum_fusion.5), calls=%async_computation.1 | async-start | bytes 1572864 | tf_op jit(solution)/shard_map/all_to_all | solution.py:377
  305.8 29.6 %copy-start.26 = (bf16[2048,192]{1,0:T(8,128)(2,1)S(1)}, bf16[2048,192]{1,0:T(8,128)(2,1)}, u32[]{:S(2)}) copy-start(bf16[2048,192]{1,0:T(8,128)(2,1)} %copy-done.25) | copy-start | bytes 2359300
  334.3 12.0 %collective-permute-start = (bf16[4096,384]{1,0:T(8,128)(2,1)}, bf16[4096,384]{1,0:T(8,128)(2,1)}, u32[]{:S(2)}, u32[]{:S(2)}) collective-permute-start(bf16[4096,384]{1,0:T(8,128)(2,1)} %get-tuple-element.79), channel_id=1, source_target_pairs={{0,4},{4,0},{8,12},{12,8},{16,20},{20,16},{24,28},{28,24},{1,5},{5... | collective-permute-start | bytes 9437192 | tf_op jit(solution)/shard_map/ppermute | solution.py:394
  336.6 15.2 %all-to-all-start = ((bf16[4,512,192]{1,2,0:T(8,128)(2,1)}), bf16[4,512,192]{1,2,0:T(8,128)(2,1)}, u32[]{:S(2)}, u32[]{:S(2)}) async-start(bf16[4,512,192]{1,2,0:T(8,128)(2,1)} %copy.144), calls=%async_computation | async-start | bytes 1572864 | tf_op jit(solution)/shard_map/all_to_all | solution.py:377
  341.0 72.5 %reduce-scatter.3.cloned.1.call-start = ((), (), s32[]{:S(2)}) async-start(), calls=%async_computation.5 | async-start | bytes 3932160 | tf_op jit(solution)/shard_map/reduce_scatter | solution.py:1989
  350.6 248.5 %reduce-scatter.5.cloned.1.call-start = ((), (), s32[]{:S(2)}) async-start(), calls=%async_computation.6 | async-start | bytes 3932160 | tf_op jit(solution)/shard_map/reduce_scatter | solution.py:2017
  353.3 14.5 %slice-start.2 = ((s8[4718592]{0:T(1024)(128)(4,1)}), s8[4194304]{0:T(1024)(128)(4,1)S(1)}, s32[]{:S(2)}) async-start(s8[4718592]{0:T(1024)(128)(4,1)} %bitcast.374), calls=%async_computation.9 | async-start | bytes 8388608
  356.1 20.1 %copy-start.38 = (f32[512,768]{1,0:T(8,128)}, f32[512,768]{1,0:T(8,128)S(1)}, u32[]{:S(2)}) copy-start(f32[512,768]{1,0:T(8,128)S(1)} %get-tuple-element.264) | copy-start | bytes 4718596
  357.2 10.6 %copy-start.41 = (bf16[2,512,768]{2,1,0:T(8,128)(2,1)S(1)}, bf16[2,512,768]{2,1,0:T(8,128)(2,1)}, u32[]{:S(2)}) copy-start(bf16[2,512,768]{2,1,0:T(8,128)(2,1)} %param.62) | copy-start | bytes 4718596
  357.2 10.6 %slice-start.3 = ((s8[4718592]{0:T(1024)(128)(4,1)}), s8[524288]{0:T(1024)(128)(4,1)S(1)}, s32[]{:S(2)}) async-start(s8[4718592]{0:T(1024)(128)(4,1)} %bitcast.374), calls=%async_computation.10 | async-start | bytes 1048576
  357.2 16.0 %slice-start.8 = ((s8[4718592]{0:T(1024)(128)(4,1)}), s8[4194304]{0:T(1024)(128)(4,1)S(1)}, s32[]{:S(2)}) async-start(s8[4718592]{0:T(1024)(128)(4,1)} %bitcast.385), calls=%async_computation.15 | async-start | bytes 8388608
  425.4 23.5 %all-to-all-start.2 = ((bf16[4,512,192]{1,2,0:T(8,128)(2,1)}), bf16[4,512,192]{1,2,0:T(8,128)(2,1)}, u32[]{:S(2)}, u32[]{:S(2)}) async-start(bf16[4,512,192]{1,2,0:T(8,128)(2,1)} %pad_maximum_fusion.6), calls=%async_computation.4 | async-start | bytes 1572864 | tf_op jit(solution)/shard_map/all_to_all | solution.py:377
  429.8 47.6 %collective-permute-start.1 = (bf16[4,4,96,768]{3,2,1,0:T(8,128)(2,1)}, bf16[4,4,96,768]{3,2,1,0:T(8,128)(2,1)}, u32[]{:S(2)}, u32[]{:S(2)}) collective-permute-start(bf16[4,4,96,768]{3,2,1,0:T(8,128)(2,1)} %bitcast.333), channel_id=1, source_target_pairs={{0,4},{4,0},{8,12},{12,8},{16,20},{20,16},{24,28},{28,24},{1,5},{5... | collective-permute-start | bytes 7077896 | tf_op jit(solution)/shard_map/ppermute | solution.py:394
  430.7 46.7 %collective-permute-start.2 = (bf16[4,4,96,768]{3,2,1,0:T(8,128)(2,1)}, bf16[4,4,96,768]{3,2,1,0:T(8,128)(2,1)}, u32[]{:S(2)}, u32[]{:S(2)}) collective-permute-start(bf16[4,4,96,768]{3,2,1,0:T(8,128)(2,1)} %bitcast.332), channel_id=1, source_target_pairs={{0,4},{4,0},{8,12},{12,8},{16,20},{20,16},{24,28},{28,24},{1,5},{5... | collective-permute-start | bytes 7077896 | tf_op jit(solution)/shard_map/ppermute | solution.py:394
  432.4 6.9 %copy-start.37 = (f32[512,768]{1,0:T(8,128)S(1)}, f32[512,768]{1,0:T(8,128)}, u32[]{:S(2)}) copy-start(f32[512,768]{1,0:T(8,128)} %copy-done.35) | copy-start | bytes 4718596
  432.5 6.9 %copy-start.47 = (bf16[512,3072]{1,0:T(8,128)(2,1)S(1)}, bf16[512,3072]{1,0:T(8,128)(2,1)}, u32[]{:S(2)}) copy-start(bf16[512,3072]{1,0:T(8,128)(2,1)} %get-tuple-element.240.refs_4_) | copy-start | bytes 9437188
  432.5 6.9 %slice-start.5 = ((s8[4718592]{0:T(1024)(128)(4,1)}), s8[524288]{0:T(1024)(128)(4,1)S(1)}, s32[]{:S(2)}) async-start(s8[4718592]{0:T(1024)(128)(4,1)} %bitcast.377), calls=%async_computation.12 | async-start | bytes 1048576
  432.5 45.0 %collective-permute-start.3 = (bf16[4,4,32,768]{3,2,1,0:T(8,128)(2,1)}, bf16[4,4,32,768]{3,2,1,0:T(8,128)(2,1)}, u32[]{:S(2)}, u32[]{:S(2)}) collective-permute-start(bf16[4,4,32,768]{3,2,1,0:T(8,128)(2,1)} %get-tuple-element.222), channel_id=1, source_target_pairs={{0,4},{4,0},{8,12},{12,8},{16,20},{20,16},{24,28},{28,24},{1,5},{5... | collective-permute-start | bytes 2359304 | tf_op jit(solution)/shard_map/ppermute | solution.py:394
  551.2 38.6 %copy-start.42 = (f32[1,512,768]{2,1,0:T(8,128)S(1)}, f32[1,512,768]{2,1,0:T(8,128)}, u32[]{:S(2)}) copy-start(f32[1,512,768]{2,1,0:T(8,128)} %slice_convert_fusion) | copy-start | bytes 4718596
  551.2 38.6 %copy-start.75 = (f32[768]{0:T(1024)S(1)}, f32[768]{0:T(1024)}, u32[]{:S(2)}) copy-start(f32[768]{0:T(1024)} %copy-done.74) | copy-start | bytes 9220
  551.2 39.4 %copy-start.59 = (bf16[2048,576]{1,0:T(8,128)(2,1)S(1)}, bf16[2048,576]{1,0:T(8,128)(2,1)}, u32[]{:S(2)}) copy-start(bf16[2048,576]{1,0:T(8,128)(2,1)} %copy-done.58) | copy-start | bytes 7077892
  (96 other events, 255.1 us)
Sparse Core Ops, SparseCore 0:
  350.7 62.7 reduce-scatter.2
  422.8 52.4 reduce-scatter.4

commit v5 on v4

--- a/solution.py
+++ b/solution.py
@@ -127,25 +127,17 @@
     return slice(first + head * BLOCK, first + (head + 1) * BLOCK)
 
 
-def forward_kernel(slots, heads, index_ref, valid_ref, query_ref, *refs):
-    *pieces, context_ref, logsum_ref, store, wide_query, wide_context = refs
-    rows = query_ref.shape[0]
-    blocks = rows // BLOCK
-    head = pl.program_id(0)
-    fill_store(store, pieces)
-
-    def take_query(own):
-        query = query_ref[:, head_columns(own, heads * PAIR)]
-        wide_query[...] = jnp.concatenate([query, jnp.zeros_like(query)], axis=1)
-
-    each_head(heads, take_query)
+def forward_head(slots, head, index_ref, valid_ref, store, wide_query, wide_context, logsum_ref):
+    blocks = wide_query.shape[0] // BLOCK
 
     def step(group, carry):
         ids = [group * UNROLL + unit for unit in range(UNROLL)]
-        listed = [
-            listed_blocks(index_ref, store, (head * blocks + block) * slots, slots)
-            for block in ids
-        ]
+        listed = []
+        for block in ids:
+            first = (head * blocks + block) * slots
+            listed.append(
+                jnp.concatenate([store[index_ref[first + slot]] for slot in range(slots)], axis=0)
+            )
         scores = [
             mask_scores(contract(wide_query[block_rows(block), :], pairs, NT), valid_ref, block)
             for block, pairs in zip(ids, listed)
@@ -164,6 +156,27 @@
         return carry
 
     lax.fori_loop(0, blocks // UNROLL, step, 0)
+
+
+def widen(query):
+    return jnp.concatenate([query, jnp.zeros_like(query)], axis=1)
+
+
+def forward_kernel(slots, heads, index_ref, valid_ref, query_ref, *refs):
+    *pieces, context_ref, logsum_ref, store, wide_query, wide_context = refs
+    place = 0
+    for piece in pieces:
+        count = piece.shape[0] // BLOCK
+        store[place : place + count] = piece[...].reshape(count, BLOCK, PAIR)
+        place += count
+
+    def take_query(own):
+        wide_query[...] = widen(query_ref[:, head_columns(own, heads * PAIR)])
+
+    each_head(heads, take_query)
+    forward_head(
+        slots, pl.program_id(0), index_ref, valid_ref, store, wide_query, wide_context, logsum_ref
+    )
 
     def give_context(own):
         context_ref[:, head_columns(own)] = wide_context[:, BLOCK:]
@@ -269,7 +282,7 @@
             in_specs=[whole(joined)] + [per_head(piece) for piece in pieces],
             out_specs=[whole(context), per_head(logsum)],
             scratch_shapes=[
-                pltpu.VMEM((stored, PAIR), bf16),
+                pltpu.VMEM((stored // BLOCK, BLOCK, PAIR), bf16),
                 pltpu.VMEM((rows, PAIR), bf16),
                 pltpu.VMEM((rows, PAIR), bf16),
             ],
@@ -985,55 +998,102 @@
 def third_kernel(
     parts,
     cuts,
+    slots,
+    heads,
+    index_ref,
+    valid_ref,
     longs_ref,
     column_ref,
-    sent_ref,
-    near_ref,
-    far_ref,
-    context_ref,
+    joined_ref,
     *refs,
 ):
     count = len(cuts)
+    pieces, refs = refs[:3], refs[3:]
+    near_ref, far_ref, context_ref, logsum_ref, refs = refs[0], refs[1], refs[2], refs[3], refs[4:]
     outs, refs = refs[:count], refs[count:]
-    keep_sem, block_sems, sems = refs[0], refs[1:3], refs[3:7]
+    stores, wide_query, wide_context, sent, refs = refs[:2], refs[2], refs[3], refs[4], refs[5:]
+    load_sem, keep_sem, block_sems, sems = refs[0], refs[1], refs[2:4], refs[4:8]
     chip, core, beside, above, facing = plane_ids()
     enter(neighbours(True, False))
     other = {SEQ: 2 * chip + 1 - core}
     longs = ColumnSpread(
-        parts, longs_ref, near_ref, far_ref, other, keep_sem.at[0], sems[:2], sems[2:4]
+        parts, longs_ref, near_ref, far_ref, other, keep_sem, sems[:2], sems[2:4]
     )
     weights = []
     for index, (first, last) in enumerate(cuts):
-        own = refs[7 + 7 * index : 14 + 7 * index]
+        own = refs[8 + 7 * index : 15 + 7 * index]
         weights.append(
             WeightSpread(
                 column_ref, pl.ds(first, last - first), outs[index], own[0], own[1:3], own[3:7]
             )
         )
 
+    def loads(head):
+        copies, place = [], 0
+        for index, piece in enumerate(pieces):
+            rows = piece.shape[0]
+            copies.append(
+                pltpu.make_async_copy(
+                    piece.at[:, :, pl.ds(head * PAIR, PAIR)],
+                    stores[head % 2].at[pl.ds(place, rows)],
+                    load_sem.at[head, index],
+                )
+            )
+            place += rows
+        return copies
+
+    def load(head):
+        for copy in loads(head):
+            copy.start()
+
+    def work(head):
+        for copy in loads(head):
+            copy.wait()
+        if head + 1 < heads:
+            load(head + 1)
+        wide_query[...] = widen(joined_ref[:, head_columns(head, heads * PAIR)])
+        forward_head(
+            slots,
+            head,
+            index_ref,
+            valid_ref,
+            stores[head % 2],
+            wide_query,
+            wide_context,
+            logsum_ref.at[:, pl.ds(head * PAIR, PAIR)],
+        )
+        rows = sent.shape[1]
+        for place in range(sent.shape[0]):
+            sent[place, :, head_columns(head)] = wide_context[
+                place * rows : (place + 1) * rows, BLOCK:
+            ]
+
     def send_block(index):
         target = (beside, above, facing)[index]
         return remote(
-            sent_ref.at[target],
+            sent.at[target],
             context_ref.at[chip],
             block_sems[0].at[index],
             block_sems[1].at[index],
             {SEQ: 2 * target + core},
         )
 
-    keep_block = pltpu.make_async_copy(sent_ref.at[chip], context_ref.at[chip], keep_sem.at[1])
+    load(0)
     longs.start()
     for weight in weights:
         weight.start()
-    for index in range(3):
-        send_block(index).start()
-    keep_block.start()
+    work(0)
     for part in range(parts):
         longs.step(1, part)
     for weight in weights:
         weight.forward()
+    work(1)
     for part in range(parts):
         longs.step(2, part)
+    work(2)
+    for index in range(3):
+        send_block(index).start()
+    context_ref[chip] = sent[chip]
     for weight in weights:
         weight.arrive()
     for part in range(parts):
@@ -1043,26 +1103,52 @@
         weight.finish()
     for index in range(3):
         send_block(index).wait()
-    keep_block.wait()
-
-
-def third_exchange(longs, column, sent, cuts, collective_id, parts=2):
+
+
+def third_exchange(
+    longs, column, index, valid, joined, pieces, cuts, heads, slots, collective_id, parts=2
+):
     near = jax.ShapeDtypeStruct((column.shape[0],) + longs.shape, longs.dtype)
+    chips = lax.axis_size(SEQ) // 2
+    rows = joined.shape[0]
+    stored = sum(piece.shape[0] for piece in pieces) + rows
+    context = jax.ShapeDtypeStruct((chips, rows // chips, heads * BLOCK), joined.dtype)
     resident = pl.BlockSpec(memory_space=pltpu.VMEM)
+    scalars = pl.BlockSpec(memory_space=pltpu.SMEM)
+    anywhere = pl.BlockSpec(memory_space=pl.ANY)
     dma = pltpu.SemaphoreType.DMA
     sems = [sem for _ in cuts for sem in weight_sems()]
     return pl.pallas_call(
-        functools.partial(third_kernel, parts, cuts),
-        out_shape=[near, near, jax.ShapeDtypeStruct(sent.shape, sent.dtype)]
-        + [weight_shape(column, rows) for rows in cuts],
-        in_specs=[resident] * 3,
-        out_specs=[resident] * (3 + len(cuts)),
-        scratch_shapes=[dma((2,)), dma((3,)), dma((3,))] + column_sems(parts) + sems,
+        functools.partial(third_kernel, parts, cuts, slots, heads),
+        out_shape=[near, near, context, jax.ShapeDtypeStruct((rows, heads * PAIR), f32)]
+        + [weight_shape(column, cut) for cut in cuts],
+        in_specs=[scalars] * 2 + [resident] * 3 + [anywhere] * 3,
+        out_specs=[resident] * (4 + len(cuts)),
+        scratch_shapes=[
+            pltpu.VMEM((stored // BLOCK, BLOCK, PAIR), bf16),
+            pltpu.VMEM((stored // BLOCK, BLOCK, PAIR), bf16),
+            pltpu.VMEM((rows, PAIR), bf16),
+            pltpu.VMEM((rows, PAIR), bf16),
+            pltpu.VMEM(context.shape, bf16),
+            dma((heads, 3)),
+            dma,
+            dma((3,)),
+            dma((3,)),
+        ]
+        + column_sems(parts)
+        + sems,
         compiler_params=pltpu.CompilerParams(
-            collective_id=collective_id, has_side_effects=True, vmem_limit_bytes=48 * 2**20
+            collective_id=collective_id, has_side_effects=True, vmem_limit_bytes=52 * 2**20
         ),
-        cost_estimate=lasting(58),
-    )(longs, column, sent)
+        cost_estimate=lasting(62),
+    )(
+        index,
+        valid,
+        longs,
+        column,
+        joined,
+        *(piece.reshape(-1, BLOCK, piece.shape[1]) for piece in pieces + [joined]),
+    )
 
 
 class ColumnReduce:
@@ -1877,14 +1963,11 @@
 
     def attend(micro):
         held = stage[micro]
-        index = held.index
-        if micro:
-            index = after(index, stage[micro - 1].grad_context_sent)
+        index = after(held.index, stage[micro - 1].grad_context_sent)
         held.context_sent, held.logsum = attend_forward(
             index, held.valid, held.joined, held.pieces, heads, slots
         )
-        if micro:
-            held.context = plane_exchange(held.context_sent, 0, 1)
+        held.context = plane_exchange(held.context_sent, 0, 1)
 
     def feed_forward(micro):
         held = stage[micro]
@@ -1966,13 +2049,17 @@
     near, far, one, outer_full = second_exchange(longs, stage[1].low, column, cuts[2:4], 2)
     stage[1].one = one.reshape(group_rows, model_width)
     keep_pieces(0, near, far)
-    attend(0)
     longs = long_blocks(1)
-    near, far, context, rest, inner_full = third_exchange(
+    near, far, context, stage[0].logsum, rest, inner_full = third_exchange(
         longs,
         column,
-        stage[0].context_sent.reshape(chips, own_rows, local_width),
+        stage[0].index,
+        stage[0].valid,
+        stage[0].joined,
+        stage[0].pieces,
         (cuts[0:2], cuts[1:3]),
+        heads,
+        slots,
         7,
     )
     keep_pieces(1, near, far)

time: 672 us -> 657 us (0.978)
  Pallas kernels: 414 us -> 402 us
    pallas_call x2 -> x1, Pallas kernels: 37.5 us -> 18.8 us  [attend_forward(): pl.pallas_call(functools.partial(forward_kernel, slots, heads), grid_spec...]
    unnamed x246 -> x236, local copies, waits for them, and re-layouts: 38.5 us -> 34.9 us
  transfers between devices with their start and end apart: 9 -> 9, of which waited for: 3 -> 3; matrix products, arithmetic and copies ran while one was open for 10% -> 11% of each run, Pallas kernels for 25% -> 26%
where the time goes in v5:
time: 657 us; the launch traced here: 648 us
  Pallas kernels  402 us (61%)
  matrix products  71.2 us (11%)
  local copies, waits for them, and re-layouts  70.6 us (11%)
  other arithmetic  45.9 us (7%)
  between operations  26.5 us (4%)
  starting transfers between devices  17.1 us (3%)
  waiting for transfers between devices  14.6 us (2%)
    dot_general x24, matrix products, contract(): return lax.dot_general(left, right, dims, preferred_element_type=f32)  71.2 us
    pallas_call x1, Pallas kernels, fourth_exchange(): pl.pallas_call(functools.partial(fourth_kernel, parts, cuts), out_shape=[...  68.1 us
    pallas_call x1, Pallas kernels, second_exchange(): pl.pallas_call(functools.partial(second_kernel, parts, rows), out_shape=[...  65.5 us
    pallas_call x1, Pallas kernels, third_exchange(): pl.pallas_call(functools.partial(third_kernel, parts, cuts, slots, heads)...  63.6 us
    pallas_call x2, Pallas kernels, attend_backward(): pl.pallas_call(functools.partial(backward_kernel, slots, heads, len(piece...  54.1 us
    pallas_call x1, Pallas kernels, first_exchange(): pl.pallas_call(functools.partial(first_kernel, parts), out_shape=[jax.Sha...  38.8 us
    pallas_call x1, Pallas kernels, sixth_exchange(): pl.pallas_call(functools.partial(sixth_kernel, parts), out_shape=[jax.Sha...  38.7 us
    pallas_call x1, Pallas kernels, fifth_exchange(): pl.pallas_call(fifth_kernel, out_shape=[jax.ShapeDtypeStruct(rows.shape[1...  38.6 us
  transfers between devices with their start and end apart: 9, of which 3 were waited for; matrix products, arithmetic and copies ran while one was open for 11% of the time, Pallas kernels for 26%

profile of v5, /device:TPU:13, one launch (start us, length us, event | category | flops | bytes accessed | tf_op | source)
XLA Modules:
  0.0 647.8 jit_solution(13007064528295300)
XLA Ops:
  15.7 2.9 add_convert_fusion.7
  22.1 38.8 %shard_map.539 = (bf16[4,512,768]{2,1,0:T(8,128)(2,1)S(1)}, bf16[896,640]{1,0:T(8,128)(2,1)S(1)}, bf16[4,224,768]{2,1,0:T(8,128)(2,1)S(1)}, s32[4,8,128]{2,1,0:T(8,128)S(1)}) custom-call(bf16[512,768]{1,0:T(8,128)(2,1)S(1)} %get-tuple-element.214.own_ref, bf16[896,640]{1,0:T(8,128)(2,1)S(1)} %fusion.59.weight_ref, bf16[224,768]{1,0:T(8,128)(2,1)S(1)} %copy-done.15, ...), custom_call_target="tpu_custom_call" | custom-call | bytes 110700000 | tf_op jit(solution)/shard_map/pallas_call | solution.py:842
  73.3 3.2 fusion.102
  77.9 4.5 add_convert_fusion.2.joined_ref.query_ref.refs_2_
  84.2 65.5 %shard_map.540 = (bf16[4,1024,384]{2,1,0:T(8,128)(2,1)S(1)}, bf16[4,1024,384]{2,1,0:T(8,128)(2,1)}, bf16[4,512,768]{2,1,0:T(8,128)(2,1)}, bf16[2,4,4,96,768]{4,3,2,1,0:T(8,128)(2,1)}) custom-call(bf16[1024,384]{1,0:T(8,128)(2,1)S(1)} %pad_maximum_fusion.3.longs_ref, bf16[512,768]{1,0:T(8,128)(2,1)S(1)} %copy-done.10, ...), custom_call_target="tpu_custom_call" | custom-call | bytes 214020000 | tf_op jit(solution)/shard_map/pallas_call | solution.py:977
  151.4 4.5 add_convert_fusion.1.query_ref.refs_2_
  159.3 63.6 %shard_map.541 = (bf16[4,1024,384]{2,1,0:T(8,128)(2,1)}, bf16[4,1024,384]{2,1,0:T(8,128)(2,1)}, bf16[4,512,192]{2,1,0:T(8,128)(2,1)S(1)}, f32[2048,384]{1,0:T(8,...) custom-call(s32[768]{0:T(1024)S(1)} %and_add_fusion.1.index_ref, ...), custom_call_target="tpu_custom_call" | custom-call | bytes 228780000 | tf_op jit(solution)/shard_map/pallas_call | solution.py:1121
  235.9 4.8 fusion.113
  240.9 5.8 convert_reduce_fusion.1
  246.7 3.5 multiply_reduce_fusion.2
  256.6 4.9 all-to-all-start.1
  268.5 18.8 %shard_map.542 = (bf16[2048,192]{1,0:T(8,128)(2,1)S(1)}, f32[2048,384]{1,0:T(8,128)S(1)}) custom-call(s32[768]{0:T(1024)S(1)} %and_add_fusion.index_ref, s32[64]{0:T(128)S(1)} %reshape.568.valid_ref, bf16[2048,576]{1,0:T(8,128)(2,1)S(1)} %add_convert_fusion.1.query_ref.refs_2_, bf16[4096,384]{1,0:T(8,128)(2,1)S(1)} %bitcast.317, ...), custom_call_target="tpu_custom_call" | custom-call | bytes 66420000 | tf_op jit(solution)/shard_map/pallas_call | solution.py:277
  291.4 27.0 %shard_map.543 = (bf16[4096,384]{1,0:T(8,128)(2,1)}, bf16[4096,384]{1,0:T(8,128)(2,1)}, bf16[2048,576]{1,0:T(8,128)(2,1)S(1)}) custom-call(s32[768]{0:T(1024)S(1)} %and_add_fusion.1.index_ref, s32[64]{0:T(128)S(1)} %reshape.565.valid_ref, bf16[2048,576]{1,0:T(8,128)(2,1)} %copy-done.26, bf16[2048,192]{1,0:T(8,128)(2,1)S(1)} %bitcast.322, ...), custom_call_target="tpu_custom_call" | custom-call | bytes 92250000 | tf_op jit(solution)/shard_map/pallas_call | solution.py:301
  323.0 4.3 all-to-all-start
  332.7 4.3 add_convert_fusion
  339.7 2.8 fusion.112
  343.6 10.2 %multiply_convert_fusion.1 = (bf16[512,3072]{1,0:T(8,128)(2,1)}, bf16[512,3072]{1,0:T(8,128)(2,1)}, f32[512,3072]{1,0:T(8,128)S(1)}) fusion(f32[512,3072]{1,0:T(8,128)} %copy-done.103, f32[3072]{0:T(1024)S(1)} %copy-done.79, bf16[512,768]{1,0:T(8,128)(2,1)S(1)} %add_convert_fusion.4.refs_3_, bf16[3072,768]{1,0:T(8,128)(2,1)} %bitcast.383), kind=kOutput, calls=%fused_computation.21 | convolution fusion | flops 2434793472 | bytes 24391680 | tf_op jit(solution)/shard_map/dot_general | solution.py:32
  353.9 5.3 convert_reduce_fusion
  359.2 3.0 multiply_reduce_fusion.1
  367.0 15.7 %shard_map.544 = (bf16[1536,768]{1,0:T(8,128)(2,1)S(1)}, bf16[1536,768]{1,0:T(8,128)(2,1)S(1)}, bf16[1536,768]{1,0:T(8,128)(2,1)S(1)}, bf16[1536,768]{1,0:T(8,128)(2,1)}, bf16[768,768]{1,0:T(8,128)(2,1)S(1)}) custom-call(s32[1]{0:T(128)} %bitcast.60.core_ref, bf16[512,3072]{1,0:T(8,128)(2,1)} %copy-done.41, bf16[512,3072]{1,0:T(8,128)(2,1)} %copy-done.44, ...), custom_call_target="tpu_custom_call" | custom-call | bytes 55350000 | tf_op jit(solution)/shard_map/pallas_call | solution.py:373
  387.9 8.6 %reduce-scatter.3.cloned.1.call-done = bf16[1024,384]{1,0:T(8,128)(2,1)} async-done(((bf16[4096,384]{1,0:T(8,128)(2,1)}), bf16[1024,384]{1,0:T(8,128)(2,1)}) %reduce-scatter.3.cloned.1.call-update) | async-done | bytes 786448 | tf_op jit(solution)/shard_map/reduce_scatter | solution.py:2076
  401.4 4.2 convolution_convert_fusion.1
  408.4 4.4 all-to-all-start.2
  416.7 5.7 fusion.49
  426.4 5.5 all-to-all-done.2
  433.3 27.1 %shard_map.545 = (bf16[4096,384]{1,0:T(8,128)(2,1)}, bf16[4096,384]{1,0:T(8,128)(2,1)}, bf16[2048,576]{1,0:T(8,128)(2,1)S(1)}) custom-call(s32[768]{0:T(1024)S(1)} %and_add_fusion.index_ref, s32[64]{0:T(128)S(1)} %reshape.568.valid_ref, bf16[2048,576]{1,0:T(8,128)(2,1)} %copy-done.2, bf16[2048,192]{1,0:T(8,128)(2,1)S(1)} %bitcast.323, ...), custom_call_target="tpu_custom_call" | custom-call | bytes 92250000 | tf_op jit(solution)/shard_map/pallas_call | solution.py:301
  460.4 68.1 %shard_map.546 = (bf16[1024,384]{1,0:T(8,128)(2,1)S(1)}, bf16[4,224,768]{2,1,0:T(8,128)(2,1)}) custom-call(bf16[4,1024,384]{2,1,0:T(8,128)(2,1)} %bitcast.343, bf16[4,1024,384]{2,1,0:T(8,128)(2,1)} %bitcast.344, bf16[4,4,96,768]{3,2,1,0:T(8,128)(2,1)} %bitcast.324, bf16[4,4,96,768]{3,2,1,0:T(8,128)(2,1)} %bitcast.355, ...), custom_call_target="tpu_custom_call" | custom-call | bytes 228780000 | tf_op jit(solution)/shard_map/pallas_call | solution.py:1411
  530.1 4.0 convolution_convert_fusion
  534.2 38.6 %shard_map.547 = (f32[2,256,768]{2,1,0:T(8,128)S(1)}, bf16[224,768]{1,0:T(8,128)(2,1)S(1)}) custom-call(bf16[4,2,256,768]{3,2,1,0:T(8,128)(2,1)} %bitcast.342, bf16[4,224,768]{2,1,0:T(8,128)(2,1)S(1)} %copy-done.16), custom_call_target="tpu_custom_call" | custom-call | bytes 110700000 | tf_op jit(solution)/shard_map/pallas_call | solution.py:1477
  584.2 38.7 %shard_map.548 = (bf16[768,640]{1,0:T(8,128)(2,1)S(1)}, bf16[4,2,224,768]{3,2,1,0:T(8,128)(2,1)S(1)}, f32[8,768]{1,0:T(8,128)S(1)}) custom-call(bf16[768,640]{1,0:T(8,128)(2,1)S(1)} %pad.48.terms_ref, bf16[224,768]{1,0:T(8,128)(2,1)S(1)} %get-tuple-element.95.own_ref, f32[8,768]{1,0:T(8,128)S(1)} %pad_maximum_fusion.8.rows_ref), custom_call_target="tpu_custom_call" | custom-call | bytes 129150000 | tf_op jit(solution)/shard_map/pallas_call | solution.py:1738
  632.3 3.2 copy.154
  636.1 2.7 fusion.32
  (429 shorter events, 117.0 us)
Async XLA Ops:
  22.1 40.7 %copy-start.89 = (s32[2,18]{1,0:T(2,128)S(1)}, s32[2,18]{1,0:T(2,128)}, u32[]{:S(2)}) copy-start(s32[2,18]{1,0:T(2,128)} %param.45) | copy-start | bytes 436
  62.6 21.3 %copy-start.6 = (bf16[4,224,768]{2,1,0:T(8,128)(2,1)}, bf16[4,224,768]{2,1,0:T(8,128)(2,1)S(1)}, u32[]{:S(2)}) copy-start(bf16[4,224,768]{2,1,0:T(8,128)(2,1)S(1)} %get-tuple-element.61.column_ref) | copy-start | bytes 4128772
  62.7 10.6 %copy-start.73 = (s32[768]{0:T(1024)S(1)}, s32[768]{0:T(1024)}, u32[]{:S(2)}) copy-start(s32[768]{0:T(1024)} %constant.137.clone) | copy-start | bytes 9220
  62.7 10.6 %copy-start.74 = (s32[768]{0:T(1024)S(1)}, s32[768]{0:T(1024)}, u32[]{:S(2)}) copy-start(s32[768]{0:T(1024)} %constant.136.clone) | copy-start | bytes 9220
  62.7 10.6 %copy-start.82 = (pred[768]{0:T(1024)(128)(4,1)S(1)}, pred[768]{0:T(1024)(128)(4,1)}, u32[]{:S(2)}) copy-start(pred[768]{0:T(1024)(128)(4,1)} %constant.138.clone) | copy-start | bytes 2308
  62.7 15.2 %copy-start.62 = (bf16[768,192]{1,0:T(8,128)(2,1)}, bf16[768,192]{1,0:T(8,128)(2,1)S(1)}, u32[]{:S(2)}) copy-start(bf16[768,192]{1,0:T(8,128)(2,1)S(1)} %slice_multiply_fusion) | copy-start | bytes 884740
  62.8 88.5 %copy-start.59 = (bf16[768,384]{1,0:T(8,128)(2,1)}, bf16[768,384]{1,0:T(8,128)(2,1)S(1)}, u32[]{:S(2)}) copy-start(bf16[768,384]{1,0:T(8,128)(2,1)S(1)} %slice.218) | copy-start | bytes 1769476
  84.0 67.4 %copy-start.63 = (bf16[768,192]{1,0:T(8,128)(2,1)S(1)}, bf16[768,192]{1,0:T(8,128)(2,1)}, u32[]{:S(2)}) copy-start(bf16[768,192]{1,0:T(8,128)(2,1)} %copy-done.62) | copy-start | bytes 884740
  155.9 108.8 %copy-start.2 = (bf16[2048,576]{1,0:T(8,128)(2,1)}, bf16[2048,576]{1,0:T(8,128)(2,1)S(1)}, u32[]{:S(2)}) copy-start(bf16[2048,576]{1,0:T(8,128)(2,1)S(1)} %add_convert_fusion.1.query_ref.refs_2_) | copy-start | bytes 7077892
  235.9 10.8 %slice-start.6 = ((s8[4718592]{0:T(1024)(128)(4,1)}), s8[4194304]{0:T(1024)(128)(4,1)S(1)}, s32[]{:S(2)}) async-start(s8[4718592]{0:T(1024)(128)(4,1)} %bitcast.384), calls=%async_computation.13 | async-start | bytes 8388608
  256.6 33.3 %all-to-all-start.1 = ((bf16[4,512,192]{1,2,0:T(8,128)(2,1)}), bf16[4,512,192]{1,2,0:T(8,128)(2,1)}, u32[]{:S(2)}, u32[]{:S(2)}) async-start(bf16[4,512,192]{1,2,0:T(8,128)(2,1)} %pad_maximum_fusion.5), calls=%async_computation.1 | async-start | bytes 1572864 | tf_op jit(solution)/shard_map/all_to_all | solution.py:390
  291.4 30.4 %copy-start.20 = (bf16[2048,192]{1,0:T(8,128)(2,1)S(1)}, bf16[2048,192]{1,0:T(8,128)(2,1)}, u32[]{:S(2)}) copy-start(bf16[2048,192]{1,0:T(8,128)(2,1)} %copy-done.19) | copy-start | bytes 2359300
  319.9 12.8 %collective-permute-start = (bf16[4096,384]{1,0:T(8,128)(2,1)}, bf16[4096,384]{1,0:T(8,128)(2,1)}, u32[]{:S(2)}, u32[]{:S(2)}) collective-permute-start(bf16[4096,384]{1,0:T(8,128)(2,1)} %get-tuple-element.77), channel_id=1, source_target_pairs={{0,4},{4,0},{8,12},{12,8},{16,20},{20,16},{24,28},{28,24},{1,5},{5... | collective-permute-start | bytes 9437192 | tf_op jit(solution)/shard_map/ppermute | solution.py:407
  323.0 15.3 %all-to-all-start = ((bf16[4,512,192]{1,2,0:T(8,128)(2,1)}), bf16[4,512,192]{1,2,0:T(8,128)(2,1)}, u32[]{:S(2)}, u32[]{:S(2)}) async-start(bf16[4,512,192]{1,2,0:T(8,128)(2,1)} %copy.144), calls=%async_computation | async-start | bytes 1572864 | tf_op jit(solution)/shard_map/all_to_all | solution.py:390
  327.3 69.2 %reduce-scatter.3.cloned.1.call-start = ((), (), s32[]{:S(2)}) async-start(), calls=%async_computation.5 | async-start | bytes 3932160 | tf_op jit(solution)/shard_map/reduce_scatter | solution.py:2076
  337.1 244.9 %reduce-scatter.5.cloned.1.call-start = ((), (), s32[]{:S(2)}) async-start(), calls=%async_computation.6 | async-start | bytes 3932160 | tf_op jit(solution)/shard_map/reduce_scatter | solution.py:2104
  339.7 14.1 %slice-start.2 = ((s8[4718592]{0:T(1024)(128)(4,1)}), s8[4194304]{0:T(1024)(128)(4,1)S(1)}, s32[]{:S(2)}) async-start(s8[4718592]{0:T(1024)(128)(4,1)} %bitcast.376), calls=%async_computation.9 | async-start | bytes 8388608
  342.5 19.8 %copy-start.33 = (f32[512,768]{1,0:T(8,128)}, f32[512,768]{1,0:T(8,128)S(1)}, u32[]{:S(2)}) copy-start(f32[512,768]{1,0:T(8,128)S(1)} %get-tuple-element.262) | copy-start | bytes 4718596
  343.6 10.3 %copy-start.36 = (bf16[2,512,768]{2,1,0:T(8,128)(2,1)S(1)}, bf16[2,512,768]{2,1,0:T(8,128)(2,1)}, u32[]{:S(2)}) copy-start(bf16[2,512,768]{2,1,0:T(8,128)(2,1)} %param.62) | copy-start | bytes 4718596
  343.6 10.3 %slice-start.3 = ((s8[4718592]{0:T(1024)(128)(4,1)}), s8[524288]{0:T(1024)(128)(4,1)S(1)}, s32[]{:S(2)}) async-start(s8[4718592]{0:T(1024)(128)(4,1)} %bitcast.376), calls=%async_computation.10 | async-start | bytes 1048576
  343.6 15.6 %slice-start.8 = ((s8[4718592]{0:T(1024)(128)(4,1)}), s8[4194304]{0:T(1024)(128)(4,1)S(1)}, s32[]{:S(2)}) async-start(s8[4718592]{0:T(1024)(128)(4,1)} %bitcast.387), calls=%async_computation.15 | async-start | bytes 8388608
  408.4 23.4 %all-to-all-start.2 = ((bf16[4,512,192]{1,2,0:T(8,128)(2,1)}), bf16[4,512,192]{1,2,0:T(8,128)(2,1)}, u32[]{:S(2)}, u32[]{:S(2)}) async-start(bf16[4,512,192]{1,2,0:T(8,128)(2,1)} %pad_maximum_fusion.6), calls=%async_computation.4 | async-start | bytes 1572864 | tf_op jit(solution)/shard_map/all_to_all | solution.py:390
  412.8 47.6 %collective-permute-start.1 = (bf16[4,4,96,768]{3,2,1,0:T(8,128)(2,1)}, bf16[4,4,96,768]{3,2,1,0:T(8,128)(2,1)}, u32[]{:S(2)}, u32[]{:S(2)}) collective-permute-start(bf16[4,4,96,768]{3,2,1,0:T(8,128)(2,1)} %bitcast.332), channel_id=1, source_target_pairs={{0,4},{4,0},{8,12},{12,8},{16,20},{20,16},{24,28},{28,24},{1,5},{5... | collective-permute-start | bytes 7077896 | tf_op jit(solution)/shard_map/ppermute | solution.py:407
  413.7 46.7 %collective-permute-start.2 = (bf16[4,4,96,768]{3,2,1,0:T(8,128)(2,1)}, bf16[4,4,96,768]{3,2,1,0:T(8,128)(2,1)}, u32[]{:S(2)}, u32[]{:S(2)}) collective-permute-start(bf16[4,4,96,768]{3,2,1,0:T(8,128)(2,1)} %bitcast.331), channel_id=1, source_target_pairs={{0,4},{4,0},{8,12},{12,8},{16,20},{20,16},{24,28},{28,24},{1,5},{5... | collective-permute-start | bytes 7077896 | tf_op jit(solution)/shard_map/ppermute | solution.py:407
  415.5 6.9 %slice-start.4 = ((s8[4718592]{0:T(1024)(128)(4,1)}), s8[4194304]{0:T(1024)(128)(4,1)S(1)}, s32[]{:S(2)}) async-start(s8[4718592]{0:T(1024)(128)(4,1)} %bitcast.379), calls=%async_computation.11 | async-start | bytes 8388608
  415.5 6.9 %copy-start.32 = (f32[512,768]{1,0:T(8,128)S(1)}, f32[512,768]{1,0:T(8,128)}, u32[]{:S(2)}) copy-start(f32[512,768]{1,0:T(8,128)} %copy-done.30) | copy-start | bytes 4718596
  415.5 6.9 %copy-start.42 = (bf16[512,3072]{1,0:T(8,128)(2,1)S(1)}, bf16[512,3072]{1,0:T(8,128)(2,1)}, u32[]{:S(2)}) copy-start(bf16[512,3072]{1,0:T(8,128)(2,1)} %get-tuple-element.238.refs_4_) | copy-start | bytes 9437188
  415.5 6.9 %slice-start.5 = ((s8[4718592]{0:T(1024)(128)(4,1)}), s8[524288]{0:T(1024)(128)(4,1)S(1)}, s32[]{:S(2)}) async-start(s8[4718592]{0:T(1024)(128)(4,1)} %bitcast.379), calls=%async_computation.12 | async-start | bytes 1048576
  415.5 44.9 %collective-permute-start.3 = (bf16[4,4,32,768]{3,2,1,0:T(8,128)(2,1)}, bf16[4,4,32,768]{3,2,1,0:T(8,128)(2,1)}, u32[]{:S(2)}, u32[]{:S(2)}) collective-permute-start(bf16[4,4,32,768]{3,2,1,0:T(8,128)(2,1)} %get-tuple-element.220), channel_id=1, source_target_pairs={{0,4},{4,0},{8,12},{12,8},{16,20},{20,16},{24,28},{28,24},{1,5},{5... | collective-permute-start | bytes 2359304 | tf_op jit(solution)/shard_map/ppermute | solution.py:407
  534.1 38.6 %copy-start.37 = (f32[1,512,768]{2,1,0:T(8,128)S(1)}, f32[1,512,768]{2,1,0:T(8,128)}, u32[]{:S(2)}) copy-start(f32[1,512,768]{2,1,0:T(8,128)} %slice_convert_fusion) | copy-start | bytes 4718596
  534.1 38.6 %copy-start.70 = (f32[768]{0:T(1024)S(1)}, f32[768]{0:T(1024)}, u32[]{:S(2)}) copy-start(f32[768]{0:T(1024)} %copy-done.69) | copy-start | bytes 9220
  534.1 39.4 %copy-start.54 = (bf16[2048,576]{1,0:T(8,128)(2,1)S(1)}, bf16[2048,576]{1,0:T(8,128)(2,1)}, u32[]{:S(2)}) copy-start(bf16[2048,576]{1,0:T(8,128)(2,1)} %copy-done.53) | copy-start | bytes 7077892
  (91 other events, 236.7 us)
Sparse Core Ops, SparseCore 0:
  337.2 59.2 reduce-scatter.2
  405.8 52.4 reduce-scatter.4

commit v6 on v5

--- a/solution.py
+++ b/solution.py
@@ -1901,7 +1901,7 @@
     long_lasts = jnp.max(jnp.where(is_long, starts, -1), axis=1)
     first_groups = lax.shift_right_logical(jnp.stack([long_firsts, long_lasts]), group_bits)
     own_groups = first_groups + ((own_class - first_groups) & (classes - 1))
-    long_rows = lax.shift_right_logical(own_groups, class_bits) * own_rows
+    in_slot = lax.shift_right_logical(own_groups, class_bits)[:, :, None] == np.arange(chips)
     randoms = randoms.reshape(chips, -1)[:, :random_count]
     randoms = randoms.reshape(chips, micro_count, tp_count, SHORT_BLK, heads, rands)
     randoms = lax.dynamic_index_in_dim(randoms, tp_place, axis=2, keepdims=False)
@@ -1913,13 +1913,13 @@
         group = slot * classes + own_class
         number = group * SHORT_BLK + block
         in_long = [
-            (number >= start[micro]) & (number < start[micro] + LONG_BLK)
-            for start in (long_firsts, long_lasts)
+            (number >= start) & (number < start + LONG_BLK)
+            for start in (long_firsts[micro : micro + 1], long_lasts[micro : micro + 1])
         ]
         window_first = jnp.where(
             in_long[0],
-            long_firsts[micro],
-            jnp.where(in_long[1], long_lasts[micro], group * SHORT_BLK),
+            long_firsts[micro : micro + 1],
+            jnp.where(in_long[1], long_lasts[micro : micro + 1], group * SHORT_BLK),
         )
         any_long = in_long[0] | in_long[1]
         window_final = window_first + jnp.where(any_long, LONG_BLK, SHORT_BLK)
@@ -1944,17 +1944,14 @@
         counts = jnp.where(entry == 0, number > window_first, number + 1 < window_final)
         counts = counts.astype(jnp.int32)[: chips * SHORT_BLK * slots]
         held.valid = counts.reshape(-1, slots)[:, :2].reshape(-1)
-        held.long_rows = [long_rows[doc, micro] for doc in range(long_docs)]
+        held.in_slot = [in_slot[doc, micro].reshape(chips, 1, 1) for doc in range(long_docs)]
 
     def long_blocks(micro):
         held = stage[micro]
         held.joined = (contract(held.one, joined_weight, NN) + joined_bias).astype(bf16)
+        parts = held.joined.reshape(chips, own_rows, -1)[:, :, :pair_width]
         longs = jnp.concatenate(
-            [
-                lax.dynamic_slice(held.joined, (start, 0), (own_rows, pair_width))
-                for start in held.long_rows
-            ],
-            axis=0,
+            [jnp.sum(jnp.where(chosen, parts, 0), axis=0) for chosen in held.in_slot], axis=0
         )
         return longs
 
@@ -2028,11 +2025,11 @@
     def input_rows(micro, long_sum):
         held = stage[micro]
         shape = (chips, own_rows, pair_width + local_width)
-        place, lane = np.indices(shape, np.int32, sparse=True)[::2]
+        lane = np.arange(shape[2], dtype=np.int32)
         joined = held.grad_joined.reshape(shape)
-        for doc, start in enumerate(held.long_rows):
+        for doc, chosen in enumerate(held.in_slot):
             long_part = jnp.pad(slot_rows(long_sum, doc), ((0, 0), (0, local_width)))
-            joined = jnp.where((place * own_rows == start) & (lane < pair_width), long_part, joined)
+            joined = jnp.where(chosen & (lane < pair_width), long_part, joined)
         held.grad_joined = joined.reshape(group_rows, -1)
         rows = contract(held.grad_joined, joined_weight, NT)
         return rows.astype(bf16).reshape(chips, own_rows, model_width)

time: 657 us -> 648 us (0.986)
  between operations: 26.5 us -> 18.8 us
    unnamed x236 -> x250, local copies, waits for them, and re-layouts: 34.9 us -> 31.8 us
  transfers between devices with their start and end apart: 9 -> 9, of which waited for: 3 -> 3; matrix products, arithmetic and copies ran while one was open for 11% -> 10% of each run, Pallas kernels for 26% -> 26%
where the time goes in v6:
time: 648 us; the launch traced here: 644 us
  Pallas kernels  408 us (63%)
  matrix products  72.3 us (11%)
  local copies, waits for them, and re-layouts  66.3 us (10%)
  other arithmetic  45.3 us (7%)
  between operations  18.8 us (3%)
  starting transfers between devices  16.5 us (3%)
  waiting for transfers between devices  16.1 us (2%)
    dot_general x24, matrix products, contract(): return lax.dot_general(left, right, dims, preferred_element_type=f32)  72.3 us
    pallas_call x1, Pallas kernels, second_exchange(): pl.pallas_call(functools.partial(second_kernel, parts, rows), out_shape=[...  69.8 us
    pallas_call x1, Pallas kernels, fourth_exchange(): pl.pallas_call(functools.partial(fourth_kernel, parts, cuts), out_shape=[...  68 us
    pallas_call x1, Pallas kernels, third_exchange(): pl.pallas_call(functools.partial(third_kernel, parts, cuts, slots, heads)...  65.9 us
    pallas_call x2, Pallas kernels, attend_backward(): pl.pallas_call(functools.partial(backward_kernel, slots, heads, len(piece...  54.1 us
    pallas_call x1, Pallas kernels, first_exchange(): pl.pallas_call(functools.partial(first_kernel, parts), out_shape=[jax.Sha...  38.8 us
    pallas_call x1, Pallas kernels, sixth_exchange(): pl.pallas_call(functools.partial(sixth_kernel, parts), out_shape=[jax.Sha...  38.7 us
    pallas_call x1, Pallas kernels, fifth_exchange(): pl.pallas_call(fifth_kernel, out_shape=[jax.ShapeDtypeStruct(rows.shape[1...  38.6 us
  transfers between devices with their start and end apart: 9, of which 3 were waited for; matrix products, arithmetic and copies ran while one was open for 10% of the time, Pallas kernels for 26%

profile of v6, /device:TPU:13, one launch (start us, length us, event | category | flops | bytes accessed | tf_op | source)
XLA Modules:
  0.0 643.8 jit_solution(12631590976327571343)
XLA Ops:
  15.7 2.9 add_convert_fusion.7
  22.1 38.8 %shard_map.512 = (bf16[4,512,768]{2,1,0:T(8,128)(2,1)S(1)}, bf16[896,640]{1,0:T(8,128)(2,1)S(1)}, bf16[4,224,768]{2,1,0:T(8,128)(2,1)S(1)}, s32[4,8,128]{2,1,0:T(8,128)S(1)}) custom-call(bf16[512,768]{1,0:T(8,128)(2,1)S(1)} %get-tuple-element.214.own_ref, bf16[896,640]{1,0:T(8,128)(2,1)S(1)} %fusion.59.weight_ref, bf16[224,768]{1,0:T(8,128)(2,1)S(1)} %copy-done.15, ...), custom_call_target="tpu_custom_call" | custom-call | bytes 110700000 | tf_op jit(solution)/shard_map/pallas_call | solution.py:842
  67.1 3.1 fusion.102
  70.5 4.5 add_convert_fusion.2.joined_ref.query_ref.refs_2_
  76.8 69.8 %shard_map.513 = (bf16[4,1024,384]{2,1,0:T(8,128)(2,1)S(1)}, bf16[4,1024,384]{2,1,0:T(8,128)(2,1)}, bf16[4,512,768]{2,1,0:T(8,128)(2,1)}, bf16[2,4,4,96,768]{4,3,2,1,0:T(8,128)(2,1)}) custom-call(bf16[1024,384]{1,0:T(8,128)(2,1)S(1)} %pad_maximum_fusion.3.longs_ref, bf16[512,768]{1,0:T(8,128)(2,1)S(1)} %copy-done.10, ...), custom_call_target="tpu_custom_call" | custom-call | bytes 214020000 | tf_op jit(solution)/shard_map/pallas_call | solution.py:977
  146.6 5.6 add_convert_fusion.1.query_ref.refs_2_
  154.9 65.9 %shard_map.514 = (bf16[4,1024,384]{2,1,0:T(8,128)(2,1)}, bf16[4,1024,384]{2,1,0:T(8,128)(2,1)}, bf16[4,512,192]{2,1,0:T(8,128)(2,1)S(1)}, f32[2048,384]{1,0:T(8,...) custom-call(s32[768]{0:T(1024)S(1)} %and_add_fusion.1.index_ref, ...), custom_call_target="tpu_custom_call" | custom-call | bytes 228780000 | tf_op jit(solution)/shard_map/pallas_call | solution.py:1121
  233.9 4.8 fusion.112
  238.9 5.8 convert_reduce_fusion.1
  244.7 3.5 multiply_reduce_fusion.2
  254.5 4.6 all-to-all-start.1
  265.9 18.8 %shard_map.515 = (bf16[2048,192]{1,0:T(8,128)(2,1)S(1)}, f32[2048,384]{1,0:T(8,128)S(1)}) custom-call(s32[768]{0:T(1024)S(1)} %and_add_fusion.index_ref, s32[64]{0:T(128)S(1)} %reshape.598.valid_ref, bf16[2048,576]{1,0:T(8,128)(2,1)S(1)} %add_convert_fusion.1.query_ref.refs_2_, bf16[4096,384]{1,0:T(8,128)(2,1)S(1)} %bitcast.320, ...), custom_call_target="tpu_custom_call" | custom-call | bytes 66420000 | tf_op jit(solution)/shard_map/pallas_call | solution.py:277
  288.8 27.0 %shard_map.516 = (bf16[4096,384]{1,0:T(8,128)(2,1)}, bf16[4096,384]{1,0:T(8,128)(2,1)}, bf16[2048,576]{1,0:T(8,128)(2,1)S(1)}) custom-call(s32[768]{0:T(1024)S(1)} %and_add_fusion.1.index_ref, s32[64]{0:T(128)S(1)} %reshape.595.valid_ref, bf16[2048,576]{1,0:T(8,128)(2,1)} %copy-done.26, bf16[2048,192]{1,0:T(8,128)(2,1)S(1)} %bitcast.325, ...), custom_call_target="tpu_custom_call" | custom-call | bytes 92250000 | tf_op jit(solution)/shard_map/pallas_call | solution.py:301
  320.1 4.3 all-to-all-start
  327.3 4.3 add_convert_fusion
  332.4 3.0 all-to-all-done
  336.9 2.8 fusion.111
  340.7 10.2 %multiply_convert_fusion.1 = (bf16[512,3072]{1,0:T(8,128)(2,1)}, bf16[512,3072]{1,0:T(8,128)(2,1)}, f32[512,3072]{1,0:T(8,128)S(1)}) fusion(f32[512,3072]{1,0:T(8,128)} %copy-done.110, f32[3072]{0:T(1024)S(1)} %copy-done.79, bf16[512,768]{1,0:T(8,128)(2,1)S(1)} %add_convert_fusion.4.refs_3_, bf16[3072,768]{1,0:T(8,128)(2,1)} %bitcast.387), kind=kOutput, calls=%fused_computation.21 | convolution fusion | flops 2434793472 | bytes 24391680 | tf_op jit(solution)/shard_map/dot_general | solution.py:32
  351.0 5.3 convert_reduce_fusion
  356.3 3.0 multiply_reduce_fusion.1
  364.1 15.6 %shard_map.517 = (bf16[1536,768]{1,0:T(8,128)(2,1)S(1)}, bf16[1536,768]{1,0:T(8,128)(2,1)S(1)}, bf16[1536,768]{1,0:T(8,128)(2,1)S(1)}, bf16[1536,768]{1,0:T(8,128)(2,1)}, bf16[768,768]{1,0:T(8,128)(2,1)S(1)}) custom-call(s32[1]{0:T(128)} %bitcast.65.core_ref, bf16[512,3072]{1,0:T(8,128)(2,1)} %copy-done.41, bf16[512,3072]{1,0:T(8,128)(2,1)} %copy-done.44, ...), custom_call_target="tpu_custom_call" | custom-call | bytes 55350000 | tf_op jit(solution)/shard_map/pallas_call | solution.py:373
  385.0 7.5 %reduce-scatter.3.cloned.1.call-done = bf16[1024,384]{1,0:T(8,128)(2,1)} async-done(((bf16[4096,384]{1,0:T(8,128)(2,1)}), bf16[1024,384]{1,0:T(8,128)(2,1)}) %reduce-scatter.3.cloned.1.call-update) | async-done | bytes 786448 | tf_op jit(solution)/shard_map/reduce_scatter | solution.py:2073
  397.5 4.2 convolution_convert_fusion.1
  404.4 4.4 all-to-all-start.2
  412.7 5.6 fusion.49
  422.4 5.5 all-to-all-done.2
  429.4 27.1 %shard_map.518 = (bf16[4096,384]{1,0:T(8,128)(2,1)}, bf16[4096,384]{1,0:T(8,128)(2,1)}, bf16[2048,576]{1,0:T(8,128)(2,1)S(1)}) custom-call(s32[768]{0:T(1024)S(1)} %and_add_fusion.index_ref, s32[64]{0:T(128)S(1)} %reshape.598.valid_ref, bf16[2048,576]{1,0:T(8,128)(2,1)} %copy-done.2, bf16[2048,192]{1,0:T(8,128)(2,1)S(1)} %bitcast.326, ...), custom_call_target="tpu_custom_call" | custom-call | bytes 92250000 | tf_op jit(solution)/shard_map/pallas_call | solution.py:301
  456.5 68.0 %shard_map.519 = (bf16[1024,384]{1,0:T(8,128)(2,1)S(1)}, bf16[4,224,768]{2,1,0:T(8,128)(2,1)}) custom-call(bf16[4,1024,384]{2,1,0:T(8,128)(2,1)} %bitcast.347, bf16[4,1024,384]{2,1,0:T(8,128)(2,1)} %bitcast.348, bf16[4,4,96,768]{3,2,1,0:T(8,128)(2,1)} %bitcast.327, bf16[4,4,96,768]{3,2,1,0:T(8,128)(2,1)} %bitcast.359, ...), custom_call_target="tpu_custom_call" | custom-call | bytes 228780000 | tf_op jit(solution)/shard_map/pallas_call | solution.py:1411
  526.1 4.0 convolution_convert_fusion
  530.1 38.6 %shard_map.520 = (f32[2,256,768]{2,1,0:T(8,128)S(1)}, bf16[224,768]{1,0:T(8,128)(2,1)S(1)}) custom-call(bf16[4,2,256,768]{3,2,1,0:T(8,128)(2,1)} %bitcast.346, bf16[4,224,768]{2,1,0:T(8,128)(2,1)S(1)} %copy-done.16), custom_call_target="tpu_custom_call" | custom-call | bytes 110700000 | tf_op jit(solution)/shard_map/pallas_call | solution.py:1477
  580.2 38.7 %shard_map.521 = (bf16[768,640]{1,0:T(8,128)(2,1)S(1)}, bf16[4,2,224,768]{3,2,1,0:T(8,128)(2,1)S(1)}, f32[8,768]{1,0:T(8,128)S(1)}) custom-call(bf16[768,640]{1,0:T(8,128)(2,1)S(1)} %pad.48.terms_ref, bf16[224,768]{1,0:T(8,128)(2,1)S(1)} %get-tuple-element.95.own_ref, f32[8,768]{1,0:T(8,128)S(1)} %pad_maximum_fusion.8.rows_ref), custom_call_target="tpu_custom_call" | custom-call | bytes 129150000 | tf_op jit(solution)/shard_map/pallas_call | solution.py:1738
  628.3 3.2 copy.151
  (443 shorter events, 114.2 us)
Async XLA Ops:
  61.0 15.5 %copy-start.6 = (bf16[4,224,768]{2,1,0:T(8,128)(2,1)}, bf16[4,224,768]{2,1,0:T(8,128)(2,1)S(1)}, u32[]{:S(2)}) copy-start(bf16[4,224,768]{2,1,0:T(8,128)(2,1)S(1)} %get-tuple-element.61.column_ref) | copy-start | bytes 4128772
  61.1 13.9 %copy-start.62 = (bf16[768,192]{1,0:T(8,128)(2,1)}, bf16[768,192]{1,0:T(8,128)(2,1)S(1)}, u32[]{:S(2)}) copy-start(bf16[768,192]{1,0:T(8,128)(2,1)S(1)} %slice_multiply_fusion) | copy-start | bytes 884740
  61.2 85.4 %copy-start.59 = (bf16[768,384]{1,0:T(8,128)(2,1)}, bf16[768,384]{1,0:T(8,128)(2,1)S(1)}, u32[]{:S(2)}) copy-start(bf16[768,384]{1,0:T(8,128)(2,1)S(1)} %slice.222) | copy-start | bytes 1769476
  70.5 81.8 %copy-start.83 = (pred[4]{0:T(512)(128)(4,1)}, pred[4]{0:T(512)(128)(4,1)S(1)}, u32[]{:S(2)}) copy-start(pred[4]{0:T(512)(128)(4,1)S(1)} %get-tuple-element.246) | copy-start | bytes 16
  70.5 81.8 %copy-start.89 = (pred[4]{0:T(512)(128)(4,1)}, pred[4]{0:T(512)(128)(4,1)S(1)}, u32[]{:S(2)}) copy-start(pred[4]{0:T(512)(128)(4,1)S(1)} %get-tuple-element.249) | copy-start | bytes 16
  76.5 70.1 %copy-start.63 = (bf16[768,192]{1,0:T(8,128)(2,1)S(1)}, bf16[768,192]{1,0:T(8,128)(2,1)}, u32[]{:S(2)}) copy-start(bf16[768,192]{1,0:T(8,128)(2,1)} %copy-done.62) | copy-start | bytes 884740
  152.3 109.9 %copy-start.2 = (bf16[2048,576]{1,0:T(8,128)(2,1)}, bf16[2048,576]{1,0:T(8,128)(2,1)S(1)}, u32[]{:S(2)}) copy-start(bf16[2048,576]{1,0:T(8,128)(2,1)S(1)} %add_convert_fusion.1.query_ref.refs_2_) | copy-start | bytes 7077892
  232.0 6.8 %copy-start.78 = (f32[3072]{0:T(1024)}, f32[3072]{0:T(1024)S(1)}, u32[]{:S(2)}) copy-start(f32[3072]{0:T(1024)S(1)} %reshape.596) | copy-start | bytes 36868
  232.0 6.8 %slice-start = ((s8[4718592]{0:T(1024)(128)(4,1)}), s8[4194304]{0:T(1024)(128)(4,1)S(1)}, s32[]{:S(2)}) async-start(s8[4718592]{0:T(1024)(128)(4,1)} %bitcast.377), calls=%async_computation.7 | async-start | bytes 8388608
  233.9 10.8 %slice-start.6 = ((s8[4718592]{0:T(1024)(128)(4,1)}), s8[4194304]{0:T(1024)(128)(4,1)S(1)}, s32[]{:S(2)}) async-start(s8[4718592]{0:T(1024)(128)(4,1)} %bitcast.388), calls=%async_computation.13 | async-start | bytes 8388608
  254.5 32.8 %all-to-all-start.1 = ((bf16[4,512,192]{1,2,0:T(8,128)(2,1)}), bf16[4,512,192]{1,2,0:T(8,128)(2,1)}, u32[]{:S(2)}, u32[]{:S(2)}) async-start(bf16[4,512,192]{1,2,0:T(8,128)(2,1)} %pad_maximum_fusion.5), calls=%async_computation.1 | async-start | bytes 1572864 | tf_op jit(solution)/shard_map/all_to_all | solution.py:390
  288.8 30.1 %copy-start.20 = (bf16[2048,192]{1,0:T(8,128)(2,1)S(1)}, bf16[2048,192]{1,0:T(8,128)(2,1)}, u32[]{:S(2)}) copy-start(bf16[2048,192]{1,0:T(8,128)(2,1)} %copy-done.19) | copy-start | bytes 2359300
  317.3 10.0 %collective-permute-start = (bf16[4096,384]{1,0:T(8,128)(2,1)}, bf16[4096,384]{1,0:T(8,128)(2,1)}, u32[]{:S(2)}, u32[]{:S(2)}) collective-permute-start(bf16[4096,384]{1,0:T(8,128)(2,1)} %get-tuple-element.77), channel_id=1, source_target_pairs={{0,4},{4,0},{8,12},{12,8},{16,20},{20,16},{24,28},{28,24},{1,5},{5... | collective-permute-start | bytes 9437192 | tf_op jit(solution)/shard_map/ppermute | solution.py:407
  320.1 15.3 %all-to-all-start = ((bf16[4,512,192]{1,2,0:T(8,128)(2,1)}), bf16[4,512,192]{1,2,0:T(8,128)(2,1)}, u32[]{:S(2)}, u32[]{:S(2)}) async-start(bf16[4,512,192]{1,2,0:T(8,128)(2,1)} %copy.141), calls=%async_computation | async-start | bytes 1572864 | tf_op jit(solution)/shard_map/all_to_all | solution.py:390
  324.5 68.1 %reduce-scatter.3.cloned.1.call-start = ((), (), s32[]{:S(2)}) async-start(), calls=%async_computation.5 | async-start | bytes 3932160 | tf_op jit(solution)/shard_map/reduce_scatter | solution.py:2073
  331.7 246.2 %reduce-scatter.5.cloned.1.call-start = ((), (), s32[]{:S(2)}) async-start(), calls=%async_computation.6 | async-start | bytes 3932160 | tf_op jit(solution)/shard_map/reduce_scatter | solution.py:2101
  336.8 14.1 %slice-start.2 = ((s8[4718592]{0:T(1024)(128)(4,1)}), s8[4194304]{0:T(1024)(128)(4,1)S(1)}, s32[]{:S(2)}) async-start(s8[4718592]{0:T(1024)(128)(4,1)} %bitcast.380), calls=%async_computation.9 | async-start | bytes 8388608
  339.7 19.7 %copy-start.33 = (f32[512,768]{1,0:T(8,128)}, f32[512,768]{1,0:T(8,128)S(1)}, u32[]{:S(2)}) copy-start(f32[512,768]{1,0:T(8,128)S(1)} %get-tuple-element.258) | copy-start | bytes 4718596
  340.7 10.2 %copy-start.36 = (bf16[2,512,768]{2,1,0:T(8,128)(2,1)S(1)}, bf16[2,512,768]{2,1,0:T(8,128)(2,1)}, u32[]{:S(2)}) copy-start(bf16[2,512,768]{2,1,0:T(8,128)(2,1)} %param.59) | copy-start | bytes 4718596
  340.7 10.2 %slice-start.3 = ((s8[4718592]{0:T(1024)(128)(4,1)}), s8[524288]{0:T(1024)(128)(4,1)S(1)}, s32[]{:S(2)}) async-start(s8[4718592]{0:T(1024)(128)(4,1)} %bitcast.380), calls=%async_computation.10 | async-start | bytes 1048576
  340.7 15.6 %slice-start.8 = ((s8[4718592]{0:T(1024)(128)(4,1)}), s8[4194304]{0:T(1024)(128)(4,1)S(1)}, s32[]{:S(2)}) async-start(s8[4718592]{0:T(1024)(128)(4,1)} %bitcast.391), calls=%async_computation.15 | async-start | bytes 8388608
  404.4 23.5 %all-to-all-start.2 = ((bf16[4,512,192]{1,2,0:T(8,128)(2,1)}), bf16[4,512,192]{1,2,0:T(8,128)(2,1)}, u32[]{:S(2)}, u32[]{:S(2)}) async-start(bf16[4,512,192]{1,2,0:T(8,128)(2,1)} %pad_maximum_fusion.6), calls=%async_computation.4 | async-start | bytes 1572864 | tf_op jit(solution)/shard_map/all_to_all | solution.py:390
  408.9 47.6 %collective-permute-start.1 = (bf16[4,4,96,768]{3,2,1,0:T(8,128)(2,1)}, bf16[4,4,96,768]{3,2,1,0:T(8,128)(2,1)}, u32[]{:S(2)}, u32[]{:S(2)}) collective-permute-start(bf16[4,4,96,768]{3,2,1,0:T(8,128)(2,1)} %bitcast.335), channel_id=1, source_target_pairs={{0,4},{4,0},{8,12},{12,8},{16,20},{20,16},{24,28},{28,24},{1,5},{5... | collective-permute-start | bytes 7077896 | tf_op jit(solution)/shard_map/ppermute | solution.py:407
  409.8 46.7 %collective-permute-start.2 = (bf16[4,4,96,768]{3,2,1,0:T(8,128)(2,1)}, bf16[4,4,96,768]{3,2,1,0:T(8,128)(2,1)}, u32[]{:S(2)}, u32[]{:S(2)}) collective-permute-start(bf16[4,4,96,768]{3,2,1,0:T(8,128)(2,1)} %bitcast.334), channel_id=1, source_target_pairs={{0,4},{4,0},{8,12},{12,8},{16,20},{20,16},{24,28},{28,24},{1,5},{5... | collective-permute-start | bytes 7077896 | tf_op jit(solution)/shard_map/ppermute | solution.py:407
  411.5 6.9 %slice-start.4 = ((s8[4718592]{0:T(1024)(128)(4,1)}), s8[4194304]{0:T(1024)(128)(4,1)S(1)}, s32[]{:S(2)}) async-start(s8[4718592]{0:T(1024)(128)(4,1)} %bitcast.383), calls=%async_computation.11 | async-start | bytes 8388608
  411.5 6.9 %copy-start.32 = (f32[512,768]{1,0:T(8,128)S(1)}, f32[512,768]{1,0:T(8,128)}, u32[]{:S(2)}) copy-start(f32[512,768]{1,0:T(8,128)} %copy-done.30) | copy-start | bytes 4718596
  411.5 6.9 %copy-start.42 = (bf16[512,3072]{1,0:T(8,128)(2,1)S(1)}, bf16[512,3072]{1,0:T(8,128)(2,1)}, u32[]{:S(2)}) copy-start(bf16[512,3072]{1,0:T(8,128)(2,1)} %get-tuple-element.238.refs_4_) | copy-start | bytes 9437188
  411.5 6.9 %slice-start.5 = ((s8[4718592]{0:T(1024)(128)(4,1)}), s8[524288]{0:T(1024)(128)(4,1)S(1)}, s32[]{:S(2)}) async-start(s8[4718592]{0:T(1024)(128)(4,1)} %bitcast.383), calls=%async_computation.12 | async-start | bytes 1048576
  411.5 45.0 %collective-permute-start.3 = (bf16[4,4,32,768]{3,2,1,0:T(8,128)(2,1)}, bf16[4,4,32,768]{3,2,1,0:T(8,128)(2,1)}, u32[]{:S(2)}, u32[]{:S(2)}) collective-permute-start(bf16[4,4,32,768]{3,2,1,0:T(8,128)(2,1)} %get-tuple-element.220), channel_id=1, source_target_pairs={{0,4},{4,0},{8,12},{12,8},{16,20},{20,16},{24,28},{28,24},{1,5},{5... | collective-permute-start | bytes 2359304 | tf_op jit(solution)/shard_map/ppermute | solution.py:407
  530.1 38.6 %copy-start.37 = (f32[1,512,768]{2,1,0:T(8,128)S(1)}, f32[1,512,768]{2,1,0:T(8,128)}, u32[]{:S(2)}) copy-start(f32[1,512,768]{2,1,0:T(8,128)} %slice_convert_fusion) | copy-start | bytes 4718596
  530.1 38.6 %copy-start.70 = (f32[768]{0:T(1024)S(1)}, f32[768]{0:T(1024)}, u32[]{:S(2)}) copy-start(f32[768]{0:T(1024)} %copy-done.69) | copy-start | bytes 9220
  530.1 39.4 %copy-start.54 = (bf16[2048,576]{1,0:T(8,128)(2,1)S(1)}, bf16[2048,576]{1,0:T(8,128)(2,1)}, u32[]{:S(2)}) copy-start(bf16[2048,576]{1,0:T(8,128)(2,1)} %copy-done.53) | copy-start | bytes 7077892
  (98 other events, 260.0 us)
Sparse Core Ops, SparseCore 0:
  331.8 60.6 reduce-scatter.2
  401.9 52.4 reduce-scatter.4

commit v7 on v6

--- a/solution.py
+++ b/solution.py
@@ -13,7 +13,7 @@
 LONG_BLK = 64
 SHORT_BLK = 8
 PAIR = 2 * BLOCK
-UNROLL = 4
+UNROLL = 8
 SEQ = "seq"
 TP = "tp"
 

time: 648 us -> 630 us (0.972)
  Pallas kernels: 408 us -> 387 us
    pallas_call x2, Pallas kernels: 54.1 us -> 45.6 us  [attend_backward(): pl.pallas_call(functools.partial(backward_kernel, slots, heads, len(piece...]
  transfers between devices with their start and end apart: 9 -> 9, of which waited for: 3 -> 3; matrix products, arithmetic and copies ran while one was open for 10% -> 11% of each run, Pallas kernels for 26% -> 26%
where the time goes in v7:
time: 630 us; the launch traced here: 623 us
  Pallas kernels  387 us (61%)
  matrix products  72.9 us (12%)
  local copies, waits for them, and re-layouts  66.1 us (10%)
  other arithmetic  45.3 us (7%)
  between operations  18.8 us (3%)
  starting transfers between devices  16.8 us (3%)
  waiting for transfers between devices  16.3 us (3%)
    dot_general x24, matrix products, contract(): return lax.dot_general(left, right, dims, preferred_element_type=f32)  72.9 us
    pallas_call x1, Pallas kernels, fourth_exchange(): pl.pallas_call(functools.partial(fourth_kernel, parts, cuts), out_shape=[...  68.1 us
    pallas_call x1, Pallas kernels, second_exchange(): pl.pallas_call(functools.partial(second_kernel, parts, rows), out_shape=[...  65.5 us
    pallas_call x1, Pallas kernels, third_exchange(): pl.pallas_call(functools.partial(third_kernel, parts, cuts, slots, heads)...  62 us
    pallas_call x2, Pallas kernels, attend_backward(): pl.pallas_call(functools.partial(backward_kernel, slots, heads, len(piece...  45.6 us
    pallas_call x1, Pallas kernels, first_exchange(): pl.pallas_call(functools.partial(first_kernel, parts), out_shape=[jax.Sha...  38.8 us
    pallas_call x1, Pallas kernels, sixth_exchange(): pl.pallas_call(functools.partial(sixth_kernel, parts), out_shape=[jax.Sha...  38.8 us
    pallas_call x1, Pallas kernels, fifth_exchange(): pl.pallas_call(fifth_kernel, out_shape=[jax.ShapeDtypeStruct(rows.shape[1...  38.4 us
  transfers between devices with their start and end apart: 9, of which 3 were waited for; matrix products, arithmetic and copies ran while one was open for 11% of the time, Pallas kernels for 26%

profile of v7, /device:TPU:13, one launch (start us, length us, event | category | flops | bytes accessed | tf_op | source)
XLA Modules:
  0.0 622.9 jit_solution(15623856505554395197)
XLA Ops:
  15.7 2.9 add_convert_fusion.7
  22.1 38.8 %shard_map.512 = (bf16[4,512,768]{2,1,0:T(8,128)(2,1)S(1)}, bf16[896,640]{1,0:T(8,128)(2,1)S(1)}, bf16[4,224,768]{2,1,0:T(8,128)(2,1)S(1)}, s32[4,8,128]{2,1,0:T(8,128)S(1)}) custom-call(bf16[512,768]{1,0:T(8,128)(2,1)S(1)} %get-tuple-element.214.own_ref, bf16[896,640]{1,0:T(8,128)(2,1)S(1)} %fusion.59.weight_ref, bf16[224,768]{1,0:T(8,128)(2,1)S(1)} %copy-done.15, ...), custom_call_target="tpu_custom_call" | custom-call | bytes 110700000 | tf_op jit(solution)/shard_map/pallas_call | solution.py:842
  67.1 3.1 fusion.102
  70.5 4.5 add_convert_fusion.2.joined_ref.query_ref.refs_2_
  76.8 65.5 %shard_map.513 = (bf16[4,1024,384]{2,1,0:T(8,128)(2,1)S(1)}, bf16[4,1024,384]{2,1,0:T(8,128)(2,1)}, bf16[4,512,768]{2,1,0:T(8,128)(2,1)}, bf16[2,4,4,96,768]{4,3,2,1,0:T(8,128)(2,1)}) custom-call(bf16[1024,384]{1,0:T(8,128)(2,1)S(1)} %pad_maximum_fusion.3.longs_ref, bf16[512,768]{1,0:T(8,128)(2,1)S(1)} %copy-done.10, ...), custom_call_target="tpu_custom_call" | custom-call | bytes 214020000 | tf_op jit(solution)/shard_map/pallas_call | solution.py:977
  142.2 5.6 add_convert_fusion.1.query_ref.refs_2_
  150.6 62.0 %shard_map.514 = (bf16[4,1024,384]{2,1,0:T(8,128)(2,1)}, bf16[4,1024,384]{2,1,0:T(8,128)(2,1)}, bf16[4,512,192]{2,1,0:T(8,128)(2,1)S(1)}, f32[2048,384]{1,0:T(8,...) custom-call(s32[768]{0:T(1024)S(1)} %and_add_fusion.1.index_ref, ...), custom_call_target="tpu_custom_call" | custom-call | bytes 228780000 | tf_op jit(solution)/shard_map/pallas_call | solution.py:1121
  225.6 4.8 fusion.112
  230.5 6.2 convert_reduce_fusion.1
  236.8 3.5 multiply_reduce_fusion.2
  246.6 4.4 all-to-all-start.1
  257.9 14.0 %shard_map.515 = (bf16[2048,192]{1,0:T(8,128)(2,1)S(1)}, f32[2048,384]{1,0:T(8,128)S(1)}) custom-call(s32[768]{0:T(1024)S(1)} %and_add_fusion.index_ref, s32[64]{0:T(128)S(1)} %reshape.598.valid_ref, bf16[2048,576]{1,0:T(8,128)(2,1)S(1)} %add_convert_fusion.1.query_ref.refs_2_, bf16[4096,384]{1,0:T(8,128)(2,1)S(1)} %bitcast.320, ...), custom_call_target="tpu_custom_call" | custom-call | bytes 66420000 | tf_op jit(solution)/shard_map/pallas_call | solution.py:277
  275.9 22.8 %shard_map.516 = (bf16[4096,384]{1,0:T(8,128)(2,1)}, bf16[4096,384]{1,0:T(8,128)(2,1)}, bf16[2048,576]{1,0:T(8,128)(2,1)S(1)}) custom-call(s32[768]{0:T(1024)S(1)} %and_add_fusion.1.index_ref, s32[64]{0:T(128)S(1)} %reshape.595.valid_ref, bf16[2048,576]{1,0:T(8,128)(2,1)} %copy-done.26, bf16[2048,192]{1,0:T(8,128)(2,1)S(1)} %bitcast.325, ...), custom_call_target="tpu_custom_call" | custom-call | bytes 92250000 | tf_op jit(solution)/shard_map/pallas_call | solution.py:301
  303.2 4.3 all-to-all-start
  310.4 4.3 add_convert_fusion
  315.5 3.0 all-to-all-done
  320.0 2.8 fusion.111
  323.9 10.2 %multiply_convert_fusion.1 = (bf16[512,3072]{1,0:T(8,128)(2,1)}, bf16[512,3072]{1,0:T(8,128)(2,1)}, f32[512,3072]{1,0:T(8,128)S(1)}) fusion(f32[512,3072]{1,0:T(8,128)} %copy-done.110, f32[3072]{0:T(1024)S(1)} %copy-done.79, bf16[512,768]{1,0:T(8,128)(2,1)S(1)} %add_convert_fusion.4.refs_3_, bf16[3072,768]{1,0:T(8,128)(2,1)} %bitcast.387), kind=kOutput, calls=%fused_computation.21 | convolution fusion | flops 2434793472 | bytes 24391680 | tf_op jit(solution)/shard_map/dot_general | solution.py:32
  334.1 5.3 convert_reduce_fusion
  339.4 3.0 multiply_reduce_fusion.1
  347.2 15.6 %shard_map.517 = (bf16[1536,768]{1,0:T(8,128)(2,1)S(1)}, bf16[1536,768]{1,0:T(8,128)(2,1)S(1)}, bf16[1536,768]{1,0:T(8,128)(2,1)S(1)}, bf16[1536,768]{1,0:T(8,128)(2,1)}, bf16[768,768]{1,0:T(8,128)(2,1)S(1)}) custom-call(s32[1]{0:T(128)} %bitcast.65.core_ref, bf16[512,3072]{1,0:T(8,128)(2,1)} %copy-done.41, bf16[512,3072]{1,0:T(8,128)(2,1)} %copy-done.44, ...), custom_call_target="tpu_custom_call" | custom-call | bytes 55350000 | tf_op jit(solution)/shard_map/pallas_call | solution.py:373
  368.1 7.7 %reduce-scatter.3.cloned.1.call-done = bf16[1024,384]{1,0:T(8,128)(2,1)} async-done(((bf16[4096,384]{1,0:T(8,128)(2,1)}), bf16[1024,384]{1,0:T(8,128)(2,1)}) %reduce-scatter.3.cloned.1.call-update) | async-done | bytes 786448 | tf_op jit(solution)/shard_map/reduce_scatter | solution.py:2073
  380.8 4.4 convolution_convert_fusion.1
  387.9 4.4 all-to-all-start.2
  396.2 5.6 fusion.49
  405.9 5.5 all-to-all-done.2
  412.9 22.8 %shard_map.518 = (bf16[4096,384]{1,0:T(8,128)(2,1)}, bf16[4096,384]{1,0:T(8,128)(2,1)}, bf16[2048,576]{1,0:T(8,128)(2,1)S(1)}) custom-call(s32[768]{0:T(1024)S(1)} %and_add_fusion.index_ref, s32[64]{0:T(128)S(1)} %reshape.598.valid_ref, bf16[2048,576]{1,0:T(8,128)(2,1)} %copy-done.2, bf16[2048,192]{1,0:T(8,128)(2,1)S(1)} %bitcast.326, ...), custom_call_target="tpu_custom_call" | custom-call | bytes 92250000 | tf_op jit(solution)/shard_map/pallas_call | solution.py:301
  435.7 68.1 %shard_map.519 = (bf16[1024,384]{1,0:T(8,128)(2,1)S(1)}, bf16[4,224,768]{2,1,0:T(8,128)(2,1)}) custom-call(bf16[4,1024,384]{2,1,0:T(8,128)(2,1)} %bitcast.347, bf16[4,1024,384]{2,1,0:T(8,128)(2,1)} %bitcast.348, bf16[4,4,96,768]{3,2,1,0:T(8,128)(2,1)} %bitcast.327, bf16[4,4,96,768]{3,2,1,0:T(8,128)(2,1)} %bitcast.359, ...), custom_call_target="tpu_custom_call" | custom-call | bytes 228780000 | tf_op jit(solution)/shard_map/pallas_call | solution.py:1411
  505.4 4.0 convolution_convert_fusion
  509.5 38.4 %shard_map.520 = (f32[2,256,768]{2,1,0:T(8,128)S(1)}, bf16[224,768]{1,0:T(8,128)(2,1)S(1)}) custom-call(bf16[4,2,256,768]{3,2,1,0:T(8,128)(2,1)} %bitcast.346, bf16[4,224,768]{2,1,0:T(8,128)(2,1)S(1)} %copy-done.16), custom_call_target="tpu_custom_call" | custom-call | bytes 110700000 | tf_op jit(solution)/shard_map/pallas_call | solution.py:1477
  559.3 38.8 %shard_map.521 = (bf16[768,640]{1,0:T(8,128)(2,1)S(1)}, bf16[4,2,224,768]{3,2,1,0:T(8,128)(2,1)S(1)}, f32[8,768]{1,0:T(8,128)S(1)}) custom-call(bf16[768,640]{1,0:T(8,128)(2,1)S(1)} %pad.48.terms_ref, bf16[224,768]{1,0:T(8,128)(2,1)S(1)} %get-tuple-element.95.own_ref, f32[8,768]{1,0:T(8,128)S(1)} %pad_maximum_fusion.8.rows_ref), custom_call_target="tpu_custom_call" | custom-call | bytes 129150000 | tf_op jit(solution)/shard_map/pallas_call | solution.py:1738
  607.4 3.2 copy.151
  (443 shorter events, 114.5 us)
Async XLA Ops:
  61.0 15.5 %copy-start.6 = (bf16[4,224,768]{2,1,0:T(8,128)(2,1)}, bf16[4,224,768]{2,1,0:T(8,128)(2,1)S(1)}, u32[]{:S(2)}) copy-start(bf16[4,224,768]{2,1,0:T(8,128)(2,1)S(1)} %get-tuple-element.61.column_ref) | copy-start | bytes 4128772
  61.1 13.9 %copy-start.62 = (bf16[768,192]{1,0:T(8,128)(2,1)}, bf16[768,192]{1,0:T(8,128)(2,1)S(1)}, u32[]{:S(2)}) copy-start(bf16[768,192]{1,0:T(8,128)(2,1)S(1)} %slice_multiply_fusion) | copy-start | bytes 884740
  61.2 81.0 %copy-start.59 = (bf16[768,384]{1,0:T(8,128)(2,1)}, bf16[768,384]{1,0:T(8,128)(2,1)S(1)}, u32[]{:S(2)}) copy-start(bf16[768,384]{1,0:T(8,128)(2,1)S(1)} %slice.222) | copy-start | bytes 1769476
  70.5 77.5 %copy-start.83 = (pred[4]{0:T(512)(128)(4,1)}, pred[4]{0:T(512)(128)(4,1)S(1)}, u32[]{:S(2)}) copy-start(pred[4]{0:T(512)(128)(4,1)S(1)} %get-tuple-element.246) | copy-start | bytes 16
  70.5 77.5 %copy-start.89 = (pred[4]{0:T(512)(128)(4,1)}, pred[4]{0:T(512)(128)(4,1)S(1)}, u32[]{:S(2)}) copy-start(pred[4]{0:T(512)(128)(4,1)S(1)} %get-tuple-element.249) | copy-start | bytes 16
  76.5 65.8 %copy-start.63 = (bf16[768,192]{1,0:T(8,128)(2,1)S(1)}, bf16[768,192]{1,0:T(8,128)(2,1)}, u32[]{:S(2)}) copy-start(bf16[768,192]{1,0:T(8,128)(2,1)} %copy-done.62) | copy-start | bytes 884740
  147.9 106.2 %copy-start.2 = (bf16[2048,576]{1,0:T(8,128)(2,1)}, bf16[2048,576]{1,0:T(8,128)(2,1)S(1)}, u32[]{:S(2)}) copy-start(bf16[2048,576]{1,0:T(8,128)(2,1)S(1)} %add_convert_fusion.1.query_ref.refs_2_) | copy-start | bytes 7077892
  223.7 6.8 %copy-start.78 = (f32[3072]{0:T(1024)}, f32[3072]{0:T(1024)S(1)}, u32[]{:S(2)}) copy-start(f32[3072]{0:T(1024)S(1)} %reshape.596) | copy-start | bytes 36868
  223.7 6.8 %slice-start = ((s8[4718592]{0:T(1024)(128)(4,1)}), s8[4194304]{0:T(1024)(128)(4,1)S(1)}, s32[]{:S(2)}) async-start(s8[4718592]{0:T(1024)(128)(4,1)} %bitcast.377), calls=%async_computation.7 | async-start | bytes 8388608
  225.6 11.2 %slice-start.6 = ((s8[4718592]{0:T(1024)(128)(4,1)}), s8[4194304]{0:T(1024)(128)(4,1)S(1)}, s32[]{:S(2)}) async-start(s8[4718592]{0:T(1024)(128)(4,1)} %bitcast.388), calls=%async_computation.13 | async-start | bytes 8388608
  246.6 27.9 %all-to-all-start.1 = ((bf16[4,512,192]{1,2,0:T(8,128)(2,1)}), bf16[4,512,192]{1,2,0:T(8,128)(2,1)}, u32[]{:S(2)}, u32[]{:S(2)}) async-start(bf16[4,512,192]{1,2,0:T(8,128)(2,1)} %pad_maximum_fusion.5), calls=%async_computation.1 | async-start | bytes 1572864 | tf_op jit(solution)/shard_map/all_to_all | solution.py:390
  275.9 26.1 %copy-start.20 = (bf16[2048,192]{1,0:T(8,128)(2,1)S(1)}, bf16[2048,192]{1,0:T(8,128)(2,1)}, u32[]{:S(2)}) copy-start(bf16[2048,192]{1,0:T(8,128)(2,1)} %copy-done.19) | copy-start | bytes 2359300
  300.2 10.3 %collective-permute-start = (bf16[4096,384]{1,0:T(8,128)(2,1)}, bf16[4096,384]{1,0:T(8,128)(2,1)}, u32[]{:S(2)}, u32[]{:S(2)}) collective-permute-start(bf16[4096,384]{1,0:T(8,128)(2,1)} %get-tuple-element.77), channel_id=1, source_target_pairs={{0,4},{4,0},{8,12},{12,8},{16,20},{20,16},{24,28},{28,24},{1,5},{5... | collective-permute-start | bytes 9437192 | tf_op jit(solution)/shard_map/ppermute | solution.py:407
  303.2 15.3 %all-to-all-start = ((bf16[4,512,192]{1,2,0:T(8,128)(2,1)}), bf16[4,512,192]{1,2,0:T(8,128)(2,1)}, u32[]{:S(2)}, u32[]{:S(2)}) async-start(bf16[4,512,192]{1,2,0:T(8,128)(2,1)} %copy.141), calls=%async_computation | async-start | bytes 1572864 | tf_op jit(solution)/shard_map/all_to_all | solution.py:390
  307.6 68.2 %reduce-scatter.3.cloned.1.call-start = ((), (), s32[]{:S(2)}) async-start(), calls=%async_computation.5 | async-start | bytes 3932160 | tf_op jit(solution)/shard_map/reduce_scatter | solution.py:2073
  314.8 242.2 %reduce-scatter.5.cloned.1.call-start = ((), (), s32[]{:S(2)}) async-start(), calls=%async_computation.6 | async-start | bytes 3932160 | tf_op jit(solution)/shard_map/reduce_scatter | solution.py:2101
  320.0 14.1 %slice-start.2 = ((s8[4718592]{0:T(1024)(128)(4,1)}), s8[4194304]{0:T(1024)(128)(4,1)S(1)}, s32[]{:S(2)}) async-start(s8[4718592]{0:T(1024)(128)(4,1)} %bitcast.380), calls=%async_computation.9 | async-start | bytes 8388608
  322.8 19.7 %copy-start.33 = (f32[512,768]{1,0:T(8,128)}, f32[512,768]{1,0:T(8,128)S(1)}, u32[]{:S(2)}) copy-start(f32[512,768]{1,0:T(8,128)S(1)} %get-tuple-element.258) | copy-start | bytes 4718596
  323.9 10.2 %copy-start.36 = (bf16[2,512,768]{2,1,0:T(8,128)(2,1)S(1)}, bf16[2,512,768]{2,1,0:T(8,128)(2,1)}, u32[]{:S(2)}) copy-start(bf16[2,512,768]{2,1,0:T(8,128)(2,1)} %param.59) | copy-start | bytes 4718596
  323.9 10.2 %slice-start.3 = ((s8[4718592]{0:T(1024)(128)(4,1)}), s8[524288]{0:T(1024)(128)(4,1)S(1)}, s32[]{:S(2)}) async-start(s8[4718592]{0:T(1024)(128)(4,1)} %bitcast.380), calls=%async_computation.10 | async-start | bytes 1048576
  323.9 15.5 %slice-start.8 = ((s8[4718592]{0:T(1024)(128)(4,1)}), s8[4194304]{0:T(1024)(128)(4,1)S(1)}, s32[]{:S(2)}) async-start(s8[4718592]{0:T(1024)(128)(4,1)} %bitcast.391), calls=%async_computation.15 | async-start | bytes 8388608
  387.9 23.5 %all-to-all-start.2 = ((bf16[4,512,192]{1,2,0:T(8,128)(2,1)}), bf16[4,512,192]{1,2,0:T(8,128)(2,1)}, u32[]{:S(2)}, u32[]{:S(2)}) async-start(bf16[4,512,192]{1,2,0:T(8,128)(2,1)} %pad_maximum_fusion.6), calls=%async_computation.4 | async-start | bytes 1572864 | tf_op jit(solution)/shard_map/all_to_all | solution.py:390
  392.4 43.3 %collective-permute-start.1 = (bf16[4,4,96,768]{3,2,1,0:T(8,128)(2,1)}, bf16[4,4,96,768]{3,2,1,0:T(8,128)(2,1)}, u32[]{:S(2)}, u32[]{:S(2)}) collective-permute-start(bf16[4,4,96,768]{3,2,1,0:T(8,128)(2,1)} %bitcast.335), channel_id=1, source_target_pairs={{0,4},{4,0},{8,12},{12,8},{16,20},{20,16},{24,28},{28,24},{1,5},{5... | collective-permute-start | bytes 7077896 | tf_op jit(solution)/shard_map/ppermute | solution.py:407
  393.3 42.4 %collective-permute-start.2 = (bf16[4,4,96,768]{3,2,1,0:T(8,128)(2,1)}, bf16[4,4,96,768]{3,2,1,0:T(8,128)(2,1)}, u32[]{:S(2)}, u32[]{:S(2)}) collective-permute-start(bf16[4,4,96,768]{3,2,1,0:T(8,128)(2,1)} %bitcast.334), channel_id=1, source_target_pairs={{0,4},{4,0},{8,12},{12,8},{16,20},{20,16},{24,28},{28,24},{1,5},{5... | collective-permute-start | bytes 7077896 | tf_op jit(solution)/shard_map/ppermute | solution.py:407
  395.0 6.9 %slice-start.4 = ((s8[4718592]{0:T(1024)(128)(4,1)}), s8[4194304]{0:T(1024)(128)(4,1)S(1)}, s32[]{:S(2)}) async-start(s8[4718592]{0:T(1024)(128)(4,1)} %bitcast.383), calls=%async_computation.11 | async-start | bytes 8388608
  395.0 6.9 %copy-start.32 = (f32[512,768]{1,0:T(8,128)S(1)}, f32[512,768]{1,0:T(8,128)}, u32[]{:S(2)}) copy-start(f32[512,768]{1,0:T(8,128)} %copy-done.30) | copy-start | bytes 4718596
  395.0 6.9 %copy-start.42 = (bf16[512,3072]{1,0:T(8,128)(2,1)S(1)}, bf16[512,3072]{1,0:T(8,128)(2,1)}, u32[]{:S(2)}) copy-start(bf16[512,3072]{1,0:T(8,128)(2,1)} %get-tuple-element.238.refs_4_) | copy-start | bytes 9437188
  395.0 6.9 %slice-start.5 = ((s8[4718592]{0:T(1024)(128)(4,1)}), s8[524288]{0:T(1024)(128)(4,1)S(1)}, s32[]{:S(2)}) async-start(s8[4718592]{0:T(1024)(128)(4,1)} %bitcast.383), calls=%async_computation.12 | async-start | bytes 1048576
  395.0 40.7 %collective-permute-start.3 = (bf16[4,4,32,768]{3,2,1,0:T(8,128)(2,1)}, bf16[4,4,32,768]{3,2,1,0:T(8,128)(2,1)}, u32[]{:S(2)}, u32[]{:S(2)}) collective-permute-start(bf16[4,4,32,768]{3,2,1,0:T(8,128)(2,1)} %get-tuple-element.220), channel_id=1, source_target_pairs={{0,4},{4,0},{8,12},{12,8},{16,20},{20,16},{24,28},{28,24},{1,5},{5... | collective-permute-start | bytes 2359304 | tf_op jit(solution)/shard_map/ppermute | solution.py:407
  509.5 38.4 %copy-start.37 = (f32[1,512,768]{2,1,0:T(8,128)S(1)}, f32[1,512,768]{2,1,0:T(8,128)}, u32[]{:S(2)}) copy-start(f32[1,512,768]{2,1,0:T(8,128)} %slice_convert_fusion) | copy-start | bytes 4718596
  509.5 38.4 %copy-start.70 = (f32[768]{0:T(1024)S(1)}, f32[768]{0:T(1024)}, u32[]{:S(2)}) copy-start(f32[768]{0:T(1024)} %copy-done.69) | copy-start | bytes 9220
  509.5 39.2 %copy-start.54 = (bf16[2048,576]{1,0:T(8,128)(2,1)S(1)}, bf16[2048,576]{1,0:T(8,128)(2,1)}, u32[]{:S(2)}) copy-start(bf16[2048,576]{1,0:T(8,128)(2,1)} %copy-done.53) | copy-start | bytes 7077892
  (98 other events, 261.3 us)
Sparse Core Ops, SparseCore 0:
  314.9 60.8 reduce-scatter.2
  385.3 52.4 reduce-scatter.4
